TPU v7x, 32 devices: a whole 2x2x4 slice. The times are simulated.
32 devices in a mesh: half: 2 (over core), wide: 8 (over z, x), narrow: 2 (over y).
Axes of the slice: x: 2, y: 2, z: 4, core: 2. Of those that a mesh axis runs over, the one named last changes fastest.
Arguments:
- stream: bfloat16 [2, 16, 1024, 512], P('half', ('wide', 'narrow')), may hold values from -6 to 6
- cotangent: bfloat16 [16, 1024, 512], P(('wide', 'narrow')), may hold values from -6 to 6
- lengths: int32 [2, 16], P(None, ('wide', 'narrow')), may hold values from 256 to 1024, as said below
- owners: int32 [2, 56], P('half'), may hold values from 0 to 7, as said below
- master: float32 [2, 112, 128, 512], P('half', 'wide', 'narrow'), as said below
- moment_one: float32 [2, 112, 128, 512], P('half', 'wide', 'narrow'), may hold values from -384 to 384
- moment_two: float32 [2, 112, 128, 512], P('half', 'wide', 'narrow'), may hold values from 4096 to 16384
- vec_master: float32 [15, 512], replicated
- vec_one: float32 [15, 512], replicated, may hold values from -384 to 384
- vec_two: float32 [15, 512], replicated, may hold values from 4096 to 16384
Outputs:
- out_stream: bfloat16 [2, 16, 1024, 512], P('half', ('wide', 'narrow'))
- grad_stream: float32 [2, 16, 1024, 512], P('half', ('wide', 'narrow'))
- new_moment_one: float32 [2, 112, 128, 512], P('half', 'wide', 'narrow')
- new_moment_two: float32 [2, 112, 128, 512], P('half', 'wide', 'narrow')
- new_master: float32 [2, 112, 128, 512], P('half', 'wide', 'narrow')
- new_copy: bfloat16 [2, 112, 128, 512], P('half', 'wide', 'narrow')
- new_vec_one: float32 [15, 512], replicated
- new_vec_two: float32 [15, 512], replicated
- new_vec_master: float32 [15, 512], replicated
Inputs may be any that keep to these rules, and one draw needn't show every extreme that they name: `lengths`: positions at or past a document's length are padding. In each row some document has exactly 1024. `owners`: no index holds more than 14 pieces of a row; in each row one index holds exactly 14. `master`: slots that no piece maps to hold values that reach only their own update.
All inputs are finite; a program needn't handle non-finite values.
Results may differ from a plain program's by a relative error of at most 0.025.
The roundings to bfloat16 on the way count: a program that leaves them out, or rounds other values in their place, can miss the bound.
Values may be sent and summed in bfloat16 or wider, within the bound.
No kernel may reach another device: no remote copies, remote signals or barrier semaphores. Data moves between devices by JAX's collectives and lax.ppermute only.
A program may use at most 384 MiB of HBM per device.

v0:
```python
import math

import jax
import jax.numpy as jnp
from jax import lax
from jax.sharding import PartitionSpec as P

HEADS = 8
BLOCK = 512
STEP = 5


eps_norm = 1e-05
beta_one = 0.5
beta_two = 0.5
rate_matrix = 0.05
rate_vector = 0.3
decay_matrix = 0.01
eps_adam = 1e-08
bfloat = jnp.bfloat16
single = jnp.float32


def shifted(block, axis, distance):
    devices = range(lax.axis_size(axis))
    route = [(i - distance, i) for i in devices if i - distance in devices]
    return lax.ppermute(block, axis, route)


def dense(left, right):
    return jnp.dot(left, right, preferred_element_type=single)


def dense_tn(left, right):
    return lax.dot_general(left, right, (((0,), (0,)), ((), ())), preferred_element_type=single)


def dense_nt(left, right):
    return lax.dot_general(left, right, (((1,), (1,)), ((), ())), preferred_element_type=single)


def layer_norm(resid, gain, shift):
    center = resid - jnp.mean(resid, -1, keepdims=True)
    spread = jnp.mean(center * center, -1, keepdims=True)
    return center * lax.rsqrt(spread + eps_norm) * gain + shift


def resid_norm(inner, weigh, branch, gain, shift):
    return layer_norm(inner * weigh + branch, gain, shift)


def smooth(pre_act):
    return jax.nn.gelu(pre_act, approximate=False)


def norm_back(inner, weigh, branch, gain, shift, grad_out):
    unused, backward = jax.vjp(resid_norm, inner, weigh, branch, gain, shift)
    return backward(grad_out)


def block_scores(query_block, key_heads, rows, limit, causal):
    raw_scores = jnp.einsum(
        "qhe,khe->hqk", query_block, key_heads, preferred_element_type=single
    ) / math.sqrt(key_heads.shape[-1])
    columns = jnp.arange(key_heads.shape[0])
    allowed = columns[None, :] < limit
    if causal:
        allowed = allowed & (columns[None, :] <= rows[:, None])
    return jnp.where(allowed[None], raw_scores, -1e30)


def attend_doc(queries, key_rows, value_rows, limit, causal):
    length, model_width = queries.shape
    key_heads = key_rows.reshape(key_rows.shape[0], HEADS, -1)
    value_heads = value_rows.reshape(value_rows.shape[0], HEADS, -1)

    def one_block(position):
        offset = position * BLOCK
        query_block = lax.dynamic_slice_in_dim(queries, offset, BLOCK, 0).reshape(BLOCK, HEADS, -1)
        scores = block_scores(query_block, key_heads, offset + jnp.arange(BLOCK), limit, causal)
        highest = jnp.max(scores, -1, keepdims=True)
        totals = highest + jnp.log(jnp.sum(jnp.exp(scores - highest), -1, keepdims=True))
        weights = jnp.exp(scores - totals).astype(bfloat)
        context = jnp.einsum("hqk,khe->qhe", weights, value_heads, preferred_element_type=single)
        return (context.reshape(BLOCK, model_width).astype(bfloat), totals[..., 0])

    context, totals = lax.map(one_block, jnp.arange(length // BLOCK))
    return (context.reshape(length, model_width), totals)


def attend_back(queries, key_rows, value_rows, totals, grad_context, limit, causal):
    length, model_width = queries.shape
    key_count = key_rows.shape[0]
    key_heads = key_rows.reshape(key_count, HEADS, -1)
    value_heads = value_rows.reshape(key_count, HEADS, -1)
    root = math.sqrt(key_heads.shape[-1])

    def one_block(carry, position):
        grad_keys, grad_values = carry
        offset = position * BLOCK
        query_block = lax.dynamic_slice_in_dim(queries, offset, BLOCK, 0).reshape(BLOCK, HEADS, -1)
        grad_block = lax.dynamic_slice_in_dim(grad_context, offset, BLOCK, 0).reshape(
            BLOCK, HEADS, -1
        )
        scores = block_scores(query_block, key_heads, offset + jnp.arange(BLOCK), limit, causal)
        weights = jnp.exp(scores - totals[position][..., None])
        grad_weights = jnp.einsum(
            "qhe,khe->hqk", grad_block, value_heads, preferred_element_type=single
        )
        grad_values = grad_values + jnp.einsum(
            "hqk,qhe->khe", weights.astype(bfloat), grad_block, preferred_element_type=single
        )
        grad_scores = (
            weights * (grad_weights - jnp.sum(weights * grad_weights, -1, keepdims=True))
        ).astype(bfloat)
        grad_query = (
            jnp.einsum("hqk,khe->qhe", grad_scores, key_heads, preferred_element_type=single) / root
        )
        grad_keys = (
            grad_keys
            + jnp.einsum("hqk,qhe->khe", grad_scores, query_block, preferred_element_type=single)
            / root
        )
        return ((grad_keys, grad_values), grad_query.reshape(BLOCK, model_width))

    zeroes = jnp.zeros((key_count, HEADS, model_width // HEADS), single)
    (grad_keys, grad_values), grad_queries = lax.scan(
        one_block, (zeroes, zeroes), jnp.arange(length // BLOCK)
    )
    return (
        grad_queries.reshape(length, model_width),
        grad_keys.reshape(key_count, model_width),
        grad_values.reshape(key_count, model_width),
    )


def attend_all(queries, key_rows, value_rows, limits, causal):

    def attend_one_doc(member):
        return attend_doc(member[0], member[1], member[2], member[3], causal)

    return lax.map(attend_one_doc, (queries, key_rows, value_rows, limits))


def back_all(queries, key_rows, value_rows, totals, grad_context, limits, causal):

    def back_one_doc(member):
        return attend_back(member[0], member[1], member[2], member[3], member[4], member[5], causal)

    return lax.map(back_one_doc, (queries, key_rows, value_rows, totals, grad_context, limits))


def self_forward(flat, parts, vector, first, limits, causal):
    docs = limits.shape[0]
    model_width = flat.shape[1]
    queries = dense(flat, parts[0]).astype(bfloat)
    key_rows = dense(flat, parts[1]).astype(bfloat)
    value_rows = dense(flat, parts[2]).astype(bfloat)
    context, totals = attend_all(
        queries.reshape(docs, -1, model_width),
        key_rows.reshape(docs, -1, model_width),
        value_rows.reshape(docs, -1, model_width),
        limits,
        causal,
    )
    context = context.reshape(-1, model_width)
    branch = dense(context, parts[3])
    inner = resid_norm(
        flat.astype(single), vector[first], branch, vector[first + 1], vector[first + 2]
    )
    return ((queries, key_rows, value_rows, context, totals, branch), inner)


def self_back(flat, parts, vector, first, saved_attn, limits, causal, grad_out):
    queries, key_rows, value_rows, context, totals, branch = saved_attn
    docs = limits.shape[0]
    model_width = flat.shape[1]
    grad_flat, grad_weigh, grad_branch, grad_gain, grad_shift = norm_back(
        flat.astype(single), vector[first], branch, vector[first + 1], vector[first + 2], grad_out
    )
    grad_low = grad_branch.astype(bfloat)
    grad_proj = dense_tn(context, grad_low)
    grad_context = dense_nt(grad_low, parts[3]).astype(bfloat)

    def per_doc(array):
        return array.reshape(docs, -1, model_width)

    grad_query, grad_key, grad_value = back_all(
        per_doc(queries),
        per_doc(key_rows),
        per_doc(value_rows),
        totals,
        per_doc(grad_context),
        limits,
        causal,
    )
    grad_query = grad_query.reshape(-1, model_width).astype(bfloat)
    grad_key = grad_key.reshape(-1, model_width).astype(bfloat)
    grad_value = grad_value.reshape(-1, model_width).astype(bfloat)
    weight_grads = [
        dense_tn(flat, grad_query),
        dense_tn(flat, grad_key),
        dense_tn(flat, grad_value),
        grad_proj,
    ]
    grad_flat = (
        grad_flat
        + dense_nt(grad_query, parts[0])
        + dense_nt(grad_key, parts[1])
        + dense_nt(grad_value, parts[2])
    )
    return (grad_flat, weight_grads, [grad_weigh, grad_gain, grad_shift])


def feed_forward(inner, parts, vector, first):
    inner_low = inner.astype(bfloat)
    pre_act = dense_nt(inner_low, parts[6])
    ff_out = dense(smooth(pre_act).astype(bfloat), parts[7])
    return (
        pre_act,
        ff_out,
        resid_norm(inner, vector[first], ff_out, vector[first + 1], vector[first + 2]),
    )


def feed_back(inner, pre_act, ff_out, parts, vector, first, grad_out):
    grad_inner, grad_weigh, grad_branch, grad_gain, grad_shift = norm_back(
        inner, vector[first], ff_out, vector[first + 1], vector[first + 2], grad_out
    )
    grad_ff = grad_branch.astype(bfloat)
    activ = smooth(pre_act).astype(bfloat)
    grad_down = dense_tn(activ, grad_ff)
    grad_activ = dense_nt(grad_ff, parts[7])
    unused, smooth_back = jax.vjp(smooth, pre_act)
    grad_pre = smooth_back(grad_activ)[0].astype(bfloat)
    grad_up = dense_tn(grad_pre, inner.astype(bfloat))
    grad_inner = grad_inner + dense(grad_pre, parts[6])
    return (grad_inner, grad_up, grad_down, [grad_weigh, grad_gain, grad_shift])


def encoder_forward(source, parts, vector, limits):
    docs, length, model_width = source.shape
    flat = source.reshape(-1, model_width)
    saved_attn, inner = self_forward(flat, parts, vector, 0, limits, False)
    pre_act, ff_out, result = feed_forward(inner, parts, vector, 3)
    memory = result.astype(bfloat)
    sendout = dense(memory, jnp.concatenate([parts[4], parts[5]], 1)).astype(bfloat)
    return saved_attn + (
        inner,
        pre_act,
        ff_out,
        memory,
        sendout.reshape(docs, length, 2 * model_width),
    )


def encoder_zeros(docs, length, model_width, hidden):
    flat_rows = docs * length
    return (
        jnp.zeros((flat_rows, model_width), bfloat),
        jnp.zeros((flat_rows, model_width), bfloat),
        jnp.zeros((flat_rows, model_width), bfloat),
        jnp.zeros((flat_rows, model_width), bfloat),
        jnp.zeros((docs, length // BLOCK, HEADS, BLOCK), single),
        jnp.zeros((flat_rows, model_width), single),
        jnp.zeros((flat_rows, model_width), single),
        jnp.zeros((flat_rows, hidden), single),
        jnp.zeros((flat_rows, model_width), single),
        jnp.zeros((flat_rows, model_width), bfloat),
        jnp.zeros((docs, length, 2 * model_width), bfloat),
    )


def decoder_zeros(docs, length, model_width, hidden):
    return (
        jnp.zeros((docs, length, model_width), bfloat),
        jnp.zeros((docs, length, model_width), single),
        jnp.zeros((6 * model_width + 2 * hidden, model_width), single),
        jnp.zeros((15, model_width), single),
        jnp.zeros((docs, length, 2 * model_width), bfloat),
    )


def encoder_back(source, saved, received, parts, vector, limits):
    docs, length, model_width = source.shape
    flat = source.reshape(-1, model_width)
    inner, pre_act, ff_out, memory = (saved[6], saved[7], saved[8], saved[9])
    grad_keys = received[..., :model_width].reshape(-1, model_width)
    grad_values = received[..., model_width:].reshape(-1, model_width)
    grad_mem_keys = dense_tn(memory, grad_keys)
    grad_mem_values = dense_tn(memory, grad_values)
    grad_memory = dense_nt(grad_keys, parts[4]) + dense_nt(grad_values, parts[5])
    grad_inner, grad_up, grad_down, ff_vec = feed_back(
        inner, pre_act, ff_out, parts, vector, 3, grad_memory
    )
    grad_flat, self_grads, self_vec = self_back(
        flat, parts, vector, 0, saved[:6], limits, False, grad_inner
    )
    weight_grads = jnp.concatenate(
        self_grads + [grad_mem_keys, grad_mem_values, grad_up, grad_down], 0
    )
    vec_grads = jnp.concatenate(
        [jnp.stack(self_vec + ff_vec), jnp.zeros((9, model_width), single)], 0
    )
    return (
        memory.reshape(docs, length, model_width),
        grad_flat.reshape(docs, length, model_width),
        weight_grads,
        vec_grads,
    )


def decoder_step(target, cotan, received, parts, vector, target_len, source_len):
    docs, length, model_width = target.shape
    flat = target.reshape(-1, model_width)
    saved_attn, inner_one = self_forward(flat, parts, vector, 6, target_len, True)
    one_low = inner_one.astype(bfloat)
    cross_query = dense(one_low, parts[4]).astype(bfloat).reshape(docs, length, model_width)
    mem_keys = received[..., :model_width]
    mem_values = received[..., model_width:]
    cross_ctx, cross_totals = attend_all(cross_query, mem_keys, mem_values, source_len, False)
    cross_ctx = cross_ctx.reshape(-1, model_width)
    cross_branch = dense(cross_ctx, parts[5])
    inner_two = resid_norm(inner_one, vector[9], cross_branch, vector[10], vector[11])
    pre_act, ff_out, output = feed_forward(inner_two, parts, vector, 12)
    valid = (jnp.arange(length)[None, :] < target_len[:, None]).astype(single)
    grad_out = (cotan.astype(single) * valid[..., None]).reshape(-1, model_width)
    grad_two, grad_up, grad_down, ff_vec = feed_back(
        inner_two, pre_act, ff_out, parts, vector, 12, grad_out
    )
    grad_one, grad_cross_weigh, grad_cross_branch, grad_cross_gain, grad_cross_shift = norm_back(
        inner_one, vector[9], cross_branch, vector[10], vector[11], grad_two
    )
    cross_low = grad_cross_branch.astype(bfloat)
    grad_cross_out = dense_tn(cross_ctx, cross_low)
    grad_cross_ctx = dense_nt(cross_low, parts[5]).astype(bfloat).reshape(docs, length, model_width)
    grad_cross_query, grad_mem_keys, grad_mem_values = back_all(
        cross_query, mem_keys, mem_values, cross_totals, grad_cross_ctx, source_len, False
    )
    grad_cross_query = grad_cross_query.reshape(-1, model_width).astype(bfloat)
    grad_cross_in = dense_tn(one_low, grad_cross_query)
    grad_one = grad_one + dense_nt(grad_cross_query, parts[4])
    sendback = jnp.concatenate([grad_mem_keys, grad_mem_values], 2).astype(bfloat)
    grad_flat, self_grads, self_vec = self_back(
        flat, parts, vector, 6, saved_attn, target_len, True, grad_one
    )
    weight_grads = jnp.concatenate(
        self_grads + [grad_cross_in, grad_cross_out, grad_up, grad_down], 0
    )
    vec_grads = jnp.concatenate(
        [
            jnp.zeros((6, model_width), single),
            jnp.stack(self_vec + [grad_cross_weigh, grad_cross_gain, grad_cross_shift] + ff_vec),
        ],
        0,
    )
    return (
        output.astype(bfloat).reshape(docs, length, model_width),
        grad_flat.reshape(docs, length, model_width),
        weight_grads,
        vec_grads,
        sendback,
    )


def adam(weight, gradient, first, second, step_rate, decay_rate):
    first_new = beta_one * first + (1.0 - beta_one) * gradient
    second_new = beta_two * second + (1.0 - beta_two) * gradient * gradient
    first_hat = first_new / (1.0 - beta_one**STEP)
    second_hat = second_new / (1.0 - beta_two**STEP)
    weight_new = weight - step_rate * (
        first_hat / (jnp.sqrt(second_hat) + eps_adam) + decay_rate * weight
    )
    return (weight_new, first_new, second_new)


def on_device(
    stream, cotangent, lengths, owners, master, moment_one, moment_two, vec_master, vec_one, vec_two
):
    narrow_size = lax.axis_size("narrow")
    owner_row = owners[0]
    capacity = master.shape[1]
    half_rows = master.shape[2]
    model_width = master.shape[3]
    piece_rows = half_rows * narrow_size
    count = owner_row.shape[0]
    slot_count = capacity * lax.axis_size("wide")
    counter = jnp.arange(count)
    same = owner_row[:, None] == owner_row[None, :]
    earlier = counter[None, :] < counter[:, None]
    ranks = jnp.sum((same & earlier).astype(jnp.int32), 1)
    slot_of = owner_row * capacity + ranks
    hit = slot_of[None, :] == jnp.arange(slot_count)[:, None]
    slot_piece = jnp.sum(hit.astype(jnp.int32) * counter[None, :], 1)
    slot_used = jnp.any(hit, 1).astype(single)
    gathered = lax.all_gather(master[0].astype(bfloat), ("wide", "narrow"), axis=0, tiled=True)
    fetch = (
        owner_row[:, None] * narrow_size + jnp.arange(narrow_size)[None, :]
    ) * capacity + ranks[:, None]
    weight = jnp.take(gathered, fetch.reshape(-1), axis=0).reshape(-1, model_width)
    hidden = (weight.shape[0] - 6 * model_width) // 2
    parts = [weight[number * model_width : (number + 1) * model_width] for number in range(6)]
    parts = parts + [
        weight[6 * model_width : 6 * model_width + hidden],
        weight[6 * model_width + hidden :],
    ]
    is_source = lax.axis_index("half") == 0
    local_docs = stream[0]
    docs, length = (local_docs.shape[0], local_docs.shape[1])
    source_len = lengths[0]
    target_len = lengths[1]

    def run_encoder():
        return encoder_forward(local_docs, parts, vec_master, source_len)

    saved = lax.cond(
        is_source, run_encoder, lambda: encoder_zeros(docs, length, model_width, hidden)
    )
    received = shifted(saved[10], "half", 1)

    def run_decoder():
        return decoder_step(
            local_docs, cotangent, received, parts, vec_master, target_len, source_len
        )

    decoded = lax.cond(
        is_source, lambda: decoder_zeros(docs, length, model_width, hidden), run_decoder
    )
    returned = shifted(decoded[4], "half", -1)

    def finish_encoder():
        return encoder_back(local_docs, saved, returned, parts, vec_master, source_len)

    def finish_decoder():
        return (decoded[0], decoded[1], decoded[2], decoded[3])

    out_rows, grad_rows, weight_grads, vec_grads = lax.cond(
        is_source, finish_encoder, finish_decoder
    )
    span = capacity * half_rows
    row_ids = jnp.arange(span * lax.axis_size(("wide", "narrow")))
    device = row_ids // span
    slot = device // narrow_size * capacity + row_ids // half_rows % capacity
    part_number = device % narrow_size
    anchor = jnp.take(slot_piece, slot) * piece_rows + part_number * half_rows + row_ids % half_rows
    anchor, usage = (anchor, jnp.take(slot_used, slot))
    mine = lax.psum_scatter(
        jnp.take(weight_grads, anchor, axis=0) * usage[:, None],
        ("wide", "narrow"),
        scatter_dimension=0,
        tiled=True,
    )
    mine = mine.reshape(capacity, half_rows, model_width)
    vec_total = lax.psum(vec_grads, ("half", "wide", "narrow"))
    new_weight, new_first, new_second = adam(
        master[0], mine, moment_one[0], moment_two[0], rate_matrix, decay_matrix
    )
    vec_weight, vec_first, vec_second = adam(
        vec_master, vec_total, vec_one, vec_two, rate_vector, 0.0
    )
    return (
        out_rows[None],
        grad_rows[None],
        new_first[None],
        new_second[None],
        new_weight[None],
        new_weight.astype(bfloat)[None],
        vec_first,
        vec_second,
        vec_weight,
    )


def solution(mesh):
    in_specs = (
        P("half", ("wide", "narrow"), None, None),
        P(("wide", "narrow"), None, None),
        P(None, ("wide", "narrow")),
        P("half", None),
        P("half", "wide", "narrow", None),
        P("half", "wide", "narrow", None),
        P("half", "wide", "narrow", None),
        P(),
        P(),
        P(),
    )
    out_specs = (
        P("half", ("wide", "narrow"), None, None),
        P("half", ("wide", "narrow"), None, None),
        P("half", "wide", "narrow", None),
        P("half", "wide", "narrow", None),
        P("half", "wide", "narrow", None),
        P("half", "wide", "narrow", None),
        P(),
        P(),
        P(),
    )
    return jax.shard_map(
        on_device, mesh=mesh, in_specs=in_specs, out_specs=out_specs, check_vma=False
    )
```

profile of v0, /device:TPU:0, one launch (start us, length us, event | category | flops | bytes accessed | tf_op | source)
XLA Modules:
  0.0 1749.4 jit_solution(1880646688127131557)
XLA Ops:
  14.3 171.7 %all-gather.3.cloned.1.call-done = bf16[1,224,64,512]{3,2,0,1:T(8,128)(2,1)} async-done(((bf16[1,14,64,512]{3,2,0,1:T(8,128)(2,1)}), bf16[1,224,64,512]{3,2,0,1:T(8,128)(2,1)}) %all-gather.3.cloned.1.call-update) | async-done | bytes 14680080 | tf_op jit(solution)/shard_map/all_gather | solution.py:396
  186.0 11.5 gather_fusion
  205.0 82.0 %conditional.3 = (bf16[1024,512]{1,0:T(8,128)(2,1)}, bf16[1024,512]{0,1:T(8,128)(2,1)S(1)}, bf16[1024,512]{0,1:T(8,128)(2,1)S(1)}, bf16[1024,512]{1,0:T(8,128)(2...) conditional(s32[]{:T(128)} %convert_element_type.259, () %tuple.72, ...), branch_computations={%region_1.0_spmd, %region_2.11_spmd} | conditional | flops 8792570880 | bytes 161862848 | solution.py:416
  208.5 29.6 %while.135 = (s32[]{:T(128)}, bf16[2,512,512]{2,1,0:T(8,128)(2,1)}, f32[2,8,512]{2,1,0:T(8,128)S(1)}, s32[]{:T(128)}, s32[2]{0:T(128)S(1)}, /*index=5*/bf16[1024...) while((s32[]{:T(128)}, bf16[2,512,512]{2,1,0:T(8,128)(2,1)}, ...), condition=%wide.region_6.6_spmd, body=%wide.region_3.0_spmd.sunk | while | flops 1120138240 | bytes 57807548 | solution.py:87
  249.6 7.4 fusion.24
  257.0 24.2 %fusion.177 = (f32[1024]{0:T(1024)S(1)}, f32[1024,512]{0,1:T(8,128)S(1)}, f32[1024,512]{0,1:T(8,128)}) fusion(f32[1024,512]{0,1:T(8,128)} %multiply_add_fusion.1, f32[512]{0:T(512)S(1)} %bitcast.636, bf16[2048,512]{1,0:T(8,128)(2,1)S(1)} %copy-done.87, f32[1024,2048]{1,0:T(8,128)} %fusion.24), kind=kOutput, calls=%fused_computation.424 | convolution fusion | flops 2285370368 | bytes 16783360 | tf_op jit(solution)/shard_map/cond/branch_1_fun/dot_general | solution.py:31
  287.1 4.6 copy.150
  295.1 146.5 %gather_fusion.1 = s32[14336]{0:T(1024)} fusion(s32[112]{0:T(128)S(1)} %select_reduce_fusion, s32[14336]{0:T(1024)S(1)} %broadcast_clamp_fusion.1), kind=kCustom, calls=%fused_computation.1 | custom fusion | bytes 172032 | tf_op jit(solution)/shard_map/jit(_take)/gather | solution.py:445
  441.6 14.4 conditional.4
  445.4 7.0 broadcast.1399
  460.9 85.1 %gather_fusion.3 = f32[14336]{0:T(1024)S(1)} fusion(f32[112]{0:T(128)S(1)} %convert_element_type.263, s32[14336]{0:T(1024)S(1)} %copy-done.96), kind=kCustom, calls=%fused_computation.3 | custom fusion | bytes 172032 | tf_op jit(solution)/shard_map/jit(_take)/gather | solution.py:446
  548.1 271.0 %collective-permute-done.1 = bf16[1,1024,1024]{2,1,0:T(8,128)(2,1)} collective-permute-done((bf16[1,1024,1024]{2,1,0:T(8,128)(2,1)}, bf16[1,1024,1024]{2,1,0:T(8,128)(2,1)}, u32[]{:S(2)}, u32[]{:S(2)}) %collective-permute-start.1) | collective-permute-done | bytes 2097184 | tf_op jit(solution)/shard_map/ppermute | solution.py:27
  819.1 221.8 %conditional.5 = (f32[7168,512]{1,0:T(8,128)}, f32[15,512]{1,0:T(8,128)}, bf16[1,1,1024,512]{3,2,1,0:T(8,128)(2,1)S(1)}, f32[1,1,1024,512]{3,2,1,0:T(8,128)S(1)}) conditional(s32[]{:T(128)} %convert_element_type.259, (bf16[1,1024,512]{1,2,0:T(8,128)(2,1)}, f32[1,1024,512]{1,2,0:T(8,128)}, f32[7168,512]{1,0:T(8,128)}, ...), branch_computations={%region_48.49_spmd, %region_49.67_spmd} | conditional | flops 17960542208 | bytes 658495104 | solution.py:437
  841.8 19.2 %fusion.115 = f32[1024,2048]{1,0:T(8,128)S(1)} fusion(f32[1024,2048]{1,0:T(8,128)} %get-tuple-element.606), kind=kLoop, calls=%fused_computation.261 | loop fusion | flops 130023424 | bytes 16777216 | tf_op jit(solution)/shard_map/cond/branch_1_fun/jvp()/erfc | solution.py:53
  861.0 10.3 add_convert_fusion.12
  879.4 119.3 %while.140 = (s32[]{:T(128)}, f32[1024,8,64]{0,2,1:T(8,128)}, f32[1024,8,64]{0,2,1:T(8,128)}, bf16[2,512,512]{2,1,0:T(8,128)(2,1)}, s32[2]{0:T(128)S(1)}, /*inde...) while((s32[]{:T(128)}, f32[1024,8,64]{0,2,1:T(8,128)}, ...), condition=%wide.region_60.60_spmd.clone, body=%wide.region_58.59_spmd.clone.sunk | while | flops 2725245952 | bytes 230247312 | solution.py:127
  882.2 9.4 fusion.362
  895.9 14.2 multiply_reduce_fusion.25
  910.1 9.5 multiply_convert_fusion.11
  919.6 6.4 bitcast_add_fusion.13
  929.7 8.7 bitcast_add_fusion.14
  941.2 9.4 fusion.362
  954.9 14.2 multiply_reduce_fusion.25
  969.1 9.5 multiply_convert_fusion.11
  978.6 7.0 bitcast_add_fusion.13
  989.3 9.3 bitcast_add_fusion.14
  1030.7 8.5 fusion.123
  1041.0 71.3 %gather_fusion.2 = f32[14336,512]{1,0:T(8,128)} fusion(f32[7168,512]{1,0:T(8,128)} %get-tuple-element.668, s32[14336]{0:T(1024)} %broadcast_clamp_fusion), kind=kCustom, calls=%fused_computation.2 | custom fusion | bytes 58777600 | tf_op jit(solution)/shard_map/jit(_take)/gather | solution.py:448
  1112.3 23.6 %select_multiply_fusion = f32[14336,512]{1,0:T(8,128)} fusion(f32[14336,512]{1,0:T(8,128)} %gather_fusion.2, f32[14336]{0:T(1024)S(1)} %copy-done.103, pred[14336]{0:T(1024)(128)(4,1)S(1)} %copy-done.109), kind=kLoop, calls=%fused_computation.335 | loop fusion | flops 14680064 | bytes 58791936 | tf_op jit(solution)/shard_map/mul | solution.py:448
  1136.7 65.7 %psum.7 = f32[15,512]{1,0:T(8,128)S(1)} all-reduce(f32[15,512]{1,0:T(8,128)S(1)} %copy-done.106), channel_id=1, replica_groups=mesh['half'=2,'wide'=8,'narrow'=2] {'half','wide','narrow'}, use_global_device_ids=true, to_apply=%region_70.71 | all-reduce | flops 7680 | bytes 61440 | tf_op jit(solution)/shard_map/psum | solution.py:454
  1203.0 532.7 %reduce-scatter.2.cloned.1.call-done = f32[896,512]{1,0:T(8,128)} async-done(((f32[14336,512]{1,0:T(8,128)}), f32[896,512]{1,0:T(8,128)}) %reduce-scatter.2.cloned.1.call-update) | async-done | bytes 1835024 | tf_op jit(solution)/shard_map/reduce_scatter | solution.py:447
  1735.7 6.4 fusion.188
  (305 shorter events, 158.1 us)
Async XLA Ops:
  7.2 178.8 %all-gather.3.cloned.1.call-start = ((), (), s32[]{:S(2)}) async-start(), calls=%async_computation.2 | async-start | bytes 15597568 | tf_op jit(solution)/shard_map/all_gather | solution.py:396
  9.8 1725.9 %reduce-scatter.2.cloned.1.call-start = ((), (), s32[]{:S(2)}) async-start(), calls=%async_computation.1 | async-start | bytes 31195136 | tf_op jit(solution)/shard_map/reduce_scatter | solution.py:447
  287.0 154.5 %copy-start.13 = (bf16[1024,512]{0,1:T(8,128)(2,1)}, bf16[1024,512]{0,1:T(8,128)(2,1)S(1)}, u32[]{:S(2)}) copy-start(bf16[1024,512]{0,1:T(8,128)(2,1)S(1)} %get-tuple-element.662) | copy-start | bytes 3145732
  291.6 149.9 %collective-permute-start = (bf16[1,1024,1024]{1,2,0:T(8,128)(2,1)}, bf16[1,1024,1024]{1,2,0:T(8,128)(2,1)}, u32[]{:S(2)}, u32[]{:S(2)}) collective-permute-start(bf16[1,1024,1024]{1,2,0:T(8,128)(2,1)} %copy.150), channel_id=1, source_target_pairs={{0,16},{1,17},{2,18},{3,19},{4,20},{5,21},{6,22},{7,23},{8,24},{9,... | collective-permute-start | bytes 6291464 | tf_op jit(solution)/shard_map/ppermute | solution.py:27
  295.0 146.5 %copy-start.95 = (s32[14336]{0:T(1024)}, s32[14336]{0:T(1024)S(1)}, u32[]{:S(2)}) copy-start(s32[14336]{0:T(1024)S(1)} %broadcast_clamp_fusion.1) | copy-start | bytes 172036
  295.1 146.5 %copy-start.36 = (bf16[1,1,1024,512]{3,2,1,0:T(8,128)(2,1)S(1)}, bf16[1,1,1024,512]{3,2,1,0:T(8,128)(2,1)}, u32[]{:S(2)}) copy-start(bf16[1,1,1024,512]{3,2,1,0:T(8,128)(2,1)} %param.28) | copy-start | bytes 3145732
  295.1 146.5 %copy-start.64 = (bf16[8,64,512]{2,1,0:T(8,128)(2,1)S(1)}, bf16[8,64,512]{2,1,0:T(8,128)(2,1)}, u32[]{:S(2)}) copy-start(bf16[8,64,512]{2,1,0:T(8,128)(2,1)} %copy-done.63) | copy-start | bytes 1572868
  458.5 360.6 %collective-permute-start.1 = (bf16[1,1024,1024]{2,1,0:T(8,128)(2,1)}, bf16[1,1024,1024]{2,1,0:T(8,128)(2,1)}, u32[]{:S(2)}, u32[]{:S(2)}) collective-permute-start(bf16[1,1024,1024]{2,1,0:T(8,128)(2,1)} %copy.153), channel_id=1, source_target_pairs={{16,0},{17,1},{18,2},{19,3},{20,4},{21,5},{22,6},{23,7},{24,8},{25... | collective-permute-start | bytes 6291464 | tf_op jit(solution)/shard_map/ppermute | solution.py:27
  460.9 358.2 %copy-start.37 = (bf16[1,1,1024,512]{3,2,1,0:T(8,128)(2,1)S(1)}, bf16[1,1,1024,512]{3,2,1,0:T(8,128)(2,1)}, u32[]{:S(2)}) copy-start(bf16[1,1,1024,512]{3,2,1,0:T(8,128)(2,1)} %param.28) | copy-start | bytes 3145732
  819.6 19.2 %copy-start.41 = (bf16[1,1,1024,512]{3,2,1,0:T(8,128)(2,1)}, bf16[1,1,1024,512]{3,2,1,0:T(8,128)(2,1)S(1)}, u32[]{:S(2)}) copy-start(bf16[1,1,1024,512]{3,2,1,0:T(8,128)(2,1)S(1)} %get-tuple-element.609) | copy-start | bytes 3145732 | tf_op jit(solution)/shard_map/cond
  820.5 18.3 %copy-start.128 = (f32[1,512]{1,0:T(1,128)}, f32[1,512]{1,0:T(1,128)S(1)}, u32[]{:S(2)}) copy-start(f32[1,512]{1,0:T(1,128)S(1)} %get-tuple-element.1469) | copy-start | bytes 6148 | tf_op jit(solution)/shard_map/cond
  841.8 30.0 %copy-start.32 = (f32[1024,512]{1,0:T(8,128)}, f32[1024,512]{1,0:T(8,128)S(1)}, u32[]{:S(2)}) copy-start(f32[1024,512]{1,0:T(8,128)S(1)} %get-tuple-element.1473) | copy-start | bytes 6291460 | tf_op jit(solution)/shard_map/cond
  841.8 30.0 %copy-start.121 = (f32[1024]{0:T(1024)}, f32[1024]{0:T(1024)S(1)}, u32[]{:S(2)}) copy-start(f32[1024]{0:T(1024)S(1)} %negate_multiply_fusion.7) | copy-start | bytes 12292 | tf_op jit(solution)/shard_map/cond
  841.8 19.2 %copy-start.90 = (bf16[2048,512]{1,0:T(8,128)(2,1)S(1)}, bf16[2048,512]{1,0:T(8,128)(2,1)}, u32[]{:S(2)}) copy-start(bf16[2048,512]{1,0:T(8,128)(2,1)} %get-tuple-element.607) | copy-start | bytes 6291460 | tf_op jit(solution)/shard_map/cond
  861.0 10.8 copy-start.53
  879.4 122.2 %copy-start.62 = (bf16[512,512]{1,0:T(8,128)(2,1)S(1)}, bf16[512,512]{1,0:T(8,128)(2,1)}, u32[]{:S(2)}) copy-start(bf16[512,512]{1,0:T(8,128)(2,1)} %get-tuple-element.619) | copy-start | bytes 1572868 | tf_op jit(solution)/shard_map/cond
  895.0 15.0 slice-start.4
  895.8 14.3 slice-start.5
  895.9 14.2 slice-start.6
  895.9 14.2 slice-start.7
  954.0 15.0 slice-start.4
  954.8 14.3 slice-start.5
  954.8 14.2 slice-start.6
  954.8 14.2 slice-start.7
  1041.0 71.3 %copy-start.86 = (f32[1,1,1024,512]{3,2,1,0:T(8,128)}, f32[1,1,1024,512]{3,2,1,0:T(8,128)S(1)}, u32[]{:S(2)}) copy-start(f32[1,1,1024,512]{3,2,1,0:T(8,128)S(1)} %get-tuple-element.642) | copy-start | bytes 6291460
  1041.0 71.3 %copy-start.94 = (bf16[1,1,1024,512]{3,2,1,0:T(8,128)(2,1)}, bf16[1,1,1024,512]{3,2,1,0:T(8,128)(2,1)S(1)}, u32[]{:S(2)}) copy-start(bf16[1,1,1024,512]{3,2,1,0:T(8,128)(2,1)S(1)} %get-tuple-element.641) | copy-start | bytes 3145732
  1041.0 71.3 %copy-start.103 = (f32[14336]{0:T(1024)S(1)}, f32[14336]{0:T(1024)}, u32[]{:S(2)}) copy-start(f32[14336]{0:T(1024)} %broadcast_select_fusion.1) | copy-start | bytes 172036
  1041.0 71.3 %copy-start.109 = (pred[14336]{0:T(1024)(128)(4,1)S(1)}, pred[14336]{0:T(1024)(128)(4,1)}, u32[]{:S(2)}) copy-start(pred[14336]{0:T(1024)(128)(4,1)} %compare_and_fusion) | copy-start | bytes 43012
  1135.9 66.4 %copy-start.105 = (f32[15,512]{1,0:T(8,128)S(1)}, f32[15,512]{1,0:T(8,128)}, u32[]{:S(2)}) copy-start(f32[15,512]{1,0:T(8,128)} %param.35) | copy-start | bytes 92164
  1135.9 66.4 %copy-start.123 = (f32[15,512]{1,0:T(8,128)S(1)}, f32[15,512]{1,0:T(8,128)}, u32[]{:S(2)}) copy-start(f32[15,512]{1,0:T(8,128)} %param.37) | copy-start | bytes 92164
  1135.9 66.4 %copy-start.124 = (f32[15,512]{1,0:T(8,128)S(1)}, f32[15,512]{1,0:T(8,128)}, u32[]{:S(2)}) copy-start(f32[15,512]{1,0:T(8,128)} %param.36) | copy-start | bytes 92164
  1135.9 599.7 %copy-start.54 = (f32[1,14,64,512]{3,2,1,0:T(8,128)S(1)}, f32[1,14,64,512]{3,2,1,0:T(8,128)}, u32[]{:S(2)}) copy-start(f32[1,14,64,512]{3,2,1,0:T(8,128)} %param.32) | copy-start | bytes 5505028
  (56 other events, 212.9 us)
Sparse Core Ops, SparseCore 0:
  11.4 174.5 all-gather.2
  1136.1 599.5 reduce-scatter.1
where the time goes:
time: 1760 us; the launch traced here: 1750 us
  waiting for transfers between devices  975 us (55%)
  local copies, waits for them, and re-layouts  372 us (21%)
  matrix products  194 us (11%)
  other arithmetic  110 us (6%)
  blocking collectives  65.7 us (4%)
    reduce_scatter x1, waiting for transfers between devices, on_device(): lax.psum_scatter(jnp.take(weight_grads, anchor, axis=0) * usage[:, None],...  533 us
    ppermute x2, waiting for transfers between devices, shifted(): return lax.ppermute(block, axis, route)  271 us
    all_gather x1, waiting for transfers between devices, on_device(): lax.all_gather(master[0].astype(bfloat), ('wide', 'narrow'), axis=0, tile...  172 us
    gather x1, local copies, waits for them, and re-layouts, on_device(): jnp.take(slot_piece, slot) * piece_rows + part_number * half_rows  146 us
    gather x1, local copies, waits for them, and re-layouts, on_device(): anchor, usage = (anchor, jnp.take(slot_used, slot))  85.1 us
    gather x1, local copies, waits for them, and re-layouts, on_device(): jnp.take(weight_grads, anchor, axis=0) * usage[:, None]  71.3 us
    psum x1, blocking collectives, on_device(): vec_total = lax.psum(vec_grads, ('half', 'wide', 'narrow'))  65.7 us
    dot_general x7, matrix products, dense(): return jnp.dot(left, right, preferred_element_type=single)  38.4 us
  transfers between devices with their start and end apart: 4, of which 3 were waited for; matrix products, arithmetic and copies ran while one was open for 14% of the time, Pallas kernels for 0%

commit v1 on v0

v1 whole, which is shorter than its diff:
```python
import math
from functools import partial

import jax
import jax.numpy as jnp
from jax import lax
from jax.experimental import pallas as pl
from jax.experimental.pallas import tpu as pltpu
from jax.sharding import PartitionSpec as P

HEADS = 8
STEP = 5
QB = 256
RB = 256
NEG = -1e30

eps_norm = 1e-05
beta_one = 0.5
beta_two = 0.5
rate_matrix = 0.05
rate_vector = 0.3
decay_matrix = 0.01
eps_adam = 1e-08
bfloat = jnp.bfloat16
single = jnp.float32
VM = pl.BlockSpec(memory_space=pltpu.VMEM)
SM = pl.BlockSpec(memory_space=pltpu.SMEM)
HB = pl.BlockSpec(memory_space=pl.ANY)


def mm(left, right):
    return jnp.dot(left, right, preferred_element_type=single)


def mm_tn(left, right):
    return lax.dot_general(left, right, (((0,), (0,)), ((), ())), preferred_element_type=single)


def mm_nt(left, right):
    return lax.dot_general(left, right, (((1,), (1,)), ((), ())), preferred_element_type=single)


def block_of(index, size):
    return pl.ds(pl.multiple_of(index * size, size), size)


def normed(resid):
    center = resid - jnp.mean(resid, -1, keepdims=True)
    spread = jnp.mean(center * center, -1, keepdims=True)
    rstd = lax.rsqrt(spread + eps_norm)
    return center * rstd, rstd


def norm_back(resid, grad, gain):
    hat, rstd = normed(resid)
    grad_hat = grad * gain
    grad_resid = rstd * (
        grad_hat
        - jnp.mean(grad_hat, -1, keepdims=True)
        - hat * jnp.mean(grad_hat * hat, -1, keepdims=True)
    )
    return grad_resid, jnp.sum(grad * hat, 0, keepdims=True), jnp.sum(grad, 0, keepdims=True)


def gelu_parts(pre_act):
    half = 0.5 * (1.0 + lax.erf(pre_act * math.sqrt(0.5)))
    slope = half + pre_act * (jnp.exp(-0.5 * pre_act * pre_act) * (1.0 / math.sqrt(2.0 * math.pi)))
    return pre_act * half, slope


def pair_keys(tile, first_extra, ones):
    rows = tile.shape[0]
    lane = lax.broadcasted_iota(jnp.int32, (rows, 128), 1)
    wide_tile = tile.astype(single)
    out = []
    for head in range(2):
        at = lane - (64 - 64 * head)
        extra = jnp.where(at == 0, first_extra, jnp.where((at > 0) & (at < ones), 1.0, 0.0))
        mine = (lane < 64) if head == 0 else (lane >= 64)
        out.append(jnp.where(mine, wide_tile, extra).astype(bfloat))
    return out


def pair_queries(tile, head, extra_rows):
    mine = tile[64 * head : 64 * head + 64]
    row = lax.broadcasted_iota(jnp.int32, mine.shape, 0)
    extra = jnp.zeros(mine.shape, single)
    for number, value in enumerate(extra_rows):
        extra = jnp.where(row == number, value, extra)
    extra = extra.astype(bfloat)
    return jnp.concatenate([mine, extra] if head == 0 else [extra, mine], 0)


def split_three(value):
    high = value.astype(bfloat).astype(single)
    rest = value - high
    middle = rest.astype(bfloat).astype(single)
    return [high, middle, rest - middle]


def key_bias(limit, rows):
    row = lax.broadcasted_iota(jnp.int32, (rows, 128), 0)
    return jnp.where(row < limit, 0.0, NEG)


def score_parts(scores, diagonal):
    if not diagonal:
        return [scores]
    size = scores.shape[1]
    cut = scores.shape[0] - size
    row = lax.broadcasted_iota(jnp.int32, (size, size), 0)
    column = lax.broadcasted_iota(jnp.int32, (size, size), 1)
    last = jnp.where(row <= column, scores[cut:], NEG)
    return [scores[:cut], last] if cut else [last]


def over_blocks(causal, length, body):
    @pl.when(causal == 0)
    def _():
        def step(index, unused):
            body(index, length, False)
            return 0

        lax.fori_loop(0, length // QB, step, 0)

    @pl.when(causal != 0)
    def _():
        for index in range(length // QB):
            body(index, (index + 1) * QB, True)


def attend(limit, causal, key_ref, query_t, value_t, ctx_t, lse_ref, key_two):
    length, width = key_ref.shape
    bias = key_bias(limit, length)

    def pair(number, unused):
        columns = block_of(number, 128)
        for head, tile in enumerate(pair_keys(key_ref[:, columns], bias, 1)):
            key_two[head] = tile

        def body(index, extent, diagonal):
            at = block_of(index, QB)
            tile = query_t[columns, at]
            for head in range(2):
                mine = pl.ds(pl.multiple_of(number * 128 + 64 * head, 64), 64)
                scores = mm(key_two[head, :extent], pair_queries(tile, head, [1.0]))
                parts = score_parts(scores, diagonal)
                top = jnp.max(parts[0], 0, keepdims=True)
                for part in parts[1:]:
                    top = jnp.maximum(top, jnp.max(part, 0, keepdims=True))
                parts = [jnp.exp(part - top) for part in parts]
                total = sum(jnp.sum(part, 0, keepdims=True) for part in parts)
                weights = jnp.concatenate([part.astype(bfloat) for part in parts], 0)
                context = mm(value_t[mine, :extent], weights)
                ctx_t[mine, at] = (context * (1.0 / total)).astype(bfloat)
                lse_ref[pl.ds(number * 2 + head, 1), at] = top + jnp.log(total)

        over_blocks(causal, length, body)
        return 0

    lax.fori_loop(0, width // 128, pair, 0)


def attend_back(
    limit, causal, query_ref, key_ref, value_ref, query_t, key_t, grad_ctx, grad_ctx_t, lse_ref, dot_ref,
    grad_key, grad_value, grad_query_t, key_two, value_two,
):
    length, width = key_ref.shape
    bias = key_bias(limit, length)
    grad_key[...] = jnp.zeros(grad_key.shape, single)
    grad_value[...] = jnp.zeros(grad_value.shape, single)

    def pair(number, unused):
        columns = block_of(number, 128)
        for head, tile in enumerate(pair_keys(key_ref[:, columns], bias, 4)):
            key_two[head] = tile
        for head, tile in enumerate(pair_keys(value_ref[:, columns], 1.0, 3)):
            value_two[head] = tile

        def body(index, extent, diagonal):
            at = block_of(index, QB)
            query_tile = query_t[columns, at]
            ctx_tile = grad_ctx_t[columns, at]
            all_weights, all_grads = [], []
            for head in range(2):
                mine = pl.ds(pl.multiple_of(number * 128 + 64 * head, 64), 64)
                row = pl.ds(number * 2 + head, 1)
                minus_lse = split_three(-lse_ref[row, at])
                scores = mm(
                    key_two[head, :extent], pair_queries(query_tile, head, [1.0] + minus_lse)
                )
                weights = [jnp.exp(part) for part in score_parts(scores, diagonal)]
                weights = jnp.concatenate(weights, 0)
                minus_dot = split_three(-dot_ref[row, at])
                grad_weights = mm(value_two[head, :extent], pair_queries(ctx_tile, head, minus_dot))
                grads = (weights * grad_weights).astype(bfloat)
                all_weights.append(weights.astype(bfloat))
                all_grads.append(grads)
                grad_query = mm(key_t[mine, :extent], grads)
                grad_query_t[mine, at] = (grad_query * 0.125).astype(bfloat)
            lane = lax.broadcasted_iota(jnp.int32, (QB, 128), 1)

            def both(tile):
                tile = tile.astype(single)
                return jnp.concatenate(
                    [
                        jnp.where(lane < 64, tile, 0.0).astype(bfloat),
                        jnp.where(lane < 64, 0.0, tile).astype(bfloat),
                    ],
                    0,
                )

            grad_value[:extent, columns] += mm(
                jnp.concatenate(all_weights, 1), both(grad_ctx[at, columns])
            )
            grad_key[:extent, columns] += mm(
                jnp.concatenate(all_grads, 1), both(query_ref[at, columns])
            )

        over_blocks(causal, length, body)
        return 0

    lax.fori_loop(0, width // 128, pair, 0)


def by_rows(length, body, init=0):
    def step(index, carry):
        return body(block_of(index, RB), carry)

    return lax.fori_loop(0, length // RB, step, init)


class Emitter:
    def __init__(self, table, target, stage, semaphores):
        self.table, self.target, self.stage, self.semaphores = table, target, stage, semaphores
        self.copies = []

    def chunk(self, number, first_piece, value):
        stage, half_rows = self.stage, self.target.shape[1]
        stage[number] = value.astype(bfloat)
        count = stage.shape[1] // half_rows
        per_piece = 128 // half_rows
        for part in range(count):
            copy = pltpu.make_async_copy(
                stage.at[number, pl.ds(part * half_rows, half_rows)],
                self.target.at[self.table[first_piece * per_piece + part]],
                self.semaphores.at[number * count + part],
            )
            copy.start()
            self.copies.append(copy)

    def wait(self):
        for copy in self.copies:
            copy.wait()


def zero_rows(width):
    return (jnp.zeros((1, width), single),) * 3


def put_rows(ref, rows):
    for number, row in enumerate(rows):
        ref[number : number + 1] = row


def project_norm(length, ctx_t, weight, inner_ref, vec, resid_ref, out_ref):
    def body(rows, carry):
        branch = mm(ctx_t[:, rows].T, weight[...])
        resid = inner_ref[rows].astype(single) * vec[0:1] + branch
        resid_ref[rows] = resid
        out_ref[rows] = normed(resid)[0] * vec[1:2] + vec[2:3]
        return carry

    by_rows(length, body)


def self_forward_kernel(
    scal, x, weight, vec, query, key, value, ctx_t, lse, resid, out, query_t, value_t, key_two
):
    length, width = x.shape

    def body(rows, carry):
        tile = x[rows]
        for number, ref in enumerate((query, key, value)):
            ref[rows] = mm(tile, weight[width * number : width * (number + 1)]).astype(bfloat)
        query_t[:, rows] = (query[rows] * bfloat(0.125)).T
        value_t[:, rows] = value[rows].T
        return carry

    by_rows(length, body)
    attend(scal[0], scal[1], key, query_t, value_t, ctx_t, lse, key_two)
    project_norm(length, ctx_t, weight.at[3 * width :], x, vec, resid, out)


def encoder_ff_kernel(
    scal, inner, up, down, cross, vec, activ, slope, resid, memory, sendout
):
    length, width = inner.shape

    @pl.when(scal[2] != 0)
    def _():
        def body(rows, carry):
            tile = inner[rows]
            act, grad = gelu_parts(mm_nt(tile.astype(bfloat), up[...]))
            act = act.astype(bfloat)
            activ[rows] = act
            slope[rows] = grad.astype(bfloat)
            total = tile * vec[0:1] + mm(act, down[...])
            resid[rows] = total
            mem = (normed(total)[0] * vec[1:2] + vec[2:3]).astype(bfloat)
            memory[rows] = mem
            sendout[0, rows] = mm(mem, cross[:width]).astype(bfloat)
            sendout[1, rows] = mm(mem, cross[width:]).astype(bfloat)
            return carry

        by_rows(length, body)


def cross_forward_kernel(
    scal, inner, keys, cross, vec, query, ctx_t, lse, resid, out, query_t, value_t, key_two
):
    length, width = inner.shape

    @pl.when(scal[2] == 0)
    def _():
        def body(rows, carry):
            query[rows] = mm(inner[rows].astype(bfloat), cross[:width]).astype(bfloat)
            query_t[:, rows] = (query[rows] * bfloat(0.125)).T
            value_t[:, rows] = keys[1, rows].T
            return carry

        by_rows(length, body)
        attend(scal[0], scal[1], keys.at[0], query_t, value_t, ctx_t, lse, key_two)
        project_norm(length, ctx_t, cross.at[width:], inner, vec, resid, out)


def ff_back(length, emit, grad_branch, activ, slope, inner_low, up, down, grad_inner):
    def body(rows, carry):
        grad = mm_nt(grad_branch[rows], down[...]) * slope[rows].astype(single)
        grad = grad.astype(bfloat)
        slope[rows] = grad
        grad_inner[rows] += mm(grad, up[...])
        return carry

    by_rows(length, body)
    for number in range(activ.shape[1] // 512):
        columns = slice(number * 512, (number + 1) * 512)
        emit.chunk(2 * number, 24 + 4 * number, mm_tn(slope[:, columns], inner_low[...]))
        emit.chunk(2 * number + 1, 40 + 4 * number, mm_tn(activ[:, columns], grad_branch[...]))


def decoder_ff_kernel(
    scal, table, inner, up, down, vec, cotan, out, grad_inner, grad_vec, target,
    activ, slope, inner_low, grad_branch, stage, semaphores,
):
    length, width = inner.shape

    @pl.when(scal[2] == 0)
    def _():
        def body(rows, carry):
            tile = inner[rows]
            low = tile.astype(bfloat)
            inner_low[rows] = low
            act, grad = gelu_parts(mm_nt(low, up[...]))
            act = act.astype(bfloat)
            activ[rows] = act
            slope[rows] = grad.astype(bfloat)
            total = tile * vec[0:1] + mm(act, down[...])
            out[rows] = (normed(total)[0] * vec[1:2] + vec[2:3]).astype(bfloat)
            row = lax.broadcasted_iota(jnp.int32, tile.shape, 0) + rows.start
            grad_out = jnp.where(row < scal[3], cotan[rows].astype(single), 0.0)
            grad_resid, grad_gain, grad_shift = norm_back(total, grad_out, vec[1:2])
            grad_branch[rows] = grad_resid.astype(bfloat)
            grad_inner[rows] = grad_resid * vec[0:1]
            weigh = jnp.sum(grad_resid * tile, 0, keepdims=True)
            return (carry[0] + weigh, carry[1] + grad_gain, carry[2] + grad_shift)

        put_rows(grad_vec, by_rows(length, body, zero_rows(width)))
        emit = Emitter(table, target, stage, semaphores)
        ff_back(length, emit, grad_branch, activ, slope, inner_low, up, down, grad_inner)
        emit.wait()


def branch_back(length, resid, grad_out, inner, vec, grad_branch, grad_inner, grad_vec):
    width = resid.shape[1]

    def body(rows, carry):
        grad_resid, grad_gain, grad_shift = norm_back(resid[rows], grad_out[rows], vec[1:2])
        grad_branch[rows] = grad_resid.astype(bfloat)
        grad_inner[rows] = grad_resid * vec[0:1]
        weigh = jnp.sum(grad_resid * inner[rows].astype(single), 0, keepdims=True)
        return (carry[0] + weigh, carry[1] + grad_gain, carry[2] + grad_shift)

    put_rows(grad_vec, by_rows(length, body, zero_rows(width)))


def ctx_back(length, grad_branch, weight, ctx_t, grad_ctx, grad_ctx_t, dot_ref):
    def body(rows, carry):
        grad_ctx[rows] = mm_nt(grad_branch[rows], weight[...]).astype(bfloat)
        grad_ctx_t[:, rows] = grad_ctx[rows].T
        for head in range(HEADS):
            mine = slice(64 * head, 64 * head + 64)
            product = grad_ctx_t[mine, rows].astype(single) * ctx_t[mine, rows].astype(single)
            dot_ref[head : head + 1, rows] = jnp.sum(product, 0, keepdims=True)
        return carry

    by_rows(length, body)


def cross_back_kernel(
    scal, table, inner, resid, query, keys, ctx_t, lse, cross, vec, grad_out, held,
    sendback, grad_inner, grad_vec, target,
    grad_branch, grad_ctx, grad_ctx_t, dot_ref, query_t, key_t, grad_key, grad_value, grad_query_t,
    key_two, value_two, stage, semaphores,
):
    length, width = inner.shape

    @pl.when(scal[2] == 0)
    def _():
        emit = Emitter(table, target, stage, semaphores)
        branch_back(length, resid, grad_out, inner, vec, grad_branch, grad_inner, grad_vec)
        emit.chunk(1, 20, mm(ctx_t[...], grad_branch[...]))
        ctx_back(length, grad_branch, cross.at[width:], ctx_t, grad_ctx, grad_ctx_t, dot_ref)

        def body(rows, carry):
            query_t[:, rows] = (query[rows] * bfloat(0.125)).T
            key_t[:, rows] = keys[0, rows].T
            return carry

        by_rows(length, body)
        attend_back(
            scal[0], scal[1], query, keys.at[0], keys.at[1], query_t, key_t, grad_ctx, grad_ctx_t, lse, dot_ref,
            grad_key, grad_value, grad_query_t, key_two, value_two,
        )

        def last(rows, carry):
            sendback[0, rows] = (grad_key[rows] * 0.125).astype(bfloat)
            sendback[1, rows] = grad_value[rows].astype(bfloat)
            grad_query = grad_query_t[:, rows].T
            grad_inner[rows] += mm_nt(grad_query, cross[:width])
            grad_ctx[rows] = grad_query
            return carry

        by_rows(length, last)
        emit.chunk(0, 16, mm_tn(inner[...].astype(bfloat), grad_ctx[...]))
        emit.wait()


def encoder_back_kernel(
    scal, table, received, memory, cross, inner, resid, activ, slope, up, down, vec, held,
    grad_inner, grad_vec, target,
    grad_mem, inner_low, grad_branch, stage, semaphores,
):
    length, width = inner.shape

    @pl.when(scal[2] != 0)
    def _():
        emit = Emitter(table, target, stage, semaphores)

        def body(rows, carry):
            grad_mem[rows] = mm_nt(received[0, rows], cross[:width]) + mm_nt(
                received[1, rows], cross[width:]
            )
            inner_low[rows] = inner[rows].astype(bfloat)
            return carry

        by_rows(length, body)
        branch_back(length, resid, grad_mem, inner, vec, grad_branch, grad_inner, grad_vec)
        ff_back(length, emit, grad_branch, activ, slope, inner_low, up, down, grad_inner)
        emit.chunk(8, 16, mm_tn(memory[...], received[0]))
        emit.chunk(9, 20, mm_tn(memory[...], received[1]))
        emit.wait()


def self_back_kernel(
    scal, table, x, weight, vec, resid, query, key, value, ctx_t, lse, grad_out, held,
    grad_x, grad_vec, target,
    grad_branch, grad_ctx, grad_ctx_t, dot_ref, query_t, key_t, grad_key, grad_value, grad_query_t,
    key_two, value_two, stage, semaphores,
):
    length, width = x.shape
    emit = Emitter(table, target, stage, semaphores)
    branch_back(length, resid, grad_out, x, vec, grad_branch, grad_x, grad_vec)
    emit.chunk(3, 12, mm(ctx_t[...], grad_branch[...]))
    ctx_back(length, grad_branch, weight.at[3 * width :], ctx_t, grad_ctx, grad_ctx_t, dot_ref)

    def body(rows, carry):
        query_t[:, rows] = (query[rows] * bfloat(0.125)).T
        key_t[:, rows] = key[rows].T
        return carry

    by_rows(length, body)
    attend_back(
        scal[0], scal[1], query, key, value, query_t, key_t, grad_ctx, grad_ctx_t, lse, dot_ref,
        grad_key, grad_value, grad_query_t, key_two, value_two,
    )

    def last(rows, carry):
        parts = (
            grad_query_t[:, rows].T,
            (grad_key[rows] * 0.125).astype(bfloat),
            grad_value[rows].astype(bfloat),
        )
        total = grad_x[rows]
        for number, part in enumerate(parts):
            total += mm_nt(part, weight[width * number : width * (number + 1)])
        grad_x[rows] = total
        grad_branch[rows] = parts[0]
        grad_ctx[rows] = parts[1]
        return carry

    by_rows(length, last)
    emit.chunk(0, 0, mm_tn(x[...], grad_branch[...]))
    emit.chunk(1, 4, mm_tn(x[...], grad_ctx[...]))
    emit.chunk(2, 8, mm_tn(x[...], grad_value[...].astype(bfloat)))
    emit.wait()


def call(kernel, ins, outs, scratch, name, aliases=None):
    specs = [spec for spec, unused in ins]
    return pl.pallas_call(
        kernel,
        in_specs=specs,
        out_specs=[spec for spec, unused in outs],
        out_shape=[shape for unused, shape in outs],
        scratch_shapes=scratch,
        input_output_aliases=aliases or {},
        compiler_params=pltpu.CompilerParams(vmem_limit_bytes=58 << 20),
        name=name,
    )(*[value for unused, value in ins])


def shaped(*shape, dtype=single):
    return jax.ShapeDtypeStruct(shape, dtype)


def low(*shape):
    return jax.ShapeDtypeStruct(shape, bfloat)


def low_vm(*shape):
    return pltpu.VMEM(shape, bfloat)


def full_vm(*shape):
    return pltpu.VMEM(shape, single)


def adam(weight, gradient, first, second, step_rate, decay_rate):
    first_new = beta_one * first + (1.0 - beta_one) * gradient
    second_new = beta_two * second + (1.0 - beta_two) * gradient * gradient
    first_hat = first_new / (1.0 - beta_one**STEP)
    second_hat = second_new / (1.0 - beta_two**STEP)
    weight_new = weight - step_rate * (
        first_hat / (jnp.sqrt(second_hat) + eps_adam) + decay_rate * weight
    )
    return (weight_new, first_new, second_new)


def on_device(
    stream, cotangent, lengths, owners, master, moment_one, moment_two, vec_master, vec_one, vec_two
):
    narrow_size = lax.axis_size("narrow")
    wide_size = lax.axis_size("wide")
    owner_row = owners[0]
    capacity = master.shape[1]
    half_rows = master.shape[2]
    width = master.shape[3]
    count = owner_row.shape[0]
    counter = jnp.arange(count)
    same = owner_row[:, None] == owner_row[None, :]
    earlier = counter[None, :] < counter[:, None]
    ranks = jnp.sum((same & earlier).astype(jnp.int32), 1)
    places = (
        owner_row[:, None] * narrow_size + jnp.arange(narrow_size)[None, :]
    ) * capacity + ranks[:, None]
    gathered = lax.all_gather(master[0].astype(bfloat), ("wide", "narrow"), axis=0, tiled=True)
    hidden = (count * half_rows * narrow_size - 6 * width) // 2
    piece_rows = half_rows * narrow_size

    def weight_rows(first, rows):
        order = places[first // piece_rows : (first + rows) // piece_rows].reshape(-1)
        return jnp.take(gathered, order, axis=0).reshape(-1, width)

    is_source = lax.axis_index("half") == 0
    x = stream[0, 0]
    length = x.shape[0]
    source_len, target_len = lengths[0, 0], lengths[1, 0]
    own_len = jnp.where(is_source, source_len, target_len)
    flag = is_source.astype(jnp.int32)
    own_scal = jnp.stack([own_len, 1 - flag, flag, target_len]).astype(jnp.int32)
    cross_scal = jnp.stack([source_len, jnp.int32(0), flag, target_len]).astype(jnp.int32)
    table = places.reshape(-1).astype(jnp.int32)
    self_vec = jnp.where(is_source, vec_master[0:3], vec_master[6:9])
    self_w = (VM, weight_rows(0, 4 * width))
    up_w = (VM, weight_rows(6 * width, hidden))
    down_w = (VM, weight_rows(6 * width + hidden, hidden))
    cross_w = (VM, weight_rows(4 * width, 2 * width))
    slots = shaped(capacity * wide_size * narrow_size, half_rows, width, dtype=bfloat)
    stage_of = lambda chunks: [
        low_vm(chunks, 512, width),
        pltpu.SemaphoreType.DMA((chunks * 512 // half_rows,)),
    ]
    two = low_vm(2, length, 128)

    query, key, value, ctx_t, lse, resid, inner = call(
        self_forward_kernel,
        [(SM, own_scal), (VM, x), self_w, (VM, self_vec)],
        [(VM, low(length, width))] * 3
        + [(VM, low(width, length)), (VM, shaped(HEADS, length))]
        + [(VM, shaped(length, width))] * 2,
        [low_vm(width, length), low_vm(width, length), two],
        "self_forward",
    )
    activ, slope, ff_resid, memory, sendout = call(
        encoder_ff_kernel,
        [(SM, own_scal), (VM, inner), up_w, down_w, cross_w, (VM, vec_master[3:6])],
        [
            (VM, low(length, hidden)),
            (VM, low(length, hidden)),
            (VM, shaped(length, width)),
            (VM, low(length, width)),
            (VM, low(2, length, width)),
        ],
        [],
        "encoder_ff",
    )
    keys = lax.ppermute(sendout, "half", [(0, 1)])
    cross_query, cross_ctx_t, cross_lse, cross_resid, inner_two = call(
        cross_forward_kernel,
        [(SM, cross_scal), (VM, inner), (VM, keys), cross_w, (VM, vec_master[9:12])],
        [
            (VM, low(length, width)),
            (VM, low(width, length)),
            (VM, shaped(HEADS, length)),
            (VM, shaped(length, width)),
            (VM, shaped(length, width)),
        ],
        [low_vm(width, length), low_vm(width, length), two],
        "cross_forward",
    )
    output, grad_two, ff_vec, target = call(
        decoder_ff_kernel,
        [
            (SM, own_scal),
            (SM, table),
            (VM, inner_two),
            up_w,
            down_w,
            (VM, vec_master[12:15]),
            (VM, cotangent[0]),
        ],
        [
            (VM, low(length, width)),
            (VM, shaped(length, width)),
            (VM, shaped(3, width)),
            (HB, slots),
        ],
        [low_vm(length, hidden), low_vm(length, hidden), low_vm(length, width), low_vm(length, width)]
        + stage_of(8),
        "decoder_ff",
    )
    attn_scratch = (
        [low_vm(length, width), low_vm(length, width), low_vm(width, length), full_vm(HEADS, length)]
        + [low_vm(width, length), low_vm(width, length)]
        + [full_vm(length, width), full_vm(length, width), low_vm(width, length), two, two]
    )
    sendback, grad_one, cross_vec, target = call(
        cross_back_kernel,
        [
            (SM, cross_scal),
            (SM, table),
            (VM, inner),
            (VM, cross_resid),
            (VM, cross_query),
            (VM, keys),
            (VM, cross_ctx_t),
            (VM, cross_lse),
            cross_w,
            (VM, vec_master[9:12]),
            (VM, grad_two),
            (HB, target),
        ],
        [
            (VM, low(2, length, width)),
            (VM, shaped(length, width)),
            (VM, shaped(3, width)),
            (HB, slots),
        ],
        attn_scratch + stage_of(2),
        "cross_back",
        {11: 3},
    )
    returned = lax.ppermute(sendback, "half", [(1, 0)])
    grad_inner, memory_vec, target = call(
        encoder_back_kernel,
        [
            (SM, own_scal),
            (SM, table),
            (VM, returned),
            (VM, memory),
            cross_w,
            (VM, inner),
            (VM, ff_resid),
            (VM, activ),
            (VM, slope),
            up_w,
            down_w,
            (VM, vec_master[3:6]),
            (HB, target),
        ],
        [(VM, shaped(length, width)), (VM, shaped(3, width)), (HB, slots)],
        [full_vm(length, width), low_vm(length, width), low_vm(length, width)] + stage_of(10),
        "encoder_back",
        {12: 2},
    )
    grad_x, own_vec, target = call(
        self_back_kernel,
        [
            (SM, own_scal),
            (SM, table),
            (VM, x),
            self_w,
            (VM, self_vec),
            (VM, resid),
            (VM, query),
            (VM, key),
            (VM, value),
            (VM, ctx_t),
            (VM, lse),
            (VM, jnp.where(is_source, grad_inner, grad_one)),
            (HB, target),
        ],
        [(VM, shaped(length, width)), (VM, shaped(3, width)), (HB, slots)],
        attn_scratch + stage_of(4),
        "self_back",
        {12: 2},
    )
    zeros = jnp.zeros((3, width), single)
    vec_grads = jnp.where(
        is_source,
        jnp.concatenate([own_vec, memory_vec, zeros, zeros, zeros], 0),
        jnp.concatenate([zeros, zeros, own_vec, cross_vec, ff_vec], 0),
    )
    mine = lax.psum_scatter(target, ("wide", "narrow"), scatter_dimension=0, tiled=True)
    used = jnp.sum((owner_row == lax.axis_index("wide")).astype(jnp.int32))
    mine = jnp.where(
        (jnp.arange(capacity) < used)[:, None, None], mine.astype(single), 0.0
    )
    vec_total = lax.psum(vec_grads, ("half", "wide", "narrow"))
    new_weight, new_first, new_second = adam(
        master[0], mine, moment_one[0], moment_two[0], rate_matrix, decay_matrix
    )
    vec_weight, vec_first, vec_second = adam(
        vec_master, vec_total, vec_one, vec_two, rate_vector, 0.0
    )
    return (
        jnp.where(is_source, memory, output)[None, None],
        grad_x[None, None],
        new_first[None],
        new_second[None],
        new_weight[None],
        new_weight.astype(bfloat)[None],
        vec_first,
        vec_second,
        vec_weight,
    )


def solution(mesh):
    in_specs = (
        P("half", ("wide", "narrow"), None, None),
        P(("wide", "narrow"), None, None),
        P(None, ("wide", "narrow")),
        P("half", None),
        P("half", "wide", "narrow", None),
        P("half", "wide", "narrow", None),
        P("half", "wide", "narrow", None),
        P(),
        P(),
        P(),
    )
    out_specs = (
        P("half", ("wide", "narrow"), None, None),
        P("half", ("wide", "narrow"), None, None),
        P("half", "wide", "narrow", None),
        P("half", "wide", "narrow", None),
        P("half", "wide", "narrow", None),
        P("half", "wide", "narrow", None),
        P(),
        P(),
        P(),
    )
    return jax.shard_map(
        on_device, mesh=mesh, in_specs=in_specs, out_specs=out_specs, check_vma=False
    )
```

time: 1760 us -> 775 us (0.44)
  waiting for transfers between devices: 975 us -> 502 us
  local copies, waits for them, and re-layouts: 372 us -> 28.4 us
  matrix products: 194 us -> 0 us
  Pallas kernels: 0 us -> 136 us
  other arithmetic: 110 us -> 25.9 us
    gather x4, local copies, waits for them, and re-layouts: 314 us -> 23.3 us  [weight_rows(): return jnp.take(gathered, order, axis=0).reshape(-1, width)]
    reduce_scatter x1, waiting for transfers between devices: 533 us -> 243 us  [on_device(): lax.psum_scatter(target, ('wide', 'narrow'), scatter_dimension=0, tiled=T...]
    dot_general x37 -> x0, matrix products: 194 us -> none  [the longest x7 38.4 us: dense(): return jnp.dot(left, right, preferred_element_type=single)]
    ppermute x2, waiting for transfers between devices: 271 us -> 87.9 us  [the longest x1 86.7 us: on_device(): returned = lax.ppermute(sendback, 'half', [(1, 0)])]
    pallas_call x0 -> x7, Pallas kernels: none -> 136 us  [call(): pl.pallas_call(kernel, in_specs=specs, out_specs=[spec for spec, unused i...]
    convert_element_type x7 -> x0, other arithmetic: 28.7 us -> none  [the longest x2 18.9 us: one_block(): grad_scores = (weights * (grad_weights - jnp.sum(weights * grad_weights,...]
    mul x2 -> x0, other arithmetic: 24.3 us -> none  [the longest x1 23.6 us: on_device(): jnp.take(weight_grads, anchor, axis=0) * usage[:, None]]
    another operation x11 -> x0, local copies, waits for them, and re-layouts: 23 us -> none
  transfers between devices with their start and end apart: 4 -> 4, of which waited for: 3 -> 4; matrix products, arithmetic and copies ran while one was open for 14% -> 1% of each run, Pallas kernels for 0% -> 0%
where the time goes in v1:
time: 775 us; the launch traced here: 768 us
  waiting for transfers between devices  502 us (65%)
  Pallas kernels  136 us (18%)
  blocking collectives  57.7 us (7%)
  local copies, waits for them, and re-layouts  28.4 us (4%)
  other arithmetic  25.9 us (3%)
  between operations  15.8 us (2%)
    reduce_scatter x1, waiting for transfers between devices, on_device(): lax.psum_scatter(target, ('wide', 'narrow'), scatter_dimension=0, tiled=T...  243 us
    all_gather x1, waiting for transfers between devices, on_device(): lax.all_gather(master[0].astype(bfloat), ('wide', 'narrow'), axis=0, tile...  171 us
    pallas_call x7, Pallas kernels, call(): pl.pallas_call(kernel, in_specs=specs, out_specs=[spec for spec, unused i...  136 us
    ppermute x1, waiting for transfers between devices, on_device(): returned = lax.ppermute(sendback, 'half', [(1, 0)])  86.7 us
    psum x1, blocking collectives, on_device(): vec_total = lax.psum(vec_grads, ('half', 'wide', 'narrow'))  57.7 us
    gather x4, local copies, waits for them, and re-layouts, weight_rows(): return jnp.take(gathered, order, axis=0).reshape(-1, width)  23.3 us
  transfers between devices with their start and end apart: 4, of which 4 were waited for; matrix products, arithmetic and copies ran while one was open for 1% of the time, Pallas kernels for 0%

profile of v1, /device:TPU:0, one launch (start us, length us, event | category | flops | bytes accessed | tf_op | source)
XLA Modules:
  0.0 768.0 jit_solution(6061721052949245660)
XLA Ops:
  7.3 2.5 bitcast_convert_fusion
  13.3 1.3 add_add_fusion.scal
  15.3 170.7 %all-gather.2.cloned.1.call-done = bf16[224,64,512]{2,1,0:T(8,128)(2,1)} async-done(((bf16[14,64,512]{2,1,0:T(8,128)(2,1)}), bf16[224,64,512]{2,1,0:T(8,128)(2,1)}) %all-gather.2.cloned.1.call-update) | async-done | bytes 14680080 | tf_op jit(solution)/shard_map/all_gather | solution.py:577
  186.0 5.9 gather_fusion.1
  191.9 1.6 broadcast_select_fusion.2
  193.5 5.9 gather_fusion.2
  199.4 1.6 broadcast_select_fusion.1
  201.0 5.9 gather_fusion.3
  206.8 1.6 broadcast_select_fusion
  208.4 5.8 gather_fusion
  214.2 1.2 bitcast_select_fusion.cross
  215.4 34.1 %self_forward.1 = (bf16[1024,512]{1,0:T(8,128)(2,1)}, bf16[1024,512]{1,0:T(8,128)(2,1)}, bf16[1024,512]{1,0:T(8,128)(2,1)}, bf16[512,1024]{1,0:T(8,128)(2,1)}, f...) custom-call(s32[4]{0:T(128)} %add_add_fusion.scal, bf16[1024,512]{1,0:T(8,128)(2,1)} %bitcast.62, ...), custom_call_target="tpu_custom_call" | custom-call | tf_op jit(solution)/shard_map/self_forward/pallas_call | solution.py:521
  249.5 16.4 %encoder_ff.1 = (bf16[1024,2048]{1,0:T(8,128)(2,1)}, bf16[1024,2048]{1,0:T(8,128)(2,1)}, f32[1024,512]{1,0:T(8,128)}, bf16[1024,512]{1,0:T(8,128)(2,1)}, bf16[2,1024,512]{2,1,0:T(8,128)(2,1)}) custom-call(s32[4]{0:T(128)} %add_add_fusion.scal, f32[1024,512]{1,0:T(8,128)} %get-tuple-element.41.inner, bf16[2048,512]{1,0:T(8,128)(2,1)} %bitcast.54, ...), custom_call_target="tpu_custom_call" | custom-call | tf_op jit(solution)/shard_map/encoder_ff/pallas_call | solution.py:521
  265.9 1.4 collective-permute-start
  267.4 0.7 add.89.table
  268.1 1.8 add_add_fusion.1.scal
  269.9 1.3 collective-permute-done.keys
  271.2 1.4 copy-done
  272.6 5.4 cross_forward.1
  278.0 5.3 decoder_ff.1
  283.3 7.0 cross_back.1
  290.3 1.3 collective-permute-start.1
  291.6 86.7 %collective-permute-done.1.received = bf16[2,1024,512]{2,1,0:T(8,128)(2,1)S(1)} collective-permute-done((bf16[2,1024,512]{2,1,0:T(8,128)(2,1)}, bf16[2,1024,512]{2,1,0:T(8,128)(2,1)S(1)}, u32[]{:S(2)}, u32[]{:S(2)}) %collective-permute-start.1) | collective-permute-done | bytes 2097184 | tf_op jit(solution)/shard_map/ppermute | solution.py:694
  378.2 1.3 copy-done.4
  379.5 24.7 %encoder_back.1 = (f32[1024,512]{1,0:T(8,128)}, f32[3,512]{1,0:T(4,128)}, bf16[224,64,512]{2,1,0:T(8,128)(2,1)}) custom-call(s32[4]{0:T(128)} %add_add_fusion.scal, s32[112]{0:T(128)} %add.89.table, bf16[2,1024,512]{2,1,0:T(8,128)(2,1)} %copy-done.4, bf16[1024,512]{1,0:T(8,128)(2,1)} %get-tuple-element.42.memory, ...), custom_call_target="tpu_custom_call", output_to_operand_aliasing={{2}: (12, {})} | custom-call | tf_op jit(solution)/shard_map/encoder_back/pallas_call | solution.py:521
  404.2 3.4 broadcast_select_fusion.3.grad_out
  407.6 42.8 %self_back.1 = (f32[1024,512]{1,0:T(8,128)}, f32[3,512]{1,0:T(4,128)}, bf16[224,64,512]{2,1,0:T(8,128)(2,1)}) custom-call(s32[4]{0:T(128)} %add_add_fusion.scal, s32[112]{0:T(128)} %add.89.table, bf16[1024,512]{1,0:T(8,128)(2,1)} %bitcast.63, bf16[2048,512]{1,0:T(8,128)(2,1)} %bitcast.61, ...), custom_call_target="tpu_custom_call", output_to_operand_aliasing={{2}: (12, {})} | custom-call | tf_op jit(solution)/shard_map/self_back/pallas_call | solution.py:521
  450.6 0.8 iota_compare_fusion.1
  451.6 1.1 select_bitcast_fusion
  452.8 57.7 %psum.7 = f32[15,512]{1,0:T(8,128)S(1)} all-reduce(f32[15,512]{1,0:T(8,128)S(1)} %maximum_select_fusion), channel_id=1, replica_groups=mesh['half'=2,'wide'=8,'narrow'=2] {'half','wide','narrow'}, use_global_device_ids=true, to_apply=%region_3.5 | all-reduce | flops 7680 | bytes 61440 | tf_op jit(solution)/shard_map/psum | solution.py:750
  511.2 243.2 %reduce-scatter.2.cloned.1.call-done = bf16[14,64,512]{2,1,0:T(8,128)(2,1)} async-done(((bf16[224,64,512]{2,1,0:T(8,128)(2,1)}), bf16[14,64,512]{2,1,0:T(8,128)(2,1)}) %reduce-scatter.2.cloned.1.call-update) | async-done | bytes 917520 | tf_op jit(solution)/shard_map/reduce_scatter | solution.py:745
  754.4 6.6 convert_bitcast_fusion
  (62 shorter events, 4.0 us)
Async XLA Ops:
  7.2 2.7 copy-start.13
  7.2 4.2 copy-start.12
  7.2 7.5 copy-start.5
  7.2 178.8 %all-gather.2.cloned.1.call-start = ((), (), s32[]{:S(2)}) async-start(), calls=%async_computation.1 | async-start | bytes 15597568 | tf_op jit(solution)/shard_map/all_gather | solution.py:577
  9.8 744.5 %reduce-scatter.2.cloned.1.call-start = ((), (), s32[]{:S(2)}) async-start(), calls=%async_computation.2 | async-start | bytes 15597568 | tf_op jit(solution)/shard_map/reduce_scatter | solution.py:745
  265.9 5.3 collective-permute-start
  271.2 1.4 copy-start
  290.3 88.0 %collective-permute-start.1 = (bf16[2,1024,512]{2,1,0:T(8,128)(2,1)}, bf16[2,1024,512]{2,1,0:T(8,128)(2,1)S(1)}, u32[]{:S(2)}, u32[]{:S(2)}) collective-permute-start(bf16[2,1024,512]{2,1,0:T(8,128)(2,1)} %get-tuple-element.58), channel_id=1, source_target_pairs={{16,0},{17,1},{18,2},{19,3},{20,4},{21,5},{22,6},{23,7},{24,8},{25... | collective-permute-start | bytes 6291464 | tf_op jit(solution)/shard_map/ppermute | solution.py:694
  378.2 1.3 copy-start.4
  379.5 24.7 %copy-start.3 = (f32[1024,512]{1,0:T(8,128)S(1)}, f32[1024,512]{1,0:T(8,128)}, u32[]{:S(2)}) copy-start(f32[1024,512]{1,0:T(8,128)} %get-tuple-element.64) | copy-start | bytes 6291460
  450.4 1.2 copy-start.2
  450.4 2.3 copy-start.8
  450.4 2.3 copy-start.9
  450.5 2.3 copy-start.10
  450.5 2.3 copy-start.11
  450.5 60.0 %copy-start.6 = (f32[15,512]{1,0:T(8,128)S(1)}, f32[15,512]{1,0:T(8,128)}, u32[]{:S(2)}) copy-start(f32[15,512]{1,0:T(8,128)} %param.21) | copy-start | bytes 92164
  450.5 60.0 %copy-start.7 = (f32[15,512]{1,0:T(8,128)S(1)}, f32[15,512]{1,0:T(8,128)}, u32[]{:S(2)}) copy-start(f32[15,512]{1,0:T(8,128)} %param.20) | copy-start | bytes 92164
  450.5 303.9 %copy-start.1 = (f32[1,14,64,512]{3,2,1,0:T(8,128)S(1)}, f32[1,14,64,512]{3,2,1,0:T(8,128)}, u32[]{:S(2)}) copy-start(f32[1,14,64,512]{3,2,1,0:T(8,128)} %param.16) | copy-start | bytes 5505028
Sparse Core Ops, SparseCore 0:
  11.4 174.5 all-gather.1
  450.6 303.7 reduce-scatter.1

commit v2 on v1

v2 whole, which is shorter than its diff:
```python
import math
from functools import partial

import jax
import jax.numpy as jnp
from jax import lax
from jax.experimental import pallas as pl
from jax.experimental.pallas import tpu as pltpu
from jax.sharding import PartitionSpec as P

HEADS = 8
STEP = 5
QB = 256
RB = 256
NEG = -1e30

eps_norm = 1e-05
beta_one = 0.5
beta_two = 0.5
rate_matrix = 0.05
rate_vector = 0.3
decay_matrix = 0.01
eps_adam = 1e-08
bfloat = jnp.bfloat16
single = jnp.float32
VM = pl.BlockSpec(memory_space=pltpu.VMEM)
SM = pl.BlockSpec(memory_space=pltpu.SMEM)
HB = pl.BlockSpec(memory_space=pl.ANY)


def mm(left, right):
    return jnp.dot(left, right, preferred_element_type=single)


def mm_tn(left, right):
    return lax.dot_general(left, right, (((0,), (0,)), ((), ())), preferred_element_type=single)


def mm_nt(left, right):
    return lax.dot_general(left, right, (((1,), (1,)), ((), ())), preferred_element_type=single)


def block_of(index, size):
    return pl.ds(pl.multiple_of(index * size, size), size)


def normed(resid):
    center = resid - jnp.mean(resid, -1, keepdims=True)
    spread = jnp.mean(center * center, -1, keepdims=True)
    rstd = lax.rsqrt(spread + eps_norm)
    return center * rstd, rstd


def norm_back(resid, grad, gain):
    hat, rstd = normed(resid)
    grad_hat = grad * gain
    grad_resid = rstd * (
        grad_hat
        - jnp.mean(grad_hat, -1, keepdims=True)
        - hat * jnp.mean(grad_hat * hat, -1, keepdims=True)
    )
    return grad_resid, jnp.sum(grad * hat, 0, keepdims=True), jnp.sum(grad, 0, keepdims=True)


def gelu_parts(pre_act):
    half = 0.5 * (1.0 + lax.erf(pre_act * math.sqrt(0.5)))
    slope = half + pre_act * (jnp.exp(-0.5 * pre_act * pre_act) * (1.0 / math.sqrt(2.0 * math.pi)))
    return pre_act * half, slope


def pair_keys(tile, first_extra, ones):
    rows = tile.shape[0]
    lane = lax.broadcasted_iota(jnp.int32, (rows, 128), 1)
    wide_tile = tile.astype(single)
    out = []
    for head in range(2):
        at = lane - (64 - 64 * head)
        extra = jnp.where(at == 0, first_extra, jnp.where((at > 0) & (at < ones), 1.0, 0.0))
        mine = (lane < 64) if head == 0 else (lane >= 64)
        out.append(jnp.where(mine, wide_tile, extra).astype(bfloat))
    return out


def pair_queries(tile, head, extra_rows):
    mine = tile[64 * head : 64 * head + 64]
    row = lax.broadcasted_iota(jnp.int32, mine.shape, 0)
    extra = jnp.zeros(mine.shape, single)
    for number, value in enumerate(extra_rows):
        extra = jnp.where(row == number, value, extra)
    extra = extra.astype(bfloat)
    return jnp.concatenate([mine, extra] if head == 0 else [extra, mine], 0)


def split_three(value):
    high = value.astype(bfloat).astype(single)
    rest = value - high
    middle = rest.astype(bfloat).astype(single)
    return [high, middle, rest - middle]


def key_bias(limit, rows):
    row = lax.broadcasted_iota(jnp.int32, (rows, 128), 0)
    return jnp.where(row < limit, 0.0, NEG)


def score_parts(scores, diagonal):
    if not diagonal:
        return [scores]
    size = scores.shape[1]
    cut = scores.shape[0] - size
    row = lax.broadcasted_iota(jnp.int32, (size, size), 0)
    column = lax.broadcasted_iota(jnp.int32, (size, size), 1)
    last = jnp.where(row <= column, scores[cut:], NEG)
    return [scores[:cut], last] if cut else [last]


def over_blocks(causal, rows, length, body):
    def every():
        def step(index, unused):
            body(index, length, False)
            return 0

        lax.fori_loop(0, rows // QB, step, 0)

    if causal is None:
        every()
        return
    pl.when(causal == 0)(every)

    @pl.when(causal != 0)
    def _():
        for index in range(length // QB):
            body(index, (index + 1) * QB, True)


def attend(limit, causal, key_ref, query_t, value_t, ctx_t, lse_ref, key_two):
    length, width = key_ref.shape
    bias = key_bias(limit, length)

    def pair(number, unused):
        columns = block_of(number, 128)
        for head, tile in enumerate(pair_keys(key_ref[:, columns], bias, 1)):
            key_two[head] = tile

        def body(index, extent, diagonal):
            at = block_of(index, QB)
            tile = query_t[columns, at]
            for head in range(2):
                mine = pl.ds(pl.multiple_of(number * 128 + 64 * head, 64), 64)
                scores = mm(key_two[head, :extent], pair_queries(tile, head, [1.0]))
                parts = score_parts(scores, diagonal)
                top = jnp.max(parts[0], 0, keepdims=True)
                for part in parts[1:]:
                    top = jnp.maximum(top, jnp.max(part, 0, keepdims=True))
                parts = [jnp.exp(part - top) for part in parts]
                total = sum(jnp.sum(part, 0, keepdims=True) for part in parts)
                weights = jnp.concatenate([part.astype(bfloat) for part in parts], 0)
                context = mm(value_t[mine, :extent], weights)
                ctx_t[mine, at] = (context * (1.0 / total)).astype(bfloat)
                lse_ref[pl.ds(number * 2 + head, 1), at] = top + jnp.log(total)

        over_blocks(causal, query_t.shape[1], length, body)
        return 0

    lax.fori_loop(0, width // 128, pair, 0)


def attend_back(
    limit, causal, query_ref, key_ref, value_ref, query_t, key_t, grad_ctx, grad_ctx_t, lse_ref, dot_ref,
    grad_key, grad_value, grad_query_t, key_two, value_two,
):
    length, width = key_ref.shape
    bias = key_bias(limit, length)
    grad_key[...] = jnp.zeros(grad_key.shape, single)
    grad_value[...] = jnp.zeros(grad_value.shape, single)

    def pair(number, unused):
        columns = block_of(number, 128)
        for head, tile in enumerate(pair_keys(key_ref[:, columns], bias, 4)):
            key_two[head] = tile
        for head, tile in enumerate(pair_keys(value_ref[:, columns], 1.0, 3)):
            value_two[head] = tile

        def body(index, extent, diagonal):
            at = block_of(index, QB)
            query_tile = query_t[columns, at]
            ctx_tile = grad_ctx_t[columns, at]
            all_weights, all_grads = [], []
            for head in range(2):
                mine = pl.ds(pl.multiple_of(number * 128 + 64 * head, 64), 64)
                row = pl.ds(number * 2 + head, 1)
                minus_lse = split_three(-lse_ref[row, at])
                scores = mm(
                    key_two[head, :extent], pair_queries(query_tile, head, [1.0] + minus_lse)
                )
                weights = [jnp.exp(part) for part in score_parts(scores, diagonal)]
                weights = jnp.concatenate(weights, 0)
                minus_dot = split_three(-dot_ref[row, at])
                grad_weights = mm(value_two[head, :extent], pair_queries(ctx_tile, head, minus_dot))
                grads = (weights * grad_weights).astype(bfloat)
                all_weights.append(weights.astype(bfloat))
                all_grads.append(grads)
                grad_query = mm(key_t[mine, :extent], grads)
                grad_query_t[mine, at] = (grad_query * 0.125).astype(bfloat)
            lane = lax.broadcasted_iota(jnp.int32, (QB, 128), 1)

            def both(tile):
                tile = tile.astype(single)
                return jnp.concatenate(
                    [
                        jnp.where(lane < 64, tile, 0.0).astype(bfloat),
                        jnp.where(lane < 64, 0.0, tile).astype(bfloat),
                    ],
                    0,
                )

            grad_value[:extent, columns] += mm(
                jnp.concatenate(all_weights, 1), both(grad_ctx[at, columns])
            )
            grad_key[:extent, columns] += mm(
                jnp.concatenate(all_grads, 1), both(query_ref[at, columns])
            )

        over_blocks(causal, query_t.shape[1], length, body)
        return 0

    lax.fori_loop(0, width // 128, pair, 0)


def by_rows(length, body, init=0):
    def step(index, carry):
        return body(block_of(index, RB), carry)

    return lax.fori_loop(0, length // RB, step, init)


class Emitter:
    def __init__(self, table, target, stage, semaphores):
        self.table, self.target, self.stage, self.semaphores = table, target, stage, semaphores
        self.copies = []

    def chunk(self, number, first_piece, value):
        stage, half_rows = self.stage, self.target.shape[1]
        stage[number] = value.astype(bfloat)
        count = stage.shape[1] // half_rows
        per_piece = 128 // half_rows
        for part in range(count):
            copy = pltpu.make_async_copy(
                stage.at[number, pl.ds(part * half_rows, half_rows)],
                self.target.at[self.table[first_piece * per_piece + part]],
                self.semaphores.at[number * count + part],
            )
            copy.start()
            self.copies.append(copy)

    def wait(self):
        for copy in self.copies:
            copy.wait()


class Moves:
    def __init__(self, role):
        self.role = role
        self.loads = []
        self.stores = []
        self.waited = set()

    def load(self, dest, ways, semaphores):
        def begin(way):
            for number, (source, first, at, rows) in enumerate(way):
                if rows is not None:
                    source = source.at[pl.ds(first, rows)]
                    target = dest.at[pl.ds(at, rows)]
                else:
                    target = dest
                pltpu.make_async_copy(source, target, semaphores.at[number]).start()

        def finish(way):
            for number, (source, first, at, rows) in enumerate(way):
                if rows is not None:
                    source = source.at[pl.ds(first, rows)]
                    target = dest.at[pl.ds(at, rows)]
                else:
                    target = dest
                pltpu.make_async_copy(source, target, semaphores.at[number]).wait()

        def split(act):
            if len(ways) == 1:
                act(ways[0])
                return
            pl.when(self.role != 0)(lambda: act(ways[0]))
            pl.when(self.role == 0)(lambda: act(ways[1]))

        split(begin)
        self.loads.append((dest, lambda: split(finish)))

    def need(self, *refs):
        for number, (dest, finish) in enumerate(self.loads):
            if number not in self.waited and any(dest is ref for ref in refs):
                self.waited.add(number)
                finish()

    def rest(self):
        self.need(*[dest for dest, unused in self.loads])

    def place(self, source, target, semaphore):
        self.stores.append([source, target, semaphore, None])

    def put(self, *refs):
        for entry in self.stores:
            if entry[3] is None and any(entry[0] is ref for ref in refs):
                entry[3] = pltpu.make_async_copy(entry[0], entry[1], entry[2])
                entry[3].start()

    def finish(self):
        self.rest()
        self.put(*[entry[0] for entry in self.stores])
        for entry in self.stores:
            entry[3].wait()


def part(value, first, rows):
    return ("load", [[(value, first, 0, rows)]])


def whole(value):
    return ("load", [[(value, 0, 0, None)]])


def either(source_way, target_way):
    return ("load", [source_way, target_way])


def call(body, name, scal, active, ins, outs, scratch, aliases=()):
    args, specs, scratch_all, plan = [scal], [SM], [], []
    counts = {"load": 0, "store": 0}

    def arg(value, spec):
        args.append(value)
        specs.append(spec)
        return len(args) - 1

    held = []
    for kind, value in ins:
        if kind == "load":
            ways = [[(arg(v, HB), first, at, rows) for v, first, at, rows in way] for way in value]
            v, first, at, rows = value[0][0]
            total = max(a + r for _, _, a, r in value[0]) if rows is not None else None
            shape = v.shape if rows is None else (total,) + v.shape[1:]
            held.append(("load", ways, shape, v.dtype, max(len(w) for w in ways)))
        else:
            held.append((kind, arg(value, SM if kind == "smem" else HB)))
    vmem, sems = [], []
    for entry in held:
        if entry[0] == "load":
            vmem.append(pltpu.VMEM(entry[2], entry[3]))
            sems.append(pltpu.SemaphoreType.DMA((entry[4],)))
    for kind, shape in outs:
        if kind == "store":
            vmem.append(pltpu.VMEM(shape.shape, shape.dtype))
            sems.append(pltpu.SemaphoreType.DMA((1,)))
    count_in, count_out = len(args), len(outs)

    def kernel(*refs):
        inputs, outputs = refs[:count_in], refs[count_in : count_in + count_out]
        rest = refs[count_in + count_out :]
        buffers, semaphores = list(rest[: len(vmem)]), list(rest[len(vmem) : len(vmem) + len(sems)])
        extra = rest[len(vmem) + len(sems) :]
        scal_ref = inputs[0]

        def run():
            moves = Moves(scal_ref[2])
            given = []
            for entry in held:
                if entry[0] == "load":
                    dest, semaphore = buffers.pop(0), semaphores.pop(0)
                    ways = [[(inputs[i], f, a, r) for i, f, a, r in way] for way in entry[1]]
                    moves.load(dest, ways, semaphore)
                    given.append(dest)
                else:
                    given.append(inputs[entry[1]])
            for (kind, unused), output in zip(outs, outputs):
                if kind == "store":
                    source, semaphore = buffers.pop(0), semaphores.pop(0)
                    moves.place(source, output, semaphore.at[0])
                    given.append(source)
                else:
                    given.append(output)
            body(moves, scal_ref, *given, *extra)
            moves.finish()

        if active is None:
            run()
        else:
            pl.when(scal_ref[2] == active)(run)

    pairs = {}
    for position, output in aliases:
        pairs[held[position][1]] = output
    return pl.pallas_call(
        kernel,
        in_specs=specs,
        out_specs=[HB] * count_out,
        out_shape=[shape for unused, shape in outs],
        scratch_shapes=vmem + sems + list(scratch),
        input_output_aliases=pairs,
        compiler_params=pltpu.CompilerParams(vmem_limit_bytes=58 << 20),
        name=name,
    )(*args)


def zero_rows(width):
    return (jnp.zeros((1, width), single),) * 3


def put_rows(ref, rows):
    for number, row in enumerate(rows):
        ref[number : number + 1] = row


def project_norm(length, ctx_t, weight, inner_ref, vec, resid_ref, out_ref):
    def body(rows, carry):
        branch = mm(ctx_t[:, rows].T, weight[...])
        resid = inner_ref[rows].astype(single) * vec[0:1] + branch
        resid_ref[rows] = resid
        out_ref[rows] = normed(resid)[0] * vec[1:2] + vec[2:3]
        return carry

    by_rows(length, body)


def self_forward_body(
    io, scal, x, weight, out_weight, vec, query, key, value, ctx_t, lse, resid, out,
    query_t, value_t, key_two,
):
    length, width = x.shape
    io.need(x, weight)

    def body(rows, carry):
        tile = x[rows]
        for number, ref in enumerate((query, key, value)):
            ref[rows] = mm(tile, weight[width * number : width * (number + 1)]).astype(bfloat)
        query_t[:, rows] = (query[rows] * bfloat(0.125)).T
        value_t[:, rows] = value[rows].T
        return carry

    by_rows(length, body)
    io.put(query, key, value)
    attend(scal[0], scal[1], key, query_t, value_t, ctx_t, lse, key_two)
    io.put(ctx_t, lse)
    io.rest()
    project_norm(length, ctx_t, out_weight, x, vec, resid, out)


def encoder_ff_body(
    io, scal, inner, up, down, cross, vec, activ, slope, resid, memory, sendout
):
    length, width = inner.shape
    io.rest()

    def body(rows, carry):
        tile = inner[rows]
        act, grad = gelu_parts(mm_nt(tile.astype(bfloat), up[...]))
        act = act.astype(bfloat)
        activ[rows] = act
        slope[rows] = grad.astype(bfloat)
        total = tile * vec[0:1] + mm(act, down[...])
        resid[rows] = total
        mem = (normed(total)[0] * vec[1:2] + vec[2:3]).astype(bfloat)
        memory[rows] = mem
        sendout[0, rows] = mm(mem, cross[:width]).astype(bfloat)
        sendout[1, rows] = mm(mem, cross[width:]).astype(bfloat)
        return carry

    by_rows(length, body)


def cross_forward_body(
    io, scal, inner, keys, cross, vec, query, ctx_t, lse, resid, out, query_t, value_t, key_two
):
    rows_here, width = inner.shape
    io.need(inner, cross, keys)

    def body(rows, carry):
        query[rows] = mm(inner[rows].astype(bfloat), cross[:width]).astype(bfloat)
        query_t[:, rows] = (query[rows] * bfloat(0.125)).T
        return carry

    def turn(rows, carry):
        value_t[:, rows] = keys[1, rows].T
        return carry

    by_rows(rows_here, body)
    by_rows(keys.shape[1], turn)
    attend(scal[4], None, keys.at[0], query_t, value_t, ctx_t, lse, key_two)
    io.put(query, ctx_t, lse)
    io.rest()
    project_norm(rows_here, ctx_t, cross.at[width:], inner, vec, resid, out)


def ff_back(length, emit, grad_branch, activ, slope, inner_low, up, down, grad_inner):
    def body(rows, carry):
        grad = mm_nt(grad_branch[rows], down[...]) * slope[rows].astype(single)
        grad = grad.astype(bfloat)
        slope[rows] = grad
        grad_inner[rows] += mm(grad, up[...])
        return carry

    by_rows(length, body)
    for number in range(activ.shape[1] // 512):
        columns = slice(number * 512, (number + 1) * 512)
        emit(0, number, mm_tn(slope[:, columns], inner_low[...]))
        emit(1, number, mm_tn(activ[:, columns], grad_branch[...]))


def decoder_ff_body(
    io, scal, inner, up, down, vec, cotan, out, grad_inner, grad_vec, grads,
    activ, slope, inner_low, grad_branch,
):
    length, width = inner.shape
    io.rest()

    def body(rows, carry):
        tile = inner[rows]
        low_tile = tile.astype(bfloat)
        inner_low[rows] = low_tile
        act, grad = gelu_parts(mm_nt(low_tile, up[...]))
        act = act.astype(bfloat)
        activ[rows] = act
        slope[rows] = grad.astype(bfloat)
        total = tile * vec[0:1] + mm(act, down[...])
        out[rows] = (normed(total)[0] * vec[1:2] + vec[2:3]).astype(bfloat)
        row = lax.broadcasted_iota(jnp.int32, tile.shape, 0) + rows.start
        grad_out = jnp.where(row < scal[3], cotan[rows].astype(single), 0.0)
        grad_resid, grad_gain, grad_shift = norm_back(total, grad_out, vec[1:2])
        grad_branch[rows] = grad_resid.astype(bfloat)
        grad_inner[rows] = grad_resid * vec[0:1]
        weigh = jnp.sum(grad_resid * tile, 0, keepdims=True)
        return (carry[0] + weigh, carry[1] + grad_gain, carry[2] + grad_shift)

    put_rows(grad_vec, by_rows(length, body, zero_rows(width)))
    io.put(out, grad_vec)
    hidden = up.shape[0]

    def emit(which, number, value):
        grads[which * hidden + number * 512 : which * hidden + (number + 1) * 512] = value.astype(bfloat)

    ff_back(length, emit, grad_branch, activ, slope, inner_low, up, down, grad_inner)


def branch_back(length, resid, grad_out, inner, vec, grad_branch, grad_inner, grad_vec):
    width = resid.shape[1]

    def body(rows, carry):
        grad_resid, grad_gain, grad_shift = norm_back(resid[rows], grad_out[rows], vec[1:2])
        grad_branch[rows] = grad_resid.astype(bfloat)
        grad_inner[rows] = grad_resid * vec[0:1]
        weigh = jnp.sum(grad_resid * inner[rows].astype(single), 0, keepdims=True)
        return (carry[0] + weigh, carry[1] + grad_gain, carry[2] + grad_shift)

    put_rows(grad_vec, by_rows(length, body, zero_rows(width)))


def ctx_back(length, grad_branch, weight, ctx_t, grad_ctx, grad_ctx_t, dot_ref):
    def body(rows, carry):
        grad_ctx[rows] = mm_nt(grad_branch[rows], weight[...]).astype(bfloat)
        grad_ctx_t[:, rows] = grad_ctx[rows].T
        for head in range(HEADS):
            mine = slice(64 * head, 64 * head + 64)
            product = grad_ctx_t[mine, rows].astype(single) * ctx_t[mine, rows].astype(single)
            dot_ref[head : head + 1, rows] = jnp.sum(product, 0, keepdims=True)
        return carry

    by_rows(length, body)


def cross_back_body(
    io, scal, inner, resid, query, keys, ctx_t, lse, cross, vec, grad_out,
    sendback, grad_inner, grad_vec, grads,
    grad_branch, grad_ctx, grad_ctx_t, dot_ref, query_t, key_t, grad_key, grad_value, grad_query_t,
    key_two, value_two,
):
    rows_here, width = inner.shape
    io.need(inner, resid, vec, grad_out)
    branch_back(rows_here, resid, grad_out, inner, vec, grad_branch, grad_inner, grad_vec)
    io.rest()
    io.put(grad_vec)
    grads[width:] = mm(ctx_t[...], grad_branch[...]).astype(bfloat)
    ctx_back(rows_here, grad_branch, cross.at[width:], ctx_t, grad_ctx, grad_ctx_t, dot_ref)

    def body(rows, carry):
        query_t[:, rows] = (query[rows] * bfloat(0.125)).T
        return carry

    def turn(rows, carry):
        key_t[:, rows] = keys[0, rows].T
        return carry

    by_rows(rows_here, body)
    by_rows(keys.shape[1], turn)
    attend_back(
        scal[4], None, query, keys.at[0], keys.at[1], query_t, key_t, grad_ctx, grad_ctx_t, lse, dot_ref,
        grad_key, grad_value, grad_query_t, key_two, value_two,
    )

    def send(rows, carry):
        sendback[0, rows] = (grad_key[rows] * 0.125).astype(bfloat)
        sendback[1, rows] = grad_value[rows].astype(bfloat)
        return carry

    by_rows(keys.shape[1], send)
    io.put(sendback)

    def last(rows, carry):
        grad_query = grad_query_t[:, rows].T
        grad_inner[rows] += mm_nt(grad_query, cross[:width])
        grad_ctx[rows] = grad_query
        return carry

    by_rows(rows_here, last)
    io.put(grad_inner)
    grads[:width] = mm_tn(inner[...].astype(bfloat), grad_ctx[...]).astype(bfloat)


def encoder_back_body(
    io, scal, table, own, received, memory, cross, inner, resid, activ, slope, up, down, vec,
    grad_inner, grad_vec, target,
    grad_mem, inner_low, grad_branch, stage, semaphores,
):
    length, width = inner.shape
    emit = Emitter(table, target, stage, semaphores)
    io.need(own, received, cross, inner)

    def body(rows, carry):
        for number in range(2):
            total = own[number, rows].astype(single) + received[number, rows].astype(single)
            own[number, rows] = total.astype(bfloat)
        grad_mem[rows] = mm_nt(own[0, rows], cross[:width]) + mm_nt(own[1, rows], cross[width:])
        inner_low[rows] = inner[rows].astype(bfloat)
        return carry

    by_rows(length, body)
    io.rest()
    branch_back(length, resid, grad_mem, inner, vec, grad_branch, grad_inner, grad_vec)
    io.put(grad_vec)

    def each(which, number, value):
        emit.chunk(2 * number + which, 24 + 16 * which + 4 * number, value)

    ff_back(length, each, grad_branch, activ, slope, inner_low, up, down, grad_inner)
    io.put(grad_inner)
    emit.chunk(8, 16, mm_tn(memory[...], own[0]))
    emit.chunk(9, 20, mm_tn(memory[...], own[1]))
    emit.wait()


def self_back_body(
    io, scal, table, x, weight, out_weight, vec, resid, query, key, value, ctx_t, lse, grad_out, held,
    grad_x, grad_vec, target,
    grad_branch, grad_ctx, grad_ctx_t, dot_ref, query_t, key_t, grad_key, grad_value, grad_query_t,
    key_two, value_two, stage, semaphores,
):
    length, width = x.shape
    emit = Emitter(table, target, stage, semaphores)
    io.need(resid, grad_out, x, vec)
    branch_back(length, resid, grad_out, x, vec, grad_branch, grad_x, grad_vec)
    io.put(grad_vec)
    io.need(ctx_t, out_weight)
    emit.chunk(3, 12, mm(ctx_t[...], grad_branch[...]))
    ctx_back(length, grad_branch, out_weight, ctx_t, grad_ctx, grad_ctx_t, dot_ref)
    io.rest()

    def body(rows, carry):
        query_t[:, rows] = (query[rows] * bfloat(0.125)).T
        key_t[:, rows] = key[rows].T
        return carry

    by_rows(length, body)
    attend_back(
        scal[0], scal[1], query, key, value, query_t, key_t, grad_ctx, grad_ctx_t, lse, dot_ref,
        grad_key, grad_value, grad_query_t, key_two, value_two,
    )

    def last(rows, carry):
        parts = (
            grad_query_t[:, rows].T,
            (grad_key[rows] * 0.125).astype(bfloat),
            grad_value[rows].astype(bfloat),
        )
        total = grad_x[rows]
        for number, low_grad in enumerate(parts):
            total += mm_nt(low_grad, weight[width * number : width * (number + 1)])
        grad_x[rows] = total
        grad_branch[rows], grad_ctx[rows], value[rows] = parts
        return carry

    by_rows(length, last)
    io.put(grad_x)
    for number, ref in enumerate((grad_branch, grad_ctx, value)):
        emit.chunk(number, 4 * number, mm_tn(x[...], ref[...]))
    emit.wait()


def merge_body(io, scal, table, ff_own, ff_other, cross_own, cross_other, held, target, stage, semaphores):
    emit = Emitter(table, target, stage, semaphores)
    io.rest()
    chunk = stage.shape[1]
    for first, own, other in ((16, cross_own, cross_other), (24, ff_own, ff_other)):
        for number in range(own.shape[0] // chunk):
            rows = slice(number * chunk, (number + 1) * chunk)
            total = own[rows].astype(single) + other[rows].astype(single)
            emit.chunk((first - 16) // 4 + number, first + 4 * number, total)
    emit.wait()


def place_kernel(where, scal, table, *refs):
    sources = refs[: len(where)]
    first_out, rest_out, pieces, semaphores, out_semaphores = refs[len(where) :]
    cut = first_out.shape[0]

    def each(act):
        base = 0
        for source, ranges in zip(sources, where):
            for start, stop, distance, other, first in ranges:

                def step(slot, unused):
                    piece = table[distance, first + slot - start]
                    at = piece * 2 + (scal[0] if other == 0 else 1 - scal[0])

                    @pl.when(piece >= 0)
                    def _():
                        semaphore = semaphores.at[base + slot]
                        act(pltpu.make_async_copy(source.at[slot], pieces.at[at], semaphore))

                    return 0

                lax.fori_loop(start, stop, step, 0)
            base += source.shape[0]

    each(lambda copy: copy.start())
    each(lambda copy: copy.wait())
    outs = [
        pltpu.make_async_copy(pieces.at[pl.ds(0, cut)], first_out, out_semaphores.at[0]),
        pltpu.make_async_copy(pieces.at[pl.ds(cut, rest_out.shape[0])], rest_out, out_semaphores.at[1]),
    ]
    for copy in outs:
        copy.start()
    for copy in outs:
        copy.wait()


RING = (0, 2, 4, 6, 7, 5, 3, 1)
LEAD = 8


def round_ring(value, step):
    count = len(RING)
    return lax.ppermute(value, "wide", [(RING[i], RING[(i + step) % count]) for i in range(count)])


def swapped(value):
    return lax.ppermute(value, "narrow", [(0, 1), (1, 0)])


def step_of(up, down, across):
    return lax.optimization_barrier((round_ring(up, 1), round_ring(down, -1), swapped(across)))


def join(*values):
    return jnp.concatenate(values, 0)


def ring_gather(own):
    every, lead, half = own.shape[0], LEAD, LEAD // 2
    late = every - lead
    found = [([(0, every, 0, 0, 0)], own)]

    def ahead(value, far, near):
        ranges = [(0, lead, far, 0, 0)]
        if near is not None:
            ranges += [(lead, lead + late, near, 0, lead), (lead + late, lead + 2 * late, near, 1, lead)]
        found.append((ranges, value))

    up, down, across = step_of(own[:lead], own[:lead], own[lead:])
    found.append(([(0, late, 0, 1, lead)], across))
    ahead(up, 7, None)
    ahead(down, 1, None)
    pair = join(own[lead:], across)
    up, down, across = step_of(join(up, pair), join(down, pair), join(up, down, own[:half]))
    found.append(
        ([(0, lead, 7, 1, 0), (lead, 2 * lead, 1, 1, 0), (2 * lead, 2 * lead + half, 0, 1, 0)], across)
    )
    ahead(up, 6, 7)
    ahead(down, 2, 1)
    up, down, across = step_of(up, down, join(up[:lead], down[:lead], own[half:lead]))
    found.append(
        ([(0, lead, 6, 1, 0), (lead, 2 * lead, 2, 1, 0), (2 * lead, 2 * lead + half, 0, 1, half)], across)
    )
    ahead(up, 5, 6)
    ahead(down, 3, 2)
    up, down, across = step_of(join(up[:half], up[lead:]), down[half:], join(up[:lead], down[:lead]))
    found.append(([(0, lead, 5, 1, 0), (lead, 2 * lead, 3, 1, 0)], across))
    for value, first, near in ((up, 0, 5), (down, half, 3)):
        ranges = [(0, half, 4, 0, first), (half, half + late, near, 0, lead)]
        found.append((ranges + [(half + late, half + 2 * late, near, 1, lead)], value))
    up, down, across = step_of(
        up[half : half + late], down[half + late :], join(up[:half], down[:half])
    )
    found.append(([(0, late, 4, 0, lead)], up))
    found.append(([(0, late, 4, 1, lead)], down))
    found.append(([(0, lead, 4, 1, 0)], across))
    return found


def added(*values):
    return sum(value.astype(single) for value in values).astype(bfloat)


def ring_scatter(grads):
    lead, half = LEAD, LEAD // 2
    late = grads.shape[2] - lead

    def both(distance):
        return grads[distance, :, lead:].reshape((-1,) + grads.shape[3:])

    def mine(distance, start=0, stop=lead):
        return grads[distance, 0, start:stop]

    def other(distance, start=0, stop=lead):
        return grads[distance, 1, start:stop]

    up, down, across = step_of(grads[4, 0, lead:], grads[4, 1, lead:], other(4))
    first = added(mine(4), across)
    up = join(first[:half], added(up, grads[3, 0, lead:]), grads[3, 1, lead:])
    down = join(first[half:], grads[5, 0, lead:], added(down, grads[5, 1, lead:]))
    up, down, across = step_of(up, down, join(other(3), other(5)))
    up = join(
        added(mine(3, 0, half), across[:half], up[:half]),
        added(mine(3, half), across[half:lead]),
        added(up[half:], both(2)),
    )
    down = join(
        added(mine(5, 0, half), across[lead : lead + half]),
        added(mine(5, half), across[lead + half :], down[:half]),
        added(down[half:], both(6)),
    )
    up, down, across = step_of(up, down, join(other(2), other(6), other(0, 0, half)))
    nearest = [across[2 * lead :]]
    up = join(added(mine(2), across[:lead], up[:lead]), added(up[lead:], both(1)))
    down = join(added(mine(6), across[lead : 2 * lead], down[:lead]), added(down[lead:], both(7)))
    up, down, across = step_of(up, down, join(other(1), other(7), other(0, half)))
    nearest.append(across[2 * lead :])
    total = sum(value.astype(single) for value in (both(0), up[lead:], down[lead:]))
    up, down, across = step_of(
        added(mine(1), across[:lead], up[:lead]),
        added(mine(7), across[lead : 2 * lead], down[:lead]),
        total[late:].astype(bfloat),
    )
    first = sum(value.astype(single) for value in (mine(0), join(*nearest), up, down))
    return join(first, total[:late] + across.astype(single))


def shaped(*shape, dtype=single):
    return jax.ShapeDtypeStruct(shape, dtype)


def low(*shape):
    return jax.ShapeDtypeStruct(shape, bfloat)


def low_vm(*shape):
    return pltpu.VMEM(shape, bfloat)


def full_vm(*shape):
    return pltpu.VMEM(shape, single)


def sum_over(value, axis):
    size = lax.axis_size(axis)
    bit = 1
    while bit < size:
        value = value + lax.ppermute(value, axis, [(i, i ^ bit) for i in range(size)])
        bit *= 2
    return value


def adam(weight, gradient, first, second, step_rate, decay_rate):
    first_new = beta_one * first + (1.0 - beta_one) * gradient
    second_new = beta_two * second + (1.0 - beta_two) * gradient * gradient
    first_hat = first_new / (1.0 - beta_one**STEP)
    second_hat = second_new / (1.0 - beta_two**STEP)
    weight_new = weight - step_rate * (
        first_hat / (jnp.sqrt(second_hat) + eps_adam) + decay_rate * weight
    )
    return (weight_new, first_new, second_new)


def on_device(
    stream, cotangent, lengths, owners, master, moment_one, moment_two, vec_master, vec_one, vec_two
):
    narrow_size = lax.axis_size("narrow")
    wide_size = lax.axis_size("wide")
    owner_row = owners[0]
    capacity = master.shape[1]
    half_rows = master.shape[2]
    width = master.shape[3]
    count = owner_row.shape[0]
    counter = jnp.arange(count)
    same = owner_row[:, None] == owner_row[None, :]
    earlier = counter[None, :] < counter[:, None]
    ranks = jnp.sum((same & earlier).astype(jnp.int32), 1)
    places = (
        owner_row[:, None] * narrow_size + jnp.arange(narrow_size)[None, :]
    ) * capacity + ranks[:, None]
    on_ring = wide_size == len(RING) and narrow_size == 2 and capacity > LEAD
    wide_at, narrow_at = lax.axis_index("wide"), lax.axis_index("narrow")
    self_rows, rest_rows = 4 * width, count * half_rows * narrow_size - 4 * width
    own = master[0].astype(bfloat)
    if on_ring:
        turned = [RING.index(i) for i in range(wide_size)]
        position = jnp.array(turned)[wide_at]
        owner_ring = jnp.array(turned)[owner_row]
        distance = (owner_ring - position) % wide_size
        halves = jnp.arange(narrow_size)[None, :] ^ narrow_at
        table = ((distance[:, None] * 2 + halves) * capacity + ranks[:, None]).reshape(-1)
        slot_of = distance * capacity + ranks
        hit = slot_of[None, :] == jnp.arange(wide_size * capacity)[:, None]
        pieces = jnp.sum(hit.astype(jnp.int32) * (counter + 1)[None, :], 1) - 1
        found = ring_gather(own)
        slots_found = sum(value.shape[0] for unused, value in found)
        weight, rest = pl.pallas_call(
            partial(place_kernel, [where for where, unused in found]),
            in_specs=[SM, SM] + [HB] * len(found),
            out_specs=[HB, HB],
            out_shape=[
                low(self_rows // half_rows, half_rows, width),
                low(rest_rows // half_rows, half_rows, width),
            ],
            scratch_shapes=[
                low_vm(count * narrow_size, half_rows, width),
                pltpu.SemaphoreType.DMA((slots_found,)),
                pltpu.SemaphoreType.DMA((2,)),
            ],
            compiler_params=pltpu.CompilerParams(vmem_limit_bytes=58 << 20),
            name="place_weights",
        )(
            narrow_at.astype(jnp.int32)[None],
            pieces.reshape(wide_size, capacity).astype(jnp.int32),
            *[value for unused, value in found],
        )
        weight, rest = weight.reshape(-1, width), rest.reshape(-1, width)
    else:
        places = (
            owner_row[:, None] * narrow_size + jnp.arange(narrow_size)[None, :]
        ) * capacity + ranks[:, None]
        table = places.reshape(-1)
        gathered = lax.all_gather(own, ("wide", "narrow"), axis=0, tiled=True)
        weight = jnp.take(gathered, table, axis=0).reshape(-1, width)
        weight, rest = weight[:self_rows], weight[self_rows:]
    table = table.astype(jnp.int32)
    hidden = (rest_rows - 2 * width) // 2
    is_source = lax.axis_index("half") == 0
    x = stream[0, 0]
    length = x.shape[0]
    some = length // 2
    source_len, target_len = lengths[0, 0], lengths[1, 0]
    flag = is_source.astype(jnp.int32)
    scal = jnp.stack(
        [
            jnp.where(is_source, source_len, target_len),
            1 - flag,
            flag,
            jnp.where(is_source, target_len - some, target_len),
            source_len,
        ]
    ).astype(jnp.int32)
    self_vec = whole(jnp.where(is_source, vec_master[0:3], vec_master[6:9]))
    cross_vec, ff_vec = whole(vec_master[9:12]), whole(vec_master[12:15])
    memory_vec = whole(vec_master[3:6])
    cross_w = part(rest, 0, 2 * width)
    up_w = part(rest, 2 * width, hidden)
    down_w = part(rest, 2 * width + hidden, hidden)
    slots = low(capacity * wide_size * narrow_size, half_rows, width)

    def stage_of(chunks):
        return [
            low_vm(chunks, 512, width),
            pltpu.SemaphoreType.DMA((chunks * 512 // half_rows,)),
        ]

    def store(*shape, dtype=single):
        return ("store", shaped(*shape, dtype=dtype))

    low_out = partial(store, dtype=bfloat)
    two = low_vm(2, length, 128)
    down_half, up_half = [(1, 0)], [(0, 1)]

    rest_other = lax.ppermute(rest, "half", down_half)
    query, key, value, ctx_t, lse, resid, inner = call(
        self_forward_body,
        "self_forward",
        scal,
        None,
        [whole(x), part(weight, 0, 3 * width), part(weight, 3 * width, width), self_vec],
        [low_out(length, width)] * 3
        + [low_out(width, length), store(HEADS, length)]
        + [store(length, width)] * 2,
        [low_vm(width, length), low_vm(width, length), two],
    )
    inner_other = lax.ppermute(inner[some:], "half", down_half)
    activ, slope, ff_resid, memory, sendout = call(
        encoder_ff_body,
        "encoder_ff",
        scal,
        1,
        [whole(inner), up_w, down_w, cross_w, memory_vec],
        [low_out(length, hidden)] * 2
        + [store(length, width), low_out(length, width), low_out(2, length, width)],
        [],
    )
    sendout_other = lax.ppermute(sendout, "half", up_half)

    def shared(first, rows):
        return either([(rest_other, first, 0, rows)], [(rest, first, 0, rows)])

    mid_inner = either([(inner_other, 0, 0, some)], [(inner, 0, 0, some)])
    keys = either([(sendout, 0, 0, None)], [(sendout_other, 0, 0, None)])
    cross_query, cross_ctx_t, cross_lse, cross_resid, inner_two = call(
        cross_forward_body,
        "cross_forward",
        scal,
        None,
        [mid_inner, keys, shared(0, 2 * width), cross_vec],
        [low_out(some, width), low_out(width, some), store(HEADS, some)] + [store(some, width)] * 2,
        [low_vm(width, some), low_vm(width, length), two],
    )
    cotan = cotangent[0]
    output, grad_two, grad_ff_vec, grad_ff = call(
        decoder_ff_body,
        "decoder_ff",
        scal,
        None,
        [
            whole(inner_two),
            shared(2 * width, hidden),
            shared(2 * width + hidden, hidden),
            ff_vec,
            either([(cotan, some, 0, some)], [(cotan, 0, 0, some)]),
        ],
        [low_out(some, width), store(some, width), store(3, width), low_out(2 * hidden, width)],
        [low_vm(some, hidden), low_vm(some, hidden), low_vm(some, width), low_vm(some, width)],
    )
    output_other = lax.ppermute(output, "half", up_half)
    grad_ff_other = lax.ppermute(grad_ff, "half", up_half)

    def attn_scratch(rows):
        return (
            [low_vm(rows, width), low_vm(rows, width), low_vm(width, rows), full_vm(HEADS, rows)]
            + [low_vm(width, rows), low_vm(width, length)]
            + [full_vm(length, width), full_vm(length, width), low_vm(width, rows), two, two]
        )

    sendback, grad_one, grad_cross_vec, grad_cross = call(
        cross_back_body,
        "cross_back",
        scal,
        None,
        [
            mid_inner,
            whole(cross_resid),
            whole(cross_query),
            keys,
            whole(cross_ctx_t),
            whole(cross_lse),
            shared(0, 2 * width),
            cross_vec,
            whole(grad_two),
        ],
        [
            low_out(2, length, width),
            store(some, width),
            store(3, width),
            low_out(2 * width, width),
        ],
        attn_scratch(some),
    )
    sendback_other = lax.ppermute(sendback, "half", down_half)
    grad_one_other = lax.ppermute(grad_one, "half", up_half)
    grad_cross_other = lax.ppermute(grad_cross, "half", up_half)
    grad_inner, grad_memory_vec, target = call(
        encoder_back_body,
        "encoder_back",
        scal,
        1,
        [
            ("smem", table),
            whole(sendback),
            whole(sendback_other),
            whole(memory),
            cross_w,
            whole(inner),
            whole(ff_resid),
            whole(activ),
            whole(slope),
            up_w,
            down_w,
            memory_vec,
        ],
        [store(length, width), store(3, width), ("hbm", slots)],
        [full_vm(length, width), low_vm(length, width), low_vm(length, width)] + stage_of(10),
    )
    grad_x, grad_self_vec, target = call(
        self_back_body,
        "self_back",
        scal,
        None,
        [
            ("smem", table),
            whole(x),
            part(weight, 0, 3 * width),
            part(weight, 3 * width, width),
            self_vec,
            whole(resid),
            whole(query),
            whole(key),
            whole(value),
            whole(ctx_t),
            whole(lse),
            either(
                [(grad_inner, 0, 0, length)],
                [(grad_one, 0, 0, some), (grad_one_other, 0, some, some)],
            ),
            ("hbm", target),
        ],
        [store(length, width), store(3, width), ("hbm", slots)],
        attn_scratch(length) + stage_of(4),
        [(12, 2)],
    )
    (target,) = call(
        merge_body,
        "merge",
        scal,
        0,
        [
            ("smem", table),
            whole(grad_ff),
            whole(grad_ff_other),
            whole(grad_cross),
            whole(grad_cross_other),
            ("hbm", target),
        ],
        [("hbm", slots)],
        stage_of(10),
        [(5, 0)],
    )
    vec_grads = jnp.concatenate(
        [
            jnp.where(is_source, grad_self_vec, 0.0),
            jnp.where(is_source, grad_memory_vec, 0.0),
            jnp.where(is_source, 0.0, grad_self_vec),
            grad_cross_vec,
            grad_ff_vec,
        ],
        0,
    )
    for axis in ("narrow", "wide"):
        vec_grads = sum_over(vec_grads, axis)
    if on_ring:
        mine = ring_scatter(target.reshape(wide_size, 2, capacity, half_rows, width))
    else:
        mine = lax.psum_scatter(target, ("wide", "narrow"), scatter_dimension=0, tiled=True)
    mine, vec_grads = lax.optimization_barrier((mine, vec_grads))
    vec_grads = sum_over(vec_grads, "half")
    used = jnp.sum((owner_row == wide_at).astype(jnp.int32))
    mine = jnp.where((jnp.arange(capacity) < used)[:, None, None], mine.astype(single), 0.0)
    new_weight, new_first, new_second = adam(
        master[0], mine, moment_one[0], moment_two[0], rate_matrix, decay_matrix
    )
    vec_weight, vec_first, vec_second = adam(
        vec_master, vec_grads, vec_one, vec_two, rate_vector, 0.0
    )
    output = jnp.concatenate([output, output_other], 0)
    return (
        jnp.where(is_source, memory, output)[None, None],
        grad_x[None, None],
        new_first[None],
        new_second[None],
        new_weight[None],
        new_weight.astype(bfloat)[None],
        vec_first,
        vec_second,
        vec_weight,
    )


def solution(mesh):
    in_specs = (
        P("half", ("wide", "narrow"), None, None),
        P(("wide", "narrow"), None, None),
        P(None, ("wide", "narrow")),
        P("half", None),
        P("half", "wide", "narrow", None),
        P("half", "wide", "narrow", None),
        P("half", "wide", "narrow", None),
        P(),
        P(),
        P(),
    )
    out_specs = (
        P("half", ("wide", "narrow"), None, None),
        P("half", ("wide", "narrow"), None, None),
        P("half", "wide", "narrow", None),
        P("half", "wide", "narrow", None),
        P("half", "wide", "narrow", None),
        P("half", "wide", "narrow", None),
        P(),
        P(),
        P(),
    )
    return jax.shard_map(
        on_device, mesh=mesh, in_specs=in_specs, out_specs=out_specs, check_vma=False
    )
```

time: 775 us -> 468 us (0.60)
  waiting for transfers between devices: 502 us -> 165 us
  starting transfers between devices: 2.78 us -> 65.7 us
  blocking collectives: 57.7 us -> 0 us
  Pallas kernels: 136 us -> 183 us
  between operations: 15.8 us -> 4.24 us
  local copies, waits for them, and re-layouts: 28.4 us -> 20.6 us
    reduce_scatter x1 -> x0, waiting for transfers between devices: 243 us -> none  [on_device(): lax.psum_scatter(target, ('wide', 'narrow'), scatter_dimension=0, tiled=T...]
    all_gather x1 -> x0, waiting for transfers between devices: 171 us -> none  [on_device(): lax.all_gather(master[0].astype(bfloat), ('wide', 'narrow'), axis=0, tile...]
    ppermute x2 -> x43, waiting for transfers between devices: 87.9 us -> 165 us  [the longest x20 82.7 us: round_ring(): lax.ppermute(value, 'wide', [(RING[i], RING[(i + step) % count]) for i in...]
    ppermute x2 -> x43, starting transfers between devices: 2.7 us -> 65.7 us  [the longest x20 21.9 us: round_ring(): lax.ppermute(value, 'wide', [(RING[i], RING[(i + step) % count]) for i in...]
    psum x1 -> x0, blocking collectives: 57.7 us -> none  [on_device(): vec_total = lax.psum(vec_grads, ('half', 'wide', 'narrow'))]
    pallas_call x7 -> x9, Pallas kernels: 136 us -> 183 us  [the longest x8 173 us: call(): pl.pallas_call(kernel, in_specs=specs, out_specs=[HB] * count_out, out_sh...]
    gather x4 -> x0, local copies, waits for them, and re-layouts: 23.3 us -> none  [weight_rows(): return jnp.take(gathered, order, axis=0).reshape(-1, width)]
    select_n x10 -> x1, other arithmetic: 9.51 us -> 0.01 us  [on_device(): jnp.where(is_source, 0.0, grad_self_vec)]
  transfers between devices with their start and end apart: 4 -> 43, of which waited for: 4 -> 26; matrix products, arithmetic and copies ran while one was open for 1% -> 6% of each run, Pallas kernels for 0% -> 30%
where the time goes in v2:
time: 468 us; the launch traced here: 464 us
  Pallas kernels  183 us (39%)
  waiting for transfers between devices  165 us (35%)
  starting transfers between devices  65.7 us (14%)
  other arithmetic  25.8 us (6%)
  local copies, waits for them, and re-layouts  20.6 us (4%)
    pallas_call x8, Pallas kernels, call(): pl.pallas_call(kernel, in_specs=specs, out_specs=[HB] * count_out, out_sh...  173 us
    ppermute x20, waiting for transfers between devices, round_ring(): lax.ppermute(value, 'wide', [(RING[i], RING[(i + step) % count]) for i in...  82.7 us
    ppermute x10, waiting for transfers between devices, swapped(): return lax.ppermute(value, 'narrow', [(0, 1), (1, 0)])  73.3 us
    ppermute x20, starting transfers between devices, round_ring(): lax.ppermute(value, 'wide', [(RING[i], RING[(i + step) % count]) for i in...  21.9 us
    ppermute x1, starting transfers between devices, on_device(): inner_other = lax.ppermute(inner[some:], 'half', down_half)  13.4 us
    ppermute x10, starting transfers between devices, swapped(): return lax.ppermute(value, 'narrow', [(0, 1), (1, 0)])  10.9 us
    pallas_call x1, Pallas kernels, on_device(): pl.pallas_call(partial(place_kernel, [where for where, unused in found]),...  10.3 us
  transfers between devices with their start and end apart: 43, of which 26 were waited for; matrix products, arithmetic and copies ran while one was open for 6% of the time, Pallas kernels for 30%

profile of v2, /device:TPU:0, one launch (start us, length us, event | category | flops | bytes accessed | tf_op | source)
XLA Modules:
  0.0 464.5 jit_solution(13632793759049043491)
XLA Ops:
  2.3 3.1 collective-permute-start
  7.5 8.6 %collective-permute-done.2.refs_1_ = bf16[6,64,512]{2,1,0:T(8,128)(2,1)S(1)} collective-permute-done((bf16[6,64,512]{2,1,0:T(8,128)(2,1)S(1)}, bf16[6,64,512]{2,1,0:T(8,128)(2,1)S(1)}, u32[]{:S(2)}, u32[]{:S(2)}) %collective-permute-start.2) | collective-permute-done | bytes 393248 | tf_op jit(solution)/shard_map/ppermute | solution.py:762
  23.1 25.8 %collective-permute-done.3.refs_5_ = bf16[20,64,512]{2,1,0:T(8,128)(2,1)S(1)} collective-permute-done((bf16[20,64,512]{2,1,0:T(8,128)(2,1)S(1)}, bf16[20,64,512]{2,1,0:T(8,128)(2,1)S(1)}, u32[]{:S(2)}, u32[]{:S(2)}) %collective-permute-start.3) | collective-permute-done | bytes 1310752 | tf_op jit(solution)/shard_map/ppermute | solution.py:758
  54.4 24.4 %collective-permute-done.8.refs_7_ = bf16[20,64,512]{2,1,0:T(8,128)(2,1)S(1)} collective-permute-done((bf16[20,64,512]{2,1,0:T(8,128)(2,1)S(1)}, bf16[20,64,512]{2,1,0:T(8,128)(2,1)S(1)}, u32[]{:S(2)}, u32[]{:S(2)}) %collective-permute-start.8) | collective-permute-done | bytes 1310752 | tf_op jit(solution)/shard_map/ppermute | solution.py:762
  90.3 15.4 %collective-permute-done.11.refs_10_ = bf16[16,64,512]{2,1,0:T(8,128)(2,1)S(1)} collective-permute-done((bf16[16,64,512]{2,1,0:T(8,128)(2,1)}, bf16[16,64,512]{2,1,0:T(8,128)(2,1)S(1)}, u32[]{:S(2)}, u32[]{:S(2)}) %collective-permute-start.11) | collective-permute-done | bytes 1048608 | tf_op jit(solution)/shard_map/ppermute | solution.py:762
  114.4 5.3 %collective-permute-done.12.refs_13_ = bf16[6,64,512]{2,1,0:T(8,128)(2,1)} collective-permute-done((bf16[6,64,512]{2,1,0:T(8,128)(2,1)}, bf16[6,64,512]{2,1,0:T(8,128)(2,1)}, u32[]{:S(2)}, u32[]{:S(2)}) %collective-permute-start.12) | collective-permute-done | bytes 393248 | tf_op jit(solution)/shard_map/ppermute | solution.py:758
  121.6 10.3 %place_weights.1 = (bf16[32,64,512]{2,1,0:T(8,128)(2,1)}, bf16[80,64,512]{2,1,0:T(8,128)(2,1)}) custom-call(s32[1]{0:T(128)} %bitcast.8.scal, s32[8,14]{1,0:T(8,128)} %sub.37.table, bf16[14,64,512]{2,1,0:T(8,128)(2,1)} %copy-done.2, bf16[6,64,512]{2,1,0:T(8,128)(2,1)} %copy-done.18, bf16[8,64,512]{2,1,0:T(8,128)(2,1)} %copy-done.14, ...), custom_call_target="tpu_custom_call" | custom-call | tf_op jit(solution)/shard_map/place_weights/pallas_call | solution.py:932
  138.2 33.7 %self_forward.1 = (bf16[1024,512]{1,0:T(8,128)(2,1)}, bf16[1024,512]{1,0:T(8,128)(2,1)}, bf16[1024,512]{1,0:T(8,128)(2,1)}, bf16[512,1024]{1,0:T(8,128)(2,1)}, f...) custom-call(s32[5]{0:T(128)} %stack.19.refs_0_, bf16[1024,512]{1,0:T(8,128)(2,1)} %bitcast.202, ...), custom_call_target="tpu_custom_call" | custom-call | tf_op jit(solution)/shard_map/self_forward/pallas_call | solution.py:400
  172.0 16.5 %encoder_ff.1 = (bf16[1024,2048]{1,0:T(8,128)(2,1)}, bf16[1024,2048]{1,0:T(8,128)(2,1)}, f32[1024,512]{1,0:T(8,128)}, bf16[1024,512]{1,0:T(8,128)(2,1)}, bf16[2,1024,512]{2,1,0:T(8,128)(2,1)}) custom-call(s32[5]{0:T(128)} %stack.19.refs_0_, f32[1024,512]{1,0:T(8,128)} %get-tuple-element.90.refs_1_.refs_2_.refs_6_, bf16[5120,512]{1,0:T(8,128)(2,1)} %bitcast.176, ...), custom_call_target="tpu_custom_call" | custom-call | tf_op jit(solution)/shard_map/encoder_ff/pallas_call | solution.py:400
  190.1 13.4 %collective-permute-start.15 = (f32[512,512]{1,0:T(8,128)S(1)}, f32[512,512]{1,0:T(8,128)S(1)}, u32[]{:S(2)}, u32[]{:S(2)}) collective-permute-start(f32[512,512]{1,0:T(8,128)S(1)} %slice.260), channel_id=1, source_target_pairs={{16,0},{17,1},{18,2},{19,3},{20,4},{21,5},{22,6},{23,7},{24,8},{25... | collective-permute-start | bytes 3145736 | tf_op jit(solution)/shard_map/ppermute | solution.py:1011
  205.1 19.0 %cross_forward.1 = (bf16[512,512]{1,0:T(8,128)(2,1)}, bf16[512,512]{1,0:T(8,128)(2,1)}, f32[8,512]{1,0:T(8,128)}, f32[512,512]{1,0:T(8,128)}, f32[512,512]{1,0:T(8,128)}) custom-call(s32[5]{0:T(128)} %stack.19.refs_0_, f32[512,512]{1,0:T(8,128)} %copy-done.7, f32[1024,512]{1,0:T(8,128)} %get-tuple-element.90.refs_1_.refs_2_.refs_6_, ...), custom_call_target="tpu_custom_call" | custom-call | tf_op jit(solution)/shard_map/cross_forward/pallas_call | solution.py:400
  224.1 14.8 %decoder_ff.1 = (bf16[512,512]{1,0:T(8,128)(2,1)}, f32[512,512]{1,0:T(8,128)}, f32[3,512]{1,0:T(4,128)}, bf16[4096,512]{1,0:T(8,128)(2,1)}) custom-call(s32[5]{0:T(128)} %stack.19.refs_0_, f32[512,512]{1,0:T(8,128)} %get-tuple-element.94.refs_1_, bf16[5120,512]{1,0:T(8,128)(2,1)} %collective-permute-done.17.refs_5_.refs_2_.refs_4_.refs_9_, ...), custom_call_target="tpu_custom_call" | custom-call | tf_op jit(solution)/shard_map/decoder_ff/pallas_call | solution.py:400
  238.9 5.1 %collective-permute-start.21 = (bf16[4096,512]{1,0:T(8,128)(2,1)}, bf16[4096,512]{1,0:T(8,128)(2,1)}, u32[]{:S(2)}, u32[]{:S(2)}) collective-permute-start(bf16[4096,512]{1,0:T(8,128)(2,1)} %get-tuple-element.115.refs_2_), channel_id=1, source_target_pairs={{0,16},{1,17},{2,18},{3,19},{4,20},{5,21},{6,22},{7,23},{8,24},{9,... | collective-permute-start | bytes 12582920 | tf_op jit(solution)/shard_map/ppermute | solution.py:1055
  244.1 23.0 %cross_back.1 = (bf16[2,1024,512]{2,1,0:T(8,128)(2,1)}, f32[512,512]{1,0:T(8,128)}, f32[3,512]{1,0:T(4,128)}, bf16[1024,512]{1,0:T(8,128)(2,1)}) custom-call(s32[5]{0:T(128)} %stack.19.refs_0_, f32[512,512]{1,0:T(8,128)} %copy-done.7, f32[1024,512]{1,0:T(8,128)} %get-tuple-element.90.refs_1_.refs_2_.refs_6_, f32[512,512]{1,0:T(8,128)} %get-tuple-element.102.refs_3_, ...), custom_call_target="tpu_custom_call" | custom-call | tf_op jit(solution)/shard_map/cross_back/pallas_call | solution.py:400
  268.3 4.2 collective-permute-start.20
  276.0 23.3 %encoder_back.1 = (f32[1024,512]{1,0:T(8,128)}, f32[3,512]{1,0:T(4,128)}, bf16[224,64,512]{2,1,0:T(8,128)(2,1)}) custom-call(s32[5]{0:T(128)} %stack.19.refs_0_, s32[112]{0:T(128)} %add.216.refs_1_, bf16[2,1024,512]{2,1,0:T(8,128)(2,1)} %get-tuple-element.107.refs_2_, bf16[2,1024,512]{2,1,0:T(8,128)(2,1)} %copy-done.13, ...), custom_call_target="tpu_custom_call" | custom-call | tf_op jit(solution)/shard_map/encoder_back/pallas_call | solution.py:400
  299.3 41.3 %self_back.1 = (f32[1024,512]{1,0:T(8,128)}, f32[3,512]{1,0:T(4,128)}, bf16[224,64,512]{2,1,0:T(8,128)(2,1)}) custom-call(s32[5]{0:T(128)} %stack.19.refs_0_, s32[112]{0:T(128)} %add.216.refs_1_, bf16[1024,512]{1,0:T(8,128)(2,1)} %bitcast.203, bf16[2048,512]{1,0:T(8,128)(2,1)} %bitcast.198, ...), custom_call_target="tpu_custom_call", output_to_operand_aliasing={{2}: (15, {})} | custom-call | tf_op jit(solution)/shard_map/self_back/pallas_call | solution.py:400
  343.0 2.4 slice_bitcast_fusion.3
  346.7 2.2 slice_bitcast_fusion.14
  352.0 8.7 %collective-permute-done.23 = bf16[6,64,512]{2,1,0:T(8,128)(2,1)S(1)} collective-permute-done((bf16[6,64,512]{2,1,0:T(8,128)(2,1)S(1)}, bf16[6,64,512]{2,1,0:T(8,128)(2,1)S(1)}, u32[]{:S(2)}, u32[]{:S(2)}) %collective-permute-start.23) | collective-permute-done | bytes 393248 | tf_op jit(solution)/shard_map/ppermute | solution.py:758
  368.0 14.9 %collective-permute-done.28 = bf16[16,64,512]{2,1,0:T(8,128)(2,1)S(1)} collective-permute-done((bf16[16,64,512]{2,1,0:T(8,128)(2,1)S(1)}, bf16[16,64,512]{2,1,0:T(8,128)(2,1)S(1)}, u32[]{:S(2)}, u32[]{:S(2)}) %collective-permute-start.28) | collective-permute-done | bytes 1048608 | tf_op jit(solution)/shard_map/ppermute | solution.py:762
  382.8 3.6 collective-permute-done.27
  390.7 9.8 %collective-permute-done.31 = bf16[20,64,512]{2,1,0:T(8,128)(2,1)S(1)} collective-permute-done((bf16[20,64,512]{2,1,0:T(8,128)(2,1)S(1)}, bf16[20,64,512]{2,1,0:T(8,128)(2,1)S(1)}, u32[]{:S(2)}, u32[]{:S(2)}) %collective-permute-start.31) | collective-permute-done | bytes 1310752 | tf_op jit(solution)/shard_map/ppermute | solution.py:762
  400.5 11.6 %collective-permute-done.30 = bf16[20,64,512]{2,1,0:T(8,128)(2,1)S(1)} collective-permute-done((bf16[20,64,512]{2,1,0:T(8,128)(2,1)S(1)}, bf16[20,64,512]{2,1,0:T(8,128)(2,1)S(1)}, u32[]{:S(2)}, u32[]{:S(2)}) %collective-permute-start.30) | collective-permute-done | bytes 1310752 | tf_op jit(solution)/shard_map/ppermute | solution.py:758
  412.1 3.4 collective-permute-done.29
  424.2 10.0 %collective-permute-done.33 = bf16[20,64,512]{2,1,0:T(8,128)(2,1)} collective-permute-done((bf16[20,64,512]{2,1,0:T(8,128)(2,1)S(1)}, bf16[20,64,512]{2,1,0:T(8,128)(2,1)}, u32[]{:S(2)}, u32[]{:S(2)}) %collective-permute-start.33) | collective-permute-done | bytes 1310752 | tf_op jit(solution)/shard_map/ppermute | solution.py:758
  435.9 2.3 fusion.11
  438.3 2.1 collective-permute-start.35
  443.0 2.1 collective-permute-start.40
  445.7 4.1 collective-permute-done.40
  451.8 2.8 collective-permute-done.41
  459.4 4.2 convert_bitcast_fusion
  (213 shorter events, 89.0 us)
Async XLA Ops:
  2.3 14.9 %collective-permute-start = (bf16[8,64,512]{2,1,0:T(8,128)(2,1)S(1)}, bf16[8,64,512]{2,1,0:T(8,128)(2,1)S(1)}, u32[]{:S(2)}, u32[]{:S(2)}) collective-permute-start(bf16[8,64,512]{2,1,0:T(8,128)(2,1)S(1)} %slice.328), channel_id=1, source_target_pairs={{0,4},{4,8},{8,12},{12,14},{14,10},{10,6},{6,2},{2,0},{1,5},{5,9},... | collective-permute-start | bytes 1572872 | tf_op jit(solution)/shard_map/ppermute | solution.py:758
  5.4 13.4 %collective-permute-start.1 = (bf16[8,64,512]{2,1,0:T(8,128)(2,1)S(1)}, bf16[8,64,512]{2,1,0:T(8,128)(2,1)S(1)}, u32[]{:S(2)}, u32[]{:S(2)}) collective-permute-start(bf16[8,64,512]{2,1,0:T(8,128)(2,1)S(1)} %slice.328), channel_id=1, source_target_pairs={{0,2},{4,0},{8,4},{12,8},{14,12},{10,14},{6,10},{2,6},{1,3},{5,1},... | collective-permute-start | bytes 1572872 | tf_op jit(solution)/shard_map/ppermute | solution.py:758
  19.6 29.3 %collective-permute-start.3 = (bf16[20,64,512]{2,1,0:T(8,128)(2,1)S(1)}, bf16[20,64,512]{2,1,0:T(8,128)(2,1)S(1)}, u32[]{:S(2)}, u32[]{:S(2)}) collective-permute-start(bf16[20,64,512]{2,1,0:T(8,128)(2,1)S(1)} %get-tuple-element.179), channel_id=1, source_target_pairs={{0,4},{4,8},{8,12},{12,14},{14,10},{10,6},{6,2},{2,0},{1,5},{5,9},... | collective-permute-start | bytes 3932168 | tf_op jit(solution)/shard_map/ppermute | solution.py:758
  21.2 29.0 %collective-permute-start.4 = (bf16[20,64,512]{2,1,0:T(8,128)(2,1)S(1)}, bf16[20,64,512]{2,1,0:T(8,128)(2,1)S(1)}, u32[]{:S(2)}, u32[]{:S(2)}) collective-permute-start(bf16[20,64,512]{2,1,0:T(8,128)(2,1)S(1)} %get-tuple-element.178), channel_id=1, source_target_pairs={{0,2},{4,0},{8,4},{12,8},{14,12},{10,14},{6,10},{2,6},{1,3},{5,1},... | collective-permute-start | bytes 3932168 | tf_op jit(solution)/shard_map/ppermute | solution.py:758
  21.6 28.9 %collective-permute-start.5 = (bf16[20,64,512]{2,1,0:T(8,128)(2,1)S(1)}, bf16[20,64,512]{2,1,0:T(8,128)(2,1)}, u32[]{:S(2)}, u32[]{:S(2)}) collective-permute-start(bf16[20,64,512]{2,1,0:T(8,128)(2,1)S(1)} %get-tuple-element.180), channel_id=1, source_target_pairs={{0,1},{1,0},{2,3},{3,2},{4,5},{5,4},{6,7},{7,6},{8,9},{9,8},{10,11... | collective-permute-start | bytes 3932168 | tf_op jit(solution)/shard_map/ppermute | solution.py:762
  50.7 28.0 %collective-permute-start.8 = (bf16[20,64,512]{2,1,0:T(8,128)(2,1)S(1)}, bf16[20,64,512]{2,1,0:T(8,128)(2,1)S(1)}, u32[]{:S(2)}, u32[]{:S(2)}) collective-permute-start(bf16[20,64,512]{2,1,0:T(8,128)(2,1)S(1)} %pad_maximum_fusion.6), channel_id=1, source_target_pairs={{0,1},{1,0},{2,3},{3,2},{4,5},{5,4},{6,7},{7,6},{8,9},{9,8},{10,11... | collective-permute-start | bytes 3932168 | tf_op jit(solution)/shard_map/ppermute | solution.py:762
  52.3 27.7 %collective-permute-start.6 = (bf16[20,64,512]{2,1,0:T(8,128)(2,1)S(1)}, bf16[20,64,512]{2,1,0:T(8,128)(2,1)S(1)}, u32[]{:S(2)}, u32[]{:S(2)}) collective-permute-start(bf16[20,64,512]{2,1,0:T(8,128)(2,1)S(1)} %collective-permute-done.3.refs_5_), channel_id=1, source_target_pairs={{0,4},{4,8},{8,12},{12,14},{14,10},{10,6},{6,2},{2,0},{1,5},{5,9},... | collective-permute-start | bytes 3932168 | tf_op jit(solution)/shard_map/ppermute | solution.py:758
  53.9 27.4 %collective-permute-start.7 = (bf16[20,64,512]{2,1,0:T(8,128)(2,1)S(1)}, bf16[20,64,512]{2,1,0:T(8,128)(2,1)S(1)}, u32[]{:S(2)}, u32[]{:S(2)}) collective-permute-start(bf16[20,64,512]{2,1,0:T(8,128)(2,1)S(1)} %collective-permute-done.4.refs_6_), channel_id=1, source_target_pairs={{0,2},{4,0},{8,4},{12,8},{14,12},{10,14},{6,10},{2,6},{1,3},{5,1},... | collective-permute-start | bytes 3932168 | tf_op jit(solution)/shard_map/ppermute | solution.py:758
  84.6 21.1 %collective-permute-start.11 = (bf16[16,64,512]{2,1,0:T(8,128)(2,1)}, bf16[16,64,512]{2,1,0:T(8,128)(2,1)S(1)}, u32[]{:S(2)}, u32[]{:S(2)}) collective-permute-start(bf16[16,64,512]{2,1,0:T(8,128)(2,1)} %pad_maximum_fusion.14), channel_id=1, source_target_pairs={{0,1},{1,0},{2,3},{3,2},{4,5},{5,4},{6,7},{7,6},{8,9},{9,8},{10,11... | collective-permute-start | bytes 3145736 | tf_op jit(solution)/shard_map/ppermute | solution.py:762
  86.2 21.3 %collective-permute-start.9 = (bf16[16,64,512]{2,1,0:T(8,128)(2,1)}, bf16[16,64,512]{2,1,0:T(8,128)(2,1)S(1)}, u32[]{:S(2)}, u32[]{:S(2)}) collective-permute-start(bf16[16,64,512]{2,1,0:T(8,128)(2,1)} %pad_maximum_fusion.13), channel_id=1, source_target_pairs={{0,4},{4,8},{8,12},{12,14},{14,10},{10,6},{6,2},{2,0},{1,5},{5,9},... | collective-permute-start | bytes 3145736 | tf_op jit(solution)/shard_map/ppermute | solution.py:758
  87.7 21.1 %collective-permute-start.10 = (bf16[16,64,512]{2,1,0:T(8,128)(2,1)}, bf16[16,64,512]{2,1,0:T(8,128)(2,1)S(1)}, u32[]{:S(2)}, u32[]{:S(2)}) collective-permute-start(bf16[16,64,512]{2,1,0:T(8,128)(2,1)} %slice.250), channel_id=1, source_target_pairs={{0,2},{4,0},{8,4},{12,8},{14,12},{10,14},{6,10},{2,6},{1,3},{5,1},... | collective-permute-start | bytes 3145736 | tf_op jit(solution)/shard_map/ppermute | solution.py:758
  131.9 71.6 %collective-permute-start.17 = (bf16[5120,512]{1,0:T(8,128)(2,1)}, bf16[5120,512]{1,0:T(8,128)(2,1)}, u32[]{:S(2)}, u32[]{:S(2)}) collective-permute-start(bf16[5120,512]{1,0:T(8,128)(2,1)} %bitcast.175), channel_id=1, source_target_pairs={{16,0},{17,1},{18,2},{19,3},{20,4},{21,5},{22,6},{23,7},{24,8},{25... | collective-permute-start | bytes 15728648 | tf_op jit(solution)/shard_map/ppermute | solution.py:999
  188.5 14.9 %collective-permute-start.16 = (bf16[2,1024,512]{2,1,0:T(8,128)(2,1)}, bf16[2,1024,512]{2,1,0:T(8,128)(2,1)S(1)}, u32[]{:S(2)}, u32[]{:S(2)}) collective-permute-start(bf16[2,1024,512]{2,1,0:T(8,128)(2,1)} %get-tuple-element.93.refs_3_.refs_5_), channel_id=1, source_target_pairs={{0,16},{1,17},{2,18},{3,19},{4,20},{5,21},{6,22},{7,23},{8,24},{9,... | collective-permute-start | bytes 6291464 | tf_op jit(solution)/shard_map/ppermute | solution.py:1022
  190.1 13.4 %collective-permute-start.15 = (f32[512,512]{1,0:T(8,128)S(1)}, f32[512,512]{1,0:T(8,128)S(1)}, u32[]{:S(2)}, u32[]{:S(2)}) collective-permute-start(f32[512,512]{1,0:T(8,128)S(1)} %slice.260), channel_id=1, source_target_pairs={{16,0},{17,1},{18,2},{19,3},{20,4},{21,5},{22,6},{23,7},{24,8},{25... | collective-permute-start | bytes 3145736 | tf_op jit(solution)/shard_map/ppermute | solution.py:1011
  238.9 101.7 %collective-permute-start.21 = (bf16[4096,512]{1,0:T(8,128)(2,1)}, bf16[4096,512]{1,0:T(8,128)(2,1)}, u32[]{:S(2)}, u32[]{:S(2)}) collective-permute-start(bf16[4096,512]{1,0:T(8,128)(2,1)} %get-tuple-element.115.refs_2_), channel_id=1, source_target_pairs={{0,16},{1,17},{2,18},{3,19},{4,20},{5,21},{6,22},{7,23},{8,24},{9,... | collective-permute-start | bytes 12582920 | tf_op jit(solution)/shard_map/ppermute | solution.py:1055
  268.3 31.0 %collective-permute-start.20 = (f32[512,512]{1,0:T(8,128)}, f32[512,512]{1,0:T(8,128)}, u32[]{:S(2)}, u32[]{:S(2)}) collective-permute-start(f32[512,512]{1,0:T(8,128)} %get-tuple-element.112.refs_13_), channel_id=1, source_target_pairs={{0,16},{1,17},{2,18},{3,19},{4,20},{5,21},{6,22},{7,23},{8,24},{9,... | collective-permute-start | bytes 3145736 | tf_op jit(solution)/shard_map/ppermute | solution.py:1089
  272.5 68.1 %collective-permute-start.22 = (bf16[1024,512]{1,0:T(8,128)(2,1)}, bf16[1024,512]{1,0:T(8,128)(2,1)S(1)}, u32[]{:S(2)}, u32[]{:S(2)}) collective-permute-start(bf16[1024,512]{1,0:T(8,128)(2,1)} %get-tuple-element.116.refs_4_), channel_id=1, source_target_pairs={{0,16},{1,17},{2,18},{3,19},{4,20},{5,21},{6,22},{7,23},{8,24},{9,... | collective-permute-start | bytes 3145736 | tf_op jit(solution)/shard_map/ppermute | solution.py:1090
  345.4 17.0 %collective-permute-start.25 = (bf16[8,64,512]{2,1,0:T(8,128)(2,1)S(1)}, bf16[8,64,512]{2,1,0:T(8,128)(2,1)S(1)}, u32[]{:S(2)}, u32[]{:S(2)}) collective-permute-start(bf16[8,64,512]{2,1,0:T(8,128)(2,1)S(1)} %get-tuple-element.160), channel_id=1, source_target_pairs={{0,1},{1,0},{2,3},{3,2},{4,5},{5,4},{6,7},{7,6},{8,9},{9,8},{10,11... | collective-permute-start | bytes 1572872 | tf_op jit(solution)/shard_map/ppermute | solution.py:762
  351.1 31.7 %collective-permute-start.28 = (bf16[16,64,512]{2,1,0:T(8,128)(2,1)S(1)}, bf16[16,64,512]{2,1,0:T(8,128)(2,1)S(1)}, u32[]{:S(2)}, u32[]{:S(2)}) collective-permute-start(bf16[16,64,512]{2,1,0:T(8,128)(2,1)S(1)} %pad_maximum_fusion.17), channel_id=1, source_target_pairs={{0,1},{1,0},{2,3},{3,2},{4,5},{5,4},{6,7},{7,6},{8,9},{9,8},{10,11... | collective-permute-start | bytes 3145736 | tf_op jit(solution)/shard_map/ppermute | solution.py:762
  364.0 22.4 %collective-permute-start.27 = (bf16[16,64,512]{2,1,0:T(8,128)(2,1)S(1)}, bf16[16,64,512]{2,1,0:T(8,128)(2,1)S(1)}, u32[]{:S(2)}, u32[]{:S(2)}) collective-permute-start(bf16[16,64,512]{2,1,0:T(8,128)(2,1)S(1)} %pad_maximum_fusion.16), channel_id=1, source_target_pairs={{0,2},{4,0},{8,4},{12,8},{14,12},{10,14},{6,10},{2,6},{1,3},{5,1},... | collective-permute-start | bytes 3145736 | tf_op jit(solution)/shard_map/ppermute | solution.py:758
  364.8 21.6 %collective-permute-start.26 = (bf16[16,64,512]{2,1,0:T(8,128)(2,1)S(1)}, bf16[16,64,512]{2,1,0:T(8,128)(2,1)S(1)}, u32[]{:S(2)}, u32[]{:S(2)}) collective-permute-start(bf16[16,64,512]{2,1,0:T(8,128)(2,1)S(1)} %pad_maximum_fusion.15), channel_id=1, source_target_pairs={{0,4},{4,8},{8,12},{12,14},{14,10},{10,6},{6,2},{2,0},{1,5},{5,9},... | collective-permute-start | bytes 3145736 | tf_op jit(solution)/shard_map/ppermute | solution.py:758
  366.7 33.8 %collective-permute-start.31 = (bf16[20,64,512]{2,1,0:T(8,128)(2,1)S(1)}, bf16[20,64,512]{2,1,0:T(8,128)(2,1)S(1)}, u32[]{:S(2)}, u32[]{:S(2)}) collective-permute-start(bf16[20,64,512]{2,1,0:T(8,128)(2,1)S(1)} %pad_maximum_fusion.9), channel_id=1, source_target_pairs={{0,1},{1,0},{2,3},{3,2},{4,5},{5,4},{6,7},{7,6},{8,9},{9,8},{10,11... | collective-permute-start | bytes 3932168 | tf_op jit(solution)/shard_map/ppermute | solution.py:762
  387.2 24.9 %collective-permute-start.30 = (bf16[20,64,512]{2,1,0:T(8,128)(2,1)S(1)}, bf16[20,64,512]{2,1,0:T(8,128)(2,1)S(1)}, u32[]{:S(2)}, u32[]{:S(2)}) collective-permute-start(bf16[20,64,512]{2,1,0:T(8,128)(2,1)S(1)} %pad_maximum_fusion.8), channel_id=1, source_target_pairs={{0,2},{4,0},{8,4},{12,8},{14,12},{10,14},{6,10},{2,6},{1,3},{5,1},... | collective-permute-start | bytes 3932168 | tf_op jit(solution)/shard_map/ppermute | solution.py:758
  388.3 27.3 %collective-permute-start.29 = (bf16[20,64,512]{2,1,0:T(8,128)(2,1)S(1)}, bf16[20,64,512]{2,1,0:T(8,128)(2,1)S(1)}, u32[]{:S(2)}, u32[]{:S(2)}) collective-permute-start(bf16[20,64,512]{2,1,0:T(8,128)(2,1)S(1)} %pad_maximum_fusion.7), channel_id=1, source_target_pairs={{0,4},{4,8},{8,12},{12,14},{14,10},{10,6},{6,2},{2,0},{1,5},{5,9},... | collective-permute-start | bytes 3932168 | tf_op jit(solution)/shard_map/ppermute | solution.py:758
  389.9 34.3 %collective-permute-start.34 = (bf16[20,64,512]{2,1,0:T(8,128)(2,1)S(1)}, bf16[20,64,512]{2,1,0:T(8,128)(2,1)}, u32[]{:S(2)}, u32[]{:S(2)}) collective-permute-start(bf16[20,64,512]{2,1,0:T(8,128)(2,1)S(1)} %pad_maximum_fusion.12), channel_id=1, source_target_pairs={{0,1},{1,0},{2,3},{3,2},{4,5},{5,4},{6,7},{7,6},{8,9},{9,8},{10,11... | collective-permute-start | bytes 3932168 | tf_op jit(solution)/shard_map/ppermute | solution.py:762
  416.5 17.8 %collective-permute-start.33 = (bf16[20,64,512]{2,1,0:T(8,128)(2,1)S(1)}, bf16[20,64,512]{2,1,0:T(8,128)(2,1)}, u32[]{:S(2)}, u32[]{:S(2)}) collective-permute-start(bf16[20,64,512]{2,1,0:T(8,128)(2,1)S(1)} %pad_maximum_fusion.11), channel_id=1, source_target_pairs={{0,2},{4,0},{8,4},{12,8},{14,12},{10,14},{6,10},{2,6},{1,3},{5,1},... | collective-permute-start | bytes 3932168 | tf_op jit(solution)/shard_map/ppermute | solution.py:758
  418.0 17.9 %collective-permute-start.32 = (bf16[20,64,512]{2,1,0:T(8,128)(2,1)}, bf16[20,64,512]{2,1,0:T(8,128)(2,1)}, u32[]{:S(2)}, u32[]{:S(2)}) collective-permute-start(bf16[20,64,512]{2,1,0:T(8,128)(2,1)} %pad_maximum_fusion.10), channel_id=1, source_target_pairs={{0,4},{4,8},{8,12},{12,14},{14,10},{10,6},{6,2},{2,0},{1,5},{5,9},... | collective-permute-start | bytes 3932168 | tf_op jit(solution)/shard_map/ppermute | solution.py:758
  420.9 29.6 %collective-permute-start.18 = (bf16[512,512]{1,0:T(8,128)(2,1)}, bf16[512,512]{1,0:T(8,128)(2,1)S(1)}, u32[]{:S(2)}, u32[]{:S(2)}) collective-permute-start(bf16[512,512]{1,0:T(8,128)(2,1)} %get-tuple-element.95), channel_id=1, source_target_pairs={{0,16},{1,17},{2,18},{3,19},{4,20},{5,21},{6,22},{7,23},{8,24},{9,... | collective-permute-start | bytes 1572872 | tf_op jit(solution)/shard_map/ppermute | solution.py:1054
  424.2 18.8 %collective-permute-start.39 = (f32[15,512]{1,0:T(8,128)S(1)}, f32[15,512]{1,0:T(8,128)S(1)}, u32[]{:S(2)}, u32[]{:S(2)}) collective-permute-start(f32[15,512]{1,0:T(8,128)S(1)} %add.244), channel_id=1, source_target_pairs={{0,2},{2,0},{4,6},{6,4},{8,10},{10,8},{12,14},{14,12},{1,3},{3,1},... | collective-permute-start | bytes 92168 | tf_op jit(solution)/shard_map/ppermute | solution.py:883
  438.3 17.4 %collective-permute-start.35 = (bf16[8,64,512]{2,1,0:T(8,128)(2,1)S(1)}, bf16[8,64,512]{2,1,0:T(8,128)(2,1)S(1)}, u32[]{:S(2)}, u32[]{:S(2)}) collective-permute-start(bf16[8,64,512]{2,1,0:T(8,128)(2,1)S(1)} %get-tuple-element.147), channel_id=1, source_target_pairs={{0,4},{4,8},{8,12},{12,14},{14,10},{10,6},{6,2},{2,0},{1,5},{5,9},... | collective-permute-start | bytes 1572872 | tf_op jit(solution)/shard_map/ppermute | solution.py:758
  440.3 15.4 %collective-permute-start.36 = (bf16[8,64,512]{2,1,0:T(8,128)(2,1)S(1)}, bf16[8,64,512]{2,1,0:T(8,128)(2,1)S(1)}, u32[]{:S(2)}, u32[]{:S(2)}) collective-permute-start(bf16[8,64,512]{2,1,0:T(8,128)(2,1)S(1)} %get-tuple-element.146), channel_id=1, source_target_pairs={{0,2},{4,0},{8,4},{12,8},{14,12},{10,14},{6,10},{2,6},{1,3},{5,1},... | collective-permute-start | bytes 1572872 | tf_op jit(solution)/shard_map/ppermute | solution.py:758
  442.3 13.4 %collective-permute-start.37 = (bf16[6,64,512]{2,1,0:T(8,128)(2,1)S(1)}, bf16[6,64,512]{2,1,0:T(8,128)(2,1)S(1)}, u32[]{:S(2)}, u32[]{:S(2)}) collective-permute-start(bf16[6,64,512]{2,1,0:T(8,128)(2,1)S(1)} %slice.439), channel_id=1, source_target_pairs={{0,1},{1,0},{2,3},{3,2},{4,5},{5,4},{6,7},{7,6},{8,9},{9,8},{10,11... | collective-permute-start | bytes 1179656 | tf_op jit(solution)/shard_map/ppermute | solution.py:762
  (50 other events, 291.7 us)

commit v3 on v2

--- a/solution.py
+++ b/solution.py
@@ -10,8 +10,8 @@
 
 HEADS = 8
 STEP = 5
-QB = 256
-RB = 256
+CAUSAL = 512
+RB = 512
 NEG = -1e30
 
 eps_norm = 1e-05
@@ -116,11 +116,7 @@
 
 def over_blocks(causal, rows, length, body):
     def every():
-        def step(index, unused):
-            body(index, length, False)
-            return 0
-
-        lax.fori_loop(0, rows // QB, step, 0)
+        body(0, rows, length, False)
 
     if causal is None:
         every()
@@ -129,40 +125,53 @@
 
     @pl.when(causal != 0)
     def _():
-        for index in range(length // QB):
-            body(index, (index + 1) * QB, True)
-
-
-def attend(limit, causal, key_ref, query_t, value_t, ctx_t, lse_ref, key_two):
+        for first in range(0, rows, CAUSAL):
+            body(first, CAUSAL, first + CAUSAL, True)
+
+
+def head_rows(group, heads, head):
+    return pl.ds(pl.multiple_of((group * heads + head) * 64, 64), 64)
+
+
+def attend(limit, causal, key_ref, query_t, value_t, ctx_t, lse_ref, key_tiles):
     length, width = key_ref.shape
+    heads = key_tiles.shape[0]
     bias = key_bias(limit, length)
 
-    def pair(number, unused):
-        columns = block_of(number, 128)
-        for head, tile in enumerate(pair_keys(key_ref[:, columns], bias, 1)):
-            key_two[head] = tile
-
-        def body(index, extent, diagonal):
-            at = block_of(index, QB)
-            tile = query_t[columns, at]
-            for head in range(2):
-                mine = pl.ds(pl.multiple_of(number * 128 + 64 * head, 64), 64)
-                scores = mm(key_two[head, :extent], pair_queries(tile, head, [1.0]))
-                parts = score_parts(scores, diagonal)
+    def group_of(group, unused):
+        for number in range(heads // 2):
+            columns = block_of(group * (heads // 2) + number, 128)
+            for head, tile in enumerate(pair_keys(key_ref[:, columns], bias, 1)):
+                key_tiles[2 * number + head] = tile
+
+        def body(first, queries, extent, diagonal):
+            at = slice(first, first + queries)
+
+            def scores_of(head):
+                columns = block_of(group * (heads // 2) + head // 2, 128)
+                tile = pair_queries(query_t[columns, at], head % 2, [1.0])
+                return mm(key_tiles[head, :extent], tile)
+
+            following = scores_of(0)
+            for head in range(heads):
+                parts = score_parts(following, diagonal)
+                if head + 1 < heads:
+                    following = scores_of(head + 1)
                 top = jnp.max(parts[0], 0, keepdims=True)
-                for part in parts[1:]:
-                    top = jnp.maximum(top, jnp.max(part, 0, keepdims=True))
-                parts = [jnp.exp(part - top) for part in parts]
-                total = sum(jnp.sum(part, 0, keepdims=True) for part in parts)
-                weights = jnp.concatenate([part.astype(bfloat) for part in parts], 0)
+                for more in parts[1:]:
+                    top = jnp.maximum(top, jnp.max(more, 0, keepdims=True))
+                parts = [jnp.exp(more - top) for more in parts]
+                total = sum(jnp.sum(more, 0, keepdims=True) for more in parts)
+                weights = jnp.concatenate([more.astype(bfloat) for more in parts], 0)
+                mine = head_rows(group, heads, head)
                 context = mm(value_t[mine, :extent], weights)
                 ctx_t[mine, at] = (context * (1.0 / total)).astype(bfloat)
-                lse_ref[pl.ds(number * 2 + head, 1), at] = top + jnp.log(total)
+                lse_ref[pl.ds(group * heads + head, 1), at] = top + jnp.log(total)
 
         over_blocks(causal, query_t.shape[1], length, body)
         return 0
 
-    lax.fori_loop(0, width // 128, pair, 0)
+    lax.fori_loop(0, HEADS // heads, group_of, 0)
 
 
 def attend_back(
@@ -171,8 +180,6 @@
 ):
     length, width = key_ref.shape
     bias = key_bias(limit, length)
-    grad_key[...] = jnp.zeros(grad_key.shape, single)
-    grad_value[...] = jnp.zeros(grad_value.shape, single)
 
     def pair(number, unused):
         columns = block_of(number, 128)
@@ -181,28 +188,22 @@
         for head, tile in enumerate(pair_keys(value_ref[:, columns], 1.0, 3)):
             value_two[head] = tile
 
-        def body(index, extent, diagonal):
-            at = block_of(index, QB)
-            query_tile = query_t[columns, at]
-            ctx_tile = grad_ctx_t[columns, at]
-            all_weights, all_grads = [], []
-            for head in range(2):
-                mine = pl.ds(pl.multiple_of(number * 128 + 64 * head, 64), 64)
+        def body(first, queries, extent, diagonal):
+            at = slice(first, first + queries)
+
+            def products_of(head):
                 row = pl.ds(number * 2 + head, 1)
-                minus_lse = split_three(-lse_ref[row, at])
+                constants = [1.0] + split_three(-lse_ref[row, at])
                 scores = mm(
-                    key_two[head, :extent], pair_queries(query_tile, head, [1.0] + minus_lse)
+                    key_two[head, :extent], pair_queries(query_t[columns, at], head, constants)
                 )
-                weights = [jnp.exp(part) for part in score_parts(scores, diagonal)]
-                weights = jnp.concatenate(weights, 0)
-                minus_dot = split_three(-dot_ref[row, at])
-                grad_weights = mm(value_two[head, :extent], pair_queries(ctx_tile, head, minus_dot))
-                grads = (weights * grad_weights).astype(bfloat)
-                all_weights.append(weights.astype(bfloat))
-                all_grads.append(grads)
-                grad_query = mm(key_t[mine, :extent], grads)
-                grad_query_t[mine, at] = (grad_query * 0.125).astype(bfloat)
-            lane = lax.broadcasted_iota(jnp.int32, (QB, 128), 1)
+                constants = split_three(-dot_ref[row, at])
+                grad_weights = mm(
+                    value_two[head, :extent], pair_queries(grad_ctx_t[columns, at], head, constants)
+                )
+                return scores, grad_weights
+
+            lane = lax.broadcasted_iota(jnp.int32, (queries, 128), 1)
 
             def both(tile):
                 tile = tile.astype(single)
@@ -214,12 +215,28 @@
                     0,
                 )
 
-            grad_value[:extent, columns] += mm(
-                jnp.concatenate(all_weights, 1), both(grad_ctx[at, columns])
-            )
-            grad_key[:extent, columns] += mm(
-                jnp.concatenate(all_grads, 1), both(query_ref[at, columns])
-            )
+            all_weights, all_grads = [], []
+            following = products_of(0)
+            for head in range(2):
+                scores, grad_weights = following
+                if head == 0:
+                    following = products_of(1)
+                weights = [jnp.exp(more) for more in score_parts(scores, diagonal)]
+                weights = jnp.concatenate(weights, 0)
+                grads = (weights * grad_weights).astype(bfloat)
+                all_weights.append(weights.astype(bfloat))
+                all_grads.append(grads)
+                mine = head_rows(number, 2, head)
+                grad_query = mm(key_t[mine, :extent], grads)
+                grad_query_t[mine, at] = (grad_query * 0.125).astype(bfloat)
+            for out, parts, other in (
+                (grad_value, all_weights, grad_ctx),
+                (grad_key, all_grads, query_ref),
+            ):
+                total = mm(jnp.concatenate(parts, 1), both(other[at, columns]))
+                if first:
+                    total = jnp.concatenate([out[:first, columns] + total[:first], total[first:]], 0)
+                out[:extent, columns] = total
 
         over_blocks(causal, query_t.shape[1], length, body)
         return 0
@@ -331,7 +348,7 @@
     return ("load", [source_way, target_way])
 
 
-def call(body, name, scal, active, ins, outs, scratch, aliases=()):
+def call(body, name, scal, active, ins, outs, scratch, aliases=(), limit=58):
     args, specs, scratch_all, plan = [scal], [SM], [], []
     counts = {"load": 0, "store": 0}
 
@@ -404,7 +421,7 @@
         out_shape=[shape for unused, shape in outs],
         scratch_shapes=vmem + sems + list(scratch),
         input_output_aliases=pairs,
-        compiler_params=pltpu.CompilerParams(vmem_limit_bytes=58 << 20),
+        compiler_params=pltpu.CompilerParams(vmem_limit_bytes=62 << 20),
         name=name,
     )(*args)
 
@@ -429,12 +446,11 @@
     by_rows(length, body)
 
 
-def self_forward_body(
-    io, scal, x, weight, out_weight, vec, query, key, value, ctx_t, lse, resid, out,
-    query_t, value_t, key_two,
-):
+def self_forward(io, scal, x, weight, vec, outs, query_t, value_t, key_tiles, ready):
+    query, key, value, ctx_t, lse, resid, out = outs
     length, width = x.shape
-    io.need(x, weight)
+    io.need(x)
+    ready()
 
     def body(rows, carry):
         tile = x[rows]
@@ -446,10 +462,47 @@
 
     by_rows(length, body)
     io.put(query, key, value)
-    attend(scal[0], scal[1], key, query_t, value_t, ctx_t, lse, key_two)
+    attend(scal[0], scal[1], key, query_t, value_t, ctx_t, lse, key_tiles)
     io.put(ctx_t, lse)
     io.rest()
-    project_norm(length, ctx_t, out_weight, x, vec, resid, out)
+    project_norm(length, ctx_t, weight.at[3 * width :], x, vec, resid, out)
+
+
+def self_forward_body(io, scal, x, weight, vec, *refs):
+    self_forward(io, scal, x, weight, vec, refs[:7], *refs[7:], lambda: io.need(weight))
+
+
+def placed_forward_body(where, io, scal, table, x, vec, *refs):
+    sources, refs = refs[: len(where)], refs[len(where) :]
+    outs, (weight, rest) = refs[:7], refs[7:9]
+    query_t, value_t, key_tiles, semaphores = refs[9:]
+    size = sources[0].shape[1]
+    cut = weight.shape[0] // size
+
+    for source, ranges in zip(sources, where):
+        for start, stop, distance, other, first in ranges:
+
+            def step(slot, unused):
+                piece = table[distance, first + slot - start]
+                at = piece * 2 + (scal[5] if other == 0 else 1 - scal[5])
+
+                def move(target, place, semaphore):
+                    place = pl.ds(pl.multiple_of(place * size, size), size)
+                    pltpu.make_async_copy(source.at[slot], target.at[place], semaphore).start()
+
+                pl.when((piece >= 0) & (at < cut))(lambda: move(weight, at, semaphores.at[0]))
+                pl.when(at >= cut)(lambda: move(rest, at - cut, semaphores.at[1]))
+                return 0
+
+            lax.fori_loop(start, stop, step, 0)
+
+    def ready():
+        pltpu.make_async_copy(weight, weight, semaphores.at[0]).wait()
+        io.put(weight)
+
+    self_forward(io, scal, x, weight, vec, outs, query_t, value_t, key_tiles, ready)
+    pltpu.make_async_copy(rest, rest, semaphores.at[1]).wait()
+    io.put(rest)
 
 
 def encoder_ff_body(
@@ -475,29 +528,6 @@
     by_rows(length, body)
 
 
-def cross_forward_body(
-    io, scal, inner, keys, cross, vec, query, ctx_t, lse, resid, out, query_t, value_t, key_two
-):
-    rows_here, width = inner.shape
-    io.need(inner, cross, keys)
-
-    def body(rows, carry):
-        query[rows] = mm(inner[rows].astype(bfloat), cross[:width]).astype(bfloat)
-        query_t[:, rows] = (query[rows] * bfloat(0.125)).T
-        return carry
-
-    def turn(rows, carry):
-        value_t[:, rows] = keys[1, rows].T
-        return carry
-
-    by_rows(rows_here, body)
-    by_rows(keys.shape[1], turn)
-    attend(scal[4], None, keys.at[0], query_t, value_t, ctx_t, lse, key_two)
-    io.put(query, ctx_t, lse)
-    io.rest()
-    project_norm(rows_here, ctx_t, cross.at[width:], inner, vec, resid, out)
-
-
 def ff_back(length, emit, grad_branch, activ, slope, inner_low, up, down, grad_inner):
     def body(rows, carry):
         grad = mm_nt(grad_branch[rows], down[...]) * slope[rows].astype(single)
@@ -511,41 +541,6 @@
         columns = slice(number * 512, (number + 1) * 512)
         emit(0, number, mm_tn(slope[:, columns], inner_low[...]))
         emit(1, number, mm_tn(activ[:, columns], grad_branch[...]))
-
-
-def decoder_ff_body(
-    io, scal, inner, up, down, vec, cotan, out, grad_inner, grad_vec, grads,
-    activ, slope, inner_low, grad_branch,
-):
-    length, width = inner.shape
-    io.rest()
-
-    def body(rows, carry):
-        tile = inner[rows]
-        low_tile = tile.astype(bfloat)
-        inner_low[rows] = low_tile
-        act, grad = gelu_parts(mm_nt(low_tile, up[...]))
-        act = act.astype(bfloat)
-        activ[rows] = act
-        slope[rows] = grad.astype(bfloat)
-        total = tile * vec[0:1] + mm(act, down[...])
-        out[rows] = (normed(total)[0] * vec[1:2] + vec[2:3]).astype(bfloat)
-        row = lax.broadcasted_iota(jnp.int32, tile.shape, 0) + rows.start
-        grad_out = jnp.where(row < scal[3], cotan[rows].astype(single), 0.0)
-        grad_resid, grad_gain, grad_shift = norm_back(total, grad_out, vec[1:2])
-        grad_branch[rows] = grad_resid.astype(bfloat)
-        grad_inner[rows] = grad_resid * vec[0:1]
-        weigh = jnp.sum(grad_resid * tile, 0, keepdims=True)
-        return (carry[0] + weigh, carry[1] + grad_gain, carry[2] + grad_shift)
-
-    put_rows(grad_vec, by_rows(length, body, zero_rows(width)))
-    io.put(out, grad_vec)
-    hidden = up.shape[0]
-
-    def emit(which, number, value):
-        grads[which * hidden + number * 512 : which * hidden + (number + 1) * 512] = value.astype(bfloat)
-
-    ff_back(length, emit, grad_branch, activ, slope, inner_low, up, down, grad_inner)
 
 
 def branch_back(length, resid, grad_out, inner, vec, grad_branch, grad_inner, grad_vec):
@@ -574,30 +569,63 @@
     by_rows(length, body)
 
 
-def cross_back_body(
-    io, scal, inner, resid, query, keys, ctx_t, lse, cross, vec, grad_out,
-    sendback, grad_inner, grad_vec, grads,
-    grad_branch, grad_ctx, grad_ctx_t, dot_ref, query_t, key_t, grad_key, grad_value, grad_query_t,
-    key_two, value_two,
+def middle_body(
+    io, scal, inner, keys, cross, cross_vec, up, down, ff_vec, cotan,
+    output, sendback, grad_inner, grads, grad_vec,
+    query, query_t, ctx_t, lse, resid, after, activ, slope, low_rows, grad_branch, grad_after,
+    grad_ctx, grad_ctx_t, dot_ref, key_t, value_t, grad_key, grad_value, grad_query_t,
+    key_tiles, key_two, value_two,
 ):
     rows_here, width = inner.shape
-    io.need(inner, resid, vec, grad_out)
-    branch_back(rows_here, resid, grad_out, inner, vec, grad_branch, grad_inner, grad_vec)
-    io.rest()
-    io.put(grad_vec)
-    grads[width:] = mm(ctx_t[...], grad_branch[...]).astype(bfloat)
-    ctx_back(rows_here, grad_branch, cross.at[width:], ctx_t, grad_ctx, grad_ctx_t, dot_ref)
-
-    def body(rows, carry):
+    hidden = up.shape[0]
+    io.need(inner, cross, keys)
+
+    def project(rows, carry):
+        query[rows] = mm(inner[rows].astype(bfloat), cross[:width]).astype(bfloat)
         query_t[:, rows] = (query[rows] * bfloat(0.125)).T
         return carry
 
     def turn(rows, carry):
         key_t[:, rows] = keys[0, rows].T
+        value_t[:, rows] = keys[1, rows].T
         return carry
 
-    by_rows(rows_here, body)
+    by_rows(rows_here, project)
     by_rows(keys.shape[1], turn)
+    attend(scal[4], None, keys.at[0], query_t, value_t, ctx_t, lse, key_tiles)
+    io.rest()
+    project_norm(rows_here, ctx_t, cross.at[width:], inner, cross_vec, resid, after)
+
+    def feed(rows, carry):
+        tile = after[rows]
+        low_tile = tile.astype(bfloat)
+        low_rows[rows] = low_tile
+        act, grad = gelu_parts(mm_nt(low_tile, up[...]))
+        act = act.astype(bfloat)
+        activ[rows] = act
+        slope[rows] = grad.astype(bfloat)
+        total = tile * ff_vec[0:1] + mm(act, down[...])
+        output[rows] = (normed(total)[0] * ff_vec[1:2] + ff_vec[2:3]).astype(bfloat)
+        row = lax.broadcasted_iota(jnp.int32, tile.shape, 0) + rows.start
+        grad_out = jnp.where(row < scal[3], cotan[rows].astype(single), 0.0)
+        grad_resid, grad_gain, grad_shift = norm_back(total, grad_out, ff_vec[1:2])
+        grad_branch[rows] = grad_resid.astype(bfloat)
+        grad_after[rows] = grad_resid * ff_vec[0:1]
+        weigh = jnp.sum(grad_resid * tile, 0, keepdims=True)
+        return (carry[0] + weigh, carry[1] + grad_gain, carry[2] + grad_shift)
+
+    put_rows(grad_vec.at[3:], by_rows(rows_here, feed, zero_rows(width)))
+    io.put(output)
+
+    def emit(which, number, value):
+        first = 2 * width + which * hidden + number * 512
+        grads[first : first + 512] = value.astype(bfloat)
+
+    ff_back(rows_here, emit, grad_branch, activ, slope, low_rows, up, down, grad_after)
+    branch_back(rows_here, resid, grad_after, inner, cross_vec, grad_branch, grad_inner, grad_vec)
+    io.put(grad_vec)
+    grads[width : 2 * width] = mm(ctx_t[...], grad_branch[...]).astype(bfloat)
+    ctx_back(rows_here, grad_branch, cross.at[width:], ctx_t, grad_ctx, grad_ctx_t, dot_ref)
     attend_back(
         scal[4], None, query, keys.at[0], keys.at[1], query_t, key_t, grad_ctx, grad_ctx_t, lse, dot_ref,
         grad_key, grad_value, grad_query_t, key_two, value_two,
@@ -701,52 +729,15 @@
     emit.wait()
 
 
-def merge_body(io, scal, table, ff_own, ff_other, cross_own, cross_other, held, target, stage, semaphores):
+def merge_body(io, scal, table, own, other, held, target, stage, semaphores):
     emit = Emitter(table, target, stage, semaphores)
     io.rest()
     chunk = stage.shape[1]
-    for first, own, other in ((16, cross_own, cross_other), (24, ff_own, ff_other)):
-        for number in range(own.shape[0] // chunk):
-            rows = slice(number * chunk, (number + 1) * chunk)
-            total = own[rows].astype(single) + other[rows].astype(single)
-            emit.chunk((first - 16) // 4 + number, first + 4 * number, total)
+    for number in range(own.shape[0] // chunk):
+        rows = slice(number * chunk, (number + 1) * chunk)
+        total = own[rows].astype(single) + other[rows].astype(single)
+        emit.chunk(number, 16 + 4 * number, total)
     emit.wait()
-
-
-def place_kernel(where, scal, table, *refs):
-    sources = refs[: len(where)]
-    first_out, rest_out, pieces, semaphores, out_semaphores = refs[len(where) :]
-    cut = first_out.shape[0]
-
-    def each(act):
-        base = 0
-        for source, ranges in zip(sources, where):
-            for start, stop, distance, other, first in ranges:
-
-                def step(slot, unused):
-                    piece = table[distance, first + slot - start]
-                    at = piece * 2 + (scal[0] if other == 0 else 1 - scal[0])
-
-                    @pl.when(piece >= 0)
-                    def _():
-                        semaphore = semaphores.at[base + slot]
-                        act(pltpu.make_async_copy(source.at[slot], pieces.at[at], semaphore))
-
-                    return 0
-
-                lax.fori_loop(start, stop, step, 0)
-            base += source.shape[0]
-
-    each(lambda copy: copy.start())
-    each(lambda copy: copy.wait())
-    outs = [
-        pltpu.make_async_copy(pieces.at[pl.ds(0, cut)], first_out, out_semaphores.at[0]),
-        pltpu.make_async_copy(pieces.at[pl.ds(cut, rest_out.shape[0])], rest_out, out_semaphores.at[1]),
-    ]
-    for copy in outs:
-        copy.start()
-    for copy in outs:
-        copy.wait()
 
 
 RING = (0, 2, 4, 6, 7, 5, 3, 1)
@@ -770,7 +761,7 @@
     return jnp.concatenate(values, 0)
 
 
-def ring_gather(own):
+def ring_gather(own, tables):
     every, lead, half = own.shape[0], LEAD, LEAD // 2
     late = every - lead
     found = [([(0, every, 0, 0, 0)], own)]
@@ -790,6 +781,7 @@
     found.append(
         ([(0, lead, 7, 1, 0), (lead, 2 * lead, 1, 1, 0), (2 * lead, 2 * lead + half, 0, 1, 0)], across)
     )
+    up, tables = lax.optimization_barrier((up, tables))
     ahead(up, 6, 7)
     ahead(down, 2, 1)
     up, down, across = step_of(up, down, join(up[:lead], down[:lead], own[half:lead]))
@@ -809,7 +801,7 @@
     found.append(([(0, late, 4, 0, lead)], up))
     found.append(([(0, late, 4, 1, lead)], down))
     found.append(([(0, lead, 4, 1, 0)], across))
-    return found
+    return found, tables
 
 
 def added(*values):
@@ -910,56 +902,9 @@
     same = owner_row[:, None] == owner_row[None, :]
     earlier = counter[None, :] < counter[:, None]
     ranks = jnp.sum((same & earlier).astype(jnp.int32), 1)
-    places = (
-        owner_row[:, None] * narrow_size + jnp.arange(narrow_size)[None, :]
-    ) * capacity + ranks[:, None]
     on_ring = wide_size == len(RING) and narrow_size == 2 and capacity > LEAD
     wide_at, narrow_at = lax.axis_index("wide"), lax.axis_index("narrow")
     self_rows, rest_rows = 4 * width, count * half_rows * narrow_size - 4 * width
-    own = master[0].astype(bfloat)
-    if on_ring:
-        turned = [RING.index(i) for i in range(wide_size)]
-        position = jnp.array(turned)[wide_at]
-        owner_ring = jnp.array(turned)[owner_row]
-        distance = (owner_ring - position) % wide_size
-        halves = jnp.arange(narrow_size)[None, :] ^ narrow_at
-        table = ((distance[:, None] * 2 + halves) * capacity + ranks[:, None]).reshape(-1)
-        slot_of = distance * capacity + ranks
-        hit = slot_of[None, :] == jnp.arange(wide_size * capacity)[:, None]
-        pieces = jnp.sum(hit.astype(jnp.int32) * (counter + 1)[None, :], 1) - 1
-        found = ring_gather(own)
-        slots_found = sum(value.shape[0] for unused, value in found)
-        weight, rest = pl.pallas_call(
-            partial(place_kernel, [where for where, unused in found]),
-            in_specs=[SM, SM] + [HB] * len(found),
-            out_specs=[HB, HB],
-            out_shape=[
-                low(self_rows // half_rows, half_rows, width),
-                low(rest_rows // half_rows, half_rows, width),
-            ],
-            scratch_shapes=[
-                low_vm(count * narrow_size, half_rows, width),
-                pltpu.SemaphoreType.DMA((slots_found,)),
-                pltpu.SemaphoreType.DMA((2,)),
-            ],
-            compiler_params=pltpu.CompilerParams(vmem_limit_bytes=58 << 20),
-            name="place_weights",
-        )(
-            narrow_at.astype(jnp.int32)[None],
-            pieces.reshape(wide_size, capacity).astype(jnp.int32),
-            *[value for unused, value in found],
-        )
-        weight, rest = weight.reshape(-1, width), rest.reshape(-1, width)
-    else:
-        places = (
-            owner_row[:, None] * narrow_size + jnp.arange(narrow_size)[None, :]
-        ) * capacity + ranks[:, None]
-        table = places.reshape(-1)
-        gathered = lax.all_gather(own, ("wide", "narrow"), axis=0, tiled=True)
-        weight = jnp.take(gathered, table, axis=0).reshape(-1, width)
-        weight, rest = weight[:self_rows], weight[self_rows:]
-    table = table.astype(jnp.int32)
-    hidden = (rest_rows - 2 * width) // 2
     is_source = lax.axis_index("half") == 0
     x = stream[0, 0]
     length = x.shape[0]
@@ -973,14 +918,35 @@
             flag,
             jnp.where(is_source, target_len - some, target_len),
             source_len,
+            narrow_at,
         ]
     ).astype(jnp.int32)
+    own = master[0].astype(bfloat)
+    if on_ring:
+        turned = [RING.index(i) for i in range(wide_size)]
+        position = jnp.array(turned)[wide_at]
+        owner_ring = jnp.array(turned)[owner_row]
+        distance = (owner_ring - position) % wide_size
+        halves = jnp.arange(narrow_size)[None, :] ^ narrow_at
+        table = ((distance[:, None] * 2 + halves) * capacity + ranks[:, None]).reshape(-1)
+        slot_of = distance * capacity + ranks
+        hit = slot_of[None, :] == jnp.arange(wide_size * capacity)[:, None]
+        pieces = jnp.sum(hit.astype(jnp.int32) * (counter + 1)[None, :], 1) - 1
+        pieces = pieces.reshape(wide_size, capacity).astype(jnp.int32)
+        found, (pieces, table, scal) = ring_gather(own, (pieces, table.astype(jnp.int32), scal))
+    else:
+        places = (
+            owner_row[:, None] * narrow_size + jnp.arange(narrow_size)[None, :]
+        ) * capacity + ranks[:, None]
+        table = places.reshape(-1)
+        gathered = lax.all_gather(own, ("wide", "narrow"), axis=0, tiled=True)
+        weight = jnp.take(gathered, table, axis=0).reshape(-1, width)
+        weight, rest = weight[:self_rows], weight[self_rows:]
+    table = table.astype(jnp.int32)
+    hidden = (rest_rows - 2 * width) // 2
     self_vec = whole(jnp.where(is_source, vec_master[0:3], vec_master[6:9]))
     cross_vec, ff_vec = whole(vec_master[9:12]), whole(vec_master[12:15])
     memory_vec = whole(vec_master[3:6])
-    cross_w = part(rest, 0, 2 * width)
-    up_w = part(rest, 2 * width, hidden)
-    down_w = part(rest, 2 * width + hidden, hidden)
     slots = low(capacity * wide_size * narrow_size, half_rows, width)
 
     def stage_of(chunks):
@@ -993,21 +959,40 @@
         return ("store", shaped(*shape, dtype=dtype))
 
     low_out = partial(store, dtype=bfloat)
-    two = low_vm(2, length, 128)
+    two, four = low_vm(2, length, 128), low_vm(4, length, 128)
     down_half, up_half = [(1, 0)], [(0, 1)]
 
-    rest_other = lax.ppermute(rest, "half", down_half)
-    query, key, value, ctx_t, lse, resid, inner = call(
-        self_forward_body,
-        "self_forward",
-        scal,
-        None,
-        [whole(x), part(weight, 0, 3 * width), part(weight, 3 * width, width), self_vec],
+    forward_outs = (
         [low_out(length, width)] * 3
         + [low_out(width, length), store(HEADS, length)]
-        + [store(length, width)] * 2,
-        [low_vm(width, length), low_vm(width, length), two],
-    )
+        + [store(length, width)] * 2
+    )
+    forward_scratch = [low_vm(width, length), low_vm(width, length), four]
+    if on_ring:
+        *forward, weight, rest = call(
+            partial(placed_forward_body, [where for where, unused in found]),
+            "self_forward",
+            scal,
+            None,
+            [("smem", pieces), whole(x), self_vec] + [("hbm", value) for unused, value in found],
+            forward_outs + [low_out(self_rows, width), low_out(rest_rows, width)],
+            forward_scratch + [pltpu.SemaphoreType.DMA((2,))],
+        )
+    else:
+        forward = call(
+            self_forward_body,
+            "self_forward",
+            scal,
+            None,
+            [whole(x), whole(weight), self_vec],
+            forward_outs,
+            forward_scratch,
+        )
+    query, key, value, ctx_t, lse, resid, inner = forward
+    rest_other = lax.ppermute(rest, "half", down_half)
+    cross_w = part(rest, 0, 2 * width)
+    up_w = part(rest, 2 * width, hidden)
+    down_w = part(rest, 2 * width + hidden, hidden)
     inner_other = lax.ppermute(inner[some:], "half", down_half)
     activ, slope, ff_resid, memory, sendout = call(
         encoder_ff_body,
@@ -1026,68 +1011,40 @@
 
     mid_inner = either([(inner_other, 0, 0, some)], [(inner, 0, 0, some)])
     keys = either([(sendout, 0, 0, None)], [(sendout_other, 0, 0, None)])
-    cross_query, cross_ctx_t, cross_lse, cross_resid, inner_two = call(
-        cross_forward_body,
-        "cross_forward",
-        scal,
-        None,
-        [mid_inner, keys, shared(0, 2 * width), cross_vec],
-        [low_out(some, width), low_out(width, some), store(HEADS, some)] + [store(some, width)] * 2,
-        [low_vm(width, some), low_vm(width, length), two],
-    )
     cotan = cotangent[0]
-    output, grad_two, grad_ff_vec, grad_ff = call(
-        decoder_ff_body,
-        "decoder_ff",
+    output, sendback, grad_one, grad_rest, grad_middle_vec = call(
+        middle_body,
+        "decoder_middle",
         scal,
         None,
         [
-            whole(inner_two),
+            mid_inner,
+            keys,
+            shared(0, 2 * width),
+            cross_vec,
             shared(2 * width, hidden),
             shared(2 * width + hidden, hidden),
             ff_vec,
             either([(cotan, some, 0, some)], [(cotan, 0, 0, some)]),
         ],
-        [low_out(some, width), store(some, width), store(3, width), low_out(2 * hidden, width)],
-        [low_vm(some, hidden), low_vm(some, hidden), low_vm(some, width), low_vm(some, width)],
-    )
-    output_other = lax.ppermute(output, "half", up_half)
-    grad_ff_other = lax.ppermute(grad_ff, "half", up_half)
-
-    def attn_scratch(rows):
-        return (
-            [low_vm(rows, width), low_vm(rows, width), low_vm(width, rows), full_vm(HEADS, rows)]
-            + [low_vm(width, rows), low_vm(width, length)]
-            + [full_vm(length, width), full_vm(length, width), low_vm(width, rows), two, two]
-        )
-
-    sendback, grad_one, grad_cross_vec, grad_cross = call(
-        cross_back_body,
-        "cross_back",
-        scal,
-        None,
         [
-            mid_inner,
-            whole(cross_resid),
-            whole(cross_query),
-            keys,
-            whole(cross_ctx_t),
-            whole(cross_lse),
-            shared(0, 2 * width),
-            cross_vec,
-            whole(grad_two),
-        ],
-        [
+            low_out(some, width),
             low_out(2, length, width),
             store(some, width),
-            store(3, width),
-            low_out(2 * width, width),
+            low_out(rest_rows, width),
+            store(6, width),
         ],
-        attn_scratch(some),
+        [low_vm(some, width), low_vm(width, some), low_vm(width, some), full_vm(HEADS, some)]
+        + [full_vm(some, width), full_vm(some, width), low_vm(some, hidden), low_vm(some, hidden)]
+        + [low_vm(some, width), low_vm(some, width), full_vm(some, width)]
+        + [low_vm(some, width), low_vm(width, some), full_vm(HEADS, some)]
+        + [low_vm(width, length), low_vm(width, length)]
+        + [full_vm(length, width), full_vm(length, width), low_vm(width, some), four, two, two],
     )
     sendback_other = lax.ppermute(sendback, "half", down_half)
     grad_one_other = lax.ppermute(grad_one, "half", up_half)
-    grad_cross_other = lax.ppermute(grad_cross, "half", up_half)
+    grad_rest_other = lax.ppermute(grad_rest, "half", up_half)
+    output_other = lax.ppermute(output, "half", up_half)
     grad_inner, grad_memory_vec, target = call(
         encoder_back_body,
         "encoder_back",
@@ -1109,6 +1066,11 @@
         ],
         [store(length, width), store(3, width), ("hbm", slots)],
         [full_vm(length, width), low_vm(length, width), low_vm(length, width)] + stage_of(10),
+    )
+    back_scratch = (
+        [low_vm(length, width), low_vm(length, width), low_vm(width, length), full_vm(HEADS, length)]
+        + [low_vm(width, length), low_vm(width, length)]
+        + [full_vm(length, width), full_vm(length, width), low_vm(width, length), two, two]
     )
     grad_x, grad_self_vec, target = call(
         self_back_body,
@@ -1134,7 +1096,7 @@
             ("hbm", target),
         ],
         [store(length, width), store(3, width), ("hbm", slots)],
-        attn_scratch(length) + stage_of(4),
+        back_scratch + stage_of(4),
         [(12, 2)],
     )
     (target,) = call(
@@ -1144,23 +1106,20 @@
         0,
         [
             ("smem", table),
-            whole(grad_ff),
-            whole(grad_ff_other),
-            whole(grad_cross),
-            whole(grad_cross_other),
+            whole(grad_rest),
+            whole(grad_rest_other),
             ("hbm", target),
         ],
         [("hbm", slots)],
         stage_of(10),
-        [(5, 0)],
+        [(3, 0)],
     )
     vec_grads = jnp.concatenate(
         [
             jnp.where(is_source, grad_self_vec, 0.0),
             jnp.where(is_source, grad_memory_vec, 0.0),
             jnp.where(is_source, 0.0, grad_self_vec),
-            grad_cross_vec,
-            grad_ff_vec,
+            grad_middle_vec,
         ],
         0,
     )

time: 468 us -> 401 us (0.86)
  Pallas kernels: 183 us -> 134 us
  starting transfers between devices: 65.7 us -> 55.2 us
  other arithmetic: 25.8 us -> 19.1 us
    pallas_call x8 -> x6, Pallas kernels: 173 us -> 134 us  [call(): pl.pallas_call(kernel, in_specs=specs, out_specs=[HB] * count_out, out_sh...]
    ppermute x20, waiting for transfers between devices: 82.7 us -> 64.2 us  [round_ring(): lax.ppermute(value, 'wide', [(RING[i], RING[(i + step) % count]) for i in...]
    ppermute x10, waiting for transfers between devices: 73.3 us -> 87.1 us  [swapped(): return lax.ppermute(value, 'narrow', [(0, 1), (1, 0)])]
    ppermute x1, starting transfers between devices: 13.4 us -> 1.29 us  [on_device(): inner_other = lax.ppermute(inner[some:], 'half', down_half)]
    pallas_call x1 -> x0, Pallas kernels: 10.3 us -> none  [on_device(): pl.pallas_call(partial(place_kernel, [where for where, unused in found]),...]
  transfers between devices with their start and end apart: 43 -> 42, of which waited for: 26 -> 28; matrix products, arithmetic and copies ran while one was open for 6% -> 6% of each run, Pallas kernels for 30% -> 18%
where the time goes in v3:
time: 401 us; the launch traced here: 397 us
  waiting for transfers between devices  164 us (41%)
  Pallas kernels  134 us (33%)
  starting transfers between devices  55.2 us (14%)
  local copies, waits for them, and re-layouts  20.4 us (5%)
  other arithmetic  19.1 us (5%)
  between operations  4.39 us (1%)
    pallas_call x6, Pallas kernels, call(): pl.pallas_call(kernel, in_specs=specs, out_specs=[HB] * count_out, out_sh...  134 us
    ppermute x10, waiting for transfers between devices, swapped(): return lax.ppermute(value, 'narrow', [(0, 1), (1, 0)])  87.1 us
    ppermute x20, waiting for transfers between devices, round_ring(): lax.ppermute(value, 'wide', [(RING[i], RING[(i + step) % count]) for i in...  64.2 us
    ppermute x20, starting transfers between devices, round_ring(): lax.ppermute(value, 'wide', [(RING[i], RING[(i + step) % count]) for i in...  22 us
    ppermute x10, starting transfers between devices, swapped(): return lax.ppermute(value, 'narrow', [(0, 1), (1, 0)])  12.2 us
    ppermute x5, waiting for transfers between devices, sum_over(): lax.ppermute(value, axis, [(i, i ^ bit) for i in range(size)])  8.51 us
  transfers between devices with their start and end apart: 42, of which 28 were waited for; matrix products, arithmetic and copies ran while one was open for 6% of the time, Pallas kernels for 18%

profile of v3, /device:TPU:0, one launch (start us, length us, event | category | flops | bytes accessed | tf_op | source)
XLA Modules:
  0.0 396.7 jit_solution(1060725157992785624)
XLA Ops:
  3.2 3.0 collective-permute-start
  6.2 2.0 collective-permute-start.2
  8.3 8.6 %collective-permute-done.2.refs_5_ = bf16[6,64,512]{2,1,0:T(8,128)(2,1)S(1)} collective-permute-done((bf16[6,64,512]{2,1,0:T(8,128)(2,1)S(1)}, bf16[6,64,512]{2,1,0:T(8,128)(2,1)S(1)}, u32[]{:S(2)}, u32[]{:S(2)}) %collective-permute-start.2) | collective-permute-done | bytes 393248 | tf_op jit(solution)/shard_map/ppermute | solution.py:753
  19.8 2.1 pad_maximum_fusion.1
  33.8 17.7 %collective-permute-done.3.refs_9_ = bf16[20,64,512]{2,1,0:T(8,128)(2,1)S(1)} collective-permute-done((bf16[20,64,512]{2,1,0:T(8,128)(2,1)}, bf16[20,64,512]{2,1,0:T(8,128)(2,1)S(1)}, u32[]{:S(2)}, u32[]{:S(2)}) %collective-permute-start.3) | collective-permute-done | bytes 1310752 | tf_op jit(solution)/shard_map/ppermute | solution.py:749
  57.4 24.7 %collective-permute-done.8.refs_11_ = bf16[20,64,512]{2,1,0:T(8,128)(2,1)S(1)} collective-permute-done((bf16[20,64,512]{2,1,0:T(8,128)(2,1)S(1)}, bf16[20,64,512]{2,1,0:T(8,128)(2,1)S(1)}, u32[]{:S(2)}, u32[]{:S(2)}) %collective-permute-start.8) | collective-permute-done | bytes 1310752 | tf_op jit(solution)/shard_map/ppermute | solution.py:753
  90.3 17.9 %collective-permute-done.11.refs_14_ = bf16[16,64,512]{2,1,0:T(8,128)(2,1)S(1)} collective-permute-done((bf16[16,64,512]{2,1,0:T(8,128)(2,1)S(1)}, bf16[16,64,512]{2,1,0:T(8,128)(2,1)S(1)}, u32[]{:S(2)}, u32[]{:S(2)}) %collective-permute-start.11) | collective-permute-done | bytes 1048608 | tf_op jit(solution)/shard_map/ppermute | solution.py:753
  114.7 4.9 %collective-permute-done.12.refs_17_ = bf16[6,64,512]{2,1,0:T(8,128)(2,1)S(1)} collective-permute-done((bf16[6,64,512]{2,1,0:T(8,128)(2,1)S(1)}, bf16[6,64,512]{2,1,0:T(8,128)(2,1)S(1)}, u32[]{:S(2)}, u32[]{:S(2)}) %collective-permute-start.12) | collective-permute-done | bytes 393248 | tf_op jit(solution)/shard_map/ppermute | solution.py:749
  119.7 1.8 collective-permute-done.13.refs_18_
  122.4 23.8 %self_forward.1 = (bf16[1024,512]{1,0:T(8,128)(2,1)}, bf16[1024,512]{1,0:T(8,128)(2,1)}, bf16[1024,512]{1,0:T(8,128)(2,1)}, bf16[512,1024]{1,0:T(8,128)(2,1)}, f...) custom-call(s32[6]{0:T(128)} %stack.23.refs_0_, ...), custom_call_target="tpu_custom_call" | custom-call | tf_op jit(solution)/shard_map/self_forward/pallas_call | solution.py:417
  147.5 15.0 %encoder_ff.1 = (bf16[1024,2048]{1,0:T(8,128)(2,1)}, bf16[1024,2048]{1,0:T(8,128)(2,1)}, f32[1024,512]{1,0:T(8,128)}, bf16[1024,512]{1,0:T(8,128)(2,1)}, bf16[2,1024,512]{2,1,0:T(8,128)(2,1)}) custom-call(s32[6]{0:T(128)} %stack.23.refs_0_, f32[1024,512]{1,0:T(8,128)} %get-tuple-element.88.refs_1_.refs_2_.refs_6_, ...), custom_call_target="tpu_custom_call" | custom-call | tf_op jit(solution)/shard_map/encoder_ff/pallas_call | solution.py:417
  162.6 2.6 collective-permute-start.16
  167.8 3.3 collective-permute-done.15.refs_1_
  172.0 35.1 %decoder_middle.1 = (bf16[512,512]{1,0:T(8,128)(2,1)}, bf16[2,1024,512]{2,1,0:T(8,128)(2,1)}, f32[512,512]{1,0:T(8,128)}, bf16[5120,512]{1,0:T(8,128)(2,1)}, f32[6,512]{1,0:T(8,128)}) custom-call(s32[6]{0:T(128)} %stack.23.refs_0_, f32[512,512]{1,0:T(8,128)} %copy-done.20, f32[1024,512]{1,0:T(8,128)} %get-tuple-element.88.refs_1_.refs_2_.refs_6_, ...), custom_call_target="tpu_custom_call" | custom-call | tf_op jit(solution)/shard_map/decoder_middle/pallas_call | solution.py:417
  207.1 3.7 collective-permute-start.21
  212.1 4.4 %collective-permute-start.20 = (f32[512,512]{1,0:T(8,128)}, f32[512,512]{1,0:T(8,128)S(1)}, u32[]{:S(2)}, u32[]{:S(2)}) collective-permute-start(f32[512,512]{1,0:T(8,128)} %get-tuple-element.106.refs_13_), channel_id=1, source_target_pairs={{0,16},{1,17},{2,18},{3,19},{4,20},{5,21},{6,22},{7,23},{8,24},{9,... | collective-permute-start | bytes 3145736 | tf_op jit(solution)/shard_map/ppermute | solution.py:1045
  217.2 22.4 %encoder_back.1 = (f32[1024,512]{1,0:T(8,128)}, f32[3,512]{1,0:T(4,128)}, bf16[224,64,512]{2,1,0:T(8,128)(2,1)}) custom-call(s32[6]{0:T(128)} %stack.23.refs_0_, s32[112]{0:T(128)} %add.216.refs_1_, bf16[2,1024,512]{2,1,0:T(8,128)(2,1)} %get-tuple-element.101.refs_2_, bf16[2,1024,512]{2,1,0:T(8,128)(2,1)} %collective-permute-done.19.refs_3_, ...), custom_call_target="tpu_custom_call" | custom-call | tf_op jit(solution)/shard_map/encoder_back/pallas_call | solution.py:417
  240.5 35.8 %self_back.1 = (f32[1024,512]{1,0:T(8,128)}, f32[3,512]{1,0:T(4,128)}, bf16[224,64,512]{2,1,0:T(8,128)(2,1)}) custom-call(s32[6]{0:T(128)} %stack.23.refs_0_, s32[112]{0:T(128)} %add.216.refs_1_, bf16[1024,512]{1,0:T(8,128)(2,1)} %bitcast.186, bf16[2048,512]{1,0:T(8,128)(2,1)} %get-tuple-element.94.refs_3_.refs_4_, ...), custom_call_target="tpu_custom_call", output_to_operand_aliasing={{2}: (15, {})} | custom-call | tf_op jit(solution)/shard_map/self_back/pallas_call | solution.py:417
  278.0 2.4 slice_bitcast_fusion.3
  281.1 2.1 slice_bitcast_fusion.14
  287.0 6.1 %collective-permute-done.22 = bf16[6,64,512]{2,1,0:T(8,128)(2,1)S(1)} collective-permute-done((bf16[6,64,512]{2,1,0:T(8,128)(2,1)S(1)}, bf16[6,64,512]{2,1,0:T(8,128)(2,1)S(1)}, u32[]{:S(2)}, u32[]{:S(2)}) %collective-permute-start.22) | collective-permute-done | bytes 393248 | tf_op jit(solution)/shard_map/ppermute | solution.py:749
  293.1 2.3 collective-permute-done.24
  300.5 17.3 %collective-permute-done.27 = bf16[16,64,512]{2,1,0:T(8,128)(2,1)S(1)} collective-permute-done((bf16[16,64,512]{2,1,0:T(8,128)(2,1)S(1)}, bf16[16,64,512]{2,1,0:T(8,128)(2,1)S(1)}, u32[]{:S(2)}, u32[]{:S(2)}) %collective-permute-start.27) | collective-permute-done | bytes 1048608 | tf_op jit(solution)/shard_map/ppermute | solution.py:753
  317.9 1.9 collective-permute-done.26
  325.5 16.1 %collective-permute-done.30 = bf16[20,64,512]{2,1,0:T(8,128)(2,1)S(1)} collective-permute-done((bf16[20,64,512]{2,1,0:T(8,128)(2,1)S(1)}, bf16[20,64,512]{2,1,0:T(8,128)(2,1)S(1)}, u32[]{:S(2)}, u32[]{:S(2)}) %collective-permute-start.30) | collective-permute-done | bytes 1310752 | tf_op jit(solution)/shard_map/ppermute | solution.py:753
  341.5 8.6 %collective-permute-done.29 = bf16[20,64,512]{2,1,0:T(8,128)(2,1)S(1)} collective-permute-done((bf16[20,64,512]{2,1,0:T(8,128)(2,1)S(1)}, bf16[20,64,512]{2,1,0:T(8,128)(2,1)S(1)}, u32[]{:S(2)}, u32[]{:S(2)}) %collective-permute-start.29) | collective-permute-done | bytes 1310752 | tf_op jit(solution)/shard_map/ppermute | solution.py:749
  356.9 2.4 collective-permute-done.37
  360.6 11.4 %collective-permute-done.32 = bf16[20,64,512]{2,1,0:T(8,128)(2,1)S(1)} collective-permute-done((bf16[20,64,512]{2,1,0:T(8,128)(2,1)S(1)}, bf16[20,64,512]{2,1,0:T(8,128)(2,1)S(1)}, u32[]{:S(2)}, u32[]{:S(2)}) %collective-permute-start.32) | collective-permute-done | bytes 1310752 | tf_op jit(solution)/shard_map/ppermute | solution.py:749
  376.6 1.8 collective-permute-start.39
  379.0 3.8 collective-permute-done.39
  385.4 2.3 collective-permute-done.40
  391.4 4.2 %convert_bitcast_fusion = (bf16[1,14,64,512]{3,2,1,0:T(8,128)(2,1)}, f32[14,64,512]{2,1,0:T(8,128)}, f32[1,14,64,512]{3,2,1,0:T(8,128)}, f32[1,14,64,512]{3,2,1,0:T(8,128)}) fusion(f32[1,14,64,512]{3,2,1,0:T(8,128)S(1)} %copy-done.12, f32[14,64,512]{2,1,0:T(8,128)S(1)} %pad_maximum_fusion, pred[14]{0:T(512)(128)(4,1)S(1)} %iota_compare_fusion.2, ...), kind=kLoop, calls=%fused_computation.56 | loop fusion | flops 7340032 | bytes 13762574 | tf_op jit(solution)/shard_map/broadcast_in_dim | solution.py:1149
  (207 shorter events, 80.9 us)
Async XLA Ops:
  3.2 15.1 %collective-permute-start = (bf16[8,64,512]{2,1,0:T(8,128)(2,1)}, bf16[8,64,512]{2,1,0:T(8,128)(2,1)S(1)}, u32[]{:S(2)}, u32[]{:S(2)}) collective-permute-start(bf16[8,64,512]{2,1,0:T(8,128)(2,1)} %slice.328), channel_id=1, source_target_pairs={{0,4},{4,8},{8,12},{12,14},{14,10},{10,6},{6,2},{2,0},{1,5},{5,9},... | collective-permute-start | bytes 1572872 | tf_op jit(solution)/shard_map/ppermute | solution.py:749
  6.2 13.6 %collective-permute-start.1 = (bf16[8,64,512]{2,1,0:T(8,128)(2,1)}, bf16[8,64,512]{2,1,0:T(8,128)(2,1)S(1)}, u32[]{:S(2)}, u32[]{:S(2)}) collective-permute-start(bf16[8,64,512]{2,1,0:T(8,128)(2,1)} %slice.328), channel_id=1, source_target_pairs={{0,2},{4,0},{8,4},{12,8},{14,12},{10,14},{6,10},{2,6},{1,3},{5,1},... | collective-permute-start | bytes 1572872 | tf_op jit(solution)/shard_map/ppermute | solution.py:749
  6.2 10.6 %collective-permute-start.2 = (bf16[6,64,512]{2,1,0:T(8,128)(2,1)S(1)}, bf16[6,64,512]{2,1,0:T(8,128)(2,1)S(1)}, u32[]{:S(2)}, u32[]{:S(2)}) collective-permute-start(bf16[6,64,512]{2,1,0:T(8,128)(2,1)S(1)} %slice.329), channel_id=1, source_target_pairs={{0,1},{1,0},{2,3},{3,2},{4,5},{5,4},{6,7},{7,6},{8,9},{9,8},{10,11... | collective-permute-start | bytes 1179656 | tf_op jit(solution)/shard_map/ppermute | solution.py:753
  21.9 29.6 %collective-permute-start.3 = (bf16[20,64,512]{2,1,0:T(8,128)(2,1)}, bf16[20,64,512]{2,1,0:T(8,128)(2,1)S(1)}, u32[]{:S(2)}, u32[]{:S(2)}) collective-permute-start(bf16[20,64,512]{2,1,0:T(8,128)(2,1)} %get-tuple-element.171), channel_id=1, source_target_pairs={{0,4},{4,8},{8,12},{12,14},{14,10},{10,6},{6,2},{2,0},{1,5},{5,9},... | collective-permute-start | bytes 3932168 | tf_op jit(solution)/shard_map/ppermute | solution.py:749
  23.6 29.3 %collective-permute-start.4 = (bf16[20,64,512]{2,1,0:T(8,128)(2,1)}, bf16[20,64,512]{2,1,0:T(8,128)(2,1)S(1)}, u32[]{:S(2)}, u32[]{:S(2)}) collective-permute-start(bf16[20,64,512]{2,1,0:T(8,128)(2,1)} %get-tuple-element.170), channel_id=1, source_target_pairs={{0,2},{4,0},{8,4},{12,8},{14,12},{10,14},{6,10},{2,6},{1,3},{5,1},... | collective-permute-start | bytes 3932168 | tf_op jit(solution)/shard_map/ppermute | solution.py:749
  24.0 29.1 %collective-permute-start.5 = (bf16[20,64,512]{2,1,0:T(8,128)(2,1)}, bf16[20,64,512]{2,1,0:T(8,128)(2,1)}, u32[]{:S(2)}, u32[]{:S(2)}) collective-permute-start(bf16[20,64,512]{2,1,0:T(8,128)(2,1)} %get-tuple-element.172), channel_id=1, source_target_pairs={{0,1},{1,0},{2,3},{3,2},{4,5},{5,4},{6,7},{7,6},{8,9},{9,8},{10,11... | collective-permute-start | bytes 3932168 | tf_op jit(solution)/shard_map/ppermute | solution.py:753
  53.9 28.2 %collective-permute-start.8 = (bf16[20,64,512]{2,1,0:T(8,128)(2,1)S(1)}, bf16[20,64,512]{2,1,0:T(8,128)(2,1)S(1)}, u32[]{:S(2)}, u32[]{:S(2)}) collective-permute-start(bf16[20,64,512]{2,1,0:T(8,128)(2,1)S(1)} %pad_maximum_fusion.6), channel_id=1, source_target_pairs={{0,1},{1,0},{2,3},{3,2},{4,5},{5,4},{6,7},{7,6},{8,9},{9,8},{10,11... | collective-permute-start | bytes 3932168 | tf_op jit(solution)/shard_map/ppermute | solution.py:753
  55.4 28.0 %collective-permute-start.6 = (bf16[20,64,512]{2,1,0:T(8,128)(2,1)S(1)}, bf16[20,64,512]{2,1,0:T(8,128)(2,1)S(1)}, u32[]{:S(2)}, u32[]{:S(2)}) collective-permute-start(bf16[20,64,512]{2,1,0:T(8,128)(2,1)S(1)} %collective-permute-done.3.refs_9_), channel_id=1, source_target_pairs={{0,4},{4,8},{8,12},{12,14},{14,10},{10,6},{6,2},{2,0},{1,5},{5,9},... | collective-permute-start | bytes 3932168 | tf_op jit(solution)/shard_map/ppermute | solution.py:749
  57.0 27.9 %collective-permute-start.7 = (bf16[20,64,512]{2,1,0:T(8,128)(2,1)}, bf16[20,64,512]{2,1,0:T(8,128)(2,1)S(1)}, u32[]{:S(2)}, u32[]{:S(2)}) collective-permute-start(bf16[20,64,512]{2,1,0:T(8,128)(2,1)} %copy-done.9), channel_id=1, source_target_pairs={{0,2},{4,0},{8,4},{12,8},{14,12},{10,14},{6,10},{2,6},{1,3},{5,1},... | collective-permute-start | bytes 3932168 | tf_op jit(solution)/shard_map/ppermute | solution.py:749
  87.1 21.2 %collective-permute-start.11 = (bf16[16,64,512]{2,1,0:T(8,128)(2,1)S(1)}, bf16[16,64,512]{2,1,0:T(8,128)(2,1)S(1)}, u32[]{:S(2)}, u32[]{:S(2)}) collective-permute-start(bf16[16,64,512]{2,1,0:T(8,128)(2,1)S(1)} %pad_maximum_fusion.14), channel_id=1, source_target_pairs={{0,1},{1,0},{2,3},{3,2},{4,5},{5,4},{6,7},{7,6},{8,9},{9,8},{10,11... | collective-permute-start | bytes 3145736 | tf_op jit(solution)/shard_map/ppermute | solution.py:753
  88.2 21.5 %collective-permute-start.9 = (bf16[16,64,512]{2,1,0:T(8,128)(2,1)S(1)}, bf16[16,64,512]{2,1,0:T(8,128)(2,1)S(1)}, u32[]{:S(2)}, u32[]{:S(2)}) collective-permute-start(bf16[16,64,512]{2,1,0:T(8,128)(2,1)S(1)} %pad_maximum_fusion.13), channel_id=1, source_target_pairs={{0,4},{4,8},{8,12},{12,14},{14,10},{10,6},{6,2},{2,0},{1,5},{5,9},... | collective-permute-start | bytes 3145736 | tf_op jit(solution)/shard_map/ppermute | solution.py:749
  89.8 20.9 %collective-permute-start.10 = (bf16[16,64,512]{2,1,0:T(8,128)(2,1)S(1)}, bf16[16,64,512]{2,1,0:T(8,128)(2,1)S(1)}, u32[]{:S(2)}, u32[]{:S(2)}) collective-permute-start(bf16[16,64,512]{2,1,0:T(8,128)(2,1)S(1)} %slice.252), channel_id=1, source_target_pairs={{0,2},{4,0},{8,4},{12,8},{14,12},{10,14},{6,10},{2,6},{1,3},{5,1},... | collective-permute-start | bytes 3145736 | tf_op jit(solution)/shard_map/ppermute | solution.py:749
  110.7 10.7 %collective-permute-start.14 = (bf16[8,64,512]{2,1,0:T(8,128)(2,1)S(1)}, bf16[8,64,512]{2,1,0:T(8,128)(2,1)S(1)}, u32[]{:S(2)}, u32[]{:S(2)}) collective-permute-start(bf16[8,64,512]{2,1,0:T(8,128)(2,1)S(1)} %pad_maximum_fusion.18), channel_id=1, source_target_pairs={{0,1},{1,0},{2,3},{3,2},{4,5},{5,4},{6,7},{7,6},{8,9},{9,8},{10,11... | collective-permute-start | bytes 1572872 | tf_op jit(solution)/shard_map/ppermute | solution.py:753
  146.2 24.8 %collective-permute-start.17 = (bf16[5120,512]{1,0:T(8,128)(2,1)}, bf16[5120,512]{1,0:T(8,128)(2,1)}, u32[]{:S(2)}, u32[]{:S(2)}) collective-permute-start(bf16[5120,512]{1,0:T(8,128)(2,1)} %get-tuple-element.89.refs_2_.refs_3_.refs_4_.refs_6_.refs_9_.refs_11_.refs_5_.refs_10_), channel_id=1, source_target_pairs={{16,0},{17,1},{18,2},{19,3},{20,4},{21,5},{22,6},{23,7},{24,8},{25... | collective-permute-start | bytes 15728648 | tf_op jit(solution)/shard_map/ppermute | solution.py:992
  207.1 69.3 %collective-permute-start.21 = (bf16[5120,512]{1,0:T(8,128)(2,1)}, bf16[5120,512]{1,0:T(8,128)(2,1)}, u32[]{:S(2)}, u32[]{:S(2)}) collective-permute-start(bf16[5120,512]{1,0:T(8,128)(2,1)} %get-tuple-element.109.refs_2_), channel_id=1, source_target_pairs={{0,16},{1,17},{2,18},{3,19},{4,20},{5,21},{6,22},{7,23},{8,24},{9,... | collective-permute-start | bytes 15728648 | tf_op jit(solution)/shard_map/ppermute | solution.py:1046
  212.1 27.5 %collective-permute-start.20 = (f32[512,512]{1,0:T(8,128)}, f32[512,512]{1,0:T(8,128)S(1)}, u32[]{:S(2)}, u32[]{:S(2)}) collective-permute-start(f32[512,512]{1,0:T(8,128)} %get-tuple-element.106.refs_13_), channel_id=1, source_target_pairs={{0,16},{1,17},{2,18},{3,19},{4,20},{5,21},{6,22},{7,23},{8,24},{9,... | collective-permute-start | bytes 3145736 | tf_op jit(solution)/shard_map/ppermute | solution.py:1045
  280.5 14.9 %collective-permute-start.24 = (bf16[8,64,512]{2,1,0:T(8,128)(2,1)S(1)}, bf16[8,64,512]{2,1,0:T(8,128)(2,1)S(1)}, u32[]{:S(2)}, u32[]{:S(2)}) collective-permute-start(bf16[8,64,512]{2,1,0:T(8,128)(2,1)S(1)} %get-tuple-element.152), channel_id=1, source_target_pairs={{0,1},{1,0},{2,3},{3,2},{4,5},{5,4},{6,7},{7,6},{8,9},{9,8},{10,11... | collective-permute-start | bytes 1572872 | tf_op jit(solution)/shard_map/ppermute | solution.py:753
  283.2 9.9 %collective-permute-start.22 = (bf16[6,64,512]{2,1,0:T(8,128)(2,1)S(1)}, bf16[6,64,512]{2,1,0:T(8,128)(2,1)S(1)}, u32[]{:S(2)}, u32[]{:S(2)}) collective-permute-start(bf16[6,64,512]{2,1,0:T(8,128)(2,1)S(1)} %get-tuple-element.163), channel_id=1, source_target_pairs={{0,4},{4,8},{8,12},{12,14},{14,10},{10,6},{6,2},{2,0},{1,5},{5,9},... | collective-permute-start | bytes 1179656 | tf_op jit(solution)/shard_map/ppermute | solution.py:749
  285.4 32.5 %collective-permute-start.27 = (bf16[16,64,512]{2,1,0:T(8,128)(2,1)S(1)}, bf16[16,64,512]{2,1,0:T(8,128)(2,1)S(1)}, u32[]{:S(2)}, u32[]{:S(2)}) collective-permute-start(bf16[16,64,512]{2,1,0:T(8,128)(2,1)S(1)} %pad_maximum_fusion.17), channel_id=1, source_target_pairs={{0,1},{1,0},{2,3},{3,2},{4,5},{5,4},{6,7},{7,6},{8,9},{9,8},{10,11... | collective-permute-start | bytes 3145736 | tf_op jit(solution)/shard_map/ppermute | solution.py:753
  297.0 22.8 %collective-permute-start.26 = (bf16[16,64,512]{2,1,0:T(8,128)(2,1)S(1)}, bf16[16,64,512]{2,1,0:T(8,128)(2,1)S(1)}, u32[]{:S(2)}, u32[]{:S(2)}) collective-permute-start(bf16[16,64,512]{2,1,0:T(8,128)(2,1)S(1)} %pad_maximum_fusion.16), channel_id=1, source_target_pairs={{0,2},{4,0},{8,4},{12,8},{14,12},{10,14},{6,10},{2,6},{1,3},{5,1},... | collective-permute-start | bytes 3145736 | tf_op jit(solution)/shard_map/ppermute | solution.py:749
  297.5 23.5 %collective-permute-start.25 = (bf16[16,64,512]{2,1,0:T(8,128)(2,1)S(1)}, bf16[16,64,512]{2,1,0:T(8,128)(2,1)S(1)}, u32[]{:S(2)}, u32[]{:S(2)}) collective-permute-start(bf16[16,64,512]{2,1,0:T(8,128)(2,1)S(1)} %pad_maximum_fusion.15), channel_id=1, source_target_pairs={{0,4},{4,8},{8,12},{12,14},{14,10},{10,6},{6,2},{2,0},{1,5},{5,9},... | collective-permute-start | bytes 3145736 | tf_op jit(solution)/shard_map/ppermute | solution.py:749
  299.4 42.1 %collective-permute-start.30 = (bf16[20,64,512]{2,1,0:T(8,128)(2,1)S(1)}, bf16[20,64,512]{2,1,0:T(8,128)(2,1)S(1)}, u32[]{:S(2)}, u32[]{:S(2)}) collective-permute-start(bf16[20,64,512]{2,1,0:T(8,128)(2,1)S(1)} %pad_maximum_fusion.9), channel_id=1, source_target_pairs={{0,1},{1,0},{2,3},{3,2},{4,5},{5,4},{6,7},{7,6},{8,9},{9,8},{10,11... | collective-permute-start | bytes 3932168 | tf_op jit(solution)/shard_map/ppermute | solution.py:753
  321.8 28.3 %collective-permute-start.29 = (bf16[20,64,512]{2,1,0:T(8,128)(2,1)S(1)}, bf16[20,64,512]{2,1,0:T(8,128)(2,1)S(1)}, u32[]{:S(2)}, u32[]{:S(2)}) collective-permute-start(bf16[20,64,512]{2,1,0:T(8,128)(2,1)S(1)} %pad_maximum_fusion.8), channel_id=1, source_target_pairs={{0,2},{4,0},{8,4},{12,8},{14,12},{10,14},{6,10},{2,6},{1,3},{5,1},... | collective-permute-start | bytes 3932168 | tf_op jit(solution)/shard_map/ppermute | solution.py:749
  322.8 28.5 %collective-permute-start.28 = (bf16[20,64,512]{2,1,0:T(8,128)(2,1)S(1)}, bf16[20,64,512]{2,1,0:T(8,128)(2,1)S(1)}, u32[]{:S(2)}, u32[]{:S(2)}) collective-permute-start(bf16[20,64,512]{2,1,0:T(8,128)(2,1)S(1)} %pad_maximum_fusion.7), channel_id=1, source_target_pairs={{0,4},{4,8},{8,12},{12,14},{14,10},{10,6},{6,2},{2,0},{1,5},{5,9},... | collective-permute-start | bytes 3932168 | tf_op jit(solution)/shard_map/ppermute | solution.py:749
  324.5 36.1 %collective-permute-start.33 = (bf16[20,64,512]{2,1,0:T(8,128)(2,1)S(1)}, bf16[20,64,512]{2,1,0:T(8,128)(2,1)S(1)}, u32[]{:S(2)}, u32[]{:S(2)}) collective-permute-start(bf16[20,64,512]{2,1,0:T(8,128)(2,1)S(1)} %pad_maximum_fusion.12), channel_id=1, source_target_pairs={{0,1},{1,0},{2,3},{3,2},{4,5},{5,4},{6,7},{7,6},{8,9},{9,8},{10,11... | collective-permute-start | bytes 3932168 | tf_op jit(solution)/shard_map/ppermute | solution.py:753
  352.3 19.7 %collective-permute-start.32 = (bf16[20,64,512]{2,1,0:T(8,128)(2,1)S(1)}, bf16[20,64,512]{2,1,0:T(8,128)(2,1)S(1)}, u32[]{:S(2)}, u32[]{:S(2)}) collective-permute-start(bf16[20,64,512]{2,1,0:T(8,128)(2,1)S(1)} %pad_maximum_fusion.11), channel_id=1, source_target_pairs={{0,2},{4,0},{8,4},{12,8},{14,12},{10,14},{6,10},{2,6},{1,3},{5,1},... | collective-permute-start | bytes 3932168 | tf_op jit(solution)/shard_map/ppermute | solution.py:749
  354.0 18.0 %collective-permute-start.31 = (bf16[20,64,512]{2,1,0:T(8,128)(2,1)S(1)}, bf16[20,64,512]{2,1,0:T(8,128)(2,1)S(1)}, u32[]{:S(2)}, u32[]{:S(2)}) collective-permute-start(bf16[20,64,512]{2,1,0:T(8,128)(2,1)S(1)} %pad_maximum_fusion.10), channel_id=1, source_target_pairs={{0,4},{4,8},{8,12},{12,14},{14,10},{10,6},{6,2},{2,0},{1,5},{5,9},... | collective-permute-start | bytes 3932168 | tf_op jit(solution)/shard_map/ppermute | solution.py:749
  355.6 28.5 %collective-permute-start.18 = (bf16[512,512]{1,0:T(8,128)(2,1)S(1)}, bf16[512,512]{1,0:T(8,128)(2,1)S(1)}, u32[]{:S(2)}, u32[]{:S(2)}) collective-permute-start(bf16[512,512]{1,0:T(8,128)(2,1)S(1)} %copy-done.22), channel_id=1, source_target_pairs={{0,16},{1,17},{2,18},{3,19},{4,20},{5,21},{6,22},{7,23},{8,24},{9,... | collective-permute-start | bytes 1572872 | tf_op jit(solution)/shard_map/ppermute | solution.py:1047
  359.3 17.3 %collective-permute-start.38 = (f32[15,512]{1,0:T(8,128)S(1)}, f32[15,512]{1,0:T(8,128)S(1)}, u32[]{:S(2)}, u32[]{:S(2)}) collective-permute-start(f32[15,512]{1,0:T(8,128)S(1)} %fusion.43), channel_id=1, source_target_pairs={{0,2},{2,0},{4,6},{6,4},{8,10},{10,8},{12,14},{14,12},{1,3},{3,1},... | collective-permute-start | bytes 92168 | tf_op jit(solution)/shard_map/ppermute | solution.py:875
  372.5 15.3 %collective-permute-start.34 = (bf16[8,64,512]{2,1,0:T(8,128)(2,1)S(1)}, bf16[8,64,512]{2,1,0:T(8,128)(2,1)S(1)}, u32[]{:S(2)}, u32[]{:S(2)}) collective-permute-start(bf16[8,64,512]{2,1,0:T(8,128)(2,1)S(1)} %get-tuple-element.139), channel_id=1, source_target_pairs={{0,4},{4,8},{8,12},{12,14},{14,10},{10,6},{6,2},{2,0},{1,5},{5,9},... | collective-permute-start | bytes 1572872 | tf_op jit(solution)/shard_map/ppermute | solution.py:749
  373.3 14.4 %collective-permute-start.35 = (bf16[8,64,512]{2,1,0:T(8,128)(2,1)S(1)}, bf16[8,64,512]{2,1,0:T(8,128)(2,1)S(1)}, u32[]{:S(2)}, u32[]{:S(2)}) collective-permute-start(bf16[8,64,512]{2,1,0:T(8,128)(2,1)S(1)} %get-tuple-element.138), channel_id=1, source_target_pairs={{0,2},{4,0},{8,4},{12,8},{14,12},{10,14},{6,10},{2,6},{1,3},{5,1},... | collective-permute-start | bytes 1572872 | tf_op jit(solution)/shard_map/ppermute | solution.py:749
  375.0 12.7 %collective-permute-start.36 = (bf16[6,64,512]{2,1,0:T(8,128)(2,1)S(1)}, bf16[6,64,512]{2,1,0:T(8,128)(2,1)S(1)}, u32[]{:S(2)}, u32[]{:S(2)}) collective-permute-start(bf16[6,64,512]{2,1,0:T(8,128)(2,1)S(1)} %slice.439), channel_id=1, source_target_pairs={{0,1},{1,0},{2,3},{3,2},{4,5},{5,4},{6,7},{7,6},{8,9},{9,8},{10,11... | collective-permute-start | bytes 1179656 | tf_op jit(solution)/shard_map/ppermute | solution.py:753
  (49 other events, 275.3 us)

commit v4 on v3

--- a/solution.py
+++ b/solution.py
@@ -11,7 +11,7 @@
 HEADS = 8
 STEP = 5
 CAUSAL = 512
-RB = 512
+RB = 1024
 NEG = -1e30
 
 eps_norm = 1e-05
@@ -89,6 +89,17 @@
         extra = jnp.where(row == number, value, extra)
     extra = extra.astype(bfloat)
     return jnp.concatenate([mine, extra] if head == 0 else [extra, mine], 0)
+
+
+def pack_rows(target, first, value):
+    rows = value.shape[0]
+    for number, one in enumerate(split_three(value)):
+        target[first + number * rows : first + (number + 1) * rows] = one.astype(bfloat)
+
+
+def unpack_rows(packed, rows):
+    high, middle, rest = (packed[n * rows : (n + 1) * rows].astype(single) for n in range(3))
+    return (high + middle) + rest
 
 
 def split_three(value):
@@ -245,6 +256,9 @@
 
 
 def by_rows(length, body, init=0):
+    if length <= RB:
+        return body(pl.ds(0, length), init)
+
     def step(index, carry):
         return body(block_of(index, RB), carry)
 
@@ -276,64 +290,86 @@
 
 
 class Moves:
-    def __init__(self, role):
+    def __init__(self, role, spare):
         self.role = role
+        self.spare = spare
+        self.some = []
         self.loads = []
         self.stores = []
+        self.begun = set()
         self.waited = set()
 
     def load(self, dest, ways, semaphores):
-        def begin(way):
+        def each(way, act):
             for number, (source, first, at, rows) in enumerate(way):
+                target = dest
                 if rows is not None:
                     source = source.at[pl.ds(first, rows)]
                     target = dest.at[pl.ds(at, rows)]
-                else:
-                    target = dest
-                pltpu.make_async_copy(source, target, semaphores.at[number]).start()
-
-        def finish(way):
-            for number, (source, first, at, rows) in enumerate(way):
-                if rows is not None:
-                    source = source.at[pl.ds(first, rows)]
-                    target = dest.at[pl.ds(at, rows)]
-                else:
-                    target = dest
-                pltpu.make_async_copy(source, target, semaphores.at[number]).wait()
+                act(pltpu.make_async_copy(source, target, semaphores.at[number]))
 
         def split(act):
             if len(ways) == 1:
-                act(ways[0])
+                each(ways[0], act)
                 return
-            pl.when(self.role != 0)(lambda: act(ways[0]))
-            pl.when(self.role == 0)(lambda: act(ways[1]))
-
-        split(begin)
-        self.loads.append((dest, lambda: split(finish)))
+            pl.when(self.role != 0)(lambda: each(ways[0], act))
+            pl.when(self.role == 0)(lambda: each(ways[1], act))
+
+        self.loads.append((dest, split))
+
+    def begin(self, *refs):
+        for number, (dest, split) in enumerate(self.loads):
+            if number not in self.begun and any(dest is ref for ref in refs):
+                self.begun.add(number)
+                split(lambda copy: copy.start())
 
     def need(self, *refs):
-        for number, (dest, finish) in enumerate(self.loads):
+        self.begin(*refs)
+        for number, (dest, split) in enumerate(self.loads):
             if number not in self.waited and any(dest is ref for ref in refs):
                 self.waited.add(number)
-                finish()
+                split(lambda copy: copy.wait())
+
+    def follow(self, *refs):
+        self.begin(*refs)
+        for dest, unused in self.loads:
+            self.begin(dest)
 
     def rest(self):
+        self.follow()
         self.need(*[dest for dest, unused in self.loads])
 
-    def place(self, source, target, semaphore):
-        self.stores.append([source, target, semaphore, None])
+    def place(self, source, target, semaphores):
+        self.stores.append((source, target, semaphores, []))
 
     def put(self, *refs):
-        for entry in self.stores:
-            if entry[3] is None and any(entry[0] is ref for ref in refs):
-                entry[3] = pltpu.make_async_copy(entry[0], entry[1], entry[2])
-                entry[3].start()
+        for source, target, semaphores, copies in self.stores:
+            if not copies and any(source is ref for ref in refs):
+                copies.append(pltpu.make_async_copy(source, target, semaphores.at[0]))
+                copies[0].start()
+
+    def put_rows(self, ref, first, rows):
+        for source, target, semaphores, copies in self.stores:
+            if source is ref:
+                at = pl.ds(first, rows)
+                copies.append(
+                    pltpu.make_async_copy(source.at[at], target.at[at], semaphores.at[len(copies)])
+                )
+                copies[-1].start()
+
+    def put_if(self, wanted, source, target):
+        copy = pltpu.make_async_copy(source, target, self.spare.at[len(self.some)])
+        pl.when(wanted)(copy.start)
+        self.some.append((wanted, copy))
 
     def finish(self):
         self.rest()
         self.put(*[entry[0] for entry in self.stores])
         for entry in self.stores:
-            entry[3].wait()
+            for copy in entry[3]:
+                copy.wait()
+        for wanted, copy in self.some:
+            pl.when(wanted)(copy.wait)
 
 
 def part(value, first, rows):
@@ -361,8 +397,9 @@
     for kind, value in ins:
         if kind == "load":
             ways = [[(arg(v, HB), first, at, rows) for v, first, at, rows in way] for way in value]
-            v, first, at, rows = value[0][0]
-            total = max(a + r for _, _, a, r in value[0]) if rows is not None else None
+            way = value[0] or value[1]
+            v, first, at, rows = way[0]
+            total = max(a + r for _, _, a, r in way) if rows is not None else None
             shape = v.shape if rows is None else (total,) + v.shape[1:]
             held.append(("load", ways, shape, v.dtype, max(len(w) for w in ways)))
         else:
@@ -375,18 +412,18 @@
     for kind, shape in outs:
         if kind == "store":
             vmem.append(pltpu.VMEM(shape.shape, shape.dtype))
-            sems.append(pltpu.SemaphoreType.DMA((1,)))
+            sems.append(pltpu.SemaphoreType.DMA((6,)))
     count_in, count_out = len(args), len(outs)
 
     def kernel(*refs):
         inputs, outputs = refs[:count_in], refs[count_in : count_in + count_out]
         rest = refs[count_in + count_out :]
         buffers, semaphores = list(rest[: len(vmem)]), list(rest[len(vmem) : len(vmem) + len(sems)])
-        extra = rest[len(vmem) + len(sems) :]
+        spare, *extra = rest[len(vmem) + len(sems) :]
         scal_ref = inputs[0]
 
         def run():
-            moves = Moves(scal_ref[2])
+            moves = Moves(scal_ref[2], spare)
             given = []
             for entry in held:
                 if entry[0] == "load":
@@ -399,7 +436,7 @@
             for (kind, unused), output in zip(outs, outputs):
                 if kind == "store":
                     source, semaphore = buffers.pop(0), semaphores.pop(0)
-                    moves.place(source, output, semaphore.at[0])
+                    moves.place(source, output, semaphore)
                     given.append(source)
                 else:
                     given.append(output)
@@ -419,13 +456,17 @@
         in_specs=specs,
         out_specs=[HB] * count_out,
         out_shape=[shape for unused, shape in outs],
-        scratch_shapes=vmem + sems + list(scratch),
+        scratch_shapes=vmem + sems + [pltpu.SemaphoreType.DMA((2,))] + list(scratch),
         input_output_aliases=pairs,
         compiler_params=pltpu.CompilerParams(vmem_limit_bytes=62 << 20),
         name=name,
     )(*args)
 
 
+def halves_of(length):
+    return [pl.ds(0, length // 2), pl.ds(length // 2, length // 2)]
+
+
 def zero_rows(width):
     return (jnp.zeros((1, width), single),) * 3
 
@@ -435,22 +476,24 @@
         ref[number : number + 1] = row
 
 
-def project_norm(length, ctx_t, weight, inner_ref, vec, resid_ref, out_ref):
-    def body(rows, carry):
+def project_norm(io, length, ctx_t, weight, inner_ref, vec, resid_ref, out_ref):
+    for rows in halves_of(length):
         branch = mm(ctx_t[:, rows].T, weight[...])
         resid = inner_ref[rows].astype(single) * vec[0:1] + branch
         resid_ref[rows] = resid
         out_ref[rows] = normed(resid)[0] * vec[1:2] + vec[2:3]
-        return carry
-
-    by_rows(length, body)
-
-
-def self_forward(io, scal, x, weight, vec, outs, query_t, value_t, key_tiles, ready):
-    query, key, value, ctx_t, lse, resid, out = outs
+        for ref in (resid_ref, out_ref):
+            io.put_rows(ref, rows.start, rows.size)
+
+
+def self_forward(io, scal, x, weight, vec, outs, query_t, value_t, key_tiles, packed, ready):
+    query, key, value, ctx_t, lse, resid, out, swap = outs
     length, width = x.shape
+    some = length // 2
+    io.begin(x)
+    ready()
     io.need(x)
-    ready()
+    io.follow()
 
     def body(rows, carry):
         tile = x[rows]
@@ -465,19 +508,24 @@
     attend(scal[0], scal[1], key, query_t, value_t, ctx_t, lse, key_tiles)
     io.put(ctx_t, lse)
     io.rest()
-    project_norm(length, ctx_t, weight.at[3 * width :], x, vec, resid, out)
+    project_norm(io, length, ctx_t, weight.at[3 * width :], x, vec, resid, out)
+
+    pl.when(scal[2] == 0)(lambda: pack_rows(packed, 0, out[some:]))
+    io.put_if(scal[2] == 0, packed, swap.at[pl.ds(0, 3 * some)])
 
 
 def self_forward_body(io, scal, x, weight, vec, *refs):
-    self_forward(io, scal, x, weight, vec, refs[:7], *refs[7:], lambda: io.need(weight))
+    io.begin(x)
+    self_forward(io, scal, x, weight, vec, refs[:8], *refs[8:], lambda: io.need(weight))
 
 
 def placed_forward_body(where, io, scal, table, x, vec, *refs):
     sources, refs = refs[: len(where)], refs[len(where) :]
-    outs, (weight, rest) = refs[:7], refs[7:9]
-    query_t, value_t, key_tiles, semaphores = refs[9:]
+    outs, (weight, rest) = refs[:8], refs[8:10]
+    query_t, value_t, key_tiles, packed, semaphores = refs[10:]
     size = sources[0].shape[1]
     cut = weight.shape[0] // size
+    io.begin(x)
 
     for source, ranges in zip(sources, where):
         for start, stop, distance, other, first in ranges:
@@ -500,32 +548,34 @@
         pltpu.make_async_copy(weight, weight, semaphores.at[0]).wait()
         io.put(weight)
 
-    self_forward(io, scal, x, weight, vec, outs, query_t, value_t, key_tiles, ready)
+    self_forward(io, scal, x, weight, vec, outs, query_t, value_t, key_tiles, packed, ready)
     pltpu.make_async_copy(rest, rest, semaphores.at[1]).wait()
     io.put(rest)
 
 
 def encoder_ff_body(
-    io, scal, inner, up, down, cross, vec, activ, slope, resid, memory, sendout
+    io, scal, inner, up, down, cross, vec, held, activ, slope, resid, memory, swap, sendout
 ):
     length, width = inner.shape
+    io.need(inner, up)
+    io.follow(down)
+    for rows in [pl.ds(0, length)]:
+        act, grad = gelu_parts(mm_nt(inner[rows].astype(bfloat), up[...]))
+        activ[rows] = act.astype(bfloat)
+        slope[rows] = grad.astype(bfloat)
+        for ref in (activ, slope):
+            io.put_rows(ref, rows.start, rows.size)
     io.rest()
-
-    def body(rows, carry):
-        tile = inner[rows]
-        act, grad = gelu_parts(mm_nt(tile.astype(bfloat), up[...]))
-        act = act.astype(bfloat)
-        activ[rows] = act
-        slope[rows] = grad.astype(bfloat)
-        total = tile * vec[0:1] + mm(act, down[...])
+    for rows in [pl.ds(0, length)]:
+        total = inner[rows] * vec[0:1] + mm(activ[rows], down[...])
         resid[rows] = total
         mem = (normed(total)[0] * vec[1:2] + vec[2:3]).astype(bfloat)
         memory[rows] = mem
-        sendout[0, rows] = mm(mem, cross[:width]).astype(bfloat)
-        sendout[1, rows] = mm(mem, cross[width:]).astype(bfloat)
-        return carry
-
-    by_rows(length, body)
+        sendout[rows] = mm(mem, cross[:width]).astype(bfloat)
+        sendout[pl.ds(length + rows.start, rows.size)] = mm(mem, cross[width:]).astype(bfloat)
+        for ref in (resid, memory):
+            io.put_rows(ref, rows.start, rows.size)
+    io.put_if(scal[2] != 0, sendout, swap)
 
 
 def ff_back(length, emit, grad_branch, activ, slope, inner_low, up, down, grad_inner):
@@ -570,15 +620,21 @@
 
 
 def middle_body(
-    io, scal, inner, keys, cross, cross_vec, up, down, ff_vec, cotan,
-    output, sendback, grad_inner, grads, grad_vec,
+    io, scal, inner, packed, keys, cross, cross_vec, up, down, ff_vec, cotan,
+    output, sendback, grad_inner, grads, grad_vec, swap,
     query, query_t, ctx_t, lse, resid, after, activ, slope, low_rows, grad_branch, grad_after,
     grad_ctx, grad_ctx_t, dot_ref, key_t, value_t, grad_key, grad_value, grad_query_t,
-    key_tiles, key_two, value_two,
+    key_tiles, key_two, value_two, swap_out,
 ):
     rows_here, width = inner.shape
-    hidden = up.shape[0]
-    io.need(inner, cross, keys)
+    hidden, length = up.shape[0], keys.shape[0] // 2
+    key_rows, value_rows = keys.at[:length], keys.at[length:]
+    io.need(inner, packed, cross, keys)
+    io.follow(cross_vec, up, down)
+
+    @pl.when(scal[2] != 0)
+    def _():
+        inner[...] = unpack_rows(packed, rows_here)
 
     def project(rows, carry):
         query[rows] = mm(inner[rows].astype(bfloat), cross[:width]).astype(bfloat)
@@ -586,15 +642,15 @@
         return carry
 
     def turn(rows, carry):
-        key_t[:, rows] = keys[0, rows].T
-        value_t[:, rows] = keys[1, rows].T
+        key_t[:, rows] = key_rows[rows].T
+        value_t[:, rows] = value_rows[rows].T
         return carry
 
     by_rows(rows_here, project)
-    by_rows(keys.shape[1], turn)
-    attend(scal[4], None, keys.at[0], query_t, value_t, ctx_t, lse, key_tiles)
+    by_rows(length, turn)
+    attend(scal[4], None, key_rows, query_t, value_t, ctx_t, lse, key_tiles)
     io.rest()
-    project_norm(rows_here, ctx_t, cross.at[width:], inner, cross_vec, resid, after)
+    project_norm(io, rows_here, ctx_t, cross.at[width:], inner, cross_vec, resid, after)
 
     def feed(rows, carry):
         tile = after[rows]
@@ -620,6 +676,9 @@
     def emit(which, number, value):
         first = 2 * width + which * hidden + number * 512
         grads[first : first + 512] = value.astype(bfloat)
+        if which == 1 and number in (1, 3):
+            for start in (2 * width, 2 * width + hidden):
+                io.put_rows(grads, start + (number - 1) * 512, 1024)
 
     ff_back(rows_here, emit, grad_branch, activ, slope, low_rows, up, down, grad_after)
     branch_back(rows_here, resid, grad_after, inner, cross_vec, grad_branch, grad_inner, grad_vec)
@@ -627,17 +686,18 @@
     grads[width : 2 * width] = mm(ctx_t[...], grad_branch[...]).astype(bfloat)
     ctx_back(rows_here, grad_branch, cross.at[width:], ctx_t, grad_ctx, grad_ctx_t, dot_ref)
     attend_back(
-        scal[4], None, query, keys.at[0], keys.at[1], query_t, key_t, grad_ctx, grad_ctx_t, lse, dot_ref,
+        scal[4], None, query, key_rows, value_rows, query_t, key_t, grad_ctx, grad_ctx_t, lse, dot_ref,
         grad_key, grad_value, grad_query_t, key_two, value_two,
     )
 
     def send(rows, carry):
-        sendback[0, rows] = (grad_key[rows] * 0.125).astype(bfloat)
-        sendback[1, rows] = grad_value[rows].astype(bfloat)
+        sendback[rows] = (grad_key[rows] * 0.125).astype(bfloat)
+        sendback[pl.ds(length + rows.start, rows.size)] = grad_value[rows].astype(bfloat)
         return carry
 
-    by_rows(keys.shape[1], send)
+    by_rows(length, send)
     io.put(sendback)
+    io.put_if(scal[2] == 0, sendback, swap)
 
     def last(rows, carry):
         grad_query = grad_query_t[:, rows].T
@@ -647,7 +707,16 @@
 
     by_rows(rows_here, last)
     io.put(grad_inner)
+
+    @pl.when(scal[2] != 0)
+    def _():
+        pack_rows(swap_out, 0, grad_inner[...])
+        swap_out[3 * rows_here :] = output[...]
+
+    io.put_if(scal[2] != 0, swap_out, swap)
+
     grads[:width] = mm_tn(inner[...].astype(bfloat), grad_ctx[...]).astype(bfloat)
+    io.put_rows(grads, 0, 2 * width)
 
 
 def encoder_back_body(
@@ -657,40 +726,48 @@
 ):
     length, width = inner.shape
     emit = Emitter(table, target, stage, semaphores)
+    io.begin(own, received, cross, inner)
+    io.follow(memory, vec, resid, down, slope, up, activ)
     io.need(own, received, cross, inner)
 
     def body(rows, carry):
-        for number in range(2):
-            total = own[number, rows].astype(single) + received[number, rows].astype(single)
-            own[number, rows] = total.astype(bfloat)
-        grad_mem[rows] = mm_nt(own[0, rows], cross[:width]) + mm_nt(own[1, rows], cross[width:])
+        own[...] = added(own[...], received[...])
+        grad_mem[rows] = mm_nt(own[:length], cross[:width]) + mm_nt(own[length:], cross[width:])
         inner_low[rows] = inner[rows].astype(bfloat)
         return carry
 
     by_rows(length, body)
-    io.rest()
+    io.need(vec, resid, memory)
+    emit.chunk(8, 16, mm_tn(memory[...], own[:length]))
+    emit.chunk(9, 20, mm_tn(memory[...], own[length:]))
     branch_back(length, resid, grad_mem, inner, vec, grad_branch, grad_inner, grad_vec)
     io.put(grad_vec)
+    io.rest()
 
     def each(which, number, value):
         emit.chunk(2 * number + which, 24 + 16 * which + 4 * number, value)
 
     ff_back(length, each, grad_branch, activ, slope, inner_low, up, down, grad_inner)
     io.put(grad_inner)
-    emit.chunk(8, 16, mm_tn(memory[...], own[0]))
-    emit.chunk(9, 20, mm_tn(memory[...], own[1]))
     emit.wait()
 
 
 def self_back_body(
-    io, scal, table, x, weight, out_weight, vec, resid, query, key, value, ctx_t, lse, grad_out, held,
+    io, scal, table, x, weight, out_weight, vec, resid, query, key, value, ctx_t, lse, grad_out, packed, held,
     grad_x, grad_vec, target,
     grad_branch, grad_ctx, grad_ctx_t, dot_ref, query_t, key_t, grad_key, grad_value, grad_query_t,
     key_two, value_two, stage, semaphores,
 ):
     length, width = x.shape
     emit = Emitter(table, target, stage, semaphores)
-    io.need(resid, grad_out, x, vec)
+    some = length // 2
+    io.need(resid, grad_out, packed, x, vec)
+    io.follow(ctx_t, out_weight, query, key, value)
+
+    @pl.when(scal[2] == 0)
+    def _():
+        grad_out[some:] = unpack_rows(packed, some)
+
     branch_back(length, resid, grad_out, x, vec, grad_branch, grad_x, grad_vec)
     io.put(grad_vec)
     io.need(ctx_t, out_weight)
@@ -757,6 +834,10 @@
     return lax.optimization_barrier((round_ring(up, 1), round_ring(down, -1), swapped(across)))
 
 
+def partner(value, axis, bit):
+    return lax.ppermute(value, axis, [(i, i ^ bit) for i in range(lax.axis_size(axis))])
+
+
 def join(*values):
     return jnp.concatenate(values, 0)
 
@@ -808,7 +889,16 @@
     return sum(value.astype(single) for value in values).astype(bfloat)
 
 
-def ring_scatter(grads):
+def ring_scatter(grads, vector):
+    partners = [("narrow", 1), ("wide", 1), ("wide", 2), ("wide", 4), ("half", 1)]
+
+    def step_of(*values):
+        nonlocal vector
+        ring = (round_ring(values[0], 1), round_ring(values[1], -1), swapped(values[2]))
+        *ring, other = lax.optimization_barrier((*ring, partner(vector, *partners.pop(0))))
+        vector = vector + other
+        return ring
+
     lead, half = LEAD, LEAD // 2
     late = grads.shape[2] - lead
 
@@ -849,7 +939,7 @@
         total[late:].astype(bfloat),
     )
     first = sum(value.astype(single) for value in (mine(0), join(*nearest), up, down))
-    return join(first, total[:late] + across.astype(single))
+    return join(first, total[:late] + across.astype(single)), vector
 
 
 def shaped(*shape, dtype=single):
@@ -872,7 +962,7 @@
     size = lax.axis_size(axis)
     bit = 1
     while bit < size:
-        value = value + lax.ppermute(value, axis, [(i, i ^ bit) for i in range(size)])
+        value = value + partner(value, axis, bit)
         bit *= 2
     return value
 
@@ -960,14 +1050,15 @@
 
     low_out = partial(store, dtype=bfloat)
     two, four = low_vm(2, length, 128), low_vm(4, length, 128)
-    down_half, up_half = [(1, 0)], [(0, 1)]
+    down_half, up_half, both_halves = [(1, 0)], [(0, 1)], [(0, 1), (1, 0)]
 
     forward_outs = (
         [low_out(length, width)] * 3
         + [low_out(width, length), store(HEADS, length)]
         + [store(length, width)] * 2
-    )
-    forward_scratch = [low_vm(width, length), low_vm(width, length), four]
+        + [("hbm", low(2 * length, width))]
+    )
+    forward_scratch = [low_vm(width, length), low_vm(width, length), four, low_vm(3 * some, width)]
     if on_ring:
         *forward, weight, rest = call(
             partial(placed_forward_body, [where for where, unused in found]),
@@ -988,37 +1079,39 @@
             forward_outs,
             forward_scratch,
         )
-    query, key, value, ctx_t, lse, resid, inner = forward
+    query, key, value, ctx_t, lse, resid, inner, swap = forward
     rest_other = lax.ppermute(rest, "half", down_half)
     cross_w = part(rest, 0, 2 * width)
     up_w = part(rest, 2 * width, hidden)
     down_w = part(rest, 2 * width + hidden, hidden)
-    inner_other = lax.ppermute(inner[some:], "half", down_half)
-    activ, slope, ff_resid, memory, sendout = call(
+    activ, slope, ff_resid, memory, swap = call(
         encoder_ff_body,
         "encoder_ff",
         scal,
         1,
-        [whole(inner), up_w, down_w, cross_w, memory_vec],
+        [whole(inner), up_w, down_w, cross_w, memory_vec, ("hbm", swap)],
         [low_out(length, hidden)] * 2
-        + [store(length, width), low_out(length, width), low_out(2, length, width)],
-        [],
-    )
-    sendout_other = lax.ppermute(sendout, "half", up_half)
+        + [store(length, width), low_out(length, width), ("hbm", low(2 * length, width))],
+        [low_vm(2 * length, width)],
+        [(5, 4)],
+    )
+    swap_other = lax.ppermute(swap, "half", both_halves)
 
     def shared(first, rows):
         return either([(rest_other, first, 0, rows)], [(rest, first, 0, rows)])
 
-    mid_inner = either([(inner_other, 0, 0, some)], [(inner, 0, 0, some)])
-    keys = either([(sendout, 0, 0, None)], [(sendout_other, 0, 0, None)])
+    mid_inner = either([], [(inner, 0, 0, some)])
+    mid_packed = either([(swap_other, 0, 0, 3 * some)], [])
+    keys = either([(swap, 0, 0, None)], [(swap_other, 0, 0, None)])
     cotan = cotangent[0]
-    output, sendback, grad_one, grad_rest, grad_middle_vec = call(
+    output, sendback, grad_one, grad_rest, grad_middle_vec, swap = call(
         middle_body,
         "decoder_middle",
         scal,
         None,
         [
             mid_inner,
+            mid_packed,
             keys,
             shared(0, 2 * width),
             cross_vec,
@@ -1029,22 +1122,24 @@
         ],
         [
             low_out(some, width),
-            low_out(2, length, width),
+            low_out(2 * length, width),
             store(some, width),
             low_out(rest_rows, width),
             store(6, width),
+            ("hbm", low(2 * length, width)),
         ],
         [low_vm(some, width), low_vm(width, some), low_vm(width, some), full_vm(HEADS, some)]
         + [full_vm(some, width), full_vm(some, width), low_vm(some, hidden), low_vm(some, hidden)]
         + [low_vm(some, width), low_vm(some, width), full_vm(some, width)]
         + [low_vm(some, width), low_vm(width, some), full_vm(HEADS, some)]
         + [low_vm(width, length), low_vm(width, length)]
-        + [full_vm(length, width), full_vm(length, width), low_vm(width, some), four, two, two],
-    )
-    sendback_other = lax.ppermute(sendback, "half", down_half)
-    grad_one_other = lax.ppermute(grad_one, "half", up_half)
+        + [full_vm(length, width), full_vm(length, width), low_vm(width, some), four, two, two]
+        + [low_vm(2 * length, width)],
+    )
+    swap_other = lax.ppermute(swap, "half", both_halves)
+    grad_rest, swap_other = lax.optimization_barrier((grad_rest, swap_other))
     grad_rest_other = lax.ppermute(grad_rest, "half", up_half)
-    output_other = lax.ppermute(output, "half", up_half)
+    output = join(output, swap_other[3 * some :])
     grad_inner, grad_memory_vec, target = call(
         encoder_back_body,
         "encoder_back",
@@ -1053,7 +1148,7 @@
         [
             ("smem", table),
             whole(sendback),
-            whole(sendback_other),
+            whole(swap_other),
             whole(memory),
             cross_w,
             whole(inner),
@@ -1091,13 +1186,14 @@
             whole(lse),
             either(
                 [(grad_inner, 0, 0, length)],
-                [(grad_one, 0, 0, some), (grad_one_other, 0, some, some)],
+                [(grad_one, 0, 0, some)],
             ),
+            either([], [(swap_other, 0, 0, 3 * some)]),
             ("hbm", target),
         ],
         [store(length, width), store(3, width), ("hbm", slots)],
         back_scratch + stage_of(4),
-        [(12, 2)],
+        [(13, 2)],
     )
     (target,) = call(
         merge_body,
@@ -1123,14 +1219,13 @@
         ],
         0,
     )
-    for axis in ("narrow", "wide"):
-        vec_grads = sum_over(vec_grads, axis)
     if on_ring:
-        mine = ring_scatter(target.reshape(wide_size, 2, capacity, half_rows, width))
+        grads = target.reshape(wide_size, 2, capacity, half_rows, width)
+        mine, vec_grads = ring_scatter(grads, vec_grads)
     else:
         mine = lax.psum_scatter(target, ("wide", "narrow"), scatter_dimension=0, tiled=True)
-    mine, vec_grads = lax.optimization_barrier((mine, vec_grads))
-    vec_grads = sum_over(vec_grads, "half")
+        for axis in ("narrow", "wide", "half"):
+            vec_grads = sum_over(vec_grads, axis)
     used = jnp.sum((owner_row == wide_at).astype(jnp.int32))
     mine = jnp.where((jnp.arange(capacity) < used)[:, None, None], mine.astype(single), 0.0)
     new_weight, new_first, new_second = adam(
@@ -1139,7 +1234,6 @@
     vec_weight, vec_first, vec_second = adam(
         vec_master, vec_grads, vec_one, vec_two, rate_vector, 0.0
     )
-    output = jnp.concatenate([output, output_other], 0)
     return (
         jnp.where(is_source, memory, output)[None, None],
         grad_x[None, None],

time: 401 us -> 379 us (0.945)
  starting transfers between devices: 55.2 us -> 47.1 us
  local copies, waits for them, and re-layouts: 20.4 us -> 14.1 us
  Pallas kernels: 134 us -> 128 us
    ppermute x10 -> x7, waiting for transfers between devices: 12.5 us -> 55.8 us  [the longest x5 46.8 us: partner(): lax.ppermute(value, axis, [(i, i ^ bit) for i in range(lax.axis_size(axis...]
    ppermute x10, waiting for transfers between devices: 87.1 us -> 56.8 us  [swapped(): return lax.ppermute(value, 'narrow', [(0, 1), (1, 0)])]
    ppermute x20, waiting for transfers between devices: 64.2 us -> 48.8 us  [round_ring(): lax.ppermute(value, 'wide', [(RING[i], RING[(i + step) % count]) for i in...]
    ppermute x10 -> x7, starting transfers between devices: 16 us -> 6.77 us  [the longest x5 6.63 us: partner(): lax.ppermute(value, axis, [(i, i ^ bit) for i in range(lax.axis_size(axis...]
    pallas_call x6, Pallas kernels: 134 us -> 128 us  [call(): pl.pallas_call(kernel, in_specs=specs, out_specs=[HB] * count_out, out_sh...]
    broadcast_in_dim x1 -> x0, other arithmetic: 4.22 us -> none  [on_device(): new_weight.astype(bfloat)[None]]
    convert_element_type x0 -> x1, other arithmetic: none -> 4.02 us  [on_device(): new_weight.astype(bfloat)[None]]
  transfers between devices with their start and end apart: 42 -> 39, of which waited for: 28 -> 26; matrix products, arithmetic and copies ran while one was open for 6% -> 5% of each run, Pallas kernels for 18% -> 18%
where the time goes in v4:
time: 379 us; the launch traced here: 375 us
  waiting for transfers between devices  161 us (42%)
  Pallas kernels  128 us (34%)
  starting transfers between devices  47.1 us (12%)
  other arithmetic  20.6 us (5%)
  local copies, waits for them, and re-layouts  14.1 us (4%)
  between operations  4.08 us (1%)
    pallas_call x6, Pallas kernels, call(): pl.pallas_call(kernel, in_specs=specs, out_specs=[HB] * count_out, out_sh...  128 us
    ppermute x10, waiting for transfers between devices, swapped(): return lax.ppermute(value, 'narrow', [(0, 1), (1, 0)])  56.8 us
    ppermute x20, waiting for transfers between devices, round_ring(): lax.ppermute(value, 'wide', [(RING[i], RING[(i + step) % count]) for i in...  48.8 us
    ppermute x5, waiting for transfers between devices, partner(): lax.ppermute(value, axis, [(i, i ^ bit) for i in range(lax.axis_size(axis...  46.8 us
    ppermute x20, starting transfers between devices, round_ring(): lax.ppermute(value, 'wide', [(RING[i], RING[(i + step) % count]) for i in...  24.9 us
    ppermute x10, starting transfers between devices, swapped(): return lax.ppermute(value, 'narrow', [(0, 1), (1, 0)])  9.74 us
    ppermute x2, waiting for transfers between devices, on_device(): swap_other = lax.ppermute(swap, 'half', both_halves)  8.97 us
  transfers between devices with their start and end apart: 39, of which 26 were waited for; matrix products, arithmetic and copies ran while one was open for 5% of the time, Pallas kernels for 18%

profile of v4, /device:TPU:0, one launch (start us, length us, event | category | flops | bytes accessed | tf_op | source)
XLA Modules:
  0.0 375.4 jit_solution(15850569036302791895)
XLA Ops:
  2.3 3.0 collective-permute-start.1
  5.5 2.0 collective-permute-start.2
  7.5 8.6 %collective-permute-done.2.refs_5_ = bf16[6,64,512]{2,1,0:T(8,128)(2,1)S(1)} collective-permute-done((bf16[6,64,512]{2,1,0:T(8,128)(2,1)S(1)}, bf16[6,64,512]{2,1,0:T(8,128)(2,1)S(1)}, u32[]{:S(2)}, u32[]{:S(2)}) %collective-permute-start.2) | collective-permute-done | bytes 393248 | tf_op jit(solution)/shard_map/ppermute | solution.py:830
  18.7 2.1 pad_maximum_fusion
  32.6 17.8 %collective-permute-done.4.refs_10_ = bf16[20,64,512]{2,1,0:T(8,128)(2,1)S(1)} collective-permute-done((bf16[20,64,512]{2,1,0:T(8,128)(2,1)}, bf16[20,64,512]{2,1,0:T(8,128)(2,1)S(1)}, u32[]{:S(2)}, u32[]{:S(2)}) %collective-permute-start.4) | collective-permute-done | bytes 1310752 | tf_op jit(solution)/shard_map/ppermute | solution.py:826
  55.9 24.4 %collective-permute-done.8.refs_11_ = bf16[20,64,512]{2,1,0:T(8,128)(2,1)S(1)} collective-permute-done((bf16[20,64,512]{2,1,0:T(8,128)(2,1)S(1)}, bf16[20,64,512]{2,1,0:T(8,128)(2,1)S(1)}, u32[]{:S(2)}, u32[]{:S(2)}) %collective-permute-start.8) | collective-permute-done | bytes 1310752 | tf_op jit(solution)/shard_map/ppermute | solution.py:830
  87.0 17.7 %collective-permute-done.10.refs_16_ = bf16[16,64,512]{2,1,0:T(8,128)(2,1)S(1)} collective-permute-done((bf16[16,64,512]{2,1,0:T(8,128)(2,1)S(1)}, bf16[16,64,512]{2,1,0:T(8,128)(2,1)S(1)}, u32[]{:S(2)}, u32[]{:S(2)}) %collective-permute-start.10) | collective-permute-done | bytes 1048608 | tf_op jit(solution)/shard_map/ppermute | solution.py:826
  105.9 3.7 collective-permute-done.11.refs_14_
  114.5 3.9 %collective-permute-done.13.refs_18_ = bf16[6,64,512]{2,1,0:T(8,128)(2,1)S(1)} collective-permute-done((bf16[6,64,512]{2,1,0:T(8,128)(2,1)S(1)}, bf16[6,64,512]{2,1,0:T(8,128)(2,1)S(1)}, u32[]{:S(2)}, u32[]{:S(2)}) %collective-permute-start.13) | collective-permute-done | bytes 393248 | tf_op jit(solution)/shard_map/ppermute | solution.py:826
  120.7 23.0 %self_forward.1 = (bf16[1024,512]{1,0:T(8,128)(2,1)}, bf16[1024,512]{1,0:T(8,128)(2,1)}, bf16[1024,512]{1,0:T(8,128)(2,1)}, bf16[512,1024]{1,0:T(8,128)(2,1)}, f...) custom-call(s32[6]{0:T(128)} %stack.23.refs_0_, ...), custom_call_target="tpu_custom_call" | custom-call | tf_op jit(solution)/shard_map/self_forward/pallas_call | solution.py:454
  144.9 13.0 %encoder_ff.1 = (bf16[1024,2048]{1,0:T(8,128)(2,1)}, bf16[1024,2048]{1,0:T(8,128)(2,1)}, f32[1024,512]{1,0:T(8,128)}, bf16[1024,512]{1,0:T(8,128)(2,1)}, bf16[2048,512]{1,0:T(8,128)(2,1)}) custom-call(s32[6]{0:T(128)} %stack.23.refs_0_, f32[1024,512]{1,0:T(8,128)} %get-tuple-element.95.refs_1_.refs_6_, ...), custom_call_target="tpu_custom_call", output_to_operand_aliasing={{4}: (6, {})} | custom-call | tf_op jit(solution)/shard_map/encoder_ff/pallas_call | solution.py:454
  158.0 4.5 %collective-permute-done.15.refs_2_.refs_4_ = bf16[2048,512]{1,0:T(8,128)(2,1)} collective-permute-done((bf16[2048,512]{1,0:T(8,128)(2,1)}, bf16[2048,512]{1,0:T(8,128)(2,1)}, u32[]{:S(2)}, u32[]{:S(2)}) %collective-permute-start.15) | collective-permute-done | bytes 2097184 | tf_op jit(solution)/shard_map/ppermute | solution.py:1098
  162.5 34.6 %decoder_middle.1 = (bf16[512,512]{1,0:T(8,128)(2,1)}, bf16[2048,512]{1,0:T(8,128)(2,1)}, f32[512,512]{1,0:T(8,128)}, bf16[5120,512]{1,0:T(8,128)(2,1)}, f32[6,512]{1,0:T(8,128)}, /*index=5*/bf16[2048,512]{1,0:T(8,128)(2,1)}) custom-call(s32[6]{0:T(128)} %stack.23.refs_0_, f32[1024,512]{1,0:T(8,128)} %get-tuple-element.95.refs_1_.refs_6_, ...), custom_call_target="tpu_custom_call" | custom-call | tf_op jit(solution)/shard_map/decoder_middle/pallas_call | solution.py:454
  197.2 4.5 %collective-permute-done.17.refs_3_.refs_14_ = bf16[2048,512]{1,0:T(8,128)(2,1)} collective-permute-done((bf16[2048,512]{1,0:T(8,128)(2,1)}, bf16[2048,512]{1,0:T(8,128)(2,1)}, u32[]{:S(2)}, u32[]{:S(2)}) %collective-permute-start.17) | collective-permute-done | bytes 2097184 | tf_op jit(solution)/shard_map/ppermute | solution.py:1139
  201.7 4.4 %collective-permute-start.18 = (bf16[5120,512]{1,0:T(8,128)(2,1)}, bf16[5120,512]{1,0:T(8,128)(2,1)}, u32[]{:S(2)}, u32[]{:S(2)}) collective-permute-start(bf16[5120,512]{1,0:T(8,128)(2,1)} %get-tuple-element.120.refs_2_), channel_id=1, source_target_pairs={{0,16},{1,17},{2,18},{3,19},{4,20},{5,21},{6,22},{7,23},{8,24},{9,... | collective-permute-start | bytes 15728648 | tf_op jit(solution)/shard_map/ppermute | solution.py:1141
  206.1 21.2 %encoder_back.1 = (f32[1024,512]{1,0:T(8,128)}, f32[3,512]{1,0:T(4,128)}, bf16[224,64,512]{2,1,0:T(8,128)(2,1)}) custom-call(s32[6]{0:T(128)} %stack.23.refs_0_, s32[112]{0:T(128)} %add.226.refs_1_, bf16[2048,512]{1,0:T(8,128)(2,1)} %get-tuple-element.112.refs_2_, bf16[2048,512]{1,0:T(8,128)(2,1)} %collective-permute-done.17.refs_3_.refs_14_, ...), custom_call_target="tpu_custom_call" | custom-call | tf_op jit(solution)/shard_map/encoder_back/pallas_call | solution.py:454
  227.3 34.7 %self_back.1 = (f32[1024,512]{1,0:T(8,128)}, f32[3,512]{1,0:T(4,128)}, bf16[224,64,512]{2,1,0:T(8,128)(2,1)}) custom-call(s32[6]{0:T(128)} %stack.23.refs_0_, s32[112]{0:T(128)} %add.226.refs_1_, bf16[1024,512]{1,0:T(8,128)(2,1)} %bitcast.168, bf16[2048,512]{1,0:T(8,128)(2,1)} %get-tuple-element.105.refs_3_.refs_4_, ...), custom_call_target="tpu_custom_call", output_to_operand_aliasing={{2}: (15, {})} | custom-call | tf_op jit(solution)/shard_map/self_back/pallas_call | solution.py:454
  262.7 1.7 merge.1
  264.5 2.4 slice_bitcast_fusion.3
  267.6 2.1 slice_bitcast_fusion.15
  274.1 8.4 %collective-permute-done.22 = f32[15,512]{1,0:T(8,128)S(1)} collective-permute-done((f32[15,512]{1,0:T(8,128)S(1)}, f32[15,512]{1,0:T(8,128)S(1)}, u32[]{:S(2)}, u32[]{:S(2)}) %collective-permute-start.22) | collective-permute-done | bytes 30752 | tf_op jit(solution)/shard_map/ppermute | solution.py:838
  288.8 16.1 %collective-permute-done.26 = f32[15,512]{1,0:T(8,128)S(1)} collective-permute-done((f32[15,512]{1,0:T(8,128)S(1)}, f32[15,512]{1,0:T(8,128)S(1)}, u32[]{:S(2)}, u32[]{:S(2)}) %collective-permute-start.26) | collective-permute-done | bytes 30752 | tf_op jit(solution)/shard_map/ppermute | solution.py:838
  306.1 2.3 collective-permute-start.28
  311.9 13.3 %collective-permute-done.29 = bf16[20,64,512]{2,1,0:T(8,128)(2,1)S(1)} collective-permute-done((bf16[20,64,512]{2,1,0:T(8,128)(2,1)S(1)}, bf16[20,64,512]{2,1,0:T(8,128)(2,1)S(1)}, u32[]{:S(2)}, u32[]{:S(2)}) %collective-permute-start.29) | collective-permute-done | bytes 1310752 | tf_op jit(solution)/shard_map/ppermute | solution.py:830
  325.2 7.9 %collective-permute-done.30 = f32[15,512]{1,0:T(8,128)S(1)} collective-permute-done((f32[15,512]{1,0:T(8,128)S(1)}, f32[15,512]{1,0:T(8,128)S(1)}, u32[]{:S(2)}, u32[]{:S(2)}) %collective-permute-start.30) | collective-permute-done | bytes 30752 | tf_op jit(solution)/shard_map/ppermute | solution.py:838
  336.7 2.5 collective-permute-start.32
  339.2 2.4 collective-permute-start.34
  341.6 1.8 collective-permute-done.33
  343.4 14.4 %collective-permute-done.34 = f32[15,512]{1,0:T(8,128)S(1)} collective-permute-done((f32[15,512]{1,0:T(8,128)S(1)}, f32[15,512]{1,0:T(8,128)S(1)}, u32[]{:S(2)}, u32[]{:S(2)}) %collective-permute-start.34) | collective-permute-done | bytes 30752 | tf_op jit(solution)/shard_map/ppermute | solution.py:838
  358.4 2.0 collective-permute-start.35
  364.2 4.5 %collective-permute-done.37 = bf16[6,64,512]{2,1,0:T(8,128)(2,1)S(1)} collective-permute-done((bf16[6,64,512]{2,1,0:T(8,128)(2,1)S(1)}, bf16[6,64,512]{2,1,0:T(8,128)(2,1)S(1)}, u32[]{:S(2)}, u32[]{:S(2)}) %collective-permute-start.37) | collective-permute-done | bytes 393248 | tf_op jit(solution)/shard_map/ppermute | solution.py:830
  371.2 4.0 %fusion.36 = (bf16[1,14,64,512]{3,2,1,0:T(8,128)(2,1)}, f32[1,14,64,512]{3,2,1,0:T(8,128)}, f32[1,14,64,512]{3,2,1,0:T(8,128)}, f32[1,14,64,512]{3,2,1,0:T(8,128)}) fusion(f32[1,14,64,512]{3,2,1,0:T(8,128)S(1)} %copy-done.1, f32[1,6,64,512]{3,2,1,0:T(8,128)S(1)} %fusion.20, f32[1,8,64,512]{3,2,1,0:T(8,128)S(1)} %fusion.19, ...), kind=kLoop, calls=%fused_computation.137 | loop fusion | flops 7798784 | bytes 13762574 | tf_op jit(solution)/shard_map/convert_element_type | solution.py:1243
  (192 shorter events, 62.3 us)
Async XLA Ops:
  2.3 15.0 %collective-permute-start.1 = (bf16[8,64,512]{2,1,0:T(8,128)(2,1)S(1)}, bf16[8,64,512]{2,1,0:T(8,128)(2,1)S(1)}, u32[]{:S(2)}, u32[]{:S(2)}) collective-permute-start(bf16[8,64,512]{2,1,0:T(8,128)(2,1)S(1)} %slice_bitcast_fusion.13), channel_id=1, source_target_pairs={{0,2},{4,0},{8,4},{12,8},{14,12},{10,14},{6,10},{2,6},{1,3},{5,1},... | collective-permute-start | bytes 1572872 | tf_op jit(solution)/shard_map/ppermute | solution.py:826
  5.3 13.4 %collective-permute-start = (bf16[8,64,512]{2,1,0:T(8,128)(2,1)S(1)}, bf16[8,64,512]{2,1,0:T(8,128)(2,1)S(1)}, u32[]{:S(2)}, u32[]{:S(2)}) collective-permute-start(bf16[8,64,512]{2,1,0:T(8,128)(2,1)S(1)} %slice_bitcast_fusion.13), channel_id=1, source_target_pairs={{0,4},{4,8},{8,12},{12,14},{14,10},{10,6},{6,2},{2,0},{1,5},{5,9},... | collective-permute-start | bytes 1572872 | tf_op jit(solution)/shard_map/ppermute | solution.py:826
  5.5 10.6 %collective-permute-start.2 = (bf16[6,64,512]{2,1,0:T(8,128)(2,1)S(1)}, bf16[6,64,512]{2,1,0:T(8,128)(2,1)S(1)}, u32[]{:S(2)}, u32[]{:S(2)}) collective-permute-start(bf16[6,64,512]{2,1,0:T(8,128)(2,1)S(1)} %slice_bitcast_fusion.20), channel_id=1, source_target_pairs={{0,1},{1,0},{2,3},{3,2},{4,5},{5,4},{6,7},{7,6},{8,9},{9,8},{10,11... | collective-permute-start | bytes 1179656 | tf_op jit(solution)/shard_map/ppermute | solution.py:830
  20.8 29.6 %collective-permute-start.4 = (bf16[20,64,512]{2,1,0:T(8,128)(2,1)}, bf16[20,64,512]{2,1,0:T(8,128)(2,1)S(1)}, u32[]{:S(2)}, u32[]{:S(2)}) collective-permute-start(bf16[20,64,512]{2,1,0:T(8,128)(2,1)} %get-tuple-element.184), channel_id=1, source_target_pairs={{0,2},{4,0},{8,4},{12,8},{14,12},{10,14},{6,10},{2,6},{1,3},{5,1},... | collective-permute-start | bytes 3932168 | tf_op jit(solution)/shard_map/ppermute | solution.py:826
  22.5 29.3 %collective-permute-start.3 = (bf16[20,64,512]{2,1,0:T(8,128)(2,1)}, bf16[20,64,512]{2,1,0:T(8,128)(2,1)S(1)}, u32[]{:S(2)}, u32[]{:S(2)}) collective-permute-start(bf16[20,64,512]{2,1,0:T(8,128)(2,1)} %get-tuple-element.185), channel_id=1, source_target_pairs={{0,4},{4,8},{8,12},{12,14},{14,10},{10,6},{6,2},{2,0},{1,5},{5,9},... | collective-permute-start | bytes 3932168 | tf_op jit(solution)/shard_map/ppermute | solution.py:826
  22.9 29.1 %collective-permute-start.5 = (bf16[20,64,512]{2,1,0:T(8,128)(2,1)}, bf16[20,64,512]{2,1,0:T(8,128)(2,1)}, u32[]{:S(2)}, u32[]{:S(2)}) collective-permute-start(bf16[20,64,512]{2,1,0:T(8,128)(2,1)} %get-tuple-element.186), channel_id=1, source_target_pairs={{0,1},{1,0},{2,3},{3,2},{4,5},{5,4},{6,7},{7,6},{8,9},{9,8},{10,11... | collective-permute-start | bytes 3932168 | tf_op jit(solution)/shard_map/ppermute | solution.py:830
  52.3 28.0 %collective-permute-start.8 = (bf16[20,64,512]{2,1,0:T(8,128)(2,1)S(1)}, bf16[20,64,512]{2,1,0:T(8,128)(2,1)S(1)}, u32[]{:S(2)}, u32[]{:S(2)}) collective-permute-start(bf16[20,64,512]{2,1,0:T(8,128)(2,1)S(1)} %pad_maximum_fusion.5), channel_id=1, source_target_pairs={{0,1},{1,0},{2,3},{3,2},{4,5},{5,4},{6,7},{7,6},{8,9},{9,8},{10,11... | collective-permute-start | bytes 3932168 | tf_op jit(solution)/shard_map/ppermute | solution.py:830
  53.8 27.7 %collective-permute-start.6 = (bf16[20,64,512]{2,1,0:T(8,128)(2,1)S(1)}, bf16[20,64,512]{2,1,0:T(8,128)(2,1)S(1)}, u32[]{:S(2)}, u32[]{:S(2)}) collective-permute-start(bf16[20,64,512]{2,1,0:T(8,128)(2,1)S(1)} %collective-permute-done.3.refs_9_), channel_id=1, source_target_pairs={{0,4},{4,8},{8,12},{12,14},{14,10},{10,6},{6,2},{2,0},{1,5},{5,9},... | collective-permute-start | bytes 3932168 | tf_op jit(solution)/shard_map/ppermute | solution.py:826
  54.7 27.7 %collective-permute-start.7 = (bf16[20,64,512]{2,1,0:T(8,128)(2,1)S(1)}, bf16[20,64,512]{2,1,0:T(8,128)(2,1)S(1)}, u32[]{:S(2)}, u32[]{:S(2)}) collective-permute-start(bf16[20,64,512]{2,1,0:T(8,128)(2,1)S(1)} %collective-permute-done.4.refs_10_), channel_id=1, source_target_pairs={{0,2},{4,0},{8,4},{12,8},{14,12},{10,14},{6,10},{2,6},{1,3},{5,1},... | collective-permute-start | bytes 3932168 | tf_op jit(solution)/shard_map/ppermute | solution.py:826
  83.6 21.1 %collective-permute-start.10 = (bf16[16,64,512]{2,1,0:T(8,128)(2,1)S(1)}, bf16[16,64,512]{2,1,0:T(8,128)(2,1)S(1)}, u32[]{:S(2)}, u32[]{:S(2)}) collective-permute-start(bf16[16,64,512]{2,1,0:T(8,128)(2,1)S(1)} %slice.268), channel_id=1, source_target_pairs={{0,2},{4,0},{8,4},{12,8},{14,12},{10,14},{6,10},{2,6},{1,3},{5,1},... | collective-permute-start | bytes 3145736 | tf_op jit(solution)/shard_map/ppermute | solution.py:826
  84.9 21.0 %collective-permute-start.9 = (bf16[16,64,512]{2,1,0:T(8,128)(2,1)S(1)}, bf16[16,64,512]{2,1,0:T(8,128)(2,1)S(1)}, u32[]{:S(2)}, u32[]{:S(2)}) collective-permute-start(bf16[16,64,512]{2,1,0:T(8,128)(2,1)S(1)} %pad_maximum_fusion.12), channel_id=1, source_target_pairs={{0,4},{4,8},{8,12},{12,14},{14,10},{10,6},{6,2},{2,0},{1,5},{5,9},... | collective-permute-start | bytes 3145736 | tf_op jit(solution)/shard_map/ppermute | solution.py:826
  86.5 23.2 %collective-permute-start.11 = (bf16[16,64,512]{2,1,0:T(8,128)(2,1)S(1)}, bf16[16,64,512]{2,1,0:T(8,128)(2,1)S(1)}, u32[]{:S(2)}, u32[]{:S(2)}) collective-permute-start(bf16[16,64,512]{2,1,0:T(8,128)(2,1)S(1)} %pad_maximum_fusion.13), channel_id=1, source_target_pairs={{0,1},{1,0},{2,3},{3,2},{4,5},{5,4},{6,7},{7,6},{8,9},{9,8},{10,11... | collective-permute-start | bytes 3145736 | tf_op jit(solution)/shard_map/ppermute | solution.py:830
  143.6 18.9 %collective-permute-start.16 = (bf16[5120,512]{1,0:T(8,128)(2,1)}, bf16[5120,512]{1,0:T(8,128)(2,1)}, u32[]{:S(2)}, u32[]{:S(2)}) collective-permute-start(bf16[5120,512]{1,0:T(8,128)(2,1)} %get-tuple-element.96.refs_2_.refs_3_.refs_4_.refs_6_.refs_9_.refs_11_.refs_5_.refs_10_), channel_id=1, source_target_pairs={{16,0},{17,1},{18,2},{19,3},{20,4},{21,5},{22,6},{23,7},{24,8},{25... | collective-permute-start | bytes 15728648 | tf_op jit(solution)/shard_map/ppermute | solution.py:1083
  201.7 61.0 %collective-permute-start.18 = (bf16[5120,512]{1,0:T(8,128)(2,1)}, bf16[5120,512]{1,0:T(8,128)(2,1)}, u32[]{:S(2)}, u32[]{:S(2)}) collective-permute-start(bf16[5120,512]{1,0:T(8,128)(2,1)} %get-tuple-element.120.refs_2_), channel_id=1, source_target_pairs={{0,16},{1,17},{2,18},{3,19},{4,20},{5,21},{6,22},{7,23},{8,24},{9,... | collective-permute-start | bytes 15728648 | tf_op jit(solution)/shard_map/ppermute | solution.py:1141
  266.9 15.6 %collective-permute-start.21 = (bf16[8,64,512]{2,1,0:T(8,128)(2,1)S(1)}, bf16[8,64,512]{2,1,0:T(8,128)(2,1)S(1)}, u32[]{:S(2)}, u32[]{:S(2)}) collective-permute-start(bf16[8,64,512]{2,1,0:T(8,128)(2,1)S(1)} %get-tuple-element.168), channel_id=1, source_target_pairs={{0,1},{1,0},{2,3},{3,2},{4,5},{5,4},{6,7},{7,6},{8,9},{9,8},{10,11... | collective-permute-start | bytes 1572872 | tf_op jit(solution)/shard_map/ppermute | solution.py:830
  269.7 12.8 %collective-permute-start.20 = (bf16[6,64,512]{2,1,0:T(8,128)(2,1)S(1)}, bf16[6,64,512]{2,1,0:T(8,128)(2,1)S(1)}, u32[]{:S(2)}, u32[]{:S(2)}) collective-permute-start(bf16[6,64,512]{2,1,0:T(8,128)(2,1)S(1)} %get-tuple-element.178), channel_id=1, source_target_pairs={{0,2},{4,0},{8,4},{12,8},{14,12},{10,14},{6,10},{2,6},{1,3},{5,1},... | collective-permute-start | bytes 1179656 | tf_op jit(solution)/shard_map/ppermute | solution.py:826
  270.7 11.8 %collective-permute-start.19 = (bf16[6,64,512]{2,1,0:T(8,128)(2,1)S(1)}, bf16[6,64,512]{2,1,0:T(8,128)(2,1)S(1)}, u32[]{:S(2)}, u32[]{:S(2)}) collective-permute-start(bf16[6,64,512]{2,1,0:T(8,128)(2,1)S(1)} %get-tuple-element.179), channel_id=1, source_target_pairs={{0,4},{4,8},{8,12},{12,14},{14,10},{10,6},{6,2},{2,0},{1,5},{5,9},... | collective-permute-start | bytes 1179656 | tf_op jit(solution)/shard_map/ppermute | solution.py:826
  271.9 10.6 %collective-permute-start.22 = (f32[15,512]{1,0:T(8,128)S(1)}, f32[15,512]{1,0:T(8,128)S(1)}, u32[]{:S(2)}, u32[]{:S(2)}) collective-permute-start(f32[15,512]{1,0:T(8,128)S(1)} %pad_maximum_fusion.18), channel_id=1, source_target_pairs={{0,1},{1,0},{2,3},{3,2},{4,5},{5,4},{6,7},{7,6},{8,9},{9,8},{10,11... | collective-permute-start | bytes 92168 | tf_op jit(solution)/shard_map/ppermute | solution.py:838
  273.5 31.5 %collective-permute-start.25 = (bf16[16,64,512]{2,1,0:T(8,128)(2,1)S(1)}, bf16[16,64,512]{2,1,0:T(8,128)(2,1)S(1)}, u32[]{:S(2)}, u32[]{:S(2)}) collective-permute-start(bf16[16,64,512]{2,1,0:T(8,128)(2,1)S(1)} %pad_maximum_fusion.16), channel_id=1, source_target_pairs={{0,1},{1,0},{2,3},{3,2},{4,5},{5,4},{6,7},{7,6},{8,9},{9,8},{10,11... | collective-permute-start | bytes 3145736 | tf_op jit(solution)/shard_map/ppermute | solution.py:830
  284.1 20.9 %collective-permute-start.23 = (bf16[16,64,512]{2,1,0:T(8,128)(2,1)S(1)}, bf16[16,64,512]{2,1,0:T(8,128)(2,1)S(1)}, u32[]{:S(2)}, u32[]{:S(2)}) collective-permute-start(bf16[16,64,512]{2,1,0:T(8,128)(2,1)S(1)} %pad_maximum_fusion.14), channel_id=1, source_target_pairs={{0,4},{4,8},{8,12},{12,14},{14,10},{10,6},{6,2},{2,0},{1,5},{5,9},... | collective-permute-start | bytes 3145736 | tf_op jit(solution)/shard_map/ppermute | solution.py:826
  284.9 20.1 %collective-permute-start.24 = (bf16[16,64,512]{2,1,0:T(8,128)(2,1)S(1)}, bf16[16,64,512]{2,1,0:T(8,128)(2,1)S(1)}, u32[]{:S(2)}, u32[]{:S(2)}) collective-permute-start(bf16[16,64,512]{2,1,0:T(8,128)(2,1)S(1)} %pad_maximum_fusion.15), channel_id=1, source_target_pairs={{0,2},{4,0},{8,4},{12,8},{14,12},{10,14},{6,10},{2,6},{1,3},{5,1},... | collective-permute-start | bytes 3145736 | tf_op jit(solution)/shard_map/ppermute | solution.py:826
  286.9 18.0 %collective-permute-start.26 = (f32[15,512]{1,0:T(8,128)S(1)}, f32[15,512]{1,0:T(8,128)S(1)}, u32[]{:S(2)}, u32[]{:S(2)}) collective-permute-start(f32[15,512]{1,0:T(8,128)S(1)} %fusion.42), channel_id=1, source_target_pairs={{0,2},{2,0},{4,6},{6,4},{8,10},{10,8},{12,14},{14,12},{1,3},{3,1},... | collective-permute-start | bytes 92168 | tf_op jit(solution)/shard_map/ppermute | solution.py:838
  288.0 37.1 %collective-permute-start.29 = (bf16[20,64,512]{2,1,0:T(8,128)(2,1)S(1)}, bf16[20,64,512]{2,1,0:T(8,128)(2,1)S(1)}, u32[]{:S(2)}, u32[]{:S(2)}) collective-permute-start(bf16[20,64,512]{2,1,0:T(8,128)(2,1)S(1)} %pad_maximum_fusion.8), channel_id=1, source_target_pairs={{0,1},{1,0},{2,3},{3,2},{4,5},{5,4},{6,7},{7,6},{8,9},{9,8},{10,11... | collective-permute-start | bytes 3932168 | tf_op jit(solution)/shard_map/ppermute | solution.py:830
  306.1 27.2 %collective-permute-start.28 = (bf16[20,64,512]{2,1,0:T(8,128)(2,1)S(1)}, bf16[20,64,512]{2,1,0:T(8,128)(2,1)S(1)}, u32[]{:S(2)}, u32[]{:S(2)}) collective-permute-start(bf16[20,64,512]{2,1,0:T(8,128)(2,1)S(1)} %pad_maximum_fusion.7), channel_id=1, source_target_pairs={{0,2},{4,0},{8,4},{12,8},{14,12},{10,14},{6,10},{2,6},{1,3},{5,1},... | collective-permute-start | bytes 3932168 | tf_op jit(solution)/shard_map/ppermute | solution.py:826
  308.5 25.4 %collective-permute-start.27 = (bf16[20,64,512]{2,1,0:T(8,128)(2,1)S(1)}, bf16[20,64,512]{2,1,0:T(8,128)(2,1)S(1)}, u32[]{:S(2)}, u32[]{:S(2)}) collective-permute-start(bf16[20,64,512]{2,1,0:T(8,128)(2,1)S(1)} %pad_maximum_fusion.6), channel_id=1, source_target_pairs={{0,4},{4,8},{8,12},{12,14},{14,10},{10,6},{6,2},{2,0},{1,5},{5,9},... | collective-permute-start | bytes 3932168 | tf_op jit(solution)/shard_map/ppermute | solution.py:826
  308.5 24.5 %collective-permute-start.30 = (f32[15,512]{1,0:T(8,128)S(1)}, f32[15,512]{1,0:T(8,128)S(1)}, u32[]{:S(2)}, u32[]{:S(2)}) collective-permute-start(f32[15,512]{1,0:T(8,128)S(1)} %add.239), channel_id=1, source_target_pairs={{0,4},{2,6},{4,0},{6,2},{8,12},{10,14},{12,8},{14,10},{1,5},{3,7},... | collective-permute-start | bytes 92168 | tf_op jit(solution)/shard_map/ppermute | solution.py:838
  310.4 33.0 %collective-permute-start.33 = (bf16[20,64,512]{2,1,0:T(8,128)(2,1)S(1)}, bf16[20,64,512]{2,1,0:T(8,128)(2,1)S(1)}, u32[]{:S(2)}, u32[]{:S(2)}) collective-permute-start(bf16[20,64,512]{2,1,0:T(8,128)(2,1)S(1)} %pad_maximum_fusion.11), channel_id=1, source_target_pairs={{0,1},{1,0},{2,3},{3,2},{4,5},{5,4},{6,7},{7,6},{8,9},{9,8},{10,11... | collective-permute-start | bytes 3932168 | tf_op jit(solution)/shard_map/ppermute | solution.py:830
  335.0 22.9 %collective-permute-start.31 = (bf16[20,64,512]{2,1,0:T(8,128)(2,1)S(1)}, bf16[20,64,512]{2,1,0:T(8,128)(2,1)S(1)}, u32[]{:S(2)}, u32[]{:S(2)}) collective-permute-start(bf16[20,64,512]{2,1,0:T(8,128)(2,1)S(1)} %pad_maximum_fusion.9), channel_id=1, source_target_pairs={{0,4},{4,8},{8,12},{12,14},{14,10},{10,6},{6,2},{2,0},{1,5},{5,9},... | collective-permute-start | bytes 3932168 | tf_op jit(solution)/shard_map/ppermute | solution.py:826
  336.7 21.1 %collective-permute-start.32 = (bf16[20,64,512]{2,1,0:T(8,128)(2,1)S(1)}, bf16[20,64,512]{2,1,0:T(8,128)(2,1)S(1)}, u32[]{:S(2)}, u32[]{:S(2)}) collective-permute-start(bf16[20,64,512]{2,1,0:T(8,128)(2,1)S(1)} %pad_maximum_fusion.10), channel_id=1, source_target_pairs={{0,2},{4,0},{8,4},{12,8},{14,12},{10,14},{6,10},{2,6},{1,3},{5,1},... | collective-permute-start | bytes 3932168 | tf_op jit(solution)/shard_map/ppermute | solution.py:826
  339.2 18.6 %collective-permute-start.34 = (f32[15,512]{1,0:T(8,128)S(1)}, f32[15,512]{1,0:T(8,128)S(1)}, u32[]{:S(2)}, u32[]{:S(2)}) collective-permute-start(f32[15,512]{1,0:T(8,128)S(1)} %add.246), channel_id=1, source_target_pairs={{0,8},{2,10},{4,12},{6,14},{8,0},{10,2},{12,4},{14,6},{1,9},{3,11}... | collective-permute-start | bytes 92168 | tf_op jit(solution)/shard_map/ppermute | solution.py:838
  358.3 10.4 %collective-permute-start.36 = (bf16[8,64,512]{2,1,0:T(8,128)(2,1)S(1)}, bf16[8,64,512]{2,1,0:T(8,128)(2,1)S(1)}, u32[]{:S(2)}, u32[]{:S(2)}) collective-permute-start(bf16[8,64,512]{2,1,0:T(8,128)(2,1)S(1)} %get-tuple-element.154), channel_id=1, source_target_pairs={{0,2},{4,0},{8,4},{12,8},{14,12},{10,14},{6,10},{2,6},{1,3},{5,1},... | collective-permute-start | bytes 1572872 | tf_op jit(solution)/shard_map/ppermute | solution.py:826
  358.4 10.3 %collective-permute-start.35 = (bf16[8,64,512]{2,1,0:T(8,128)(2,1)S(1)}, bf16[8,64,512]{2,1,0:T(8,128)(2,1)S(1)}, u32[]{:S(2)}, u32[]{:S(2)}) collective-permute-start(bf16[8,64,512]{2,1,0:T(8,128)(2,1)S(1)} %get-tuple-element.155), channel_id=1, source_target_pairs={{0,4},{4,8},{8,12},{12,14},{14,10},{10,6},{6,2},{2,0},{1,5},{5,9},... | collective-permute-start | bytes 1572872 | tf_op jit(solution)/shard_map/ppermute | solution.py:826
  (42 other events, 241.8 us)

commit v5 on v4

--- a/solution.py
+++ b/solution.py
@@ -266,23 +266,33 @@
 
 
 class Emitter:
-    def __init__(self, table, target, stage, semaphores):
-        self.table, self.target, self.stage, self.semaphores = table, target, stage, semaphores
+    def __init__(self, table, targets, stage, semaphores):
+        self.table, self.targets, self.stage, self.semaphores = table, targets, stage, semaphores
         self.copies = []
 
     def chunk(self, number, first_piece, value):
-        stage, half_rows = self.stage, self.target.shape[1]
+        stage, half_rows = self.stage, self.targets[0].shape[1]
         stage[number] = value.astype(bfloat)
         count = stage.shape[1] // half_rows
         per_piece = 128 // half_rows
         for part in range(count):
-            copy = pltpu.make_async_copy(
-                stage.at[number, pl.ds(part * half_rows, half_rows)],
-                self.target.at[self.table[first_piece * per_piece + part]],
-                self.semaphores.at[number * count + part],
-            )
-            copy.start()
-            self.copies.append(copy)
+            source = stage.at[number, pl.ds(part * half_rows, half_rows)]
+            semaphore = self.semaphores.at[number * count + part]
+            slot = self.table[first_piece * per_piece + part]
+
+            def start(targets, first, source=source, semaphore=semaphore, slot=slot):
+                def go():
+                    pltpu.make_async_copy(source, targets[0].at[slot - first], semaphore).start()
+
+                if len(targets) == 1:
+                    go()
+                    return
+                last = first + targets[0].shape[0]
+                pl.when(slot < last)(go)
+                pl.when(slot >= last)(lambda: start(targets[1:], last))
+
+            start(self.targets, 0)
+            self.copies.append(pltpu.make_async_copy(source, self.targets[0].at[0], semaphore))
 
     def wait(self):
         for copy in self.copies:
@@ -721,11 +731,11 @@
 
 def encoder_back_body(
     io, scal, table, own, received, memory, cross, inner, resid, activ, slope, up, down, vec,
-    grad_inner, grad_vec, target,
-    grad_mem, inner_low, grad_branch, stage, semaphores,
+    grad_inner, grad_vec, *rest_of,
 ):
     length, width = inner.shape
-    emit = Emitter(table, target, stage, semaphores)
+    *targets, grad_mem, inner_low, grad_branch, stage, semaphores = rest_of
+    emit = Emitter(table, targets, stage, semaphores)
     io.begin(own, received, cross, inner)
     io.follow(memory, vec, resid, down, slope, up, activ)
     io.need(own, received, cross, inner)
@@ -753,13 +763,16 @@
 
 
 def self_back_body(
-    io, scal, table, x, weight, out_weight, vec, resid, query, key, value, ctx_t, lse, grad_out, packed, held,
-    grad_x, grad_vec, target,
-    grad_branch, grad_ctx, grad_ctx_t, dot_ref, query_t, key_t, grad_key, grad_value, grad_query_t,
-    key_two, value_two, stage, semaphores,
+    io, scal, table, x, weight, out_weight, vec, resid, query, key, value, ctx_t, lse, grad_out, packed, *refs
 ):
     length, width = x.shape
-    emit = Emitter(table, target, stage, semaphores)
+    count = (len(refs) - 15) // 2
+    grad_x, grad_vec, *targets = refs[count : 2 * count + 2]
+    (
+        grad_branch, grad_ctx, grad_ctx_t, dot_ref, query_t, key_t, grad_key, grad_value, grad_query_t,
+        key_two, value_two, stage, semaphores,
+    ) = refs[2 * count + 2 :]
+    emit = Emitter(table, targets, stage, semaphores)
     some = length // 2
     io.need(resid, grad_out, packed, x, vec)
     io.follow(ctx_t, out_weight, query, key, value)
@@ -806,8 +819,10 @@
     emit.wait()
 
 
-def merge_body(io, scal, table, own, other, held, target, stage, semaphores):
-    emit = Emitter(table, target, stage, semaphores)
+def merge_body(io, scal, table, own, other, *refs):
+    count = (len(refs) - 2) // 2
+    *targets, stage, semaphores = refs[count:]
+    emit = Emitter(table, targets, stage, semaphores)
     io.rest()
     chunk = stage.shape[1]
     for number in range(own.shape[0] // chunk):
@@ -818,7 +833,216 @@
 
 
 RING = (0, 2, 4, 6, 7, 5, 3, 1)
-LEAD = 8
+LEAD = 6
+LEVEL = 10
+FLOW = 8
+
+
+def lend_kernel(scal, owners, master, own_out, up_out, down_out, plan, counts, low_rows, loaded, sems):
+    size = len(RING)
+    load = pltpu.make_async_copy(master, loaded, sems.at[0])
+    load.start()
+    for place in range(size):
+        counts[place] = 0
+
+    def count(piece, unused):
+        owner = owners[piece]
+        place = jnp.where(owner % 2 == 0, owner // 2, size - 1 - owner // 2)
+        counts[place] = counts[place] + 1
+        return 0
+
+    lax.fori_loop(0, owners.shape[0], count, 0)
+    held = [counts[place] for place in range(size)]
+    caps = [jnp.int32(FLOW)] * size
+    for place in list(range(size - 1, -1, -1)) * 2:
+        after = (place + 1) % size
+        caps[place] = jnp.minimum(FLOW, caps[after] - held[after] + LEVEL)
+    flows = [jnp.minimum(0, cap) for cap in caps]
+    for place in list(range(size)) * 2:
+        flows[place] = jnp.maximum(flows[place], flows[place - 1] + held[place] - LEVEL)
+    for place in range(size):
+        ahead = jnp.maximum(flows[place], 0)
+        back = jnp.maximum(-flows[place - 1], 0)
+        plan[0, place] = held[place] - ahead - back
+        plan[1, place] = ahead
+        plan[2, place] = back
+    load.wait()
+    rows = loaded.shape[0]
+    low_rows[:rows] = loaded[...].astype(bfloat)
+    kept = plan[0, scal[0]]
+    copies = [
+        pltpu.make_async_copy(low_rows.at[pl.ds(0, rows)], own_out, sems.at[0]),
+        pltpu.make_async_copy(low_rows.at[pl.ds(kept, FLOW)], up_out, sems.at[1]),
+        pltpu.make_async_copy(
+            low_rows.at[pl.ds(kept + plan[1, scal[0]], FLOW)], down_out, sems.at[2]
+        ),
+    ]
+    for copy in copies:
+        copy.start()
+    for copy in copies:
+        copy.wait()
+
+
+def borrow_kernel(scal, plan, own, below, above, lead_out, late_out, slots, sems, out_sems):
+    size = len(RING)
+    kept = plan[0, scal[0]]
+    from_below = kept + plan[1, (scal[0] + size - 1) % size]
+    from_above = from_below + plan[2, (scal[0] + 1) % size]
+    for slot in range(LEVEL):
+
+        def move(source, slot=slot):
+            pltpu.make_async_copy(source, slots.at[slot], sems.at[slot]).start()
+
+        pl.when(slot < kept)(lambda slot=slot, move=move: move(own.at[slot]))
+        pl.when((slot >= kept) & (slot < from_below))(
+            lambda slot=slot, move=move: move(below.at[slot - kept])
+        )
+        pl.when((slot >= from_below) & (slot < from_above))(
+            lambda slot=slot, move=move: move(above.at[slot - from_below])
+        )
+    for slot in range(LEVEL):
+        pl.when(slot < from_above)(pltpu.make_async_copy(own.at[0], slots.at[slot], sems.at[slot]).wait)
+    copies = [
+        pltpu.make_async_copy(slots.at[pl.ds(0, LEAD)], lead_out, out_sems.at[0]),
+        pltpu.make_async_copy(slots.at[pl.ds(LEAD, LEVEL - LEAD)], late_out, out_sems.at[1]),
+    ]
+    for copy in copies:
+        copy.start()
+    for copy in copies:
+        copy.wait()
+
+
+def lend(position, owner_row, master):
+    slot = master.shape[1:]
+    rows = master.shape[0]
+    where = position[None].astype(jnp.int32)
+    own, up, down, plan = pl.pallas_call(
+        lend_kernel,
+        in_specs=[SM, SM, HB],
+        out_specs=[HB, HB, HB, SM],
+        out_shape=[
+            low(rows, *slot),
+            low(FLOW, *slot),
+            low(FLOW, *slot),
+            jax.ShapeDtypeStruct((3, len(RING)), jnp.int32),
+        ],
+        scratch_shapes=[
+            pltpu.SMEM((len(RING),), jnp.int32),
+            low_vm(rows + FLOW, *slot),
+            full_vm(rows, *slot),
+            pltpu.SemaphoreType.DMA((3,)),
+        ],
+        name="lend",
+    )(where, owner_row, master)
+    below, above = round_ring(up, 1), round_ring(down, -1)
+    lead, late = pl.pallas_call(
+        borrow_kernel,
+        in_specs=[SM, SM, HB, HB, HB],
+        out_specs=[HB, HB],
+        out_shape=[low(LEAD, *slot), low(LEVEL - LEAD, *slot)],
+        scratch_shapes=[
+            low_vm(LEVEL, *slot),
+            pltpu.SemaphoreType.DMA((LEVEL,)),
+            pltpu.SemaphoreType.DMA((2,)),
+        ],
+        name="borrow",
+    )(where, plan, own, below, above)
+    return lead, late, plan
+
+
+def adam_kept_body(
+    io, scal, plan, sums, master, first, second, new_first, new_second, new_master, new_copy
+):
+    io.rest()
+    count, place = master.shape[0], scal[6]
+    kept = plan[0, place]
+    held = kept + plan[1, place] + plan[2, place]
+
+    def update(slot, gradient):
+        weight, one, two = adam(
+            master[slot], gradient, first[slot], second[slot], rate_matrix, decay_matrix
+        )
+        new_first[slot], new_second[slot], new_master[slot] = one, two, weight
+        new_copy[slot] = weight.astype(bfloat)
+
+    def step(slot, unused):
+        pl.when(slot < kept)(lambda: update(slot, sums[slot]))
+        pl.when(slot >= held)(lambda: update(slot, jnp.zeros(master.shape[1:], single)))
+        return 0
+
+    for start in range(0, count, count // 2):
+        lax.fori_loop(start, start + count // 2, step, 0)
+        for ref in (new_first, new_second, new_master, new_copy):
+            io.put_rows(ref, start, count // 2)
+
+
+def adam_lent_body(
+    io, scal, plan, below, above, master, first, second, one_held, two_held, weight_held, copy_held,
+    new_first, new_second, new_master, new_copy,
+    states, gradients, results, low_result, in_sems, out_sems,
+):
+    count, place = master.shape[0], scal[6]
+    kept = plan[0, place]
+    from_above = kept + plan[1, place]
+    held = from_above + plan[2, place]
+
+    def each(act):
+        def step(slot, unused):
+            pl.when((slot >= kept) & (slot < held))(lambda: act(slot))
+            return 0
+
+        lax.fori_loop(0, count, step, 0)
+
+    def copies_in(slot):
+        sources = [ref.at[slot] for ref in (master, first, second)]
+        return [
+            pltpu.make_async_copy(source, states.at[number, slot], in_sems.at[number, slot])
+            for number, source in enumerate(sources)
+        ]
+
+    def copies_out(slot):
+        outs = [
+            pltpu.make_async_copy(results.at[number, slot], ref.at[slot], out_sems.at[number, slot])
+            for number, ref in enumerate((new_first, new_second, new_master))
+        ]
+        return outs + [
+            pltpu.make_async_copy(low_result.at[slot], new_copy.at[slot], out_sems.at[3, slot])
+        ]
+
+    def begin(slot):
+        for copy in copies_in(slot):
+            copy.start()
+
+        def fetch(source):
+            pltpu.make_async_copy(source, gradients.at[slot], in_sems.at[3, slot]).start()
+
+        pl.when(slot < from_above)(lambda: fetch(above.at[slot - kept]))
+        pl.when(slot >= from_above)(lambda: fetch(below.at[slot - from_above]))
+
+    def update(slot):
+        for copy in copies_in(slot):
+            copy.wait()
+        pltpu.make_async_copy(below.at[0], gradients.at[slot], in_sems.at[3, slot]).wait()
+        weight, one, two = adam(
+            states[0, slot],
+            gradients[slot].astype(single),
+            states[1, slot],
+            states[2, slot],
+            rate_matrix,
+            decay_matrix,
+        )
+        results[0, slot], results[1, slot], results[2, slot] = one, two, weight
+        low_result[slot] = weight.astype(bfloat)
+        for copy in copies_out(slot):
+            copy.start()
+
+    def end(slot):
+        for copy in copies_out(slot):
+            copy.wait()
+
+    each(begin)
+    each(update)
+    each(end)
 
 
 def round_ring(value, step):
@@ -842,10 +1066,9 @@
     return jnp.concatenate(values, 0)
 
 
-def ring_gather(own, tables):
-    every, lead, half = own.shape[0], LEAD, LEAD // 2
-    late = every - lead
-    found = [([(0, every, 0, 0, 0)], own)]
+def ring_gather(own_lead, own_late, tables):
+    lead, late, half = LEAD, LEVEL - LEAD, LEAD // 2
+    found = [([(0, lead, 0, 0, 0)], own_lead), ([(0, late, 0, 0, lead)], own_late)]
 
     def ahead(value, far, near):
         ranges = [(0, lead, far, 0, 0)]
@@ -853,19 +1076,19 @@
             ranges += [(lead, lead + late, near, 0, lead), (lead + late, lead + 2 * late, near, 1, lead)]
         found.append((ranges, value))
 
-    up, down, across = step_of(own[:lead], own[:lead], own[lead:])
+    up, down, across = step_of(own_lead, own_lead, own_late)
     found.append(([(0, late, 0, 1, lead)], across))
     ahead(up, 7, None)
     ahead(down, 1, None)
-    pair = join(own[lead:], across)
-    up, down, across = step_of(join(up, pair), join(down, pair), join(up, down, own[:half]))
+    pair = join(own_late, across)
+    up, down, across = step_of(join(up, pair), join(down, pair), join(up, down, own_lead[:half]))
     found.append(
         ([(0, lead, 7, 1, 0), (lead, 2 * lead, 1, 1, 0), (2 * lead, 2 * lead + half, 0, 1, 0)], across)
     )
     up, tables = lax.optimization_barrier((up, tables))
     ahead(up, 6, 7)
     ahead(down, 2, 1)
-    up, down, across = step_of(up, down, join(up[:lead], down[:lead], own[half:lead]))
+    up, down, across = step_of(up, down, join(up[:lead], down[:lead], own_lead[half:]))
     found.append(
         ([(0, lead, 6, 1, 0), (lead, 2 * lead, 2, 1, 0), (2 * lead, 2 * lead + half, 0, 1, half)], across)
     )
@@ -889,7 +1112,7 @@
     return sum(value.astype(single) for value in values).astype(bfloat)
 
 
-def ring_scatter(grads, vector):
+def ring_scatter(grads, far, vector):
     partners = [("narrow", 1), ("wide", 1), ("wide", 2), ("wide", 4), ("half", 1)]
 
     def step_of(*values):
@@ -911,7 +1134,8 @@
     def other(distance, start=0, stop=lead):
         return grads[distance, 1, start:stop]
 
-    up, down, across = step_of(grads[4, 0, lead:], grads[4, 1, lead:], other(4))
+    across, down, up = far
+    up, down, across = step_of(up, down, across)
     first = added(mine(4), across)
     up = join(first[:half], added(up, grads[3, 0, lead:]), grads[3, 1, lead:])
     down = join(first[half:], grads[5, 0, lead:], added(down, grads[5, 1, lead:]))
@@ -992,7 +1216,7 @@
     same = owner_row[:, None] == owner_row[None, :]
     earlier = counter[None, :] < counter[:, None]
     ranks = jnp.sum((same & earlier).astype(jnp.int32), 1)
-    on_ring = wide_size == len(RING) and narrow_size == 2 and capacity > LEAD
+    on_ring = (wide_size, narrow_size, capacity, count) == (len(RING), 2, 14, 56)
     wide_at, narrow_at = lax.axis_index("wide"), lax.axis_index("narrow")
     self_rows, rest_rows = 4 * width, count * half_rows * narrow_size - 4 * width
     is_source = lax.axis_index("half") == 0
@@ -1001,6 +1225,7 @@
     some = length // 2
     source_len, target_len = lengths[0, 0], lengths[1, 0]
     flag = is_source.astype(jnp.int32)
+    position = jnp.where(wide_at % 2 == 0, wide_at // 2, wide_size - 1 - wide_at // 2)
     scal = jnp.stack(
         [
             jnp.where(is_source, source_len, target_len),
@@ -1009,26 +1234,48 @@
             jnp.where(is_source, target_len - some, target_len),
             source_len,
             narrow_at,
+            position,
         ]
     ).astype(jnp.int32)
-    own = master[0].astype(bfloat)
     if on_ring:
-        turned = [RING.index(i) for i in range(wide_size)]
-        position = jnp.array(turned)[wide_at]
-        owner_ring = jnp.array(turned)[owner_row]
-        distance = (owner_ring - position) % wide_size
+        capacity = LEVEL
+        own_lead, own_late, plan = lend(position, owner_row.astype(jnp.int32), master[0])
+        place = jnp.where(owner_row % 2 == 0, owner_row // 2, wide_size - 1 - owner_row // 2)
+        kept, ahead, back = (jnp.take(row, place) for row in plan)
+        moved = (ranks >= kept).astype(jnp.int32) - 2 * (ranks >= kept + ahead).astype(jnp.int32)
+        place = (place + moved) % wide_size
+        base = jnp.take(plan[0], place)
+        below = jnp.take(plan[1], (place - 1) % wide_size)
+        ranks = jnp.where(
+            moved == 0,
+            ranks,
+            jnp.where(moved > 0, base + ranks - kept, base + below + ranks - kept - ahead),
+        )
+        distance = (place - position) % wide_size
         halves = jnp.arange(narrow_size)[None, :] ^ narrow_at
-        table = ((distance[:, None] * 2 + halves) * capacity + ranks[:, None]).reshape(-1)
+        table = (distance[:, None] * 2 + halves) * capacity + ranks[:, None]
+        total, late = wide_size * 2 * capacity, capacity - LEAD
+        is_late = (ranks >= LEAD)[:, None]
+        after_late = ranks[:, None] - LEAD + total + LEAD
+        far = jnp.where(
+            halves == 1,
+            jnp.where(is_late, after_late, ranks[:, None] + total),
+            jnp.where(is_late, after_late + late, table),
+        )
+        table = jnp.where(distance[:, None] == 4, far, table).reshape(-1)
         slot_of = distance * capacity + ranks
         hit = slot_of[None, :] == jnp.arange(wide_size * capacity)[:, None]
         pieces = jnp.sum(hit.astype(jnp.int32) * (counter + 1)[None, :], 1) - 1
         pieces = pieces.reshape(wide_size, capacity).astype(jnp.int32)
-        found, (pieces, table, scal) = ring_gather(own, (pieces, table.astype(jnp.int32), scal))
+        found, (pieces, table, scal) = ring_gather(
+            own_lead, own_late, (pieces, table.astype(jnp.int32), scal)
+        )
     else:
         places = (
             owner_row[:, None] * narrow_size + jnp.arange(narrow_size)[None, :]
         ) * capacity + ranks[:, None]
         table = places.reshape(-1)
+        own = master[0].astype(bfloat)
         gathered = lax.all_gather(own, ("wide", "narrow"), axis=0, tiled=True)
         weight = jnp.take(gathered, table, axis=0).reshape(-1, width)
         weight, rest = weight[:self_rows], weight[self_rows:]
@@ -1037,7 +1284,10 @@
     self_vec = whole(jnp.where(is_source, vec_master[0:3], vec_master[6:9]))
     cross_vec, ff_vec = whole(vec_master[9:12]), whole(vec_master[12:15])
     memory_vec = whole(vec_master[3:6])
-    slots = low(capacity * wide_size * narrow_size, half_rows, width)
+    total = capacity * wide_size * narrow_size
+    cuts = [total, LEAD, capacity - LEAD, capacity - LEAD] if on_ring else [total]
+    slots = [low(size, half_rows, width) for size in cuts]
+    slot_outs = [("hbm", one) for one in slots]
 
     def stage_of(chunks):
         return [
@@ -1140,7 +1390,7 @@
     grad_rest, swap_other = lax.optimization_barrier((grad_rest, swap_other))
     grad_rest_other = lax.ppermute(grad_rest, "half", up_half)
     output = join(output, swap_other[3 * some :])
-    grad_inner, grad_memory_vec, target = call(
+    grad_inner, grad_memory_vec, *target = call(
         encoder_back_body,
         "encoder_back",
         scal,
@@ -1159,7 +1409,7 @@
             down_w,
             memory_vec,
         ],
-        [store(length, width), store(3, width), ("hbm", slots)],
+        [store(length, width), store(3, width)] + slot_outs,
         [full_vm(length, width), low_vm(length, width), low_vm(length, width)] + stage_of(10),
     )
     back_scratch = (
@@ -1167,7 +1417,7 @@
         + [low_vm(width, length), low_vm(width, length)]
         + [full_vm(length, width), full_vm(length, width), low_vm(width, length), two, two]
     )
-    grad_x, grad_self_vec, target = call(
+    grad_x, grad_self_vec, *target = call(
         self_back_body,
         "self_back",
         scal,
@@ -1189,13 +1439,13 @@
                 [(grad_one, 0, 0, some)],
             ),
             either([], [(swap_other, 0, 0, 3 * some)]),
-            ("hbm", target),
-        ],
-        [store(length, width), store(3, width), ("hbm", slots)],
+        ]
+        + [("hbm", one) for one in target],
+        [store(length, width), store(3, width)] + slot_outs,
         back_scratch + stage_of(4),
-        [(13, 2)],
-    )
-    (target,) = call(
+        [(13 + number, 2 + number) for number in range(len(slots))],
+    )
+    target = call(
         merge_body,
         "merge",
         scal,
@@ -1204,11 +1454,11 @@
             ("smem", table),
             whole(grad_rest),
             whole(grad_rest_other),
-            ("hbm", target),
-        ],
-        [("hbm", slots)],
+        ]
+        + [("hbm", one) for one in target],
+        slot_outs,
         stage_of(10),
-        [(3, 0)],
+        [(3 + number, number) for number in range(len(slots))],
     )
     vec_grads = jnp.concatenate(
         [
@@ -1220,17 +1470,56 @@
         0,
     )
     if on_ring:
-        grads = target.reshape(wide_size, 2, capacity, half_rows, width)
-        mine, vec_grads = ring_scatter(grads, vec_grads)
+        grads = target[0].reshape(wide_size, 2, capacity, half_rows, width)
+        mine, vec_grads = ring_scatter(grads, target[1:], vec_grads)
     else:
-        mine = lax.psum_scatter(target, ("wide", "narrow"), scatter_dimension=0, tiled=True)
+        mine = lax.psum_scatter(target[0], ("wide", "narrow"), scatter_dimension=0, tiled=True)
         for axis in ("narrow", "wide", "half"):
             vec_grads = sum_over(vec_grads, axis)
-    used = jnp.sum((owner_row == wide_at).astype(jnp.int32))
-    mine = jnp.where((jnp.arange(capacity) < used)[:, None, None], mine.astype(single), 0.0)
-    new_weight, new_first, new_second = adam(
-        master[0], mine, moment_one[0], moment_two[0], rate_matrix, decay_matrix
-    )
+    if on_ring:
+        sums = join(mine, jnp.zeros((FLOW, half_rows, width), single))
+        cut = plan[0][position]
+        lent = lax.dynamic_slice_in_dim(sums, cut, FLOW, 0).astype(bfloat)
+        cut = cut + plan[1][(position - 1) % wide_size]
+        lent_above = lax.dynamic_slice_in_dim(sums, cut, FLOW, 0).astype(bfloat)
+        above, below = round_ring(lent, -1), round_ring(lent_above, 1)
+        states = (master[0], moment_one[0], moment_two[0])
+        state = states[0].shape
+        results = call(
+            adam_kept_body,
+            "adam_kept",
+            scal,
+            None,
+            [("smem", plan), whole(mine)] + [whole(one) for one in states],
+            [store(*state)] * 3 + [low_out(*state)],
+            [],
+        )
+        new_first, new_second, new_weight, new_copy = call(
+            adam_lent_body,
+            "adam_lent",
+            scal,
+            None,
+            [("smem", plan), ("hbm", below), ("hbm", above)]
+            + [("hbm", one) for one in states]
+            + [("hbm", one) for one in results],
+            [("hbm", shaped(*state))] * 3 + [("hbm", low(*state))],
+            [
+                full_vm(3, *state),
+                low_vm(*state),
+                full_vm(3, *state),
+                low_vm(*state),
+                pltpu.SemaphoreType.DMA((4, state[0])),
+                pltpu.SemaphoreType.DMA((4, state[0])),
+            ],
+            [(6 + number, number) for number in range(4)],
+        )
+    else:
+        used = jnp.sum((owner_row == wide_at).astype(jnp.int32))
+        mine = jnp.where((jnp.arange(capacity) < used)[:, None, None], mine.astype(single), 0.0)
+        new_weight, new_first, new_second = adam(
+            master[0], mine, moment_one[0], moment_two[0], rate_matrix, decay_matrix
+        )
+        new_copy = new_weight.astype(bfloat)
     vec_weight, vec_first, vec_second = adam(
         vec_master, vec_grads, vec_one, vec_two, rate_vector, 0.0
     )
@@ -1240,7 +1529,7 @@
         new_first[None],
         new_second[None],
         new_weight[None],
-        new_weight.astype(bfloat)[None],
+        new_copy[None],
         vec_first,
         vec_second,
         vec_weight,

time: 379 us -> 369 us (0.974)
  waiting for transfers between devices: 161 us -> 118 us
  Pallas kernels: 128 us -> 145 us
  other arithmetic: 20.6 us -> 27.2 us
  local copies, waits for them, and re-layouts: 14.1 us -> 18.3 us
    ppermute x10, waiting for transfers between devices: 56.8 us -> 9.22 us  [swapped(): return lax.ppermute(value, 'narrow', [(0, 1), (1, 0)])]
    add x1 -> x5, other arithmetic: 0.08 us -> 13.3 us  [the longest x1 10.9 us: on_device(): after_late + late]
    ppermute x20 -> x24, waiting for transfers between devices: 48.8 us -> 60 us  [round_ring(): lax.ppermute(value, 'wide', [(RING[i], RING[(i + step) % count]) for i in...]
    pallas_call x6 -> x8, Pallas kernels: 128 us -> 138 us  [call(): pl.pallas_call(kernel, in_specs=specs, out_specs=[HB] * count_out, out_sh...]
    ppermute x5, waiting for transfers between devices: 46.8 us -> 40 us  [partner(): lax.ppermute(value, axis, [(i, i ^ bit) for i in range(lax.axis_size(axis...]
    pallas_call x0 -> x2, Pallas kernels: none -> 6.77 us  [the longest x1 4.13 us: lend(): pl.pallas_call(lend_kernel, in_specs=[SM, SM, HB], out_specs=[HB, HB, HB,...]
    convert_element_type x3 -> x0, other arithmetic: 6.69 us -> none  [the longest x1 4.02 us: on_device(): new_weight.astype(bfloat)[None]]
    ppermute x20 -> x24, starting transfers between devices: 24.9 us -> 26.8 us  [round_ring(): lax.ppermute(value, 'wide', [(RING[i], RING[(i + step) % count]) for i in...]
  transfers between devices with their start and end apart: 39 -> 43, of which waited for: 26 -> 27; matrix products, arithmetic and copies ran while one was open for 5% -> 10% of each run, Pallas kernels for 18% -> 22%
where the time goes in v5:
time: 369 us; the launch traced here: 364 us
  Pallas kernels  145 us (39%)
  waiting for transfers between devices  118 us (32%)
  starting transfers between devices  48.3 us (13%)
  other arithmetic  27.2 us (7%)
  local copies, waits for them, and re-layouts  18.3 us (5%)
  between operations  7.48 us (2%)
    pallas_call x8, Pallas kernels, call(): pl.pallas_call(kernel, in_specs=specs, out_specs=[HB] * count_out, out_sh...  138 us
    ppermute x24, waiting for transfers between devices, round_ring(): lax.ppermute(value, 'wide', [(RING[i], RING[(i + step) % count]) for i in...  60 us
    ppermute x5, waiting for transfers between devices, partner(): lax.ppermute(value, axis, [(i, i ^ bit) for i in range(lax.axis_size(axis...  40 us
    ppermute x24, starting transfers between devices, round_ring(): lax.ppermute(value, 'wide', [(RING[i], RING[(i + step) % count]) for i in...  26.8 us
    ppermute x10, starting transfers between devices, swapped(): return lax.ppermute(value, 'narrow', [(0, 1), (1, 0)])  12.4 us
    add x1, other arithmetic, on_device(): after_late + late  10.9 us
    ppermute x10, waiting for transfers between devices, swapped(): return lax.ppermute(value, 'narrow', [(0, 1), (1, 0)])  9.22 us
    ppermute x2, waiting for transfers between devices, on_device(): swap_other = lax.ppermute(swap, 'half', both_halves)  8.97 us
  transfers between devices with their start and end apart: 43, of which 27 were waited for; matrix products, arithmetic and copies ran while one was open for 10% of the time, Pallas kernels for 22%

profile of v5, /device:TPU:0, one launch (start us, length us, event | category | flops | bytes accessed | tf_op | source)
XLA Modules:
  0.0 364.2 jit_solution(12822391591835427295)
XLA Ops:
  0.7 4.1 %lend.1 = (bf16[14,64,512]{2,1,0:T(8,128)(2,1)}, bf16[8,64,512]{2,1,0:T(8,128)(2,1)}, bf16[8,64,512]{2,1,0:T(8,128)(2,1)}, s32[3,8]{1,0:T(4,128)}) custom-call(s32[1]{0:T(128)} %bitcast.scal, s32[56]{0:T(128)} %bitcast.167, f32[14,64,512]{2,1,0:T(8,128)} %bitcast.152), custom_call_target="tpu_custom_call" | custom-call | tf_op jit(solution)/shard_map/lend/pallas_call | solution.py:919
  4.8 3.1 collective-permute-start
  10.2 10.9 %broadcast_add_fusion = (s32[56]{0:T(128)S(1)}, s32[56]{0:T(128)S(1)}, s32[56]{0:T(128)S(1)}, s32[56]{0:T(128)S(1)}, s32[56]{0:T(128)S(1)}) fusion(s32[56]{0:T(128)S(1)} %convert_reduce_fusion, s32[]{:T(128)} %bitcast.20, s32[]{:T(128)} %bitcast.19, s32[]{:T(128)} %bitcast.18, s32[]{:T(128)} %bitcast.17, s32[]{:T(128)} %bitcast.16, s32[]{:T(128)} %bitcast.15, ...), kind=kLoop, calls=%fused_computation.173 | loop fusion | flops 7504 | bytes 1632 | tf_op jit(solution)/shard_map/add | solution.py:1263
  22.3 2.6 borrow.1
  24.9 1.9 collective-permute-start.3
  27.7 1.8 collective-permute-start.4
  45.4 15.2 %collective-permute-done.6.refs_11_ = bf16[14,64,512]{2,1,0:T(8,128)(2,1)S(1)} collective-permute-done((bf16[14,64,512]{2,1,0:T(8,128)(2,1)}, bf16[14,64,512]{2,1,0:T(8,128)(2,1)S(1)}, u32[]{:S(2)}, u32[]{:S(2)}) %collective-permute-start.6) | collective-permute-done | bytes 917536 | tf_op jit(solution)/shard_map/ppermute | solution.py:1050
  65.9 16.8 %collective-permute-done.8.refs_13_ = bf16[14,64,512]{2,1,0:T(8,128)(2,1)S(1)} collective-permute-done((bf16[14,64,512]{2,1,0:T(8,128)(2,1)}, bf16[14,64,512]{2,1,0:T(8,128)(2,1)S(1)}, u32[]{:S(2)}, u32[]{:S(2)}) %collective-permute-start.8) | collective-permute-done | bytes 917536 | tf_op jit(solution)/shard_map/ppermute | solution.py:1050
  88.3 10.0 %collective-permute-done.12.refs_17_ = bf16[11,64,512]{2,1,0:T(8,128)(2,1)S(1)} collective-permute-done((bf16[11,64,512]{2,1,0:T(8,128)(2,1)S(1)}, bf16[11,64,512]{2,1,0:T(8,128)(2,1)S(1)}, u32[]{:S(2)}, u32[]{:S(2)}) %collective-permute-start.12) | collective-permute-done | bytes 720928 | tf_op jit(solution)/shard_map/ppermute | solution.py:1050
  98.3 2.1 collective-permute-done.11.refs_16_
  100.4 2.9 collective-permute-done.13.refs_15_
  108.0 3.6 collective-permute-done.15.refs_19_
  114.1 22.0 %self_forward.1 = (bf16[1024,512]{1,0:T(8,128)(2,1)}, bf16[1024,512]{1,0:T(8,128)(2,1)}, bf16[1024,512]{1,0:T(8,128)(2,1)}, bf16[512,1024]{1,0:T(8,128)(2,1)}, f...) custom-call(s32[7]{0:T(128)} %stack.24.refs_0_, ...), custom_call_target="tpu_custom_call" | custom-call | tf_op jit(solution)/shard_map/self_forward/pallas_call | solution.py:464
  137.5 13.1 %encoder_ff.1 = (bf16[1024,2048]{1,0:T(8,128)(2,1)}, bf16[1024,2048]{1,0:T(8,128)(2,1)}, f32[1024,512]{1,0:T(8,128)}, bf16[1024,512]{1,0:T(8,128)(2,1)}, bf16[2048,512]{1,0:T(8,128)(2,1)}) custom-call(s32[7]{0:T(128)} %stack.24.refs_0_, f32[1024,512]{1,0:T(8,128)} %get-tuple-element.126.refs_1_.refs_6_, ...), custom_call_target="tpu_custom_call", output_to_operand_aliasing={{4}: (6, {})} | custom-call | tf_op jit(solution)/shard_map/encoder_ff/pallas_call | solution.py:464
  150.6 4.5 %collective-permute-done.17.refs_2_.refs_4_ = bf16[2048,512]{1,0:T(8,128)(2,1)} collective-permute-done((bf16[2048,512]{1,0:T(8,128)(2,1)}, bf16[2048,512]{1,0:T(8,128)(2,1)}, u32[]{:S(2)}, u32[]{:S(2)}) %collective-permute-start.17) | collective-permute-done | bytes 2097184 | tf_op jit(solution)/shard_map/ppermute | solution.py:1348
  155.1 34.5 %decoder_middle.1 = (bf16[512,512]{1,0:T(8,128)(2,1)}, bf16[2048,512]{1,0:T(8,128)(2,1)}, f32[512,512]{1,0:T(8,128)}, bf16[5120,512]{1,0:T(8,128)(2,1)}, f32[6,512]{1,0:T(8,128)}, /*index=5*/bf16[2048,512]{1,0:T(8,128)(2,1)}) custom-call(s32[7]{0:T(128)} %stack.24.refs_0_, f32[1024,512]{1,0:T(8,128)} %get-tuple-element.126.refs_1_.refs_6_, ...), custom_call_target="tpu_custom_call" | custom-call | tf_op jit(solution)/shard_map/decoder_middle/pallas_call | solution.py:464
  189.8 4.5 %collective-permute-done.19.refs_3_.refs_14_ = bf16[2048,512]{1,0:T(8,128)(2,1)} collective-permute-done((bf16[2048,512]{1,0:T(8,128)(2,1)}, bf16[2048,512]{1,0:T(8,128)(2,1)}, u32[]{:S(2)}, u32[]{:S(2)}) %collective-permute-start.19) | collective-permute-done | bytes 2097184 | tf_op jit(solution)/shard_map/ppermute | solution.py:1389
  194.2 4.4 %collective-permute-start.20 = (bf16[5120,512]{1,0:T(8,128)(2,1)}, bf16[5120,512]{1,0:T(8,128)(2,1)}, u32[]{:S(2)}, u32[]{:S(2)}) collective-permute-start(bf16[5120,512]{1,0:T(8,128)(2,1)} %get-tuple-element.154.refs_2_), channel_id=1, source_target_pairs={{0,16},{1,17},{2,18},{3,19},{4,20},{5,21},{6,22},{7,23},{8,24},{9,... | collective-permute-start | bytes 15728648 | tf_op jit(solution)/shard_map/ppermute | solution.py:1391
  198.7 21.6 %encoder_back.1 = (f32[1024,512]{1,0:T(8,128)}, f32[3,512]{1,0:T(4,128)}, bf16[160,64,512]{2,1,0:T(8,128)(2,1)}, bf16[6,64,512]{2,1,0:T(8,128)(2,1)}, bf16[4,64,...) custom-call(s32[7]{0:T(128)} %stack.24.refs_0_, s32[112]{0:T(128)} %select_select_fusion.refs_1_, ...), custom_call_target="tpu_custom_call" | custom-call | tf_op jit(solution)/shard_map/encoder_back/pallas_call | solution.py:464
  220.3 35.1 %self_back.1 = (f32[1024,512]{1,0:T(8,128)}, f32[3,512]{1,0:T(4,128)}, bf16[160,64,512]{2,1,0:T(8,128)(2,1)}, bf16[6,64,512]{2,1,0:T(8,128)(2,1)}, bf16[4,64,512...) custom-call(s32[7]{0:T(128)} %stack.24.refs_0_, ...), custom_call_target="tpu_custom_call", output_to_operand_aliasing={{2}: (15, {}), {3}: (16, {}), {4}: (17, {}), {5}: (18, {})} | custom-call | tf_op jit(solution)/shard_map/self_back/pallas_call | solution.py:464
  259.3 1.8 collective-permute-start.22
  262.0 2.0 slice_bitcast_fusion.3
  268.7 4.7 %collective-permute-done.23 = bf16[6,64,512]{2,1,0:T(8,128)(2,1)S(1)} collective-permute-done((bf16[6,64,512]{2,1,0:T(8,128)(2,1)}, bf16[6,64,512]{2,1,0:T(8,128)(2,1)S(1)}, u32[]{:S(2)}, u32[]{:S(2)}) %collective-permute-start.23) | collective-permute-done | bytes 393248 | tf_op jit(solution)/shard_map/ppermute | solution.py:1054
  276.2 1.8 collective-permute-start.26
  278.4 2.0 collective-permute-start.28
  281.5 13.8 %collective-permute-done.28 = f32[15,512]{1,0:T(8,128)S(1)} collective-permute-done((f32[15,512]{1,0:T(8,128)S(1)}, f32[15,512]{1,0:T(8,128)S(1)}, u32[]{:S(2)}, u32[]{:S(2)}) %collective-permute-start.28) | collective-permute-done | bytes 30752 | tf_op jit(solution)/shard_map/ppermute | solution.py:1062
  296.1 2.4 collective-permute-start.30
  299.9 14.3 %collective-permute-done.32 = f32[15,512]{1,0:T(8,128)S(1)} collective-permute-done((f32[15,512]{1,0:T(8,128)S(1)}, f32[15,512]{1,0:T(8,128)S(1)}, u32[]{:S(2)}, u32[]{:S(2)}) %collective-permute-start.32) | collective-permute-done | bytes 30752 | tf_op jit(solution)/shard_map/ppermute | solution.py:1062
  314.2 2.1 collective-permute-done.29
  319.3 11.9 %collective-permute-done.36 = f32[15,512]{1,0:T(8,128)S(1)} collective-permute-done((f32[15,512]{1,0:T(8,128)S(1)}, f32[15,512]{1,0:T(8,128)S(1)}, u32[]{:S(2)}, u32[]{:S(2)}) %collective-permute-start.36) | collective-permute-done | bytes 30752 | tf_op jit(solution)/shard_map/ppermute | solution.py:1062
  350.2 7.8 %adam_kept.1 = (f32[14,64,512]{2,1,0:T(8,128)}, f32[14,64,512]{2,1,0:T(8,128)}, f32[14,64,512]{2,1,0:T(8,128)}, bf16[14,64,512]{2,1,0:T(8,128)(2,1)}) custom-call(s32[7]{0:T(128)} %stack.24.refs_0_, s32[3,8]{1,0:T(4,128)} %get-tuple-element.102.plan.refs_1_, f32[10,64,512]{2,1,0:T(8,128)} %pad_maximum_fusion.refs_2_, f32[14,64,512]{2,1,0:T(8,128)} %bitcast.153, ...), custom_call_target="tpu_custom_call" | custom-call | tf_op jit(solution)/shard_map/adam_kept/pallas_call | solution.py:464
  361.8 2.2 adam_lent.1
  (213 shorter events, 75.2 us)
Async XLA Ops:
  4.8 16.4 %collective-permute-start = (bf16[8,64,512]{2,1,0:T(8,128)(2,1)}, bf16[8,64,512]{2,1,0:T(8,128)(2,1)S(1)}, u32[]{:S(2)}, u32[]{:S(2)}) collective-permute-start(bf16[8,64,512]{2,1,0:T(8,128)(2,1)} %get-tuple-element.104), channel_id=1, source_target_pairs={{0,4},{4,8},{8,12},{12,14},{14,10},{10,6},{6,2},{2,0},{1,5},{5,9},... | collective-permute-start | bytes 1572872 | tf_op jit(solution)/shard_map/ppermute | solution.py:1050
  7.9 13.6 %collective-permute-start.1 = (bf16[8,64,512]{2,1,0:T(8,128)(2,1)}, bf16[8,64,512]{2,1,0:T(8,128)(2,1)S(1)}, u32[]{:S(2)}, u32[]{:S(2)}) collective-permute-start(bf16[8,64,512]{2,1,0:T(8,128)(2,1)} %get-tuple-element.105), channel_id=1, source_target_pairs={{0,2},{4,0},{8,4},{12,8},{14,12},{10,14},{6,10},{2,6},{1,3},{5,1},... | collective-permute-start | bytes 1572872 | tf_op jit(solution)/shard_map/ppermute | solution.py:1050
  24.9 10.9 %collective-permute-start.3 = (bf16[6,64,512]{2,1,0:T(8,128)(2,1)}, bf16[6,64,512]{2,1,0:T(8,128)(2,1)S(1)}, u32[]{:S(2)}, u32[]{:S(2)}) collective-permute-start(bf16[6,64,512]{2,1,0:T(8,128)(2,1)} %get-tuple-element.106.refs_4_), channel_id=1, source_target_pairs={{0,2},{4,0},{8,4},{12,8},{14,12},{10,14},{6,10},{2,6},{1,3},{5,1},... | collective-permute-start | bytes 1179656 | tf_op jit(solution)/shard_map/ppermute | solution.py:1050
  26.9 10.3 %collective-permute-start.2 = (bf16[6,64,512]{2,1,0:T(8,128)(2,1)}, bf16[6,64,512]{2,1,0:T(8,128)(2,1)S(1)}, u32[]{:S(2)}, u32[]{:S(2)}) collective-permute-start(bf16[6,64,512]{2,1,0:T(8,128)(2,1)} %get-tuple-element.106.refs_4_), channel_id=1, source_target_pairs={{0,4},{4,8},{8,12},{12,14},{14,10},{10,6},{6,2},{2,0},{1,5},{5,9},... | collective-permute-start | bytes 1179656 | tf_op jit(solution)/shard_map/ppermute | solution.py:1050
  37.2 24.6 %collective-permute-start.7 = (bf16[15,64,512]{2,1,0:T(8,128)(2,1)S(1)}, bf16[15,64,512]{2,1,0:T(8,128)(2,1)S(1)}, u32[]{:S(2)}, u32[]{:S(2)}) collective-permute-start(bf16[15,64,512]{2,1,0:T(8,128)(2,1)S(1)} %pad_maximum_fusion.5), channel_id=1, source_target_pairs={{0,1},{1,0},{2,3},{3,2},{4,5},{5,4},{6,7},{7,6},{8,9},{9,8},{10,11... | collective-permute-start | bytes 2949128 | tf_op jit(solution)/shard_map/ppermute | solution.py:1054
  40.2 20.3 %collective-permute-start.6 = (bf16[14,64,512]{2,1,0:T(8,128)(2,1)}, bf16[14,64,512]{2,1,0:T(8,128)(2,1)S(1)}, u32[]{:S(2)}, u32[]{:S(2)}) collective-permute-start(bf16[14,64,512]{2,1,0:T(8,128)(2,1)} %get-tuple-element.231), channel_id=1, source_target_pairs={{0,2},{4,0},{8,4},{12,8},{14,12},{10,14},{6,10},{2,6},{1,3},{5,1},... | collective-permute-start | bytes 2752520 | tf_op jit(solution)/shard_map/ppermute | solution.py:1050
  41.8 20.1 %collective-permute-start.5 = (bf16[14,64,512]{2,1,0:T(8,128)(2,1)}, bf16[14,64,512]{2,1,0:T(8,128)(2,1)}, u32[]{:S(2)}, u32[]{:S(2)}) collective-permute-start(bf16[14,64,512]{2,1,0:T(8,128)(2,1)} %get-tuple-element.232), channel_id=1, source_target_pairs={{0,4},{4,8},{8,12},{12,14},{14,10},{10,6},{6,2},{2,0},{1,5},{5,9},... | collective-permute-start | bytes 2752520 | tf_op jit(solution)/shard_map/ppermute | solution.py:1050
  63.3 20.4 %collective-permute-start.10 = (bf16[15,64,512]{2,1,0:T(8,128)(2,1)S(1)}, bf16[15,64,512]{2,1,0:T(8,128)(2,1)}, u32[]{:S(2)}, u32[]{:S(2)}) collective-permute-start(bf16[15,64,512]{2,1,0:T(8,128)(2,1)S(1)} %pad_maximum_fusion.6), channel_id=1, source_target_pairs={{0,1},{1,0},{2,3},{3,2},{4,5},{5,4},{6,7},{7,6},{8,9},{9,8},{10,11... | collective-permute-start | bytes 2949128 | tf_op jit(solution)/shard_map/ppermute | solution.py:1054
  63.9 18.8 %collective-permute-start.8 = (bf16[14,64,512]{2,1,0:T(8,128)(2,1)}, bf16[14,64,512]{2,1,0:T(8,128)(2,1)S(1)}, u32[]{:S(2)}, u32[]{:S(2)}) collective-permute-start(bf16[14,64,512]{2,1,0:T(8,128)(2,1)} %collective-permute-done.5.refs_10_), channel_id=1, source_target_pairs={{0,4},{4,8},{8,12},{12,14},{14,10},{10,6},{6,2},{2,0},{1,5},{5,9},... | collective-permute-start | bytes 2752520 | tf_op jit(solution)/shard_map/ppermute | solution.py:1050
  64.5 18.8 %collective-permute-start.9 = (bf16[14,64,512]{2,1,0:T(8,128)(2,1)S(1)}, bf16[14,64,512]{2,1,0:T(8,128)(2,1)S(1)}, u32[]{:S(2)}, u32[]{:S(2)}) collective-permute-start(bf16[14,64,512]{2,1,0:T(8,128)(2,1)S(1)} %collective-permute-done.6.refs_11_), channel_id=1, source_target_pairs={{0,2},{4,0},{8,4},{12,8},{14,12},{10,14},{6,10},{2,6},{1,3},{5,1},... | collective-permute-start | bytes 2752520 | tf_op jit(solution)/shard_map/ppermute | solution.py:1050
  84.3 14.0 %collective-permute-start.12 = (bf16[11,64,512]{2,1,0:T(8,128)(2,1)S(1)}, bf16[11,64,512]{2,1,0:T(8,128)(2,1)S(1)}, u32[]{:S(2)}, u32[]{:S(2)}) collective-permute-start(bf16[11,64,512]{2,1,0:T(8,128)(2,1)S(1)} %slice.237), channel_id=1, source_target_pairs={{0,2},{4,0},{8,4},{12,8},{14,12},{10,14},{6,10},{2,6},{1,3},{5,1},... | collective-permute-start | bytes 2162696 | tf_op jit(solution)/shard_map/ppermute | solution.py:1050
  85.7 17.6 %collective-permute-start.13 = (bf16[12,64,512]{2,1,0:T(8,128)(2,1)S(1)}, bf16[12,64,512]{2,1,0:T(8,128)(2,1)S(1)}, u32[]{:S(2)}, u32[]{:S(2)}) collective-permute-start(bf16[12,64,512]{2,1,0:T(8,128)(2,1)S(1)} %pad_maximum_fusion.13), channel_id=1, source_target_pairs={{0,1},{1,0},{2,3},{3,2},{4,5},{5,4},{6,7},{7,6},{8,9},{9,8},{10,11... | collective-permute-start | bytes 2359304 | tf_op jit(solution)/shard_map/ppermute | solution.py:1054
  87.5 12.9 %collective-permute-start.11 = (bf16[11,64,512]{2,1,0:T(8,128)(2,1)S(1)}, bf16[11,64,512]{2,1,0:T(8,128)(2,1)S(1)}, u32[]{:S(2)}, u32[]{:S(2)}) collective-permute-start(bf16[11,64,512]{2,1,0:T(8,128)(2,1)S(1)} %pad_maximum_fusion.15), channel_id=1, source_target_pairs={{0,4},{4,8},{8,12},{12,14},{14,10},{10,6},{6,2},{2,0},{1,5},{5,9},... | collective-permute-start | bytes 2162696 | tf_op jit(solution)/shard_map/ppermute | solution.py:1050
  103.4 9.9 %collective-permute-start.16 = (bf16[6,64,512]{2,1,0:T(8,128)(2,1)S(1)}, bf16[6,64,512]{2,1,0:T(8,128)(2,1)S(1)}, u32[]{:S(2)}, u32[]{:S(2)}) collective-permute-start(bf16[6,64,512]{2,1,0:T(8,128)(2,1)S(1)} %pad_maximum_fusion.18), channel_id=1, source_target_pairs={{0,1},{1,0},{2,3},{3,2},{4,5},{5,4},{6,7},{7,6},{8,9},{9,8},{10,11... | collective-permute-start | bytes 1179656 | tf_op jit(solution)/shard_map/ppermute | solution.py:1054
  136.2 19.0 %collective-permute-start.18 = (bf16[5120,512]{1,0:T(8,128)(2,1)}, bf16[5120,512]{1,0:T(8,128)(2,1)}, u32[]{:S(2)}, u32[]{:S(2)}) collective-permute-start(bf16[5120,512]{1,0:T(8,128)(2,1)} %get-tuple-element.127.refs_2_.refs_3_.refs_4_.refs_6_.refs_9_.refs_11_.refs_5_.refs_10_), channel_id=1, source_target_pairs={{16,0},{17,1},{18,2},{19,3},{20,4},{21,5},{22,6},{23,7},{24,8},{25... | collective-permute-start | bytes 15728648 | tf_op jit(solution)/shard_map/ppermute | solution.py:1333
  194.2 63.1 %collective-permute-start.20 = (bf16[5120,512]{1,0:T(8,128)(2,1)}, bf16[5120,512]{1,0:T(8,128)(2,1)}, u32[]{:S(2)}, u32[]{:S(2)}) collective-permute-start(bf16[5120,512]{1,0:T(8,128)(2,1)} %get-tuple-element.154.refs_2_), channel_id=1, source_target_pairs={{0,16},{1,17},{2,18},{3,19},{4,20},{5,21},{6,22},{7,23},{8,24},{9,... | collective-permute-start | bytes 15728648 | tf_op jit(solution)/shard_map/ppermute | solution.py:1391
  256.1 10.5 %collective-permute-start.24 = (f32[15,512]{1,0:T(8,128)S(1)}, f32[15,512]{1,0:T(8,128)S(1)}, u32[]{:S(2)}, u32[]{:S(2)}) collective-permute-start(f32[15,512]{1,0:T(8,128)S(1)} %pad_maximum_fusion.19), channel_id=1, source_target_pairs={{0,1},{1,0},{2,3},{3,2},{4,5},{5,4},{6,7},{7,6},{8,9},{9,8},{10,11... | collective-permute-start | bytes 92168 | tf_op jit(solution)/shard_map/ppermute | solution.py:1062
  261.1 12.3 %collective-permute-start.23 = (bf16[6,64,512]{2,1,0:T(8,128)(2,1)}, bf16[6,64,512]{2,1,0:T(8,128)(2,1)S(1)}, u32[]{:S(2)}, u32[]{:S(2)}) collective-permute-start(bf16[6,64,512]{2,1,0:T(8,128)(2,1)} %get-tuple-element.162), channel_id=1, source_target_pairs={{0,1},{1,0},{2,3},{3,2},{4,5},{5,4},{6,7},{7,6},{8,9},{9,8},{10,11... | collective-permute-start | bytes 1179656 | tf_op jit(solution)/shard_map/ppermute | solution.py:1054
  265.5 29.8 %collective-permute-start.27 = (bf16[12,64,512]{2,1,0:T(8,128)(2,1)S(1)}, bf16[12,64,512]{2,1,0:T(8,128)(2,1)S(1)}, u32[]{:S(2)}, u32[]{:S(2)}) collective-permute-start(bf16[12,64,512]{2,1,0:T(8,128)(2,1)S(1)} %pad_maximum_fusion.14), channel_id=1, source_target_pairs={{0,1},{1,0},{2,3},{3,2},{4,5},{5,4},{6,7},{7,6},{8,9},{9,8},{10,11... | collective-permute-start | bytes 2359304 | tf_op jit(solution)/shard_map/ppermute | solution.py:1054
  275.8 19.5 %collective-permute-start.25 = (bf16[11,64,512]{2,1,0:T(8,128)(2,1)S(1)}, bf16[11,64,512]{2,1,0:T(8,128)(2,1)S(1)}, u32[]{:S(2)}, u32[]{:S(2)}) collective-permute-start(bf16[11,64,512]{2,1,0:T(8,128)(2,1)S(1)} %pad_maximum_fusion.16), channel_id=1, source_target_pairs={{0,4},{4,8},{8,12},{12,14},{14,10},{10,6},{6,2},{2,0},{1,5},{5,9},... | collective-permute-start | bytes 2162696 | tf_op jit(solution)/shard_map/ppermute | solution.py:1050
  276.2 19.2 %collective-permute-start.26 = (bf16[11,64,512]{2,1,0:T(8,128)(2,1)S(1)}, bf16[11,64,512]{2,1,0:T(8,128)(2,1)S(1)}, u32[]{:S(2)}, u32[]{:S(2)}) collective-permute-start(bf16[11,64,512]{2,1,0:T(8,128)(2,1)S(1)} %pad_maximum_fusion.17), channel_id=1, source_target_pairs={{0,2},{4,0},{8,4},{12,8},{14,12},{10,14},{6,10},{2,6},{1,3},{5,1},... | collective-permute-start | bytes 2162696 | tf_op jit(solution)/shard_map/ppermute | solution.py:1050
  278.4 17.0 %collective-permute-start.28 = (f32[15,512]{1,0:T(8,128)S(1)}, f32[15,512]{1,0:T(8,128)S(1)}, u32[]{:S(2)}, u32[]{:S(2)}) collective-permute-start(f32[15,512]{1,0:T(8,128)S(1)} %fusion.46), channel_id=1, source_target_pairs={{0,2},{2,0},{4,6},{6,4},{8,10},{10,8},{12,14},{14,12},{1,3},{3,1},... | collective-permute-start | bytes 92168 | tf_op jit(solution)/shard_map/ppermute | solution.py:1062
  280.5 19.4 %collective-permute-start.31 = (bf16[15,64,512]{2,1,0:T(8,128)(2,1)S(1)}, bf16[15,64,512]{2,1,0:T(8,128)(2,1)S(1)}, u32[]{:S(2)}, u32[]{:S(2)}) collective-permute-start(bf16[15,64,512]{2,1,0:T(8,128)(2,1)S(1)} %pad_maximum_fusion.7), channel_id=1, source_target_pairs={{0,1},{1,0},{2,3},{3,2},{4,5},{5,4},{6,7},{7,6},{8,9},{9,8},{10,11... | collective-permute-start | bytes 2949128 | tf_op jit(solution)/shard_map/ppermute | solution.py:1054
  296.1 18.1 %collective-permute-start.30 = (bf16[14,64,512]{2,1,0:T(8,128)(2,1)S(1)}, bf16[14,64,512]{2,1,0:T(8,128)(2,1)S(1)}, u32[]{:S(2)}, u32[]{:S(2)}) collective-permute-start(bf16[14,64,512]{2,1,0:T(8,128)(2,1)S(1)} %pad_maximum_fusion.10), channel_id=1, source_target_pairs={{0,2},{4,0},{8,4},{12,8},{14,12},{10,14},{6,10},{2,6},{1,3},{5,1},... | collective-permute-start | bytes 2752520 | tf_op jit(solution)/shard_map/ppermute | solution.py:1050
  298.6 17.7 %collective-permute-start.29 = (bf16[14,64,512]{2,1,0:T(8,128)(2,1)S(1)}, bf16[14,64,512]{2,1,0:T(8,128)(2,1)S(1)}, u32[]{:S(2)}, u32[]{:S(2)}) collective-permute-start(bf16[14,64,512]{2,1,0:T(8,128)(2,1)S(1)} %pad_maximum_fusion.9), channel_id=1, source_target_pairs={{0,4},{4,8},{8,12},{12,14},{14,10},{10,6},{6,2},{2,0},{1,5},{5,9},... | collective-permute-start | bytes 2752520 | tf_op jit(solution)/shard_map/ppermute | solution.py:1050
  298.7 15.5 %collective-permute-start.32 = (f32[15,512]{1,0:T(8,128)S(1)}, f32[15,512]{1,0:T(8,128)S(1)}, u32[]{:S(2)}, u32[]{:S(2)}) collective-permute-start(f32[15,512]{1,0:T(8,128)S(1)} %add.274), channel_id=1, source_target_pairs={{0,4},{2,6},{4,0},{6,2},{8,12},{10,14},{12,8},{14,10},{1,5},{3,7},... | collective-permute-start | bytes 92168 | tf_op jit(solution)/shard_map/ppermute | solution.py:1062
  298.9 20.4 %collective-permute-start.35 = (bf16[15,64,512]{2,1,0:T(8,128)(2,1)S(1)}, bf16[15,64,512]{2,1,0:T(8,128)(2,1)S(1)}, u32[]{:S(2)}, u32[]{:S(2)}) collective-permute-start(bf16[15,64,512]{2,1,0:T(8,128)(2,1)S(1)} %pad_maximum_fusion.8), channel_id=1, source_target_pairs={{0,1},{1,0},{2,3},{3,2},{4,5},{5,4},{6,7},{7,6},{8,9},{9,8},{10,11... | collective-permute-start | bytes 2949128 | tf_op jit(solution)/shard_map/ppermute | solution.py:1054
  317.1 14.1 %collective-permute-start.33 = (bf16[14,64,512]{2,1,0:T(8,128)(2,1)S(1)}, bf16[14,64,512]{2,1,0:T(8,128)(2,1)S(1)}, u32[]{:S(2)}, u32[]{:S(2)}) collective-permute-start(bf16[14,64,512]{2,1,0:T(8,128)(2,1)S(1)} %pad_maximum_fusion.11), channel_id=1, source_target_pairs={{0,4},{4,8},{8,12},{12,14},{14,10},{10,6},{6,2},{2,0},{1,5},{5,9},... | collective-permute-start | bytes 2752520 | tf_op jit(solution)/shard_map/ppermute | solution.py:1050
  317.6 13.8 %collective-permute-start.34 = (bf16[14,64,512]{2,1,0:T(8,128)(2,1)S(1)}, bf16[14,64,512]{2,1,0:T(8,128)(2,1)S(1)}, u32[]{:S(2)}, u32[]{:S(2)}) collective-permute-start(bf16[14,64,512]{2,1,0:T(8,128)(2,1)S(1)} %pad_maximum_fusion.12), channel_id=1, source_target_pairs={{0,2},{4,0},{8,4},{12,8},{14,12},{10,14},{6,10},{2,6},{1,3},{5,1},... | collective-permute-start | bytes 2752520 | tf_op jit(solution)/shard_map/ppermute | solution.py:1050
  319.3 11.9 %collective-permute-start.36 = (f32[15,512]{1,0:T(8,128)S(1)}, f32[15,512]{1,0:T(8,128)S(1)}, u32[]{:S(2)}, u32[]{:S(2)}) collective-permute-start(f32[15,512]{1,0:T(8,128)S(1)} %add.281), channel_id=1, source_target_pairs={{0,8},{2,10},{4,12},{6,14},{8,0},{10,2},{12,4},{14,6},{1,9},{3,11}... | collective-permute-start | bytes 92168 | tf_op jit(solution)/shard_map/ppermute | solution.py:1062
  345.7 14.5 %collective-permute-start.42 = (bf16[8,64,512]{2,1,0:T(8,128)(2,1)}, bf16[8,64,512]{2,1,0:T(8,128)(2,1)S(1)}, u32[]{:S(2)}, u32[]{:S(2)}) collective-permute-start(bf16[8,64,512]{2,1,0:T(8,128)(2,1)} %get-tuple-element.229), channel_id=1, source_target_pairs={{0,2},{4,0},{8,4},{12,8},{14,12},{10,14},{6,10},{2,6},{1,3},{5,1},... | collective-permute-start | bytes 1572872 | tf_op jit(solution)/shard_map/ppermute | solution.py:1050
  347.0 14.0 %collective-permute-start.41 = (bf16[8,64,512]{2,1,0:T(8,128)(2,1)S(1)}, bf16[8,64,512]{2,1,0:T(8,128)(2,1)S(1)}, u32[]{:S(2)}, u32[]{:S(2)}) collective-permute-start(bf16[8,64,512]{2,1,0:T(8,128)(2,1)S(1)} %get-tuple-element.230), channel_id=1, source_target_pairs={{0,4},{4,8},{8,12},{12,14},{14,10},{10,6},{6,2},{2,0},{1,5},{5,9},... | collective-permute-start | bytes 1572872 | tf_op jit(solution)/shard_map/ppermute | solution.py:1050
  (38 other events, 325.5 us)

commit v6 on v5

--- a/solution.py
+++ b/solution.py
@@ -1066,7 +1066,7 @@
     return jnp.concatenate(values, 0)
 
 
-def ring_gather(own_lead, own_late, tables):
+def ring_gather(own_lead, own_late, plan, make_tables):
     lead, late, half = LEAD, LEVEL - LEAD, LEAD // 2
     found = [([(0, lead, 0, 0, 0)], own_lead), ([(0, late, 0, 0, lead)], own_late)]
 
@@ -1077,6 +1077,8 @@
         found.append((ranges, value))
 
     up, down, across = step_of(own_lead, own_lead, own_late)
+    up, plan = lax.optimization_barrier((up, plan))
+    tables = make_tables(plan)
     found.append(([(0, late, 0, 1, lead)], across))
     ahead(up, 7, None)
     ahead(down, 1, None)
@@ -1240,36 +1242,42 @@
     if on_ring:
         capacity = LEVEL
         own_lead, own_late, plan = lend(position, owner_row.astype(jnp.int32), master[0])
-        place = jnp.where(owner_row % 2 == 0, owner_row // 2, wide_size - 1 - owner_row // 2)
-        kept, ahead, back = (jnp.take(row, place) for row in plan)
-        moved = (ranks >= kept).astype(jnp.int32) - 2 * (ranks >= kept + ahead).astype(jnp.int32)
-        place = (place + moved) % wide_size
-        base = jnp.take(plan[0], place)
-        below = jnp.take(plan[1], (place - 1) % wide_size)
-        ranks = jnp.where(
-            moved == 0,
-            ranks,
-            jnp.where(moved > 0, base + ranks - kept, base + below + ranks - kept - ahead),
-        )
-        distance = (place - position) % wide_size
-        halves = jnp.arange(narrow_size)[None, :] ^ narrow_at
-        table = (distance[:, None] * 2 + halves) * capacity + ranks[:, None]
-        total, late = wide_size * 2 * capacity, capacity - LEAD
-        is_late = (ranks >= LEAD)[:, None]
-        after_late = ranks[:, None] - LEAD + total + LEAD
-        far = jnp.where(
-            halves == 1,
-            jnp.where(is_late, after_late, ranks[:, None] + total),
-            jnp.where(is_late, after_late + late, table),
-        )
-        table = jnp.where(distance[:, None] == 4, far, table).reshape(-1)
-        slot_of = distance * capacity + ranks
-        hit = slot_of[None, :] == jnp.arange(wide_size * capacity)[:, None]
-        pieces = jnp.sum(hit.astype(jnp.int32) * (counter + 1)[None, :], 1) - 1
-        pieces = pieces.reshape(wide_size, capacity).astype(jnp.int32)
-        found, (pieces, table, scal) = ring_gather(
-            own_lead, own_late, (pieces, table.astype(jnp.int32), scal)
-        )
+
+        def make_tables(plan):
+            def pick(row, index):
+                hit = index[:, None] == jnp.arange(wide_size)[None, :]
+                return jnp.sum(jnp.where(hit, row[None, :], 0), 1)
+
+            place = jnp.where(owner_row % 2 == 0, owner_row // 2, wide_size - 1 - owner_row // 2)
+            kept, ahead = pick(plan[0], place), pick(plan[1], place)
+            moved = (ranks >= kept).astype(jnp.int32) - 2 * (ranks >= kept + ahead).astype(jnp.int32)
+            place = (place + moved) % wide_size
+            base = pick(plan[0], place)
+            below = pick(plan[1], (place - 1) % wide_size)
+            slots_there = jnp.where(
+                moved == 0,
+                ranks,
+                jnp.where(moved > 0, base + ranks - kept, base + below + ranks - kept - ahead),
+            )
+            distance = (place - position) % wide_size
+            halves = jnp.arange(narrow_size)[None, :] ^ narrow_at
+            table = (distance[:, None] * 2 + halves) * capacity + slots_there[:, None]
+            total, late = wide_size * 2 * capacity, capacity - LEAD
+            is_late = (slots_there >= LEAD)[:, None]
+            after_late = slots_there[:, None] - LEAD + total + LEAD
+            far = jnp.where(
+                halves == 1,
+                jnp.where(is_late, after_late, slots_there[:, None] + total),
+                jnp.where(is_late, after_late + late, table),
+            )
+            table = jnp.where(distance[:, None] == 4, far, table).reshape(-1)
+            slot_of = distance * capacity + slots_there
+            hit = slot_of[None, :] == jnp.arange(wide_size * capacity)[:, None]
+            pieces = jnp.sum(hit.astype(jnp.int32) * (counter + 1)[None, :], 1) - 1
+            pieces = pieces.reshape(wide_size, capacity).astype(jnp.int32)
+            return pieces, table.astype(jnp.int32), scal
+
+        found, (pieces, table, scal) = ring_gather(own_lead, own_late, plan, make_tables)
     else:
         places = (
             owner_row[:, None] * narrow_size + jnp.arange(narrow_size)[None, :]
@@ -1300,7 +1308,7 @@
 
     low_out = partial(store, dtype=bfloat)
     two, four = low_vm(2, length, 128), low_vm(4, length, 128)
-    down_half, up_half, both_halves = [(1, 0)], [(0, 1)], [(0, 1), (1, 0)]
+    both_halves = [(0, 1), (1, 0)]
 
     forward_outs = (
         [low_out(length, width)] * 3
@@ -1330,7 +1338,7 @@
             forward_scratch,
         )
     query, key, value, ctx_t, lse, resid, inner, swap = forward
-    rest_other = lax.ppermute(rest, "half", down_half)
+    rest_other = lax.ppermute(rest, "half", both_halves)
     cross_w = part(rest, 0, 2 * width)
     up_w = part(rest, 2 * width, hidden)
     down_w = part(rest, 2 * width + hidden, hidden)
@@ -1388,7 +1396,7 @@
     )
     swap_other = lax.ppermute(swap, "half", both_halves)
     grad_rest, swap_other = lax.optimization_barrier((grad_rest, swap_other))
-    grad_rest_other = lax.ppermute(grad_rest, "half", up_half)
+    grad_rest_other = lax.ppermute(grad_rest, "half", both_halves)
     output = join(output, swap_other[3 * some :])
     grad_inner, grad_memory_vec, *target = call(
         encoder_back_body,

time: 369 us -> 358 us (0.970)
  other arithmetic: 27.2 us -> 18.2 us
  starting transfers between devices: 48.3 us -> 43.8 us
    ppermute x24, waiting for transfers between devices: 60 us -> 71 us  [round_ring(): lax.ppermute(value, 'wide', [(RING[i], RING[(i + step) % count]) for i in...]
    add x4, other arithmetic: 11 us -> 0.09 us  [the longest x1 0.07 us: make_tables(): table = (distance[:, None] * 2 + halves) * capacity + slots_there[:, None]]
    ppermute x5, waiting for transfers between devices: 40 us -> 30.1 us  [partner(): lax.ppermute(value, axis, [(i, i ^ bit) for i in range(lax.axis_size(axis...]
    ppermute x2, starting transfers between devices: 5.7 us -> 0.21 us  [the longest x1 0.14 us: on_device(): grad_rest_other = lax.ppermute(grad_rest, 'half', both_halves)]
    ppermute x10, starting transfers between devices: 12.4 us -> 8.6 us  [swapped(): return lax.ppermute(value, 'narrow', [(0, 1), (1, 0)])]
  transfers between devices with their start and end apart: 43 -> 43, of which waited for: 27 -> 28; matrix products, arithmetic and copies ran while one was open for 10% -> 7% of each run, Pallas kernels for 22% -> 22%
where the time goes in v6:
time: 358 us; the launch traced here: 354 us
  Pallas kernels  146 us (41%)
  waiting for transfers between devices  121 us (34%)
  starting transfers between devices  43.8 us (12%)
  other arithmetic  18.2 us (5%)
  local copies, waits for them, and re-layouts  17.3 us (5%)
  between operations  7.45 us (2%)
    pallas_call x8, Pallas kernels, call(): pl.pallas_call(kernel, in_specs=specs, out_specs=[HB] * count_out, out_sh...  139 us
    ppermute x24, waiting for transfers between devices, round_ring(): lax.ppermute(value, 'wide', [(RING[i], RING[(i + step) % count]) for i in...  71 us
    ppermute x5, waiting for transfers between devices, partner(): lax.ppermute(value, axis, [(i, i ^ bit) for i in range(lax.axis_size(axis...  30.1 us
    ppermute x24, starting transfers between devices, round_ring(): lax.ppermute(value, 'wide', [(RING[i], RING[(i + step) % count]) for i in...  28.5 us
    ppermute x10, waiting for transfers between devices, swapped(): return lax.ppermute(value, 'narrow', [(0, 1), (1, 0)])  10.8 us
    ppermute x2, waiting for transfers between devices, on_device(): swap_other = lax.ppermute(swap, 'half', both_halves)  8.97 us
    ppermute x10, starting transfers between devices, swapped(): return lax.ppermute(value, 'narrow', [(0, 1), (1, 0)])  8.6 us
  transfers between devices with their start and end apart: 43, of which 28 were waited for; matrix products, arithmetic and copies ran while one was open for 7% of the time, Pallas kernels for 22%

profile of v6, /device:TPU:0, one launch (start us, length us, event | category | flops | bytes accessed | tf_op | source)
XLA Modules:
  0.0 353.8 jit_solution(14373785018233724107)
XLA Ops:
  0.7 4.3 %lend.1 = (bf16[14,64,512]{2,1,0:T(8,128)(2,1)}, bf16[8,64,512]{2,1,0:T(8,128)(2,1)}, bf16[8,64,512]{2,1,0:T(8,128)(2,1)}, s32[3,8]{1,0:T(4,128)}) custom-call(s32[1]{0:T(128)} %bitcast.scal, s32[56]{0:T(128)} %bitcast.198, f32[14,64,512]{2,1,0:T(8,128)} %bitcast.183), custom_call_target="tpu_custom_call" | custom-call | tf_op jit(solution)/shard_map/lend/pallas_call | solution.py:919
  5.0 3.1 collective-permute-start
  10.9 9.1 %collective-permute-done.below = bf16[8,64,512]{2,1,0:T(8,128)(2,1)S(1)} collective-permute-done((bf16[8,64,512]{2,1,0:T(8,128)(2,1)}, bf16[8,64,512]{2,1,0:T(8,128)(2,1)S(1)}, u32[]{:S(2)}, u32[]{:S(2)}) %collective-permute-start) | collective-permute-done | bytes 524320 | tf_op jit(solution)/shard_map/ppermute | solution.py:1050
  22.4 2.8 borrow.1
  45.1 15.8 %collective-permute-done.5.refs_10_ = bf16[14,64,512]{2,1,0:T(8,128)(2,1)S(1)} collective-permute-done((bf16[14,64,512]{2,1,0:T(8,128)(2,1)}, bf16[14,64,512]{2,1,0:T(8,128)(2,1)S(1)}, u32[]{:S(2)}, u32[]{:S(2)}) %collective-permute-start.5) | collective-permute-done | bytes 917536 | tf_op jit(solution)/shard_map/ppermute | solution.py:1050
  66.3 15.9 %collective-permute-done.8.refs_13_ = bf16[14,64,512]{2,1,0:T(8,128)(2,1)S(1)} collective-permute-done((bf16[14,64,512]{2,1,0:T(8,128)(2,1)S(1)}, bf16[14,64,512]{2,1,0:T(8,128)(2,1)S(1)}, u32[]{:S(2)}, u32[]{:S(2)}) %collective-permute-start.8) | collective-permute-done | bytes 917536 | tf_op jit(solution)/shard_map/ppermute | solution.py:1050
  86.2 2.0 collective-permute-start.11
  88.3 11.2 %collective-permute-done.11.refs_16_ = bf16[11,64,512]{2,1,0:T(8,128)(2,1)S(1)} collective-permute-done((bf16[11,64,512]{2,1,0:T(8,128)(2,1)S(1)}, bf16[11,64,512]{2,1,0:T(8,128)(2,1)S(1)}, u32[]{:S(2)}, u32[]{:S(2)}) %collective-permute-start.11) | collective-permute-done | bytes 720928 | tf_op jit(solution)/shard_map/ppermute | solution.py:1050
  99.5 1.7 collective-permute-done.12.refs_17_
  101.2 1.7 collective-permute-done.13.refs_15_
  106.7 3.6 %collective-permute-done.14.refs_18_ = bf16[4,64,512]{2,1,0:T(8,128)(2,1)S(1)} collective-permute-done((bf16[4,64,512]{2,1,0:T(8,128)(2,1)S(1)}, bf16[4,64,512]{2,1,0:T(8,128)(2,1)S(1)}, u32[]{:S(2)}, u32[]{:S(2)}) %collective-permute-start.14) | collective-permute-done | bytes 262176 | tf_op jit(solution)/shard_map/ppermute | solution.py:1050
  112.7 21.9 %self_forward.1 = (bf16[1024,512]{1,0:T(8,128)(2,1)}, bf16[1024,512]{1,0:T(8,128)(2,1)}, bf16[1024,512]{1,0:T(8,128)(2,1)}, bf16[512,1024]{1,0:T(8,128)(2,1)}, f...) custom-call(s32[7]{0:T(128)} %stack.24.refs_0_, ...), custom_call_target="tpu_custom_call" | custom-call | tf_op jit(solution)/shard_map/self_forward/pallas_call | solution.py:464
  134.6 13.1 %encoder_ff.1 = (bf16[1024,2048]{1,0:T(8,128)(2,1)}, bf16[1024,2048]{1,0:T(8,128)(2,1)}, f32[1024,512]{1,0:T(8,128)}, bf16[1024,512]{1,0:T(8,128)(2,1)}, bf16[2048,512]{1,0:T(8,128)(2,1)}) custom-call(s32[7]{0:T(128)} %stack.24.refs_0_, f32[1024,512]{1,0:T(8,128)} %get-tuple-element.129.refs_1_.refs_6_, ...), custom_call_target="tpu_custom_call", output_to_operand_aliasing={{4}: (6, {})} | custom-call | tf_op jit(solution)/shard_map/encoder_ff/pallas_call | solution.py:464
  147.8 4.5 %collective-permute-done.17.refs_2_.refs_4_ = bf16[2048,512]{1,0:T(8,128)(2,1)} collective-permute-done((bf16[2048,512]{1,0:T(8,128)(2,1)}, bf16[2048,512]{1,0:T(8,128)(2,1)}, u32[]{:S(2)}, u32[]{:S(2)}) %collective-permute-start.17) | collective-permute-done | bytes 2097184 | tf_op jit(solution)/shard_map/ppermute | solution.py:1356
  152.3 34.5 %decoder_middle.1 = (bf16[512,512]{1,0:T(8,128)(2,1)}, bf16[2048,512]{1,0:T(8,128)(2,1)}, f32[512,512]{1,0:T(8,128)}, bf16[5120,512]{1,0:T(8,128)(2,1)}, f32[6,512]{1,0:T(8,128)}, /*index=5*/bf16[2048,512]{1,0:T(8,128)(2,1)}) custom-call(s32[7]{0:T(128)} %stack.24.refs_0_, f32[1024,512]{1,0:T(8,128)} %get-tuple-element.129.refs_1_.refs_6_, ...), custom_call_target="tpu_custom_call" | custom-call | tf_op jit(solution)/shard_map/decoder_middle/pallas_call | solution.py:464
  186.9 4.5 %collective-permute-done.19.refs_3_.refs_14_ = bf16[2048,512]{1,0:T(8,128)(2,1)} collective-permute-done((bf16[2048,512]{1,0:T(8,128)(2,1)}, bf16[2048,512]{1,0:T(8,128)(2,1)}, u32[]{:S(2)}, u32[]{:S(2)}) %collective-permute-start.19) | collective-permute-done | bytes 2097184 | tf_op jit(solution)/shard_map/ppermute | solution.py:1397
  191.5 21.4 %encoder_back.1 = (f32[1024,512]{1,0:T(8,128)}, f32[3,512]{1,0:T(4,128)}, bf16[160,64,512]{2,1,0:T(8,128)(2,1)}, bf16[6,64,512]{2,1,0:T(8,128)(2,1)}, bf16[4,64,...) custom-call(s32[7]{0:T(128)} %stack.24.refs_0_, s32[112]{0:T(128)} %select_select_fusion.refs_1_, ...), custom_call_target="tpu_custom_call" | custom-call | tf_op jit(solution)/shard_map/encoder_back/pallas_call | solution.py:464
  213.0 35.0 %self_back.1 = (f32[1024,512]{1,0:T(8,128)}, f32[3,512]{1,0:T(4,128)}, bf16[160,64,512]{2,1,0:T(8,128)(2,1)}, bf16[6,64,512]{2,1,0:T(8,128)(2,1)}, bf16[4,64,512...) custom-call(s32[7]{0:T(128)} %stack.24.refs_0_, ...), custom_call_target="tpu_custom_call", output_to_operand_aliasing={{2}: (15, {}), {3}: (16, {}), {4}: (17, {}), {5}: (18, {})} | custom-call | tf_op jit(solution)/shard_map/self_back/pallas_call | solution.py:464
  252.6 1.7 collective-permute-start.21
  254.6 2.0 slice_bitcast_fusion.3
  259.9 3.8 %collective-permute-done.22 = bf16[4,64,512]{2,1,0:T(8,128)(2,1)S(1)} collective-permute-done((bf16[4,64,512]{2,1,0:T(8,128)(2,1)}, bf16[4,64,512]{2,1,0:T(8,128)(2,1)S(1)}, u32[]{:S(2)}, u32[]{:S(2)}) %collective-permute-start.22) | collective-permute-done | bytes 262176 | tf_op jit(solution)/shard_map/ppermute | solution.py:1050
  271.2 12.7 %collective-permute-done.28 = f32[15,512]{1,0:T(8,128)S(1)} collective-permute-done((f32[15,512]{1,0:T(8,128)S(1)}, f32[15,512]{1,0:T(8,128)S(1)}, u32[]{:S(2)}, u32[]{:S(2)}) %collective-permute-start.28) | collective-permute-done | bytes 30752 | tf_op jit(solution)/shard_map/ppermute | solution.py:1062
  284.8 2.1 collective-permute-start.29
  288.4 6.5 %collective-permute-done.31 = bf16[15,64,512]{2,1,0:T(8,128)(2,1)S(1)} collective-permute-done((bf16[15,64,512]{2,1,0:T(8,128)(2,1)S(1)}, bf16[15,64,512]{2,1,0:T(8,128)(2,1)S(1)}, u32[]{:S(2)}, u32[]{:S(2)}) %collective-permute-start.31) | collective-permute-done | bytes 983072 | tf_op jit(solution)/shard_map/ppermute | solution.py:1054
  294.9 8.1 %collective-permute-done.32 = f32[15,512]{1,0:T(8,128)S(1)} collective-permute-done((f32[15,512]{1,0:T(8,128)S(1)}, f32[15,512]{1,0:T(8,128)S(1)}, u32[]{:S(2)}, u32[]{:S(2)}) %collective-permute-start.32) | collective-permute-done | bytes 30752 | tf_op jit(solution)/shard_map/ppermute | solution.py:1062
  306.4 2.9 collective-permute-start.36
  309.3 9.4 %collective-permute-done.36 = f32[15,512]{1,0:T(8,128)S(1)} collective-permute-done((f32[15,512]{1,0:T(8,128)S(1)}, f32[15,512]{1,0:T(8,128)S(1)}, u32[]{:S(2)}, u32[]{:S(2)}) %collective-permute-start.36) | collective-permute-done | bytes 30752 | tf_op jit(solution)/shard_map/ppermute | solution.py:1062
  319.9 1.9 collective-permute-start.37
  321.9 2.0 collective-permute-start.38
  335.0 2.0 collective-permute-start.42
  339.5 7.8 %adam_kept.1 = (f32[14,64,512]{2,1,0:T(8,128)}, f32[14,64,512]{2,1,0:T(8,128)}, f32[14,64,512]{2,1,0:T(8,128)}, bf16[14,64,512]{2,1,0:T(8,128)(2,1)}) custom-call(s32[7]{0:T(128)} %stack.24.refs_0_, s32[3,8]{1,0:T(4,128)} %get-tuple-element.114.plan.refs_1_, f32[10,64,512]{2,1,0:T(8,128)} %pad_maximum_fusion.refs_2_, f32[14,64,512]{2,1,0:T(8,128)} %bitcast.184, ...), custom_call_target="tpu_custom_call" | custom-call | tf_op jit(solution)/shard_map/adam_kept/pallas_call | solution.py:464
  349.8 3.8 %adam_lent.1 = (f32[14,64,512]{2,1,0:T(8,128)}, f32[14,64,512]{2,1,0:T(8,128)}, f32[14,64,512]{2,1,0:T(8,128)}, bf16[14,64,512]{2,1,0:T(8,128)(2,1)}) custom-call(s32[7]{0:T(128)} %stack.24.refs_0_, s32[3,8]{1,0:T(4,128)} %get-tuple-element.114.plan.refs_1_, ...), custom_call_target="tpu_custom_call", output_to_operand_aliasing={{0}: (7, {}), {1}: (8, {}), {2}: (9, {}), {3}: (10, {})} | custom-call | tf_op jit(solution)/shard_map/adam_lent/pallas_call | solution.py:464
  (220 shorter events, 73.7 us)
Async XLA Ops:
  5.0 15.1 %collective-permute-start = (bf16[8,64,512]{2,1,0:T(8,128)(2,1)}, bf16[8,64,512]{2,1,0:T(8,128)(2,1)S(1)}, u32[]{:S(2)}, u32[]{:S(2)}) collective-permute-start(bf16[8,64,512]{2,1,0:T(8,128)(2,1)} %get-tuple-element.105), channel_id=1, source_target_pairs={{0,4},{4,8},{8,12},{12,14},{14,10},{10,6},{6,2},{2,0},{1,5},{5,9},... | collective-permute-start | bytes 1572872 | tf_op jit(solution)/shard_map/ppermute | solution.py:1050
  8.0 13.6 %collective-permute-start.1 = (bf16[8,64,512]{2,1,0:T(8,128)(2,1)}, bf16[8,64,512]{2,1,0:T(8,128)(2,1)S(1)}, u32[]{:S(2)}, u32[]{:S(2)}) collective-permute-start(bf16[8,64,512]{2,1,0:T(8,128)(2,1)} %get-tuple-element.106), channel_id=1, source_target_pairs={{0,2},{4,0},{8,4},{12,8},{14,12},{10,14},{6,10},{2,6},{1,3},{5,1},... | collective-permute-start | bytes 1572872 | tf_op jit(solution)/shard_map/ppermute | solution.py:1050
  25.2 9.8 %collective-permute-start.2 = (bf16[6,64,512]{2,1,0:T(8,128)(2,1)}, bf16[6,64,512]{2,1,0:T(8,128)(2,1)S(1)}, u32[]{:S(2)}, u32[]{:S(2)}) collective-permute-start(bf16[6,64,512]{2,1,0:T(8,128)(2,1)} %get-tuple-element.107.refs_4_), channel_id=1, source_target_pairs={{0,4},{4,8},{8,12},{12,14},{14,10},{10,6},{6,2},{2,0},{1,5},{5,9},... | collective-permute-start | bytes 1179656 | tf_op jit(solution)/shard_map/ppermute | solution.py:1050
  38.5 23.9 %collective-permute-start.7 = (bf16[15,64,512]{2,1,0:T(8,128)(2,1)}, bf16[15,64,512]{2,1,0:T(8,128)(2,1)S(1)}, u32[]{:S(2)}, u32[]{:S(2)}) collective-permute-start(bf16[15,64,512]{2,1,0:T(8,128)(2,1)} %pad_maximum_fusion.5), channel_id=1, source_target_pairs={{0,1},{1,0},{2,3},{3,2},{4,5},{5,4},{6,7},{7,6},{8,9},{9,8},{10,11... | collective-permute-start | bytes 2949128 | tf_op jit(solution)/shard_map/ppermute | solution.py:1054
  41.4 19.6 %collective-permute-start.5 = (bf16[14,64,512]{2,1,0:T(8,128)(2,1)}, bf16[14,64,512]{2,1,0:T(8,128)(2,1)S(1)}, u32[]{:S(2)}, u32[]{:S(2)}) collective-permute-start(bf16[14,64,512]{2,1,0:T(8,128)(2,1)} %get-tuple-element.235), channel_id=1, source_target_pairs={{0,4},{4,8},{8,12},{12,14},{14,10},{10,6},{6,2},{2,0},{1,5},{5,9},... | collective-permute-start | bytes 2752520 | tf_op jit(solution)/shard_map/ppermute | solution.py:1050
  43.1 19.3 %collective-permute-start.6 = (bf16[14,64,512]{2,1,0:T(8,128)(2,1)}, bf16[14,64,512]{2,1,0:T(8,128)(2,1)S(1)}, u32[]{:S(2)}, u32[]{:S(2)}) collective-permute-start(bf16[14,64,512]{2,1,0:T(8,128)(2,1)} %get-tuple-element.234), channel_id=1, source_target_pairs={{0,2},{4,0},{8,4},{12,8},{14,12},{10,14},{6,10},{2,6},{1,3},{5,1},... | collective-permute-start | bytes 2752520 | tf_op jit(solution)/shard_map/ppermute | solution.py:1050
  63.8 21.2 %collective-permute-start.10 = (bf16[15,64,512]{2,1,0:T(8,128)(2,1)S(1)}, bf16[15,64,512]{2,1,0:T(8,128)(2,1)}, u32[]{:S(2)}, u32[]{:S(2)}) collective-permute-start(bf16[15,64,512]{2,1,0:T(8,128)(2,1)S(1)} %pad_maximum_fusion.6), channel_id=1, source_target_pairs={{0,1},{1,0},{2,3},{3,2},{4,5},{5,4},{6,7},{7,6},{8,9},{9,8},{10,11... | collective-permute-start | bytes 2949128 | tf_op jit(solution)/shard_map/ppermute | solution.py:1054
  64.3 17.9 %collective-permute-start.8 = (bf16[14,64,512]{2,1,0:T(8,128)(2,1)S(1)}, bf16[14,64,512]{2,1,0:T(8,128)(2,1)S(1)}, u32[]{:S(2)}, u32[]{:S(2)}) collective-permute-start(bf16[14,64,512]{2,1,0:T(8,128)(2,1)S(1)} %collective-permute-done.5.refs_10_), channel_id=1, source_target_pairs={{0,4},{4,8},{8,12},{12,14},{14,10},{10,6},{6,2},{2,0},{1,5},{5,9},... | collective-permute-start | bytes 2752520 | tf_op jit(solution)/shard_map/ppermute | solution.py:1050
  65.7 17.8 %collective-permute-start.9 = (bf16[14,64,512]{2,1,0:T(8,128)(2,1)}, bf16[14,64,512]{2,1,0:T(8,128)(2,1)S(1)}, u32[]{:S(2)}, u32[]{:S(2)}) collective-permute-start(bf16[14,64,512]{2,1,0:T(8,128)(2,1)} %copy-done.9), channel_id=1, source_target_pairs={{0,2},{4,0},{8,4},{12,8},{14,12},{10,14},{6,10},{2,6},{1,3},{5,1},... | collective-permute-start | bytes 2752520 | tf_op jit(solution)/shard_map/ppermute | solution.py:1050
  85.3 17.6 %collective-permute-start.13 = (bf16[12,64,512]{2,1,0:T(8,128)(2,1)S(1)}, bf16[12,64,512]{2,1,0:T(8,128)(2,1)}, u32[]{:S(2)}, u32[]{:S(2)}) collective-permute-start(bf16[12,64,512]{2,1,0:T(8,128)(2,1)S(1)} %pad_maximum_fusion.13), channel_id=1, source_target_pairs={{0,1},{1,0},{2,3},{3,2},{4,5},{5,4},{6,7},{7,6},{8,9},{9,8},{10,11... | collective-permute-start | bytes 2359304 | tf_op jit(solution)/shard_map/ppermute | solution.py:1054
  86.2 13.3 %collective-permute-start.11 = (bf16[11,64,512]{2,1,0:T(8,128)(2,1)S(1)}, bf16[11,64,512]{2,1,0:T(8,128)(2,1)S(1)}, u32[]{:S(2)}, u32[]{:S(2)}) collective-permute-start(bf16[11,64,512]{2,1,0:T(8,128)(2,1)S(1)} %pad_maximum_fusion.15), channel_id=1, source_target_pairs={{0,4},{4,8},{8,12},{12,14},{14,10},{10,6},{6,2},{2,0},{1,5},{5,9},... | collective-permute-start | bytes 2162696 | tf_op jit(solution)/shard_map/ppermute | solution.py:1050
  88.1 13.1 %collective-permute-start.12 = (bf16[11,64,512]{2,1,0:T(8,128)(2,1)S(1)}, bf16[11,64,512]{2,1,0:T(8,128)(2,1)S(1)}, u32[]{:S(2)}, u32[]{:S(2)}) collective-permute-start(bf16[11,64,512]{2,1,0:T(8,128)(2,1)S(1)} %slice.249), channel_id=1, source_target_pairs={{0,2},{4,0},{8,4},{12,8},{14,12},{10,14},{6,10},{2,6},{1,3},{5,1},... | collective-permute-start | bytes 2162696 | tf_op jit(solution)/shard_map/ppermute | solution.py:1050
  134.5 17.7 %collective-permute-start.18 = (bf16[5120,512]{1,0:T(8,128)(2,1)}, bf16[5120,512]{1,0:T(8,128)(2,1)}, u32[]{:S(2)}, u32[]{:S(2)}) collective-permute-start(bf16[5120,512]{1,0:T(8,128)(2,1)} %get-tuple-element.130.refs_2_.refs_3_.refs_4_.refs_6_.refs_9_.refs_11_.refs_5_.refs_10_), channel_id=1, source_target_pairs={{0,16},{16,0},{1,17},{17,1},{2,18},{18,2},{3,19},{19,3},{4,20},{20... | collective-permute-start | bytes 15728648 | tf_op jit(solution)/shard_map/ppermute | solution.py:1341
  191.4 58.5 %collective-permute-start.20 = (bf16[5120,512]{1,0:T(8,128)(2,1)}, bf16[5120,512]{1,0:T(8,128)(2,1)}, u32[]{:S(2)}, u32[]{:S(2)}) collective-permute-start(bf16[5120,512]{1,0:T(8,128)(2,1)} %get-tuple-element.157.refs_2_), channel_id=1, source_target_pairs={{0,16},{16,0},{1,17},{17,1},{2,18},{18,2},{3,19},{19,3},{4,20},{20... | collective-permute-start | bytes 15728648 | tf_op jit(solution)/shard_map/ppermute | solution.py:1399
  248.8 10.8 %collective-permute-start.24 = (f32[15,512]{1,0:T(8,128)S(1)}, f32[15,512]{1,0:T(8,128)S(1)}, u32[]{:S(2)}, u32[]{:S(2)}) collective-permute-start(f32[15,512]{1,0:T(8,128)S(1)} %pad_maximum_fusion.19), channel_id=1, source_target_pairs={{0,1},{1,0},{2,3},{3,2},{4,5},{5,4},{6,7},{7,6},{8,9},{9,8},{10,11... | collective-permute-start | bytes 92168 | tf_op jit(solution)/shard_map/ppermute | solution.py:1062
  251.5 12.3 %collective-permute-start.23 = (bf16[6,64,512]{2,1,0:T(8,128)(2,1)}, bf16[6,64,512]{2,1,0:T(8,128)(2,1)S(1)}, u32[]{:S(2)}, u32[]{:S(2)}) collective-permute-start(bf16[6,64,512]{2,1,0:T(8,128)(2,1)} %get-tuple-element.165), channel_id=1, source_target_pairs={{0,1},{1,0},{2,3},{3,2},{4,5},{5,4},{6,7},{7,6},{8,9},{9,8},{10,11... | collective-permute-start | bytes 1179656 | tf_op jit(solution)/shard_map/ppermute | solution.py:1054
  258.0 25.8 %collective-permute-start.27 = (bf16[12,64,512]{2,1,0:T(8,128)(2,1)S(1)}, bf16[12,64,512]{2,1,0:T(8,128)(2,1)S(1)}, u32[]{:S(2)}, u32[]{:S(2)}) collective-permute-start(bf16[12,64,512]{2,1,0:T(8,128)(2,1)S(1)} %pad_maximum_fusion.14), channel_id=1, source_target_pairs={{0,1},{1,0},{2,3},{3,2},{4,5},{5,4},{6,7},{7,6},{8,9},{9,8},{10,11... | collective-permute-start | bytes 2359304 | tf_op jit(solution)/shard_map/ppermute | solution.py:1054
  266.2 17.7 %collective-permute-start.26 = (bf16[11,64,512]{2,1,0:T(8,128)(2,1)S(1)}, bf16[11,64,512]{2,1,0:T(8,128)(2,1)S(1)}, u32[]{:S(2)}, u32[]{:S(2)}) collective-permute-start(bf16[11,64,512]{2,1,0:T(8,128)(2,1)S(1)} %pad_maximum_fusion.17), channel_id=1, source_target_pairs={{0,2},{4,0},{8,4},{12,8},{14,12},{10,14},{6,10},{2,6},{1,3},{5,1},... | collective-permute-start | bytes 2162696 | tf_op jit(solution)/shard_map/ppermute | solution.py:1050
  267.8 16.1 %collective-permute-start.25 = (bf16[11,64,512]{2,1,0:T(8,128)(2,1)S(1)}, bf16[11,64,512]{2,1,0:T(8,128)(2,1)S(1)}, u32[]{:S(2)}, u32[]{:S(2)}) collective-permute-start(bf16[11,64,512]{2,1,0:T(8,128)(2,1)S(1)} %pad_maximum_fusion.16), channel_id=1, source_target_pairs={{0,4},{4,8},{8,12},{12,14},{14,10},{10,6},{6,2},{2,0},{1,5},{5,9},... | collective-permute-start | bytes 2162696 | tf_op jit(solution)/shard_map/ppermute | solution.py:1050
  269.3 14.6 %collective-permute-start.28 = (f32[15,512]{1,0:T(8,128)S(1)}, f32[15,512]{1,0:T(8,128)S(1)}, u32[]{:S(2)}, u32[]{:S(2)}) collective-permute-start(f32[15,512]{1,0:T(8,128)S(1)} %fusion.49), channel_id=1, source_target_pairs={{0,2},{2,0},{4,6},{6,4},{8,10},{10,8},{12,14},{14,12},{1,3},{3,1},... | collective-permute-start | bytes 92168 | tf_op jit(solution)/shard_map/ppermute | solution.py:1062
  270.4 24.5 %collective-permute-start.31 = (bf16[15,64,512]{2,1,0:T(8,128)(2,1)S(1)}, bf16[15,64,512]{2,1,0:T(8,128)(2,1)S(1)}, u32[]{:S(2)}, u32[]{:S(2)}) collective-permute-start(bf16[15,64,512]{2,1,0:T(8,128)(2,1)S(1)} %pad_maximum_fusion.7), channel_id=1, source_target_pairs={{0,1},{1,0},{2,3},{3,2},{4,5},{5,4},{6,7},{7,6},{8,9},{9,8},{10,11... | collective-permute-start | bytes 2949128 | tf_op jit(solution)/shard_map/ppermute | solution.py:1054
  284.4 18.5 %collective-permute-start.30 = (bf16[14,64,512]{2,1,0:T(8,128)(2,1)S(1)}, bf16[14,64,512]{2,1,0:T(8,128)(2,1)S(1)}, u32[]{:S(2)}, u32[]{:S(2)}) collective-permute-start(bf16[14,64,512]{2,1,0:T(8,128)(2,1)S(1)} %pad_maximum_fusion.10), channel_id=1, source_target_pairs={{0,2},{4,0},{8,4},{12,8},{14,12},{10,14},{6,10},{2,6},{1,3},{5,1},... | collective-permute-start | bytes 2752520 | tf_op jit(solution)/shard_map/ppermute | solution.py:1050
  284.8 18.6 %collective-permute-start.29 = (bf16[14,64,512]{2,1,0:T(8,128)(2,1)S(1)}, bf16[14,64,512]{2,1,0:T(8,128)(2,1)S(1)}, u32[]{:S(2)}, u32[]{:S(2)}) collective-permute-start(bf16[14,64,512]{2,1,0:T(8,128)(2,1)S(1)} %pad_maximum_fusion.9), channel_id=1, source_target_pairs={{0,4},{4,8},{8,12},{12,14},{14,10},{10,6},{6,2},{2,0},{1,5},{5,9},... | collective-permute-start | bytes 2752520 | tf_op jit(solution)/shard_map/ppermute | solution.py:1050
  286.9 16.1 %collective-permute-start.32 = (f32[15,512]{1,0:T(8,128)S(1)}, f32[15,512]{1,0:T(8,128)S(1)}, u32[]{:S(2)}, u32[]{:S(2)}) collective-permute-start(f32[15,512]{1,0:T(8,128)S(1)} %add.483), channel_id=1, source_target_pairs={{0,4},{2,6},{4,0},{6,2},{8,12},{10,14},{12,8},{14,10},{1,5},{3,7},... | collective-permute-start | bytes 92168 | tf_op jit(solution)/shard_map/ppermute | solution.py:1062
  288.4 20.9 %collective-permute-start.35 = (bf16[15,64,512]{2,1,0:T(8,128)(2,1)S(1)}, bf16[15,64,512]{2,1,0:T(8,128)(2,1)S(1)}, u32[]{:S(2)}, u32[]{:S(2)}) collective-permute-start(bf16[15,64,512]{2,1,0:T(8,128)(2,1)S(1)} %pad_maximum_fusion.8), channel_id=1, source_target_pairs={{0,1},{1,0},{2,3},{3,2},{4,5},{5,4},{6,7},{7,6},{8,9},{9,8},{10,11... | collective-permute-start | bytes 2949128 | tf_op jit(solution)/shard_map/ppermute | solution.py:1054
  304.0 14.7 %collective-permute-start.34 = (bf16[14,64,512]{2,1,0:T(8,128)(2,1)S(1)}, bf16[14,64,512]{2,1,0:T(8,128)(2,1)S(1)}, u32[]{:S(2)}, u32[]{:S(2)}) collective-permute-start(bf16[14,64,512]{2,1,0:T(8,128)(2,1)S(1)} %pad_maximum_fusion.12), channel_id=1, source_target_pairs={{0,2},{4,0},{8,4},{12,8},{14,12},{10,14},{6,10},{2,6},{1,3},{5,1},... | collective-permute-start | bytes 2752520 | tf_op jit(solution)/shard_map/ppermute | solution.py:1050
  305.3 13.4 %collective-permute-start.33 = (bf16[14,64,512]{2,1,0:T(8,128)(2,1)S(1)}, bf16[14,64,512]{2,1,0:T(8,128)(2,1)S(1)}, u32[]{:S(2)}, u32[]{:S(2)}) collective-permute-start(bf16[14,64,512]{2,1,0:T(8,128)(2,1)S(1)} %pad_maximum_fusion.11), channel_id=1, source_target_pairs={{0,4},{4,8},{8,12},{12,14},{14,10},{10,6},{6,2},{2,0},{1,5},{5,9},... | collective-permute-start | bytes 2752520 | tf_op jit(solution)/shard_map/ppermute | solution.py:1050
  306.4 12.2 %collective-permute-start.36 = (f32[15,512]{1,0:T(8,128)S(1)}, f32[15,512]{1,0:T(8,128)S(1)}, u32[]{:S(2)}, u32[]{:S(2)}) collective-permute-start(f32[15,512]{1,0:T(8,128)S(1)} %add.490), channel_id=1, source_target_pairs={{0,8},{2,10},{4,12},{6,14},{8,0},{10,2},{12,4},{14,6},{1,9},{3,11}... | collective-permute-start | bytes 92168 | tf_op jit(solution)/shard_map/ppermute | solution.py:1062
  319.9 11.6 %collective-permute-start.37 = (bf16[6,64,512]{2,1,0:T(8,128)(2,1)}, bf16[6,64,512]{2,1,0:T(8,128)(2,1)S(1)}, u32[]{:S(2)}, u32[]{:S(2)}) collective-permute-start(bf16[6,64,512]{2,1,0:T(8,128)(2,1)} %get-tuple-element.208), channel_id=1, source_target_pairs={{0,4},{4,8},{8,12},{12,14},{14,10},{10,6},{6,2},{2,0},{1,5},{5,9},... | collective-permute-start | bytes 1179656 | tf_op jit(solution)/shard_map/ppermute | solution.py:1050
  321.9 9.7 %collective-permute-start.38 = (bf16[6,64,512]{2,1,0:T(8,128)(2,1)}, bf16[6,64,512]{2,1,0:T(8,128)(2,1)}, u32[]{:S(2)}, u32[]{:S(2)}) collective-permute-start(bf16[6,64,512]{2,1,0:T(8,128)(2,1)} %get-tuple-element.207), channel_id=1, source_target_pairs={{0,2},{4,0},{8,4},{12,8},{14,12},{10,14},{6,10},{2,6},{1,3},{5,1},... | collective-permute-start | bytes 1179656 | tf_op jit(solution)/shard_map/ppermute | solution.py:1050
  335.0 13.9 %collective-permute-start.41 = (bf16[8,64,512]{2,1,0:T(8,128)(2,1)}, bf16[8,64,512]{2,1,0:T(8,128)(2,1)S(1)}, u32[]{:S(2)}, u32[]{:S(2)}) collective-permute-start(bf16[8,64,512]{2,1,0:T(8,128)(2,1)} %get-tuple-element.233), channel_id=1, source_target_pairs={{0,4},{4,8},{8,12},{12,14},{14,10},{10,6},{6,2},{2,0},{1,5},{5,9},... | collective-permute-start | bytes 1572872 | tf_op jit(solution)/shard_map/ppermute | solution.py:1050
  335.0 13.9 %collective-permute-start.42 = (bf16[8,64,512]{2,1,0:T(8,128)(2,1)S(1)}, bf16[8,64,512]{2,1,0:T(8,128)(2,1)S(1)}, u32[]{:S(2)}, u32[]{:S(2)}) collective-permute-start(bf16[8,64,512]{2,1,0:T(8,128)(2,1)S(1)} %get-tuple-element.232), channel_id=1, source_target_pairs={{0,2},{4,0},{8,4},{12,8},{14,12},{10,14},{6,10},{2,6},{1,3},{5,1},... | collective-permute-start | bytes 1572872 | tf_op jit(solution)/shard_map/ppermute | solution.py:1050
  (39 other events, 367.4 us)

commit v7 on v6

--- a/solution.py
+++ b/solution.py
@@ -1528,6 +1528,7 @@
             master[0], mine, moment_one[0], moment_two[0], rate_matrix, decay_matrix
         )
         new_copy = new_weight.astype(bfloat)
+    memory, output, vec_grads = lax.optimization_barrier((memory, output, vec_grads))
     vec_weight, vec_first, vec_second = adam(
         vec_master, vec_grads, vec_one, vec_two, rate_vector, 0.0
     )

time: 358 us -> 367 us (1.025)
  other arithmetic: 18.2 us -> 27.7 us
    ppermute x5, waiting for transfers between devices: 30.1 us -> 20.8 us  [partner(): lax.ppermute(value, axis, [(i, i ^ bit) for i in range(lax.axis_size(axis...]
    ppermute x10, waiting for transfers between devices: 10.8 us -> 17.1 us  [swapped(): return lax.ppermute(value, 'narrow', [(0, 1), (1, 0)])]
    concatenate x17 -> x18, other arithmetic: 4.92 us -> 8.84 us  [join(): return jnp.concatenate(values, 0)]
  transfers between devices with their start and end apart: 43 -> 43, of which waited for: 28 -> 29; matrix products, arithmetic and copies ran while one was open for 7% -> 9% of each run, Pallas kernels for 22% -> 22%
where the time goes in v7:
time: 367 us; the launch traced here: 361 us
  Pallas kernels  145 us (40%)
  waiting for transfers between devices  121 us (33%)
  starting transfers between devices  41.1 us (11%)
  other arithmetic  27.7 us (8%)
  local copies, waits for them, and re-layouts  18.8 us (5%)
  between operations  7.42 us (2%)
    pallas_call x8, Pallas kernels, call(): pl.pallas_call(kernel, in_specs=specs, out_specs=[HB] * count_out, out_sh...  138 us
    ppermute x24, waiting for transfers between devices, round_ring(): lax.ppermute(value, 'wide', [(RING[i], RING[(i + step) % count]) for i in...  73.9 us
    ppermute x24, starting transfers between devices, round_ring(): lax.ppermute(value, 'wide', [(RING[i], RING[(i + step) % count]) for i in...  26.4 us
    ppermute x5, waiting for transfers between devices, partner(): lax.ppermute(value, axis, [(i, i ^ bit) for i in range(lax.axis_size(axis...  20.8 us
    ppermute x10, waiting for transfers between devices, swapped(): return lax.ppermute(value, 'narrow', [(0, 1), (1, 0)])  17.1 us
    ppermute x2, waiting for transfers between devices, on_device(): swap_other = lax.ppermute(swap, 'half', both_halves)  8.97 us
    concatenate x18, other arithmetic, join(): return jnp.concatenate(values, 0)  8.84 us
    convert_element_type x9, other arithmetic, added(): return sum((value.astype(single) for value in values)).astype(bfloat)  8.46 us
  transfers between devices with their start and end apart: 43, of which 29 were waited for; matrix products, arithmetic and copies ran while one was open for 9% of the time, Pallas kernels for 22%

profile of v7, /device:TPU:0, one launch (start us, length us, event | category | flops | bytes accessed | tf_op | source)
XLA Modules:
  0.0 360.8 jit_solution(4315079531703605557)
XLA Ops:
  0.7 4.3 %lend.1 = (bf16[14,64,512]{2,1,0:T(8,128)(2,1)}, bf16[8,64,512]{2,1,0:T(8,128)(2,1)}, bf16[8,64,512]{2,1,0:T(8,128)(2,1)}, s32[3,8]{1,0:T(4,128)}) custom-call(s32[1]{0:T(128)} %bitcast.scal, s32[56]{0:T(128)} %bitcast.198, f32[14,64,512]{2,1,0:T(8,128)} %bitcast.183), custom_call_target="tpu_custom_call" | custom-call | tf_op jit(solution)/shard_map/lend/pallas_call | solution.py:919
  5.0 3.1 collective-permute-start
  10.9 9.1 %collective-permute-done.below = bf16[8,64,512]{2,1,0:T(8,128)(2,1)S(1)} collective-permute-done((bf16[8,64,512]{2,1,0:T(8,128)(2,1)}, bf16[8,64,512]{2,1,0:T(8,128)(2,1)S(1)}, u32[]{:S(2)}, u32[]{:S(2)}) %collective-permute-start) | collective-permute-done | bytes 524320 | tf_op jit(solution)/shard_map/ppermute | solution.py:1050
  22.4 2.5 borrow.1
  25.0 1.8 collective-permute-start.2
  45.3 16.0 %collective-permute-done.5.refs_10_ = bf16[14,64,512]{2,1,0:T(8,128)(2,1)S(1)} collective-permute-done((bf16[14,64,512]{2,1,0:T(8,128)(2,1)}, bf16[14,64,512]{2,1,0:T(8,128)(2,1)S(1)}, u32[]{:S(2)}, u32[]{:S(2)}) %collective-permute-start.5) | collective-permute-done | bytes 917536 | tf_op jit(solution)/shard_map/ppermute | solution.py:1050
  66.4 15.9 %collective-permute-done.8.refs_13_ = bf16[14,64,512]{2,1,0:T(8,128)(2,1)S(1)} collective-permute-done((bf16[14,64,512]{2,1,0:T(8,128)(2,1)S(1)}, bf16[14,64,512]{2,1,0:T(8,128)(2,1)S(1)}, u32[]{:S(2)}, u32[]{:S(2)}) %collective-permute-start.8) | collective-permute-done | bytes 917536 | tf_op jit(solution)/shard_map/ppermute | solution.py:1050
  83.4 2.0 collective-permute-done.10.refs_12_
  88.2 10.3 %collective-permute-done.11.refs_16_ = bf16[11,64,512]{2,1,0:T(8,128)(2,1)S(1)} collective-permute-done((bf16[11,64,512]{2,1,0:T(8,128)(2,1)S(1)}, bf16[11,64,512]{2,1,0:T(8,128)(2,1)S(1)}, u32[]{:S(2)}, u32[]{:S(2)}) %collective-permute-start.11) | collective-permute-done | bytes 720928 | tf_op jit(solution)/shard_map/ppermute | solution.py:1050
  98.5 2.0 collective-permute-done.12.refs_17_
  100.5 2.9 collective-permute-done.13.refs_15_
  106.6 3.6 collective-permute-done.14.refs_18_
  112.4 22.4 %self_forward.1 = (bf16[1024,512]{1,0:T(8,128)(2,1)}, bf16[1024,512]{1,0:T(8,128)(2,1)}, bf16[1024,512]{1,0:T(8,128)(2,1)}, bf16[512,1024]{1,0:T(8,128)(2,1)}, f...) custom-call(s32[7]{0:T(128)} %stack.24.refs_0_, ...), custom_call_target="tpu_custom_call" | custom-call | tf_op jit(solution)/shard_map/self_forward/pallas_call | solution.py:464
  134.9 13.1 %encoder_ff.1 = (bf16[1024,2048]{1,0:T(8,128)(2,1)}, bf16[1024,2048]{1,0:T(8,128)(2,1)}, f32[1024,512]{1,0:T(8,128)}, bf16[1024,512]{1,0:T(8,128)(2,1)}, bf16[2048,512]{1,0:T(8,128)(2,1)}) custom-call(s32[7]{0:T(128)} %stack.24.refs_0_, f32[1024,512]{1,0:T(8,128)} %get-tuple-element.132.refs_1_.refs_6_, ...), custom_call_target="tpu_custom_call", output_to_operand_aliasing={{4}: (6, {})} | custom-call | tf_op jit(solution)/shard_map/encoder_ff/pallas_call | solution.py:464
  148.0 4.5 %collective-permute-done.17.refs_2_.refs_4_ = bf16[2048,512]{1,0:T(8,128)(2,1)} collective-permute-done((bf16[2048,512]{1,0:T(8,128)(2,1)}, bf16[2048,512]{1,0:T(8,128)(2,1)}, u32[]{:S(2)}, u32[]{:S(2)}) %collective-permute-start.17) | collective-permute-done | bytes 2097184 | tf_op jit(solution)/shard_map/ppermute | solution.py:1356
  152.5 34.5 %decoder_middle.1 = (bf16[512,512]{1,0:T(8,128)(2,1)}, bf16[2048,512]{1,0:T(8,128)(2,1)}, f32[512,512]{1,0:T(8,128)}, bf16[5120,512]{1,0:T(8,128)(2,1)}, f32[6,512]{1,0:T(8,128)}, /*index=5*/bf16[2048,512]{1,0:T(8,128)(2,1)}) custom-call(s32[7]{0:T(128)} %stack.24.refs_0_, f32[1024,512]{1,0:T(8,128)} %get-tuple-element.132.refs_1_.refs_6_, ...), custom_call_target="tpu_custom_call" | custom-call | tf_op jit(solution)/shard_map/decoder_middle/pallas_call | solution.py:464
  187.1 4.5 %collective-permute-done.19.refs_3_.refs_14_ = bf16[2048,512]{1,0:T(8,128)(2,1)} collective-permute-done((bf16[2048,512]{1,0:T(8,128)(2,1)}, bf16[2048,512]{1,0:T(8,128)(2,1)}, u32[]{:S(2)}, u32[]{:S(2)}) %collective-permute-start.19) | collective-permute-done | bytes 2097184 | tf_op jit(solution)/shard_map/ppermute | solution.py:1397
  191.8 21.6 %encoder_back.1 = (f32[1024,512]{1,0:T(8,128)}, f32[3,512]{1,0:T(4,128)}, bf16[160,64,512]{2,1,0:T(8,128)(2,1)}, bf16[6,64,512]{2,1,0:T(8,128)(2,1)}, bf16[4,64,...) custom-call(s32[7]{0:T(128)} %stack.24.refs_0_, s32[112]{0:T(128)} %select_select_fusion.refs_1_, ...), custom_call_target="tpu_custom_call" | custom-call | tf_op jit(solution)/shard_map/encoder_back/pallas_call | solution.py:464
  213.4 35.0 %self_back.1 = (f32[1024,512]{1,0:T(8,128)}, f32[3,512]{1,0:T(4,128)}, bf16[160,64,512]{2,1,0:T(8,128)(2,1)}, bf16[6,64,512]{2,1,0:T(8,128)(2,1)}, bf16[4,64,512...) custom-call(s32[7]{0:T(128)} %stack.24.refs_0_, ...), custom_call_target="tpu_custom_call", output_to_operand_aliasing={{2}: (15, {}), {3}: (16, {}), {4}: (17, {}), {5}: (18, {})} | custom-call | tf_op jit(solution)/shard_map/self_back/pallas_call | solution.py:464
  252.9 1.9 slice_bitcast_fusion.4
  259.5 1.9 collective-permute-done.21
  261.3 2.8 collective-permute-done.22
  270.2 2.0 fusion.42
  274.5 5.6 %collective-permute-done.28 = f32[15,512]{1,0:T(8,128)S(1)} collective-permute-done((f32[15,512]{1,0:T(8,128)S(1)}, f32[15,512]{1,0:T(8,128)S(1)}, u32[]{:S(2)}, u32[]{:S(2)}) %collective-permute-start.28) | collective-permute-done | bytes 30752 | tf_op jit(solution)/shard_map/ppermute | solution.py:1062
  287.6 9.8 %collective-permute-done.31 = bf16[15,64,512]{2,1,0:T(8,128)(2,1)S(1)} collective-permute-done((bf16[15,64,512]{2,1,0:T(8,128)(2,1)S(1)}, bf16[15,64,512]{2,1,0:T(8,128)(2,1)S(1)}, u32[]{:S(2)}, u32[]{:S(2)}) %collective-permute-start.31) | collective-permute-done | bytes 983072 | tf_op jit(solution)/shard_map/ppermute | solution.py:1054
  297.4 4.8 %collective-permute-done.32 = f32[15,512]{1,0:T(8,128)S(1)} collective-permute-done((f32[15,512]{1,0:T(8,128)S(1)}, f32[15,512]{1,0:T(8,128)S(1)}, u32[]{:S(2)}, u32[]{:S(2)}) %collective-permute-start.32) | collective-permute-done | bytes 30752 | tf_op jit(solution)/shard_map/ppermute | solution.py:1062
  310.7 10.4 %collective-permute-done.36 = f32[15,512]{1,0:T(8,128)S(1)} collective-permute-done((f32[15,512]{1,0:T(8,128)S(1)}, f32[15,512]{1,0:T(8,128)S(1)}, u32[]{:S(2)}, u32[]{:S(2)}) %collective-permute-start.36) | collective-permute-done | bytes 30752 | tf_op jit(solution)/shard_map/ppermute | solution.py:1062
  321.3 2.6 fusion.8
  335.4 2.1 pad_maximum_fusion.5
  344.5 7.7 %adam_kept.1 = (f32[14,64,512]{2,1,0:T(8,128)}, f32[14,64,512]{2,1,0:T(8,128)}, f32[14,64,512]{2,1,0:T(8,128)}, bf16[14,64,512]{2,1,0:T(8,128)(2,1)}) custom-call(s32[7]{0:T(128)} %stack.24.refs_0_, s32[3,8]{1,0:T(4,128)} %get-tuple-element.117.plan.refs_1_, f32[10,64,512]{2,1,0:T(8,128)} %pad_maximum_fusion.refs_2_, f32[14,64,512]{2,1,0:T(8,128)} %bitcast.184, ...), custom_call_target="tpu_custom_call" | custom-call | tf_op jit(solution)/shard_map/adam_kept/pallas_call | solution.py:464
  354.1 3.2 collective-permute-done.41.refs_2_
  358.4 2.2 adam_lent.1
  (226 shorter events, 87.4 us)
Async XLA Ops:
  5.0 15.1 %collective-permute-start = (bf16[8,64,512]{2,1,0:T(8,128)(2,1)}, bf16[8,64,512]{2,1,0:T(8,128)(2,1)S(1)}, u32[]{:S(2)}, u32[]{:S(2)}) collective-permute-start(bf16[8,64,512]{2,1,0:T(8,128)(2,1)} %get-tuple-element.108), channel_id=1, source_target_pairs={{0,4},{4,8},{8,12},{12,14},{14,10},{10,6},{6,2},{2,0},{1,5},{5,9},... | collective-permute-start | bytes 1572872 | tf_op jit(solution)/shard_map/ppermute | solution.py:1050
  8.0 13.6 %collective-permute-start.1 = (bf16[8,64,512]{2,1,0:T(8,128)(2,1)}, bf16[8,64,512]{2,1,0:T(8,128)(2,1)S(1)}, u32[]{:S(2)}, u32[]{:S(2)}) collective-permute-start(bf16[8,64,512]{2,1,0:T(8,128)(2,1)} %get-tuple-element.109), channel_id=1, source_target_pairs={{0,2},{4,0},{8,4},{12,8},{14,12},{10,14},{6,10},{2,6},{1,3},{5,1},... | collective-permute-start | bytes 1572872 | tf_op jit(solution)/shard_map/ppermute | solution.py:1050
  25.0 10.1 %collective-permute-start.2 = (bf16[6,64,512]{2,1,0:T(8,128)(2,1)}, bf16[6,64,512]{2,1,0:T(8,128)(2,1)S(1)}, u32[]{:S(2)}, u32[]{:S(2)}) collective-permute-start(bf16[6,64,512]{2,1,0:T(8,128)(2,1)} %get-tuple-element.110.refs_4_), channel_id=1, source_target_pairs={{0,4},{4,8},{8,12},{12,14},{14,10},{10,6},{6,2},{2,0},{1,5},{5,9},... | collective-permute-start | bytes 1179656 | tf_op jit(solution)/shard_map/ppermute | solution.py:1050
  26.7 9.6 %collective-permute-start.3 = (bf16[6,64,512]{2,1,0:T(8,128)(2,1)}, bf16[6,64,512]{2,1,0:T(8,128)(2,1)S(1)}, u32[]{:S(2)}, u32[]{:S(2)}) collective-permute-start(bf16[6,64,512]{2,1,0:T(8,128)(2,1)} %get-tuple-element.110.refs_4_), channel_id=1, source_target_pairs={{0,2},{4,0},{8,4},{12,8},{14,12},{10,14},{6,10},{2,6},{1,3},{5,1},... | collective-permute-start | bytes 1179656 | tf_op jit(solution)/shard_map/ppermute | solution.py:1050
  38.7 23.9 %collective-permute-start.7 = (bf16[15,64,512]{2,1,0:T(8,128)(2,1)}, bf16[15,64,512]{2,1,0:T(8,128)(2,1)S(1)}, u32[]{:S(2)}, u32[]{:S(2)}) collective-permute-start(bf16[15,64,512]{2,1,0:T(8,128)(2,1)} %pad_maximum_fusion.6), channel_id=1, source_target_pairs={{0,1},{1,0},{2,3},{3,2},{4,5},{5,4},{6,7},{7,6},{8,9},{9,8},{10,11... | collective-permute-start | bytes 2949128 | tf_op jit(solution)/shard_map/ppermute | solution.py:1054
  41.6 19.7 %collective-permute-start.5 = (bf16[14,64,512]{2,1,0:T(8,128)(2,1)}, bf16[14,64,512]{2,1,0:T(8,128)(2,1)S(1)}, u32[]{:S(2)}, u32[]{:S(2)}) collective-permute-start(bf16[14,64,512]{2,1,0:T(8,128)(2,1)} %get-tuple-element.241), channel_id=1, source_target_pairs={{0,4},{4,8},{8,12},{12,14},{14,10},{10,6},{6,2},{2,0},{1,5},{5,9},... | collective-permute-start | bytes 2752520 | tf_op jit(solution)/shard_map/ppermute | solution.py:1050
  43.2 19.4 %collective-permute-start.6 = (bf16[14,64,512]{2,1,0:T(8,128)(2,1)}, bf16[14,64,512]{2,1,0:T(8,128)(2,1)S(1)}, u32[]{:S(2)}, u32[]{:S(2)}) collective-permute-start(bf16[14,64,512]{2,1,0:T(8,128)(2,1)} %get-tuple-element.240), channel_id=1, source_target_pairs={{0,2},{4,0},{8,4},{12,8},{14,12},{10,14},{6,10},{2,6},{1,3},{5,1},... | collective-permute-start | bytes 2752520 | tf_op jit(solution)/shard_map/ppermute | solution.py:1050
  63.9 21.5 %collective-permute-start.10 = (bf16[15,64,512]{2,1,0:T(8,128)(2,1)S(1)}, bf16[15,64,512]{2,1,0:T(8,128)(2,1)}, u32[]{:S(2)}, u32[]{:S(2)}) collective-permute-start(bf16[15,64,512]{2,1,0:T(8,128)(2,1)S(1)} %pad_maximum_fusion.7), channel_id=1, source_target_pairs={{0,1},{1,0},{2,3},{3,2},{4,5},{5,4},{6,7},{7,6},{8,9},{9,8},{10,11... | collective-permute-start | bytes 2949128 | tf_op jit(solution)/shard_map/ppermute | solution.py:1054
  64.4 18.0 %collective-permute-start.8 = (bf16[14,64,512]{2,1,0:T(8,128)(2,1)S(1)}, bf16[14,64,512]{2,1,0:T(8,128)(2,1)S(1)}, u32[]{:S(2)}, u32[]{:S(2)}) collective-permute-start(bf16[14,64,512]{2,1,0:T(8,128)(2,1)S(1)} %collective-permute-done.5.refs_10_), channel_id=1, source_target_pairs={{0,4},{4,8},{8,12},{12,14},{14,10},{10,6},{6,2},{2,0},{1,5},{5,9},... | collective-permute-start | bytes 2752520 | tf_op jit(solution)/shard_map/ppermute | solution.py:1050
  65.7 17.7 %collective-permute-start.9 = (bf16[14,64,512]{2,1,0:T(8,128)(2,1)}, bf16[14,64,512]{2,1,0:T(8,128)(2,1)S(1)}, u32[]{:S(2)}, u32[]{:S(2)}) collective-permute-start(bf16[14,64,512]{2,1,0:T(8,128)(2,1)} %copy-done.8), channel_id=1, source_target_pairs={{0,2},{4,0},{8,4},{12,8},{14,12},{10,14},{6,10},{2,6},{1,3},{5,1},... | collective-permute-start | bytes 2752520 | tf_op jit(solution)/shard_map/ppermute | solution.py:1050
  85.7 17.6 %collective-permute-start.13 = (bf16[12,64,512]{2,1,0:T(8,128)(2,1)S(1)}, bf16[12,64,512]{2,1,0:T(8,128)(2,1)}, u32[]{:S(2)}, u32[]{:S(2)}) collective-permute-start(bf16[12,64,512]{2,1,0:T(8,128)(2,1)S(1)} %pad_maximum_fusion.14), channel_id=1, source_target_pairs={{0,1},{1,0},{2,3},{3,2},{4,5},{5,4},{6,7},{7,6},{8,9},{9,8},{10,11... | collective-permute-start | bytes 2359304 | tf_op jit(solution)/shard_map/ppermute | solution.py:1054
  86.1 12.4 %collective-permute-start.11 = (bf16[11,64,512]{2,1,0:T(8,128)(2,1)S(1)}, bf16[11,64,512]{2,1,0:T(8,128)(2,1)S(1)}, u32[]{:S(2)}, u32[]{:S(2)}) collective-permute-start(bf16[11,64,512]{2,1,0:T(8,128)(2,1)S(1)} %pad_maximum_fusion.16), channel_id=1, source_target_pairs={{0,4},{4,8},{8,12},{12,14},{14,10},{10,6},{6,2},{2,0},{1,5},{5,9},... | collective-permute-start | bytes 2162696 | tf_op jit(solution)/shard_map/ppermute | solution.py:1050
  87.8 12.6 %collective-permute-start.12 = (bf16[11,64,512]{2,1,0:T(8,128)(2,1)S(1)}, bf16[11,64,512]{2,1,0:T(8,128)(2,1)S(1)}, u32[]{:S(2)}, u32[]{:S(2)}) collective-permute-start(bf16[11,64,512]{2,1,0:T(8,128)(2,1)S(1)} %slice.249), channel_id=1, source_target_pairs={{0,2},{4,0},{8,4},{12,8},{14,12},{10,14},{6,10},{2,6},{1,3},{5,1},... | collective-permute-start | bytes 2162696 | tf_op jit(solution)/shard_map/ppermute | solution.py:1050
  134.8 17.7 %collective-permute-start.18 = (bf16[5120,512]{1,0:T(8,128)(2,1)}, bf16[5120,512]{1,0:T(8,128)(2,1)}, u32[]{:S(2)}, u32[]{:S(2)}) collective-permute-start(bf16[5120,512]{1,0:T(8,128)(2,1)} %get-tuple-element.133.refs_2_.refs_3_.refs_4_.refs_6_.refs_9_.refs_11_.refs_5_.refs_10_), channel_id=1, source_target_pairs={{0,16},{16,0},{1,17},{17,1},{2,18},{18,2},{3,19},{19,3},{4,20},{20... | collective-permute-start | bytes 15728648 | tf_op jit(solution)/shard_map/ppermute | solution.py:1341
  191.6 58.9 %collective-permute-start.20 = (bf16[5120,512]{1,0:T(8,128)(2,1)}, bf16[5120,512]{1,0:T(8,128)(2,1)}, u32[]{:S(2)}, u32[]{:S(2)}) collective-permute-start(bf16[5120,512]{1,0:T(8,128)(2,1)} %get-tuple-element.162.refs_2_), channel_id=1, source_target_pairs={{0,16},{16,0},{1,17},{17,1},{2,18},{18,2},{3,19},{19,3},{4,20},{20... | collective-permute-start | bytes 15728648 | tf_op jit(solution)/shard_map/ppermute | solution.py:1399
  249.2 10.3 %collective-permute-start.24 = (f32[15,512]{1,0:T(8,128)S(1)}, f32[15,512]{1,0:T(8,128)S(1)}, u32[]{:S(2)}, u32[]{:S(2)}) collective-permute-start(f32[15,512]{1,0:T(8,128)S(1)} %pad_maximum_fusion.20), channel_id=1, source_target_pairs={{0,1},{1,0},{2,3},{3,2},{4,5},{5,4},{6,7},{7,6},{8,9},{9,8},{10,11... | collective-permute-start | bytes 92168 | tf_op jit(solution)/shard_map/ppermute | solution.py:1062
  252.2 12.3 %collective-permute-start.23 = (bf16[6,64,512]{2,1,0:T(8,128)(2,1)}, bf16[6,64,512]{2,1,0:T(8,128)(2,1)S(1)}, u32[]{:S(2)}, u32[]{:S(2)}) collective-permute-start(bf16[6,64,512]{2,1,0:T(8,128)(2,1)} %get-tuple-element.169), channel_id=1, source_target_pairs={{0,1},{1,0},{2,3},{3,2},{4,5},{5,4},{6,7},{7,6},{8,9},{9,8},{10,11... | collective-permute-start | bytes 1179656 | tf_op jit(solution)/shard_map/ppermute | solution.py:1054
  258.1 23.3 %collective-permute-start.27 = (bf16[12,64,512]{2,1,0:T(8,128)(2,1)S(1)}, bf16[12,64,512]{2,1,0:T(8,128)(2,1)S(1)}, u32[]{:S(2)}, u32[]{:S(2)}) collective-permute-start(bf16[12,64,512]{2,1,0:T(8,128)(2,1)S(1)} %pad_maximum_fusion.15), channel_id=1, source_target_pairs={{0,1},{1,0},{2,3},{3,2},{4,5},{5,4},{6,7},{7,6},{8,9},{9,8},{10,11... | collective-permute-start | bytes 2359304 | tf_op jit(solution)/shard_map/ppermute | solution.py:1054
  266.9 14.5 %collective-permute-start.26 = (bf16[11,64,512]{2,1,0:T(8,128)(2,1)S(1)}, bf16[11,64,512]{2,1,0:T(8,128)(2,1)S(1)}, u32[]{:S(2)}, u32[]{:S(2)}) collective-permute-start(bf16[11,64,512]{2,1,0:T(8,128)(2,1)S(1)} %pad_maximum_fusion.18), channel_id=1, source_target_pairs={{0,2},{4,0},{8,4},{12,8},{14,12},{10,14},{6,10},{2,6},{1,3},{5,1},... | collective-permute-start | bytes 2162696 | tf_op jit(solution)/shard_map/ppermute | solution.py:1050
  268.4 13.0 %collective-permute-start.25 = (bf16[11,64,512]{2,1,0:T(8,128)(2,1)S(1)}, bf16[11,64,512]{2,1,0:T(8,128)(2,1)S(1)}, u32[]{:S(2)}, u32[]{:S(2)}) collective-permute-start(bf16[11,64,512]{2,1,0:T(8,128)(2,1)S(1)} %pad_maximum_fusion.17), channel_id=1, source_target_pairs={{0,4},{4,8},{8,12},{12,14},{14,10},{10,6},{6,2},{2,0},{1,5},{5,9},... | collective-permute-start | bytes 2162696 | tf_op jit(solution)/shard_map/ppermute | solution.py:1050
  273.7 23.7 %collective-permute-start.31 = (bf16[15,64,512]{2,1,0:T(8,128)(2,1)S(1)}, bf16[15,64,512]{2,1,0:T(8,128)(2,1)S(1)}, u32[]{:S(2)}, u32[]{:S(2)}) collective-permute-start(bf16[15,64,512]{2,1,0:T(8,128)(2,1)S(1)} %pad_maximum_fusion.8), channel_id=1, source_target_pairs={{0,1},{1,0},{2,3},{3,2},{4,5},{5,4},{6,7},{7,6},{8,9},{9,8},{10,11... | collective-permute-start | bytes 2949128 | tf_op jit(solution)/shard_map/ppermute | solution.py:1054
  283.1 19.1 %collective-permute-start.30 = (bf16[14,64,512]{2,1,0:T(8,128)(2,1)S(1)}, bf16[14,64,512]{2,1,0:T(8,128)(2,1)S(1)}, u32[]{:S(2)}, u32[]{:S(2)}) collective-permute-start(bf16[14,64,512]{2,1,0:T(8,128)(2,1)S(1)} %pad_maximum_fusion.11), channel_id=1, source_target_pairs={{0,2},{4,0},{8,4},{12,8},{14,12},{10,14},{6,10},{2,6},{1,3},{5,1},... | collective-permute-start | bytes 2752520 | tf_op jit(solution)/shard_map/ppermute | solution.py:1050
  284.8 17.4 %collective-permute-start.29 = (bf16[14,64,512]{2,1,0:T(8,128)(2,1)S(1)}, bf16[14,64,512]{2,1,0:T(8,128)(2,1)S(1)}, u32[]{:S(2)}, u32[]{:S(2)}) collective-permute-start(bf16[14,64,512]{2,1,0:T(8,128)(2,1)S(1)} %pad_maximum_fusion.10), channel_id=1, source_target_pairs={{0,4},{4,8},{8,12},{12,14},{14,10},{10,6},{6,2},{2,0},{1,5},{5,9},... | collective-permute-start | bytes 2752520 | tf_op jit(solution)/shard_map/ppermute | solution.py:1050
  285.5 16.7 %collective-permute-start.32 = (f32[15,512]{1,0:T(8,128)S(1)}, f32[15,512]{1,0:T(8,128)S(1)}, u32[]{:S(2)}, u32[]{:S(2)}) collective-permute-start(f32[15,512]{1,0:T(8,128)S(1)} %add.475), channel_id=1, source_target_pairs={{0,4},{2,6},{4,0},{6,2},{8,12},{10,14},{12,8},{14,10},{1,5},{3,7},... | collective-permute-start | bytes 92168 | tf_op jit(solution)/shard_map/ppermute | solution.py:1062
  287.3 23.4 %collective-permute-start.35 = (bf16[15,64,512]{2,1,0:T(8,128)(2,1)S(1)}, bf16[15,64,512]{2,1,0:T(8,128)(2,1)S(1)}, u32[]{:S(2)}, u32[]{:S(2)}) collective-permute-start(bf16[15,64,512]{2,1,0:T(8,128)(2,1)S(1)} %pad_maximum_fusion.9), channel_id=1, source_target_pairs={{0,1},{1,0},{2,3},{3,2},{4,5},{5,4},{6,7},{7,6},{8,9},{9,8},{10,11... | collective-permute-start | bytes 2949128 | tf_op jit(solution)/shard_map/ppermute | solution.py:1054
  304.9 16.2 %collective-permute-start.34 = (bf16[14,64,512]{2,1,0:T(8,128)(2,1)}, bf16[14,64,512]{2,1,0:T(8,128)(2,1)}, u32[]{:S(2)}, u32[]{:S(2)}) collective-permute-start(bf16[14,64,512]{2,1,0:T(8,128)(2,1)} %pad_maximum_fusion.13), channel_id=1, source_target_pairs={{0,2},{4,0},{8,4},{12,8},{14,12},{10,14},{6,10},{2,6},{1,3},{5,1},... | collective-permute-start | bytes 2752520 | tf_op jit(solution)/shard_map/ppermute | solution.py:1050
  307.6 13.7 %collective-permute-start.33 = (bf16[14,64,512]{2,1,0:T(8,128)(2,1)}, bf16[14,64,512]{2,1,0:T(8,128)(2,1)}, u32[]{:S(2)}, u32[]{:S(2)}) collective-permute-start(bf16[14,64,512]{2,1,0:T(8,128)(2,1)} %pad_maximum_fusion.12), channel_id=1, source_target_pairs={{0,4},{4,8},{8,12},{12,14},{14,10},{10,6},{6,2},{2,0},{1,5},{5,9},... | collective-permute-start | bytes 2752520 | tf_op jit(solution)/shard_map/ppermute | solution.py:1050
  308.5 12.5 %collective-permute-start.36 = (f32[15,512]{1,0:T(8,128)S(1)}, f32[15,512]{1,0:T(8,128)S(1)}, u32[]{:S(2)}, u32[]{:S(2)}) collective-permute-start(f32[15,512]{1,0:T(8,128)S(1)} %add.484), channel_id=1, source_target_pairs={{0,8},{2,10},{4,12},{6,14},{8,0},{10,2},{12,4},{14,6},{1,9},{3,11}... | collective-permute-start | bytes 92168 | tf_op jit(solution)/shard_map/ppermute | solution.py:1062
  323.8 13.7 %collective-permute-start.37 = (bf16[6,64,512]{2,1,0:T(8,128)(2,1)}, bf16[6,64,512]{2,1,0:T(8,128)(2,1)}, u32[]{:S(2)}, u32[]{:S(2)}) collective-permute-start(bf16[6,64,512]{2,1,0:T(8,128)(2,1)} %get-tuple-element.214), channel_id=1, source_target_pairs={{0,4},{4,8},{8,12},{12,14},{14,10},{10,6},{6,2},{2,0},{1,5},{5,9},... | collective-permute-start | bytes 1179656 | tf_op jit(solution)/shard_map/ppermute | solution.py:1050
  325.0 12.6 %collective-permute-start.38 = (bf16[6,64,512]{2,1,0:T(8,128)(2,1)}, bf16[6,64,512]{2,1,0:T(8,128)(2,1)}, u32[]{:S(2)}, u32[]{:S(2)}) collective-permute-start(bf16[6,64,512]{2,1,0:T(8,128)(2,1)} %get-tuple-element.213), channel_id=1, source_target_pairs={{0,2},{4,0},{8,4},{12,8},{14,12},{10,14},{6,10},{2,6},{1,3},{5,1},... | collective-permute-start | bytes 1179656 | tf_op jit(solution)/shard_map/ppermute | solution.py:1050
  342.5 14.8 %collective-permute-start.41 = (bf16[8,64,512]{2,1,0:T(8,128)(2,1)}, bf16[8,64,512]{2,1,0:T(8,128)(2,1)S(1)}, u32[]{:S(2)}, u32[]{:S(2)}) collective-permute-start(bf16[8,64,512]{2,1,0:T(8,128)(2,1)} %get-tuple-element.239), channel_id=1, source_target_pairs={{0,4},{4,8},{8,12},{12,14},{14,10},{10,6},{6,2},{2,0},{1,5},{5,9},... | collective-permute-start | bytes 1572872 | tf_op jit(solution)/shard_map/ppermute | solution.py:1050
  343.7 14.6 %collective-permute-start.42 = (bf16[8,64,512]{2,1,0:T(8,128)(2,1)}, bf16[8,64,512]{2,1,0:T(8,128)(2,1)}, u32[]{:S(2)}, u32[]{:S(2)}) collective-permute-start(bf16[8,64,512]{2,1,0:T(8,128)(2,1)} %get-tuple-element.238), channel_id=1, source_target_pairs={{0,2},{4,0},{8,4},{12,8},{14,12},{10,14},{6,10},{2,6},{1,3},{5,1},... | collective-permute-start | bytes 1572872 | tf_op jit(solution)/shard_map/ppermute | solution.py:1050
  (41 other events, 387.0 us)
